TPU v7x, 32 devices: a whole 2x2x4 slice. The times are simulated.
32 devices in a mesh: tm: 4 (over y, x), rows: 8 (over z, core).
Axes of the slice: x: 2, y: 2, z: 4, core: 2. Of those that a mesh axis runs over, the one named last changes fastest.
Arguments:
- frames: bfloat16 [16, 64, 1280, 128], P('tm', 'rows'), may hold values from -30 to 30
- clip_ids: int32 [16], replicated, may hold values from 0 to 3, never falling along the last dimension, each value on 1 to 6 neighbouring positions
- conv_weight: bfloat16 [3, 3, 3, 128, 256], replicated, may hold values from -0.109375 to 0.109375
- norm_gain: float32 [256], replicated, may hold values from 0.1 to 1.9
- norm_bias: float32 [256], replicated, may hold values from -3 to 3
Outputs:
- latent: bfloat16 [16, 32, 640, 256], P('tm', None, 'rows')
Inputs may be any that keep to these rules, and one draw needn't show every extreme that they name: `clip_ids`: clip numbers never fall along the frames; each clip spans 1 to 6 frames, one exactly 6.
All inputs are finite; a program needn't handle non-finite values.
Results may differ from a plain program's by a relative error of at most 0.012.
Values may be sent and summed in bfloat16 or wider, within the bound.
No kernel may reach another device: no remote copies, remote signals or barrier semaphores. Data moves between devices by JAX's collectives and lax.ppermute only.
A program may use at most 192 MiB of HBM per device.

v0:
```python
import jax
import jax.numpy as jnp
from jax import lax
from jax.sharding import PartitionSpec as P

GROUPS = 32


def passed_along(array, axis, by):
    length = lax.axis_size(axis)
    pairs = [(i, i + by) for i in range(length) if 0 <= i + by < length]
    return lax.ppermute(array, axis, pairs)


def conv_tap(source, kernel):
    return lax.conv_general_dilated(
        source,
        kernel,
        (2, 2),
        ((0, 0), (1, 1)),
        dimension_numbers=("NHWC", "HWIO", "NHWC"),
        preferred_element_type=jnp.float32,
    )


def group_sums(block):
    values = block.astype(jnp.float32).reshape(
        block.shape[0], block.shape[1], block.shape[2], GROUPS, -1
    )
    return (jnp.sum(values, axis=(1, 2, 4)), jnp.sum(values * values, axis=(1, 2, 4)))


def finish(block, sum_first, sum_second, norm_gain, norm_bias):
    values = block.astype(jnp.float32).reshape(
        block.shape[0], block.shape[1], block.shape[2], GROUPS, -1
    )
    entries = block.shape[1] * block.shape[2] * values.shape[4] * lax.axis_size("rows")
    mean = sum_first / entries
    variance = sum_second / entries - mean * mean
    scaled = (values - mean[:, None, None, :, None]) * lax.rsqrt(variance + 1e-05)[
        :, None, None, :, None
    ]
    scaled = scaled.reshape(block.shape) * norm_gain + norm_bias
    return jax.nn.silu(scaled).astype(jnp.bfloat16)


def on_device(frames, clip_ids, conv_weight, norm_gain, norm_bias):
    frame_count = frames.shape[0]
    row_above = passed_along(frames[:, -1:], "rows", 1)
    extended = jnp.concatenate([row_above, frames], axis=1)
    stretch_start = lax.axis_index("tm") * frame_count
    sentinel = jnp.full((2,), -1, jnp.int32)
    padded = jnp.concatenate([sentinel, clip_ids, sentinel])
    window = lax.dynamic_slice_in_dim(padded, stretch_start, frame_count + 4)
    target = window[2 : frame_count + 2]
    running = jnp.zeros(
        (frame_count, frames.shape[1] // 2, frames.shape[2] // 2, conv_weight.shape[4]), jnp.float32
    )
    history_head = passed_along(extended[-2:], "tm", 1)
    history = jnp.concatenate([history_head, extended], axis=0)
    for tap_index in range(3):
        keep_mask = (window[tap_index : tap_index + frame_count] == target).astype(frames.dtype)
        running = running + conv_tap(
            history[tap_index : tap_index + frame_count] * keep_mask[:, None, None, None],
            conv_weight[tap_index],
        )
    conv = running.astype(jnp.bfloat16)
    sum_first, sum_second = lax.psum(group_sums(conv), "rows")
    banded = finish(conv, sum_first, sum_second, norm_gain, norm_bias)
    return lax.all_to_all(banded, "rows", split_axis=2, concat_axis=1, tiled=True)


def solution(mesh):
    in_specs = (P("tm", "rows", None, None), P(), P(), P(), P())
    out_specs = P("tm", None, "rows", None)
    return jax.shard_map(
        on_device, mesh=mesh, in_specs=in_specs, out_specs=out_specs, check_vma=False
    )
```

profile of v0, /device:TPU:4, one launch (start us, length us, event | category | flops | bytes accessed | tf_op | source)
XLA Modules:
  0.0 472.1 jit_solution(15300437874176355138)
XLA Ops:
  0.0 1.4 slice.31
  1.4 1.8 collective-permute-start
  3.2 2.6 collective-permute-done
  5.8 1.3 constant_dynamic-update-slice_fusion.1
  7.1 10.8 %constant_dynamic-update-slice_fusion = bf16[4,9,1280,128]{3,2,1,0:T(8,128)(2,1)} fusion(bf16[4,9,1280,128]{3,2,1,0:T(8,128)(2,1)} %constant_dynamic-update-slice_fusion.1, bf16[4,8,1280,128]{3,2,1,0:T(8,128)(2,1)} %param.5), kind=kLoop, calls=%fused_computation.40 | loop fusion | bytes 20971520 | tf_op jit(solution)/shard_map/concatenate | solution.py:50
  18.0 5.7 %slice.47 = bf16[2,9,1280,128]{3,2,1,0:T(8,128)(2,1)} slice(bf16[4,9,1280,128]{3,2,1,0:T(8,128)(2,1)} %constant_dynamic-update-slice_fusion), slice={[2:4], [0:9], [0:1280], [0:128]} | slice | bytes 11796480 | tf_op jit(solution)/shard_map/slice | solution.py:59
  23.6 3.6 collective-permute-start.1
  27.2 0.0 copy-done.3
  27.2 0.1 pad_add_fusion
  27.3 0.1 dynamic_slice.3
  27.4 0.1 compare_convert_fusion.1
  27.4 11.0 %pad.4 = bf16[9,4,1296,128]{3,2,0,1:T(8,128)(2,1)} pad(bf16[9,4,1280,128]{3,2,0,1:T(8,128)(2,1)} %bitcast.52, bf16[]{:T(256)} %constant.26), padding=0_0x0_0x1_15x0_0 | pad | bytes 23740418 | tf_op jit(solution)/shard_map/concatenate | solution.py:50
  38.4 15.4 %reshape.47 = bf16[9,4,8,162,128]{4,3,2,0,1:T(8,128)(2,1)} reshape(bf16[9,4,1296,128]{3,2,0,1:T(8,128)(2,1)} %pad.4) | data formatting | bytes 23887872 | tf_op jit(solution)/shard_map/conv_general_dilated | solution.py:16
  53.8 1.1 slice.52
  55.0 0.1 copy.88
  55.1 0.0 copy-start.2
  55.1 0.0 slice-start
  55.1 0.0 slice-start.1
  55.1 7.7 %fusion.5 = bf16[9,4,8,164,128]{4,3,2,1,0:T(8,128)(2,1)S(1)} fusion(bf16[9,4,7,2,128]{4,3,2,1,0:T(2,128)(2,1)S(1)} %copy.88, bf16[9,4,8,162,128]{4,3,2,0,1:T(8,128)(2,1)} %reshape.47), kind=kLoop, calls=%fused_computation.8 | loop fusion | flops 36274176 | bytes 24164352 | tf_op jit(solution)/shard_map/conv_general_dilated | solution.py:16
  62.9 0.0 copy-done.2
  62.9 0.0 slice-start.2
  62.9 12.1 %fusion.6 = f32[4,32,81,256]{3,1,2,0:T(8,128)} fusion(bf16[9,4,8,164,128]{4,3,2,1,0:T(8,128)(2,1)S(1)} %fusion.5, bf16[3,3,3,128,256]{4,3,2,1,0:T(8,128)(2,1)S(1)} %copy-done.2), kind=kOutput, calls=%fused_computation.9 | convolution fusion | flops 6115295232 | bytes 23592960 | tf_op jit(solution)/shard_map/conv_general_dilated | solution.py:16
  75.0 68.8 %collective-permute-done.1 = bf16[2,9,1280,128]{3,2,1,0:T(8,128)(2,1)} collective-permute-done((bf16[2,9,1280,128]{3,2,1,0:T(8,128)(2,1)}, bf16[2,9,1280,128]{3,2,1,0:T(8,128)(2,1)}, u32[]{:S(2)}, u32[]{:S(2)}) %collective-permute-start.1) | collective-permute-done | bytes 5898272 | tf_op jit(solution)/shard_map/ppermute | solution.py:12
  143.8 0.0 slice-done
  143.8 0.0 slice-done.1
  143.8 0.0 slice-done.2
  143.8 9.6 %fusion.17 = (bf16[9,4,1280,128]{3,2,0,1:T(8,128)(2,1)S(1)}, bf16[9,4,1280,128]{3,2,0,1:T(8,128)(2,1)}) fusion(bf16[2,9,1280,128]{3,2,1,0:T(8,128)(2,1)} %collective-permute-done.1, bf16[4,9,1280,128]{3,2,1,0:T(8,128)(2,1)S(1)} %bitcast.54, bf16[4]{0:T(256)(128)(2,1)S(1)} %get-tuple-element.11, bf16[4]{0:T(256)(128)(2,1)S(1)} %get-tuple-element.12), kind=kLoop, calls=%fused_computation.20 | loop fusion | flops 23592960 | bytes 41287696 | tf_op jit(solution)/shard_map/mul | solution.py:64
  153.4 6.1 %pad = bf16[9,4,1296,128]{3,2,0,1:T(8,128)(2,1)} pad(bf16[9,4,1280,128]{3,2,0,1:T(8,128)(2,1)S(1)} %get-tuple-element.7, bf16[]{:T(256)} %constant.26), padding=0_0x0_0x1_15x0_0 | pad | bytes 23740418 | tf_op jit(solution)/shard_map/mul | solution.py:64
  159.5 15.4 %reshape.45 = bf16[9,4,8,162,128]{4,3,2,0,1:T(8,128)(2,1)} reshape(bf16[9,4,1296,128]{3,2,0,1:T(8,128)(2,1)} %pad) | data formatting | bytes 23887872 | tf_op jit(solution)/shard_map/conv_general_dilated | solution.py:16
  174.9 1.1 slice.50
  176.1 0.1 copy.90
  176.2 11.1 %fusion.3 = bf16[9,4,8,164,128]{4,3,2,1,0:T(8,128)(2,1)} fusion(bf16[9,4,7,2,128]{4,3,2,1,0:T(2,128)(2,1)S(1)} %copy.90, bf16[9,4,8,162,128]{4,3,2,0,1:T(8,128)(2,1)} %reshape.45), kind=kLoop, calls=%fused_computation.6 | loop fusion | flops 36274176 | bytes 24164352 | tf_op jit(solution)/shard_map/conv_general_dilated | solution.py:16
  187.2 11.0 %pad.2 = bf16[9,4,1296,128]{3,2,0,1:T(8,128)(2,1)} pad(bf16[9,4,1280,128]{3,2,0,1:T(8,128)(2,1)} %get-tuple-element.8, bf16[]{:T(256)} %constant.26), padding=0_0x0_0x1_15x0_0 | pad | bytes 23740418 | tf_op jit(solution)/shard_map/mul | solution.py:64
  198.2 15.5 %reshape.46 = bf16[9,4,8,162,128]{4,3,2,0,1:T(8,128)(2,1)} reshape(bf16[9,4,1296,128]{3,2,0,1:T(8,128)(2,1)} %pad.2) | data formatting | bytes 23887872 | tf_op jit(solution)/shard_map/conv_general_dilated | solution.py:16
  213.7 1.1 slice.51
  214.8 0.1 copy.89
  214.9 6.2 %fusion.4 = bf16[9,4,8,164,128]{4,3,2,1,0:T(8,128)(2,1)S(1)} fusion(bf16[9,4,7,2,128]{4,3,2,1,0:T(2,128)(2,1)S(1)} %copy.89, bf16[9,4,8,162,128]{4,3,2,0,1:T(8,128)(2,1)} %reshape.46), kind=kLoop, calls=%fused_computation.7 | loop fusion | flops 36274176 | bytes 24164352 | tf_op jit(solution)/shard_map/conv_general_dilated | solution.py:16
  221.2 0.0 copy-start.4
  221.2 12.0 %fusion.8 = f32[4,32,81,256]{3,1,2,0:T(8,128)} fusion(bf16[9,4,8,164,128]{4,3,2,1,0:T(8,128)(2,1)S(1)} %fusion.4, bf16[3,3,3,128,256]{4,3,2,1,0:T(8,128)(2,1)S(1)} %copy-done.2), kind=kOutput, calls=%fused_computation.11 | convolution fusion | flops 6115295232 | bytes 23592960 | tf_op jit(solution)/shard_map/conv_general_dilated | solution.py:16
  233.2 19.6 %fusion.31 = (f32[4,32,81,256]{3,1,2,0:T(8,128)}, f32[4,32,81,256]{3,1,2,0:T(8,128)}) fusion(f32[4,32,81,256]{3,1,2,0:T(8,128)} %fusion.6, f32[4,32,81,256]{3,1,2,0:T(8,128)} %fusion.8, bf16[3,3,3,128,256]{4,3,2,1,0:T(8,128)(2,1)S(1)} %copy-done.2, bf16[9,4,8,164,128]{4,3,2,1,0:T(8,128)(2,1)} %fusion.3, pred[32,81]{0,1:T(8,128)(4,1)S(1)} %copy-done.4), kind=kOutput, calls=%fused_computation.47 | convolution fusion | flops 6136528896 | bytes 55159808 | tf_op jit(solution)/shard_map/conv_general_dilated | solution.py:16
  252.8 12.6 %copy.43 = f32[4,32,81,256]{3,0,2,1:T(4,128)S(1)} copy(f32[4,32,81,256]{3,1,2,0:T(8,128)} %get-tuple-element.14) | data formatting | bytes 21233664 | tf_op jit(solution)/shard_map/convert_element_type | solution.py:34
  265.4 1.0 slice_reduce_fusion.1
  266.4 0.1 reduce_sum.24
  266.5 12.6 %copy.45 = f32[4,32,81,256]{3,0,2,1:T(4,128)S(1)} copy(f32[4,32,81,256]{3,1,2,0:T(8,128)} %get-tuple-element.13) | data formatting | bytes 21233664 | tf_op jit(solution)/shard_map/mul | solution.py:30
  279.1 1.0 slice_reduce_fusion
  280.1 0.0 copy-start
  280.1 0.0 copy-start.1
  280.1 0.1 reduce_sum.36
  280.2 0.1 reduce_sum.25
  280.3 0.1 reduce_sum.37
  280.4 37.3 %all-reduce = (f32[4,32]{1,0:T(4,128)S(1)}, f32[4,32]{1,0:T(4,128)S(1)}) all-reduce(f32[4,32]{1,0:T(4,128)S(1)} %reduce_sum.37, f32[4,32]{1,0:T(4,128)S(1)} %reduce_sum.25), channel_id=1, replica_groups=mesh['tm'=4,'rows'=8] {'rows'}, use_global_device_ids=true, to_apply=%region_5.6 | all-reduce | flops 256 | bytes 2048 | tf_op jit(solution)/shard_map/psum | solution.py:68
  317.6 0.1 sub.16
  317.7 0.1 sub.17
  317.8 0.1 mul.62
  317.9 0.1 mul.63
  318.0 1.4 broadcast.34
  319.4 5.4 %broadcast.35 = f32[4,4,648,256]{3,0,2,1:T(4,128)} broadcast(f32[4,256]{1,0:T(4,128)S(1)} %mul.63), dimensions={1,3} | broadcast | bytes 10620928 | tf_op jit(solution)/shard_map/mul | solution.py:40
  324.8 12.8 %multiply_convert_fusion = bf16[4,32,81,256]{3,1,2,0:T(8,128)(2,1)} fusion(f32[4,32,81,256]{3,0,2,1:T(4,128)} %bitcast.56, f32[4,32,81,256]{3,1,2,0:T(8,128)} %get-tuple-element.14, f32[4,32,81,256]{3,0,2,1:T(4,128)S(1)} %bitcast.55, f32[256]{0:T(256)S(1)} %copy-done, f32[256]{0:T(256)S(1)} %copy-done.1), kind=kLoop, calls=%fused_computation.28 | loop fusion | flops 23887872 | bytes 37160960 | tf_op jit(solution)/shard_map/convert_element_type | solution.py:44
  337.6 6.6 %copy.47 = bf16[4,32,81,256]{3,0,2,1:T(4,128)(2,1)S(1)} copy(bf16[4,32,81,256]{3,1,2,0:T(8,128)(2,1)} %multiply_convert_fusion) | data formatting | bytes 10616832 | tf_op jit(solution)/shard_map/convert_element_type | solution.py:44
  344.2 1.8 slice_bitcast_fusion
  346.0 1.8 copy.48
  347.8 119.1 %all_to_all.18 = bf16[4,4,640,256]{3,1,0,2:T(4,128)(2,1)S(1)} all-to-all(bf16[4,4,640,256]{3,1,0,2:T(4,128)(2,1)S(1)} %copy.48), channel_id=1, replica_groups=mesh['tm'=4,'rows'=8] {'rows'}, dimensions={2} | all-to-all | bytes 10485760 | tf_op jit(solution)/shard_map/all_to_all | solution.py:70
  466.9 2.0 copy.49
  468.8 3.1 copy.50
  (7 shorter events, 0.0 us)
Async XLA Ops:
  1.4 4.4 collective-permute-start
  7.1 20.1 %copy-start.3 = (s32[16]{0:T(128)S(1)}, s32[16]{0:T(128)}, u32[]{:S(2)}) copy-start(s32[16]{0:T(128)} %param.6) | copy-start | bytes 196
  23.6 120.2 %collective-permute-start.1 = (bf16[2,9,1280,128]{3,2,1,0:T(8,128)(2,1)}, bf16[2,9,1280,128]{3,2,1,0:T(8,128)(2,1)}, u32[]{:S(2)}, u32[]{:S(2)}) collective-permute-start(bf16[2,9,1280,128]{3,2,1,0:T(8,128)(2,1)} %slice.47), channel_id=1, source_target_pairs={{0,8},{8,16},{16,24},{1,9},{9,17},{17,25},{2,10},{10,18},{18,26},{... | collective-permute-start | bytes 17694728 | tf_op jit(solution)/shard_map/ppermute | solution.py:12
  55.1 7.8 %copy-start.2 = (bf16[3,3,3,128,256]{4,3,2,1,0:T(8,128)(2,1)S(1)}, bf16[3,3,3,128,256]{4,3,2,1,0:T(8,128)(2,1)}, u32[]{:S(2)}) copy-start(bf16[3,3,3,128,256]{4,3,2,1,0:T(8,128)(2,1)} %param.7) | copy-start | bytes 5308420
  55.1 88.7 %slice-start = ((s8[11796480]{0:T(1024)(128)(4,1)}), s8[4194304]{0:T(1024)(128)(4,1)S(1)}, s32[]{:S(2)}) async-start(s8[11796480]{0:T(1024)(128)(4,1)} %bitcast.53), calls=%async_computation.1 | async-start | bytes 8388608
  55.1 88.7 %slice-start.1 = ((s8[11796480]{0:T(1024)(128)(4,1)}), s8[4194304]{0:T(1024)(128)(4,1)S(1)}, s32[]{:S(2)}) async-start(s8[11796480]{0:T(1024)(128)(4,1)} %bitcast.53), calls=%async_computation.2 | async-start | bytes 8388608
  62.9 80.9 %slice-start.2 = ((s8[11796480]{0:T(1024)(128)(4,1)}), s8[3407872]{0:T(1024)(128)(4,1)S(1)}, s32[]{:S(2)}) async-start(s8[11796480]{0:T(1024)(128)(4,1)} %bitcast.53), calls=%async_computation.3 | async-start | bytes 6815744
  221.2 12.0 %copy-start.4 = (pred[32,81]{0,1:T(8,128)(4,1)S(1)}, pred[32,81]{0,1:T(8,128)(4,1)}, u32[]{:S(2)}) copy-start(pred[32,81]{0,1:T(8,128)(4,1)} %constant.38) | copy-start | bytes 7780
  280.1 44.7 %copy-start = (f32[256]{0:T(256)S(1)}, f32[256]{0:T(256)}, u32[]{:S(2)}) copy-start(f32[256]{0:T(256)} %param.9) | copy-start | bytes 3076
  280.1 44.7 %copy-start.1 = (f32[256]{0:T(256)S(1)}, f32[256]{0:T(256)}, u32[]{:S(2)}) copy-start(f32[256]{0:T(256)} %param.8) | copy-start | bytes 3076
where the time goes:
time: 477 us; the launch traced here: 472 us
  blocking collectives  156 us (33%)
  local copies, waits for them, and re-layouts  145 us (30%)
  waiting for transfers between devices  71.3 us (15%)
  other arithmetic  49.7 us (10%)
  matrix products  43.8 us (9%)
  starting transfers between devices  5.39 us (1%)
    all_to_all x1, blocking collectives, on_device(): lax.all_to_all(banded, 'rows', split_axis=2, concat_axis=1, tiled=True)  119 us
    ppermute x2, waiting for transfers between devices, passed_along(): return lax.ppermute(array, axis, pairs)  71.3 us
    conv_general_dilated x6, local copies, waits for them, and re-layouts, conv_tap(): lax.conv_general_dilated(source, kernel, (2, 2), ((0, 0), (1, 1)), dimens...  49.7 us
    conv_general_dilated x3, matrix products, conv_tap(): lax.conv_general_dilated(source, kernel, (2, 2), ((0, 0), (1, 1)), dimens...  43.8 us
    psum x1, blocking collectives, on_device(): sum_first, sum_second = lax.psum(group_sums(conv), 'rows')  37.3 us
    conv_general_dilated x3, other arithmetic, conv_tap(): lax.conv_general_dilated(source, kernel, (2, 2), ((0, 0), (1, 1)), dimens...  25 us
    concatenate x2, local copies, waits for them, and re-layouts, on_device(): extended = jnp.concatenate([row_above, frames], axis=1)  21.8 us
    mul x2, local copies, waits for them, and re-layouts, on_device(): history[tap_index:tap_index + frame_count] * keep_mask[:, None, None, None]  17.1 us
  transfers between devices with their start and end apart: 2, of which 2 were waited for; matrix products, arithmetic and copies ran while one was open for 10% of the time, Pallas kernels for 0%

commit v1 on v0

v1 whole, which is shorter than its diff:
```python
import functools

import jax
import jax.numpy as jnp
from jax import lax
from jax.experimental import pallas as pl
from jax.experimental.pallas import tpu as pltpu
from jax.sharding import PartitionSpec as P

GROUPS = 32
EPS = 1e-05
VMEM_BYTES = 40 * 1024 * 1024


def passed_along(array, axis, by):
    length = lax.axis_size(axis)
    pairs = [(i, i + by) for i in range(length) if 0 <= i + by < length]
    return lax.ppermute(array, axis, pairs)


def exchanged(array, axis, flip):
    length = lax.axis_size(axis)
    return lax.ppermute(array, axis, [(i, i ^ flip) for i in range(length)])


def after(array, *earlier):
    return lax.optimization_barrier((array, *earlier))[0]


def rounded_up(rows):
    return -(-rows // 16) * 16


def split_columns(row_ref, slab_ref):
    width, ci = row_ref.shape
    half = width // 2
    slab_ref[:, ci : 2 * ci] = row_ref[pl.ds(0, half, stride=2), :]
    slab_ref[:, 2 * ci :] = row_ref[pl.ds(1, half, stride=2), :]
    slab_ref[16:, 0:ci] = row_ref[pl.ds(31, half - 16, stride=2), :]
    head = row_ref[pl.ds(1, 16, stride=2), :].astype(jnp.float32)
    zero = jnp.zeros((1, ci), jnp.float32)
    slab_ref[0:16, 0:ci] = jnp.concatenate([zero, head[:15]], axis=0).astype(jnp.bfloat16)


def split_three(total):
    high = total.astype(jnp.bfloat16).astype(jnp.float32)
    rest = total - high
    middle = rest.astype(jnp.bfloat16).astype(jnp.float32)
    return [high, middle, rest - middle]


def conv_kernel(plan, clip_ref, place_ref, x_ref, above_ref, w_ref, *refs):
    jobs, parts, part_rows, part_width = (
        plan["jobs"], plan["parts"], plan["part_rows"], plan["part_width"])
    lead, tail, steps = plan["lead"], plan["tail"], plan["steps"]

    def take(number):
        nonlocal refs
        some, refs = refs[:number], refs[number:]
        return some

    add_refs = take(plan["addends"])
    lead_refs = take(parts if lead else 0)
    sums_refs = take(plan["sums_in"])
    out_refs = take(parts if parts else len(jobs))
    sums_out = take(1 if plan["sums_out"] else 0)
    slab_ref, acc_ref, part_ref, stat_ref = refs
    step = pl.program_id(0)
    sources = x_ref.shape[0]
    half = slab_ref.shape[2]
    above = lax.rem(step + 1, 2)
    below = lax.rem(step, 2)
    start = place_ref[0]
    last = clip_ref.shape[0] - 1

    @pl.when(step == 0)
    def _():
        for source in range(sources):
            split_columns(above_ref.at[source, 0], slab_ref.at[source, 1])
        stat_ref[...] = jnp.zeros_like(stat_ref)
        for flip in range(parts if lead else 0):
            out_refs[flip][0:lead] = lead_refs[flip][...]

    for source in range(sources):
        split_columns(x_ref.at[source, 0], slab_ref.at[source, 2])
        split_columns(x_ref.at[source, 1], slab_ref.at[source, below])

    def product(source, tap):
        rows = jnp.concatenate(
            [slab_ref[source, above], slab_ref[source, 2], slab_ref[source, below]], axis=1)
        return jnp.dot(rows, w_ref[tap], preferred_element_type=jnp.float32)

    for at, (target, taps, addend) in enumerate(jobs):
        empty = addend is None
        if addend is not None:
            acc_ref[...] = add_refs[addend][0].astype(jnp.float32)
        for source, tap in taps:
            frame = plan["first"] + source
            if frame == target:
                value = product(source, tap)
                acc_ref[...] = value if empty else acc_ref[...] + value
                empty = False
                continue
            if empty:
                acc_ref[...] = jnp.zeros_like(acc_ref)
                empty = False
            same = clip_ref[start + frame] == clip_ref[jnp.minimum(start + target, last)]

            @pl.when(same)
            def _(source=source, tap=tap):
                acc_ref[...] += product(source, tap)

        if not parts:
            out_refs[at][0] = acc_ref[...].astype(jnp.bfloat16)
            continue
        rounded = acc_ref[...].astype(jnp.bfloat16).astype(jnp.float32)
        tiles = rounded.reshape(half // 8, 8, rounded.shape[1])
        stat_ref[2 * at] += jnp.sum(tiles, axis=0)
        stat_ref[2 * at + 1] += jnp.sum(tiles * tiles, axis=0)
        for part in range(parts):
            piece = rounded[part * part_width : (part + 1) * part_width]
            part_ref[part, 0:part_width] = piece.astype(jnp.bfloat16)
        mine = place_ref[1]
        for flip in range(parts):
            offset = pl.multiple_of(lead + (at * steps + step) * part_rows, 16)
            out_refs[flip][pl.ds(offset, part_rows)] = part_ref[mine ^ flip]

    if sums_out or tail:
        @pl.when(step == steps - 1)
        def _():
            if sums_out:
                sums_out[0][...] = stat_ref[...]
            if tail:
                sums = [sum(ref[at] for ref in sums_refs)
                        for at in range(sums_refs[0].shape[0] if sums_refs else 0)]
                sums += [stat_ref[at] for at in range(2 * len(jobs))]
                rows = []
                for total in sums:
                    rows += split_three(jnp.sum(total, axis=0, keepdims=True))
                blank = jnp.zeros((tail - len(rows), rows[0].shape[1]), jnp.float32)
                closing = jnp.concatenate(rows + [blank], axis=0).astype(jnp.bfloat16)
                body = lead + len(jobs) * steps * part_rows
                for flip in range(parts):
                    out_refs[flip][body : body + tail] = closing


def conv_frames(frames, halo, weight, clip_ids, place, first, sources, jobs, row=0, steps=None,
                addends=(), parts=0, leads=(), sums=(), sums_out=False, tail=0):
    _, band, width, ci = frames.shape
    co = weight.shape[2]
    half = width // 2
    steps = steps or band // 2
    part_width = half // parts if parts else half
    part_rows = rounded_up(part_width)
    lead = leads[0].shape[0] if leads else 0
    plan = dict(jobs=jobs, addends=len(addends), parts=parts, part_rows=part_rows, lead=lead,
                part_width=part_width, first=first, steps=steps, tail=tail,
                sums_in=len(sums), sums_out=sums_out)
    block = first // sources
    above = (frames, 2 * row - 1) if row else (halo, 0)
    in_specs = [
        pl.BlockSpec((sources, 2, width, ci), lambda i, *_: (block, row + i, 0, 0)),
        pl.BlockSpec((sources, 1, width, ci), lambda i, *_: (block, above[1], 0, 0)),
        pl.BlockSpec(weight.shape, lambda i, *_: (0, 0, 0)),
    ]
    in_specs += [pl.BlockSpec((1, None, half, co), lambda i, *_: (0, i, 0, 0)) for _ in addends]
    in_specs += [pl.BlockSpec(a.shape, lambda i, *_: (0, 0)) for a in leads]
    in_specs += [pl.BlockSpec(a.shape, lambda i, *_: (0, 0, 0)) for a in sums]
    if parts:
        message = (lead + len(jobs) * steps * part_rows + tail, co)
        out_shape = [jax.ShapeDtypeStruct(message, jnp.bfloat16) for _ in range(parts)]
        out_specs = [pl.BlockSpec(message, lambda i, *_: (0, 0)) for _ in range(parts)]
    else:
        out_shape = [jax.ShapeDtypeStruct((1, steps, half, co), jnp.bfloat16) for _ in jobs]
        out_specs = [pl.BlockSpec((1, None, half, co), lambda i, *_: (0, i, 0, 0)) for _ in jobs]
    if sums_out:
        shape = (2 * len(jobs), 8, co)
        out_shape.append(jax.ShapeDtypeStruct(shape, jnp.float32))
        out_specs.append(pl.BlockSpec(shape, lambda i, *_: (0, 0, 0)))
    products = sum(len(taps) for _, taps, _ in jobs)
    return pl.pallas_call(
        functools.partial(conv_kernel, plan),
        out_shape=out_shape,
        grid_spec=pltpu.PrefetchScalarGridSpec(
            num_scalar_prefetch=2,
            grid=(steps,),
            in_specs=in_specs,
            out_specs=out_specs,
            scratch_shapes=[
                pltpu.VMEM((sources, 3, half, 3 * ci), jnp.bfloat16),
                pltpu.VMEM((half, co), jnp.float32),
                pltpu.VMEM((max(parts, 1), part_rows, co), jnp.bfloat16),
                pltpu.VMEM((2 * len(jobs), 8, co), jnp.float32),
            ],
        ),
        cost_estimate=pl.CostEstimate(
            flops=2 * products * steps * half * 9 * ci * co,
            bytes_accessed=4 * sources * steps * width * ci + 2 * len(jobs) * steps * half * co,
            transcendentals=0,
        ),
        compiler_params=pltpu.CompilerParams(vmem_limit_bytes=VMEM_BYTES),
    )(clip_ids, place, frames, above[0], weight, *addends, *leads, *sums)


def norm_kernel(plan, place_ref, *refs):
    parts, jobs, entries, held = plan["parts"], plan["jobs"], plan["entries"], plan["held"]
    early_refs = refs[:parts] if plan["early"] else ()
    refs = refs[len(early_refs):]
    data_refs, tail_refs = refs[:parts], refs[parts : 2 * parts]
    gain_ref, bias_ref = refs[2 * parts : 2 * parts + 2]
    out_ref, scale_ref = refs[-2:]
    frame, row = pl.program_id(0), pl.program_id(1)
    part_width, co = out_ref.shape[-2:]

    @pl.when((frame == 0) & (row == 0))
    def _():
        total = tail_refs[0][...].astype(jnp.float32)
        for flip in range(1, parts):
            total = total + tail_refs[flip][...].astype(jnp.float32)
        size = co // GROUPS
        same = (lax.broadcasted_iota(jnp.int32, (co, co), 0) // size
                == lax.broadcasted_iota(jnp.int32, (co, co), 1) // size).astype(jnp.float32)
        grouped = jnp.dot(total, same, precision=lax.Precision.HIGHEST,
                          preferred_element_type=jnp.float32)
        for at in range(jobs):
            def taken(which):
                base = 6 * (held + at) + 3 * which
                return grouped[base : base + 1] + grouped[base + 1 : base + 2] + grouped[base + 2 : base + 3]
            mean = taken(0) / entries
            variance = taken(1) / entries - mean * mean
            scale_ref[at, 0:1] = mean
            scale_ref[at, 1:2] = lax.rsqrt(variance + EPS) * gain_ref[...]

    def write(sources):
        mean = scale_ref[frame, 0:1]
        scale = scale_ref[frame, 1:2]
        bias = bias_ref[...]
        mine = place_ref[1]
        for flip in range(parts):
            values = sources[flip][0:part_width].astype(jnp.float32)
            value = 0.5 * ((values - mean) * scale + bias)
            out_ref[0, mine ^ flip, 0] = (value + value * jnp.tanh(value)).astype(jnp.bfloat16)

    if early_refs:
        @pl.when(row == 0)
        def _():
            write(data_refs)

        @pl.when(row > 0)
        def _():
            write(early_refs)
    else:
        write(data_refs)


def norm_frames(messages, gain, bias, place, first, jobs, shape, held=0, lead=0, tail=16,
                early=(), base=None):
    frames, parts, steps, part_width, co = shape
    part_rows = rounded_up(part_width)
    group = co // GROUPS
    plan = dict(parts=parts, jobs=jobs, entries=float(parts * steps * part_width * parts * group),
                held=held, early=bool(early))
    ahead = lead // part_rows
    if early:
        at = lambda f, i, *_: (f, 0)
    else:
        at = lambda f, i, *_: (ahead + f * steps + i, 0)
    closing = messages[0].shape[0] // tail - 1
    in_specs = (
        [pl.BlockSpec((part_rows, co), lambda f, i, *_: (f * (steps - 1) + jnp.maximum(i - 1, 0), 0))
         for _ in early]
        + [pl.BlockSpec((part_rows, co), at) for _ in messages]
        + [pl.BlockSpec((tail, co), lambda f, i, *_: (closing, 0)) for _ in messages]
        + [pl.BlockSpec((1, co), lambda f, i, *_: (0, 0))] * 2
    )
    operands = [place, *early, *messages, *messages, gain, bias]
    aliases = {}
    if base is not None:
        in_specs.append(pl.BlockSpec(memory_space=pl.ANY))
        aliases = {len(operands): 0}
        operands.append(base)
    return pl.pallas_call(
        functools.partial(norm_kernel, plan),
        out_shape=jax.ShapeDtypeStruct(shape, jnp.bfloat16),
        grid_spec=pltpu.PrefetchScalarGridSpec(
            num_scalar_prefetch=1,
            grid=(jobs, steps),
            in_specs=in_specs,
            out_specs=pl.BlockSpec(
                (1, parts, 1, part_width, co), lambda f, i, *_: (first + f, 0, i, 0, 0)),
            scratch_shapes=[pltpu.VMEM((jobs, 8, co), jnp.float32)],
        ),
        input_output_aliases=aliases,
        cost_estimate=pl.CostEstimate(
            flops=8 * jobs * parts * steps * part_width * co,
            bytes_accessed=4 * jobs * parts * steps * part_width * co,
            transcendentals=jobs * parts * steps * part_width * co,
        ),
        compiler_params=pltpu.CompilerParams(vmem_limit_bytes=VMEM_BYTES),
    )(*operands)


def on_device(frames, clip_ids, conv_weight, norm_gain, norm_bias):
    count, band, width, ci = frames.shape
    co = conv_weight.shape[4]
    parts = lax.axis_size("rows")
    place = jnp.stack([lax.axis_index("tm") * count, lax.axis_index("rows")]).astype(jnp.int32)
    weight = conv_weight.reshape(3, 9 * ci, co)
    gain, bias = norm_gain.reshape(1, co), norm_bias.reshape(1, co)
    steps = band // 2
    shape = (count, parts, steps, width // 2 // parts, co)
    part_rows = rounded_up(shape[3])

    def named(name, function, *args, **keywords):
        with jax.named_scope(name):
            return function(*args, **keywords)

    halo = named("halo", passed_along, frames[:, -1:], "rows", 1)
    run = functools.partial(conv_frames, frames, halo, weight, clip_ids, place)
    far = [flip for flip in range(parts - 1, 0, -1) if 2 * flip >= parts]
    near = [flip for flip in range(parts - 1, 0, -1) if 2 * flip < parts]

    later = [(2, [(0, 0), (1, 1), (2, 2)], None), (3, [(1, 0), (2, 1), (3, 2)], None)]
    *a_sent, a_sums = named("conv_a", run, 0, 4, later, row=1, steps=steps - 1, parts=parts, sums_out=True)
    a_got = {flip: named(f"a{flip}", exchanged, a_sent[flip], "rows", flip) for flip in far}

    run = functools.partial(conv_frames, frames, after(halo, a_sums), weight, clip_ids, place)
    onward = named("conv_hist", run, 2, 2, [(4, [(0, 0), (1, 1)], None), (5, [(1, 0)], None)])
    first_add = named("hist0", passed_along, onward[0], "tm", 1)
    *top, top_sums = named("conv_top", run, 0, 4, later, row=0, steps=1, parts=parts, sums_out=True)
    second_add = named("hist1", passed_along, onward[1], "tm", 1)

    b_sent = named("conv_b", run, 0, 1, [(0, [(0, 2)], 0)], addends=(after(first_add, *[a_got[f] for f in far]),), parts=parts, leads=top,
                   sums=(a_sums, top_sums), tail=32)
    b_got = {flip: named(f"b{flip}", exchanged, b_sent[flip], "rows", flip) for flip in far}
    c_sent = named("conv_c", run, 0, 2, [(1, [(0, 1), (1, 2)], 0)], addends=(after(second_add, *[b_got[f] for f in far]),), parts=parts, tail=16)
    for flip in near:
        a_got[flip] = named(f"a{flip}", exchanged, a_sent[flip], "rows", flip)
        b_got[flip] = named(f"b{flip}", exchanged, b_sent[flip], "rows", flip)
    c_got = {flip: named(f"c{flip}", exchanged, c_sent[flip], "rows", flip) for flip in far + near}

    def whole(sent, got):
        return [sent[0]] + [got[flip] for flip in range(1, parts)]

    a_all, b_all, c_all = whole(a_sent, a_got), whole(b_sent, b_got), whole(c_sent, c_got)
    lead = 2 * part_rows
    out = named("norm_a", norm_frames, b_all, gain, bias, place, 2, 2, shape, tail=32, early=a_all)
    out = named("norm_b", norm_frames, b_all, gain, bias, place, 0, 1, shape, held=2, lead=lead, tail=32, base=out)
    out = named("norm_c", norm_frames, c_all, gain, bias, place, 1, 1, shape, tail=16, base=out)
    return out.reshape(count, parts * steps, shape[3], co)


def solution(mesh):
    in_specs = (P("tm", "rows", None, None), P(), P(), P(), P())
    out_specs = P("tm", None, "rows", None)
    return jax.shard_map(
        on_device, mesh=mesh, in_specs=in_specs, out_specs=out_specs, check_vma=False
    )
```

time: 477 us -> 192 us (0.40)
  the two profiles are of different devices: /device:TPU:4 before, /device:TPU:11 now
where the time goes in v1:
time: 192 us
  waiting for transfers between devices  93.3 us (49%)
  Pallas kernels  48.3 us (25%)
  starting transfers between devices  42.9 us (22%)
  local copies, waits for them, and re-layouts  7.35 us (4%)
    ppermute x21, waiting for transfers between devices, exchanged(): return lax.ppermute(array, axis, [(i, i ^ flip) for i in range(length)])  93.3 us
    pallas_call x5, Pallas kernels, conv_frames(): pl.pallas_call(functools.partial(conv_kernel, plan), out_shape=out_shape,...  37.8 us
    ppermute x21, starting transfers between devices, exchanged(): return lax.ppermute(array, axis, [(i, i ^ flip) for i in range(length)])  25 us
    ppermute x3, starting transfers between devices, passed_along(): return lax.ppermute(array, axis, pairs)  17.8 us
    pallas_call x3, Pallas kernels, norm_frames(): pl.pallas_call(functools.partial(norm_kernel, plan), out_shape=jax.ShapeD...  10.6 us
    unnamed x34, local copies, waits for them, and re-layouts  4.76 us
  transfers between devices with their start and end apart: 24, of which 12 were waited for; matrix products, arithmetic and copies ran while one was open for 0% of the time, Pallas kernels for 18%

profile of v1, /device:TPU:11, one launch (start us, length us, event | category | flops | bytes accessed | tf_op | source)
XLA Modules:
  0.0 192.1 jit_solution(5093091324824671485)
XLA Ops:
  0.0 2.6 %slice.3 = bf16[4,1,1280,128]{3,2,1,0:T(8,128)(2,1)} slice(bf16[4,8,1280,128]{3,2,1,0:T(8,128)(2,1)} %x_ref.9), slice={[0:4], [7:8], [0:1280], [0:128]} | slice | bytes 2621440 | tf_op jit(solution)/shard_map/slice | solution.py:318
  2.6 3.8 %collective-permute-start = (bf16[4,1,1280,128]{3,2,1,0:T(8,128)(2,1)}, bf16[4,1,1280,128]{3,2,1,0:T(8,128)(2,1)}, u32[]{:S(2)}, u32[]{:S(2)}) collective-permute-start(bf16[4,1,1280,128]{3,2,1,0:T(8,128)(2,1)} %slice.3), channel_id=1, source_target_pairs={{0,1},{1,2},{2,3},{3,4},{4,5},{5,6},{6,7},{8,9},{9,10},{10,11},{11... | collective-permute-start | bytes 3932168 | tf_op jit(solution)/shard_map/halo/ppermute | solution.py:18
  6.4 0.1 pad_add_fusion.place_ref
  6.4 0.0 copy-done.1
  6.4 4.0 %copy-done = bf16[4,8,1280,128]{3,2,1,0:T(8,128)(2,1)S(1)} copy-done((bf16[4,8,1280,128]{3,2,1,0:T(8,128)(2,1)S(1)}, bf16[4,8,1280,128]{3,2,1,0:T(8,128)(2,1)}, u32[]{:S(2)}) %copy-start) | copy-done | bytes 10485784
  10.4 10.2 %conv_a.1 = (bf16[480,256]{1,0:T(8,128)(2,1)S(1)}, bf16[480,256]{1,0:T(8,128)(2,1)S(1)}, bf16[480,256]{1,0:T(8,128)(2,1)S(1)}, bf16[480,256]{1,0:T(8,128)(2,1)S(...) custom-call(s32[16]{0:T(128)S(1)} %copy-done.6, ...), custom_call_target="tpu_custom_call" | custom-call | flops 6794772480 | bytes 9830400 | tf_op jit(solution)/shard_map/conv_a/pallas_call | solution.py:181
  20.6 0.7 copy-done.9
  21.3 0.0 collective-permute-done.above_ref
  21.4 0.0 slice-start.2
  21.4 0.0 copy-start.3
  21.4 10.3 %conv_hist.1 = (bf16[1,4,640,256]{3,2,1,0:T(8,128)(2,1)S(1)}, bf16[1,4,640,256]{3,2,1,0:T(8,128)(2,1)}) custom-call(s32[16]{0:T(128)S(1)} %copy-done.6, s32[2]{0:T(128)S(1)} %pad_add_fusion.place_ref, bf16[4,8,1280,128]{3,2,1,0:T(8,128)(2,1)} %x_ref.9, bf16[4,1,1280,128]{3,2,1,0:T(8,128)(2,1)} %collective-permute-done.above_ref, ...), custom_call_target="tpu_custom_call" | custom-call | flops 4529848320 | bytes 7864320 | tf_op jit(solution)/shard_map/conv_hist/pallas_call | solution.py:181
  31.7 0.0 copy-done.13
  31.7 5.5 %collective-permute-start.2 = (bf16[1,4,640,256]{3,2,1,0:T(8,128)(2,1)S(1)}, bf16[1,4,640,256]{3,2,1,0:T(8,128)(2,1)S(1)}, u32[]{:S(2)}, u32[]{:S(2)}) collective-permute-start(bf16[1,4,640,256]{3,2,1,0:T(8,128)(2,1)S(1)} %get-tuple-element.47), channel_id=1, source_target_pairs={{0,8},{8,16},{16,24},{1,9},{9,17},{17,25},{2,10},{10,18},{18,26},{... | collective-permute-start | bytes 3932168 | tf_op jit(solution)/shard_map/hist0/ppermute | solution.py:18
  37.3 8.5 %collective-permute-start.1 = (bf16[1,4,640,256]{3,2,1,0:T(8,128)(2,1)}, bf16[1,4,640,256]{3,2,1,0:T(8,128)(2,1)S(1)}, u32[]{:S(2)}, u32[]{:S(2)}) collective-permute-start(bf16[1,4,640,256]{3,2,1,0:T(8,128)(2,1)} %get-tuple-element.46), channel_id=1, source_target_pairs={{0,8},{8,16},{16,24},{1,9},{9,17},{17,25},{2,10},{10,18},{18,26},{... | collective-permute-start | bytes 3932168 | tf_op jit(solution)/shard_map/hist1/ppermute | solution.py:18
  45.8 0.6 collective-permute-start.3
  46.5 0.8 collective-permute-start.4
  47.3 2.3 %collective-permute-start.5 = (bf16[480,256]{1,0:T(8,128)(2,1)}, bf16[480,256]{1,0:T(8,128)(2,1)S(1)}, u32[]{:S(2)}, u32[]{:S(2)}) collective-permute-start(bf16[480,256]{1,0:T(8,128)(2,1)} %get-tuple-element.50), channel_id=1, source_target_pairs={{0,5},{1,4},{2,7},{3,6},{4,1},{5,0},{6,3},{7,2},{8,13},{9,12},{10,... | collective-permute-start | bytes 737288 | tf_op jit(solution)/shard_map/a5/ppermute | solution.py:23
  49.5 20.6 %collective-permute-done.3.refs_7_ = bf16[480,256]{1,0:T(8,128)(2,1)S(1)} collective-permute-done((bf16[480,256]{1,0:T(8,128)(2,1)S(1)}, bf16[480,256]{1,0:T(8,128)(2,1)S(1)}, u32[]{:S(2)}, u32[]{:S(2)}) %collective-permute-start.3) | collective-permute-done | bytes 245792 | tf_op jit(solution)/shard_map/a7/ppermute | solution.py:23
  70.2 0.0 collective-permute-start.6
  70.2 5.1 %conv_top.1 = (bf16[160,256]{1,0:T(8,128)(2,1)S(1)}, bf16[160,256]{1,0:T(8,128)(2,1)S(1)}, bf16[160,256]{1,0:T(8,128)(2,1)S(1)}, bf16[160,256]{1,0:T(8,128)(2,1)...) custom-call(s32[16]{0:T(128)S(1)} %copy-done.6, ...), custom_call_target="tpu_custom_call" | custom-call | flops 2264924160 | bytes 3276800 | tf_op jit(solution)/shard_map/conv_top/pallas_call | solution.py:181
  75.4 3.9 %collective-permute-done.4.refs_6_ = bf16[480,256]{1,0:T(8,128)(2,1)S(1)} collective-permute-done((bf16[480,256]{1,0:T(8,128)(2,1)}, bf16[480,256]{1,0:T(8,128)(2,1)S(1)}, u32[]{:S(2)}, u32[]{:S(2)}) %collective-permute-start.4) | collective-permute-done | bytes 245792 | tf_op jit(solution)/shard_map/a6/ppermute | solution.py:23
  79.3 3.7 %collective-permute-done.5.refs_5_ = bf16[480,256]{1,0:T(8,128)(2,1)S(1)} collective-permute-done((bf16[480,256]{1,0:T(8,128)(2,1)}, bf16[480,256]{1,0:T(8,128)(2,1)S(1)}, u32[]{:S(2)}, u32[]{:S(2)}) %collective-permute-start.5) | collective-permute-done | bytes 245792 | tf_op jit(solution)/shard_map/a5/ppermute | solution.py:23
  83.1 5.3 %collective-permute-done.6.refs_4_ = bf16[480,256]{1,0:T(8,128)(2,1)S(1)} collective-permute-done((bf16[480,256]{1,0:T(8,128)(2,1)}, bf16[480,256]{1,0:T(8,128)(2,1)S(1)}, u32[]{:S(2)}, u32[]{:S(2)}) %collective-permute-start.6) | collective-permute-done | bytes 245792 | tf_op jit(solution)/shard_map/a4/ppermute | solution.py:23
  88.3 0.0 collective-permute-done.2.refs_0_
  88.3 5.4 %conv_b.1 = (bf16[512,256]{1,0:T(8,128)(2,1)S(1)}, bf16[512,256]{1,0:T(8,128)(2,1)S(1)}, bf16[512,256]{1,0:T(8,128)(2,1)S(1)}, bf16[512,256]{1,0:T(8,128)(2,1)S(...) custom-call(s32[16]{0:T(128)S(1)} %copy-done.6, ...), custom_call_target="tpu_custom_call" | custom-call | flops 1509949440 | bytes 3932160 | tf_op jit(solution)/shard_map/conv_b/pallas_call | solution.py:181
  93.7 2.0 %collective-permute-start.7 = (bf16[512,256]{1,0:T(8,128)(2,1)S(1)}, bf16[512,256]{1,0:T(8,128)(2,1)S(1)}, u32[]{:S(2)}, u32[]{:S(2)}) collective-permute-start(bf16[512,256]{1,0:T(8,128)(2,1)S(1)} %get-tuple-element.62), channel_id=1, source_target_pairs={{0,7},{1,6},{2,5},{3,4},{4,3},{5,2},{6,1},{7,0},{8,15},{9,14},{10,... | collective-permute-start | bytes 786440 | tf_op jit(solution)/shard_map/b7/ppermute | solution.py:23
  95.7 0.7 collective-permute-start.8
  96.4 4.2 %collective-permute-start.9 = (bf16[512,256]{1,0:T(8,128)(2,1)S(1)}, bf16[512,256]{1,0:T(8,128)(2,1)S(1)}, u32[]{:S(2)}, u32[]{:S(2)}) collective-permute-start(bf16[512,256]{1,0:T(8,128)(2,1)S(1)} %get-tuple-element.64), channel_id=1, source_target_pairs={{0,5},{1,4},{2,7},{3,6},{4,1},{5,0},{6,3},{7,2},{8,13},{9,12},{10,... | collective-permute-start | bytes 786440 | tf_op jit(solution)/shard_map/b5/ppermute | solution.py:23
  100.6 0.6 collective-permute-start.10
  101.2 0.0 collective-permute-done.1.refs_0_
  101.2 0.4 collective-permute-start.21
  101.7 23.3 %collective-permute-done.7.refs_15_.refs_23_.refs_7_ = bf16[512,256]{1,0:T(8,128)(2,1)S(1)} collective-permute-done((bf16[512,256]{1,0:T(8,128)(2,1)S(1)}, bf16[512,256]{1,0:T(8,128)(2,1)S(1)}, u32[]{:S(2)}, u32[]{:S(2)}) %collective-permute-start.7) | collective-permute-done | bytes 262176 | tf_op jit(solution)/shard_map/b7/ppermute | solution.py:23
  125.0 0.0 collective-permute-start.22
  125.0 6.3 %collective-permute-done.8.refs_14_.refs_22_.refs_6_ = bf16[512,256]{1,0:T(8,128)(2,1)S(1)} collective-permute-done((bf16[512,256]{1,0:T(8,128)(2,1)S(1)}, bf16[512,256]{1,0:T(8,128)(2,1)S(1)}, u32[]{:S(2)}, u32[]{:S(2)}) %collective-permute-start.8) | collective-permute-done | bytes 262176 | tf_op jit(solution)/shard_map/b6/ppermute | solution.py:23
  131.3 0.0 collective-permute-start.23
  131.3 4.2 %collective-permute-done.9.refs_13_.refs_21_.refs_5_ = bf16[512,256]{1,0:T(8,128)(2,1)S(1)} collective-permute-done((bf16[512,256]{1,0:T(8,128)(2,1)S(1)}, bf16[512,256]{1,0:T(8,128)(2,1)S(1)}, u32[]{:S(2)}, u32[]{:S(2)}) %collective-permute-start.9) | collective-permute-done | bytes 262176 | tf_op jit(solution)/shard_map/b5/ppermute | solution.py:23
  135.5 0.0 collective-permute-start.18
  135.5 5.3 %collective-permute-done.10.refs_12_.refs_20_.refs_4_ = bf16[512,256]{1,0:T(8,128)(2,1)S(1)} collective-permute-done((bf16[512,256]{1,0:T(8,128)(2,1)S(1)}, bf16[512,256]{1,0:T(8,128)(2,1)S(1)}, u32[]{:S(2)}, u32[]{:S(2)}) %collective-permute-start.10) | collective-permute-done | bytes 262176 | tf_op jit(solution)/shard_map/b4/ppermute | solution.py:23
  140.8 2.4 %collective-permute-start.19 = (bf16[512,256]{1,0:T(8,128)(2,1)S(1)}, bf16[512,256]{1,0:T(8,128)(2,1)S(1)}, u32[]{:S(2)}, u32[]{:S(2)}) collective-permute-start(bf16[512,256]{1,0:T(8,128)(2,1)S(1)} %get-tuple-element.77), channel_id=1, source_target_pairs={{0,2},{1,3},{2,0},{3,1},{4,6},{5,7},{6,4},{7,5},{8,10},{9,11},{10,... | collective-permute-start | bytes 786440 | tf_op jit(solution)/shard_map/b2/ppermute | solution.py:23
  143.2 0.0 collective-permute-done.21.refs_1_
  143.2 0.3 collective-permute-start.20
  143.5 6.7 %conv_c.1 = (bf16[336,256]{1,0:T(8,128)(2,1)S(1)}, bf16[336,256]{1,0:T(8,128)(2,1)S(1)}, bf16[336,256]{1,0:T(8,128)(2,1)S(1)}, bf16[336,256]{1,0:T(8,128)(2,1)S(...) custom-call(s32[16]{0:T(128)S(1)} %copy-done.6, ...), custom_call_target="tpu_custom_call" | custom-call | flops 3019898880 | bytes 6553600 | tf_op jit(solution)/shard_map/conv_c/pallas_call | solution.py:181
  150.2 0.0 collective-permute-done.22.refs_2_
  150.2 0.4 collective-permute-start.11
  150.6 0.0 collective-permute-done.23.refs_3_
  150.6 1.4 collective-permute-start.12
  152.0 0.0 collective-permute-done.18.refs_9_.refs_17_.refs_1_
  152.0 0.4 collective-permute-start.13
  152.4 0.0 collective-permute-done.19.refs_10_.refs_18_.refs_2_
  152.4 2.4 %collective-permute-start.14 = (bf16[336,256]{1,0:T(8,128)(2,1)S(1)}, bf16[336,256]{1,0:T(8,128)(2,1)S(1)}, u32[]{:S(2)}, u32[]{:S(2)}) collective-permute-start(bf16[336,256]{1,0:T(8,128)(2,1)S(1)} %get-tuple-element.71), channel_id=1, source_target_pairs={{0,4},{1,5},{2,6},{3,7},{4,0},{5,1},{6,2},{7,3},{8,12},{9,13},{10,... | collective-permute-start | bytes 516104 | tf_op jit(solution)/shard_map/c4/ppermute | solution.py:23
  154.9 6.6 %collective-permute-done.20.refs_11_.refs_19_.refs_3_ = bf16[512,256]{1,0:T(8,128)(2,1)S(1)} collective-permute-done((bf16[512,256]{1,0:T(8,128)(2,1)S(1)}, bf16[512,256]{1,0:T(8,128)(2,1)S(1)}, u32[]{:S(2)}, u32[]{:S(2)}) %collective-permute-start.20) | collective-permute-done | bytes 262176 | tf_op jit(solution)/shard_map/b3/ppermute | solution.py:23
  161.5 3.0 %collective-permute-start.15 = (bf16[336,256]{1,0:T(8,128)(2,1)S(1)}, bf16[336,256]{1,0:T(8,128)(2,1)S(1)}, u32[]{:S(2)}, u32[]{:S(2)}) collective-permute-start(bf16[336,256]{1,0:T(8,128)(2,1)S(1)} %get-tuple-element.72), channel_id=1, source_target_pairs={{0,5},{1,4},{2,7},{3,6},{4,1},{5,0},{6,3},{7,2},{8,13},{9,12},{10,... | collective-permute-start | bytes 516104 | tf_op jit(solution)/shard_map/c5/ppermute | solution.py:23
  164.4 0.0 collective-permute-done.11.refs_1_.refs_9_
  164.5 0.7 collective-permute-start.16
  165.2 0.0 collective-permute-done.12.refs_2_.refs_10_
  165.2 2.4 %collective-permute-start.17 = (bf16[336,256]{1,0:T(8,128)(2,1)S(1)}, bf16[336,256]{1,0:T(8,128)(2,1)S(1)}, u32[]{:S(2)}, u32[]{:S(2)}) collective-permute-start(bf16[336,256]{1,0:T(8,128)(2,1)S(1)} %get-tuple-element.74), channel_id=1, source_target_pairs={{0,7},{1,6},{2,5},{3,4},{4,3},{5,2},{6,1},{7,0},{8,15},{9,14},{10,... | collective-permute-start | bytes 516104 | tf_op jit(solution)/shard_map/c7/ppermute | solution.py:23
  167.6 4.8 %norm_a.1.refs_18_ = bf16[4,8,4,80,256]{4,3,2,1,0:T(8,128)(2,1)} custom-call(s32[2]{0:T(128)S(1)} %pad_add_fusion.place_ref, bf16[480,256]{1,0:T(8,128)(2,1)S(1)} %get-tuple-element.79.refs_0_, bf16[480,256]{1,0:T(8,128)(2,1)S(1)} %collective-permute-done.21.refs_1_, bf16[480,256]{1,0:T(8,128)(2,1)S(1)} %collective-permute-done.22.refs_2_, ...), custom_call_target="tpu_custom_call" | custom-call | flops 10485760 | bytes 5242880 | tf_op jit(solution)/shard_map/norm_a/pallas_call | solution.py:282
  172.4 2.9 %norm_b.1.refs_18_ = bf16[4,8,4,80,256]{4,3,2,1,0:T(8,128)(2,1)} custom-call(s32[2]{0:T(128)S(1)} %pad_add_fusion.place_ref, bf16[512,256]{1,0:T(8,128)(2,1)S(1)} %get-tuple-element.75.refs_8_.refs_16_.refs_0_, bf16[512,256]{1,0:T(8,128)(2,1)S(1)} %collective-permute-done.18.refs_9_.refs_17_.refs_1_, ...), custom_call_target="tpu_custom_call", output_to_operand_aliasing={{}: (19, {})} | custom-call | flops 5242880 | bytes 2621440 | tf_op jit(solution)/shard_map/norm_b/pallas_call | solution.py:282
  175.2 0.0 collective-permute-done.13.refs_3_.refs_11_
  175.2 0.0 collective-permute-done.14.refs_4_.refs_12_
  175.2 5.1 %collective-permute-done.15.refs_5_.refs_13_ = bf16[336,256]{1,0:T(8,128)(2,1)S(1)} collective-permute-done((bf16[336,256]{1,0:T(8,128)(2,1)S(1)}, bf16[336,256]{1,0:T(8,128)(2,1)S(1)}, u32[]{:S(2)}, u32[]{:S(2)}) %collective-permute-start.15) | collective-permute-done | bytes 172064 | tf_op jit(solution)/shard_map/c5/ppermute | solution.py:23
  180.3 5.2 %collective-permute-done.16.refs_6_.refs_14_ = bf16[336,256]{1,0:T(8,128)(2,1)S(1)} collective-permute-done((bf16[336,256]{1,0:T(8,128)(2,1)S(1)}, bf16[336,256]{1,0:T(8,128)(2,1)S(1)}, u32[]{:S(2)}, u32[]{:S(2)}) %collective-permute-start.16) | collective-permute-done | bytes 172064 | tf_op jit(solution)/shard_map/c6/ppermute | solution.py:23
  185.5 3.7 %collective-permute-done.17.refs_7_.refs_15_ = bf16[336,256]{1,0:T(8,128)(2,1)S(1)} collective-permute-done((bf16[336,256]{1,0:T(8,128)(2,1)S(1)}, bf16[336,256]{1,0:T(8,128)(2,1)S(1)}, u32[]{:S(2)}, u32[]{:S(2)}) %collective-permute-start.17) | collective-permute-done | bytes 172064 | tf_op jit(solution)/shard_map/c7/ppermute | solution.py:23
  189.2 2.9 %norm_c.1 = bf16[4,8,4,80,256]{4,3,2,1,0:T(8,128)(2,1)} custom-call(s32[2]{0:T(128)S(1)} %pad_add_fusion.place_ref, bf16[336,256]{1,0:T(8,128)(2,1)S(1)} %get-tuple-element.67.refs_0_.refs_8_, bf16[336,256]{1,0:T(8,128)(2,1)S(1)} %collective-permute-done.11.refs_1_.refs_9_, ...), custom_call_target="tpu_custom_call", output_to_operand_aliasing={{}: (19, {})} | custom-call | flops 5242880 | bytes 2621440 | tf_op jit(solution)/shard_map/norm_c/pallas_call | solution.py:282
  (29 shorter events, 0.1 us)
Async XLA Ops:
  0.0 6.4 %copy-start.6 = (s32[16]{0:T(128)S(1)}, s32[16]{0:T(128)}, u32[]{:S(2)}) copy-start(s32[16]{0:T(128)} %clip_ref.9) | copy-start | bytes 196
  0.0 6.4 %copy-start.1 = (bf16[3,3,3,128,256]{4,3,2,1,0:T(8,128)(2,1)S(1)}, bf16[3,3,3,128,256]{4,3,2,1,0:T(8,128)(2,1)}, u32[]{:S(2)}) copy-start(bf16[3,3,3,128,256]{4,3,2,1,0:T(8,128)(2,1)} %param.7) | copy-start | bytes 5308420
  2.6 18.7 %collective-permute-start = (bf16[4,1,1280,128]{3,2,1,0:T(8,128)(2,1)}, bf16[4,1,1280,128]{3,2,1,0:T(8,128)(2,1)}, u32[]{:S(2)}, u32[]{:S(2)}) collective-permute-start(bf16[4,1,1280,128]{3,2,1,0:T(8,128)(2,1)} %slice.3), channel_id=1, source_target_pairs={{0,1},{1,2},{2,3},{3,4},{4,5},{5,6},{6,7},{8,9},{9,10},{10,11},{11... | collective-permute-start | bytes 3932168 | tf_op jit(solution)/shard_map/halo/ppermute | solution.py:18
  6.4 4.0 %copy-start = (bf16[4,8,1280,128]{3,2,1,0:T(8,128)(2,1)S(1)}, bf16[4,8,1280,128]{3,2,1,0:T(8,128)(2,1)}, u32[]{:S(2)}) copy-start(bf16[4,8,1280,128]{3,2,1,0:T(8,128)(2,1)} %x_ref.9) | copy-start | bytes 31457284
  10.4 10.9 %copy-start.2 = (bf16[3,3,3,128,256]{4,3,2,1,0:T(8,128)(2,1)S(1)}, bf16[3,3,3,128,256]{4,3,2,1,0:T(8,128)(2,1)}, u32[]{:S(2)}) copy-start(bf16[3,3,3,128,256]{4,3,2,1,0:T(8,128)(2,1)} %param.7) | copy-start | bytes 5308420
  10.4 59.8 %slice-start = ((s8[10485760]{0:T(1024)(128)(4,1)}), s8[4194304]{0:T(1024)(128)(4,1)S(1)}, s32[]{:S(2)}) async-start(s8[10485760]{0:T(1024)(128)(4,1)} %bitcast.6), calls=%async_computation | async-start | bytes 8388608
  10.4 59.8 %slice-start.1 = ((s8[10485760]{0:T(1024)(128)(4,1)}), s8[4194304]{0:T(1024)(128)(4,1)S(1)}, s32[]{:S(2)}) async-start(s8[10485760]{0:T(1024)(128)(4,1)} %bitcast.6), calls=%async_computation.1 | async-start | bytes 8388608
  20.6 0.7 copy-start.9
  21.3 10.4 %copy-start.7 = (bf16[480,256]{1,0:T(8,128)(2,1)}, bf16[480,256]{1,0:T(8,128)(2,1)S(1)}, u32[]{:S(2)}) copy-start(bf16[480,256]{1,0:T(8,128)(2,1)S(1)} %get-tuple-element.82) | copy-start | bytes 737284
  21.3 10.4 %copy-start.11 = (bf16[480,256]{1,0:T(8,128)(2,1)}, bf16[480,256]{1,0:T(8,128)(2,1)S(1)}, u32[]{:S(2)}) copy-start(bf16[480,256]{1,0:T(8,128)(2,1)S(1)} %get-tuple-element.80) | copy-start | bytes 737284
  21.3 10.4 %copy-start.13 = (bf16[480,256]{1,0:T(8,128)(2,1)}, bf16[480,256]{1,0:T(8,128)(2,1)S(1)}, u32[]{:S(2)}) copy-start(bf16[480,256]{1,0:T(8,128)(2,1)S(1)} %get-tuple-element.51) | copy-start | bytes 737284
  21.4 48.8 %slice-start.2 = ((s8[10485760]{0:T(1024)(128)(4,1)}), s8[2097152]{0:T(1024)(128)(4,1)S(1)}, s32[]{:S(2)}) async-start(s8[10485760]{0:T(1024)(128)(4,1)} %bitcast.6), calls=%async_computation.2 | async-start | bytes 4194304
  21.4 48.8 %copy-start.3 = (bf16[3,3,3,128,256]{4,3,2,1,0:T(8,128)(2,1)S(1)}, bf16[3,3,3,128,256]{4,3,2,1,0:T(8,128)(2,1)}, u32[]{:S(2)}) copy-start(bf16[3,3,3,128,256]{4,3,2,1,0:T(8,128)(2,1)} %param.7) | copy-start | bytes 5308420
  31.7 56.6 %collective-permute-start.2 = (bf16[1,4,640,256]{3,2,1,0:T(8,128)(2,1)S(1)}, bf16[1,4,640,256]{3,2,1,0:T(8,128)(2,1)S(1)}, u32[]{:S(2)}, u32[]{:S(2)}) collective-permute-start(bf16[1,4,640,256]{3,2,1,0:T(8,128)(2,1)S(1)} %get-tuple-element.47), channel_id=1, source_target_pairs={{0,8},{8,16},{16,24},{1,9},{9,17},{17,25},{2,10},{10,18},{18,26},{... | collective-permute-start | bytes 3932168 | tf_op jit(solution)/shard_map/hist0/ppermute | solution.py:18
  37.3 64.0 %collective-permute-start.1 = (bf16[1,4,640,256]{3,2,1,0:T(8,128)(2,1)}, bf16[1,4,640,256]{3,2,1,0:T(8,128)(2,1)S(1)}, u32[]{:S(2)}, u32[]{:S(2)}) collective-permute-start(bf16[1,4,640,256]{3,2,1,0:T(8,128)(2,1)} %get-tuple-element.46), channel_id=1, source_target_pairs={{0,8},{8,16},{16,24},{1,9},{9,17},{17,25},{2,10},{10,18},{18,26},{... | collective-permute-start | bytes 3932168 | tf_op jit(solution)/shard_map/hist1/ppermute | solution.py:18
  45.8 24.4 %collective-permute-start.3 = (bf16[480,256]{1,0:T(8,128)(2,1)S(1)}, bf16[480,256]{1,0:T(8,128)(2,1)S(1)}, u32[]{:S(2)}, u32[]{:S(2)}) collective-permute-start(bf16[480,256]{1,0:T(8,128)(2,1)S(1)} %get-tuple-element.48), channel_id=1, source_target_pairs={{0,7},{1,6},{2,5},{3,4},{4,3},{5,2},{6,1},{7,0},{8,15},{9,14},{10,... | collective-permute-start | bytes 737288 | tf_op jit(solution)/shard_map/a7/ppermute | solution.py:23
  46.5 32.9 %collective-permute-start.4 = (bf16[480,256]{1,0:T(8,128)(2,1)}, bf16[480,256]{1,0:T(8,128)(2,1)S(1)}, u32[]{:S(2)}, u32[]{:S(2)}) collective-permute-start(bf16[480,256]{1,0:T(8,128)(2,1)} %get-tuple-element.49), channel_id=1, source_target_pairs={{0,6},{1,7},{2,4},{3,5},{4,2},{5,3},{6,0},{7,1},{8,14},{9,15},{10,... | collective-permute-start | bytes 737288 | tf_op jit(solution)/shard_map/a6/ppermute | solution.py:23
  47.3 35.8 %collective-permute-start.5 = (bf16[480,256]{1,0:T(8,128)(2,1)}, bf16[480,256]{1,0:T(8,128)(2,1)S(1)}, u32[]{:S(2)}, u32[]{:S(2)}) collective-permute-start(bf16[480,256]{1,0:T(8,128)(2,1)} %get-tuple-element.50), channel_id=1, source_target_pairs={{0,5},{1,4},{2,7},{3,6},{4,1},{5,0},{6,3},{7,2},{8,13},{9,12},{10,... | collective-permute-start | bytes 737288 | tf_op jit(solution)/shard_map/a5/ppermute | solution.py:23
  70.2 18.1 %collective-permute-start.6 = (bf16[480,256]{1,0:T(8,128)(2,1)}, bf16[480,256]{1,0:T(8,128)(2,1)S(1)}, u32[]{:S(2)}, u32[]{:S(2)}) collective-permute-start(bf16[480,256]{1,0:T(8,128)(2,1)} %copy-done.13), channel_id=1, source_target_pairs={{0,4},{1,5},{2,6},{3,7},{4,0},{5,1},{6,2},{7,3},{8,12},{9,13},{10,... | collective-permute-start | bytes 737288 | tf_op jit(solution)/shard_map/a4/ppermute | solution.py:23
  88.3 12.9 %copy-start.12 = (bf16[480,256]{1,0:T(8,128)(2,1)S(1)}, bf16[480,256]{1,0:T(8,128)(2,1)}, u32[]{:S(2)}) copy-start(bf16[480,256]{1,0:T(8,128)(2,1)} %copy-done.11) | copy-start | bytes 737284
  88.3 36.6 %copy-start.10 = (bf16[480,256]{1,0:T(8,128)(2,1)S(1)}, bf16[480,256]{1,0:T(8,128)(2,1)}, u32[]{:S(2)}) copy-start(bf16[480,256]{1,0:T(8,128)(2,1)} %copy-done.9) | copy-start | bytes 737284
  88.3 42.9 %copy-start.8 = (bf16[480,256]{1,0:T(8,128)(2,1)S(1)}, bf16[480,256]{1,0:T(8,128)(2,1)}, u32[]{:S(2)}) copy-start(bf16[480,256]{1,0:T(8,128)(2,1)} %copy-done.7) | copy-start | bytes 737284
  93.7 31.2 %collective-permute-start.7 = (bf16[512,256]{1,0:T(8,128)(2,1)S(1)}, bf16[512,256]{1,0:T(8,128)(2,1)S(1)}, u32[]{:S(2)}, u32[]{:S(2)}) collective-permute-start(bf16[512,256]{1,0:T(8,128)(2,1)S(1)} %get-tuple-element.62), channel_id=1, source_target_pairs={{0,7},{1,6},{2,5},{3,4},{4,3},{5,2},{6,1},{7,0},{8,15},{9,14},{10,... | collective-permute-start | bytes 786440 | tf_op jit(solution)/shard_map/b7/ppermute | solution.py:23
  95.7 35.6 %collective-permute-start.8 = (bf16[512,256]{1,0:T(8,128)(2,1)S(1)}, bf16[512,256]{1,0:T(8,128)(2,1)S(1)}, u32[]{:S(2)}, u32[]{:S(2)}) collective-permute-start(bf16[512,256]{1,0:T(8,128)(2,1)S(1)} %get-tuple-element.63), channel_id=1, source_target_pairs={{0,6},{1,7},{2,4},{3,5},{4,2},{5,3},{6,0},{7,1},{8,14},{9,15},{10,... | collective-permute-start | bytes 786440 | tf_op jit(solution)/shard_map/b6/ppermute | solution.py:23
  96.4 39.1 %collective-permute-start.9 = (bf16[512,256]{1,0:T(8,128)(2,1)S(1)}, bf16[512,256]{1,0:T(8,128)(2,1)S(1)}, u32[]{:S(2)}, u32[]{:S(2)}) collective-permute-start(bf16[512,256]{1,0:T(8,128)(2,1)S(1)} %get-tuple-element.64), channel_id=1, source_target_pairs={{0,5},{1,4},{2,7},{3,6},{4,1},{5,0},{6,3},{7,2},{8,13},{9,12},{10,... | collective-permute-start | bytes 786440 | tf_op jit(solution)/shard_map/b5/ppermute | solution.py:23
  100.6 40.2 %collective-permute-start.10 = (bf16[512,256]{1,0:T(8,128)(2,1)S(1)}, bf16[512,256]{1,0:T(8,128)(2,1)S(1)}, u32[]{:S(2)}, u32[]{:S(2)}) collective-permute-start(bf16[512,256]{1,0:T(8,128)(2,1)S(1)} %get-tuple-element.65), channel_id=1, source_target_pairs={{0,4},{1,5},{2,6},{3,7},{4,0},{5,1},{6,2},{7,3},{8,12},{9,13},{10,... | collective-permute-start | bytes 786440 | tf_op jit(solution)/shard_map/b4/ppermute | solution.py:23
  101.2 41.9 %collective-permute-start.21 = (bf16[480,256]{1,0:T(8,128)(2,1)S(1)}, bf16[480,256]{1,0:T(8,128)(2,1)S(1)}, u32[]{:S(2)}, u32[]{:S(2)}) collective-permute-start(bf16[480,256]{1,0:T(8,128)(2,1)S(1)} %copy-done.12), channel_id=1, source_target_pairs={{0,1},{1,0},{2,3},{3,2},{4,5},{5,4},{6,7},{7,6},{8,9},{9,8},{10,11... | collective-permute-start | bytes 737288 | tf_op jit(solution)/shard_map/a1/ppermute | solution.py:23
  125.0 25.2 %collective-permute-start.22 = (bf16[480,256]{1,0:T(8,128)(2,1)S(1)}, bf16[480,256]{1,0:T(8,128)(2,1)S(1)}, u32[]{:S(2)}, u32[]{:S(2)}) collective-permute-start(bf16[480,256]{1,0:T(8,128)(2,1)S(1)} %copy-done.10), channel_id=1, source_target_pairs={{0,2},{1,3},{2,0},{3,1},{4,6},{5,7},{6,4},{7,5},{8,10},{9,11},{10,... | collective-permute-start | bytes 737288 | tf_op jit(solution)/shard_map/a2/ppermute | solution.py:23
  131.3 19.3 %collective-permute-start.23 = (bf16[480,256]{1,0:T(8,128)(2,1)S(1)}, bf16[480,256]{1,0:T(8,128)(2,1)S(1)}, u32[]{:S(2)}, u32[]{:S(2)}) collective-permute-start(bf16[480,256]{1,0:T(8,128)(2,1)S(1)} %copy-done.8), channel_id=1, source_target_pairs={{0,3},{1,2},{2,1},{3,0},{4,7},{5,6},{6,5},{7,4},{8,11},{9,10},{10,... | collective-permute-start | bytes 737288 | tf_op jit(solution)/shard_map/a3/ppermute | solution.py:23
  135.5 16.6 %collective-permute-start.18 = (bf16[512,256]{1,0:T(8,128)(2,1)S(1)}, bf16[512,256]{1,0:T(8,128)(2,1)S(1)}, u32[]{:S(2)}, u32[]{:S(2)}) collective-permute-start(bf16[512,256]{1,0:T(8,128)(2,1)S(1)} %get-tuple-element.76), channel_id=1, source_target_pairs={{0,1},{1,0},{2,3},{3,2},{4,5},{5,4},{6,7},{7,6},{8,9},{9,8},{10,11... | collective-permute-start | bytes 786440 | tf_op jit(solution)/shard_map/b1/ppermute | solution.py:23
  140.8 11.7 %collective-permute-start.19 = (bf16[512,256]{1,0:T(8,128)(2,1)S(1)}, bf16[512,256]{1,0:T(8,128)(2,1)S(1)}, u32[]{:S(2)}, u32[]{:S(2)}) collective-permute-start(bf16[512,256]{1,0:T(8,128)(2,1)S(1)} %get-tuple-element.77), channel_id=1, source_target_pairs={{0,2},{1,3},{2,0},{3,1},{4,6},{5,7},{6,4},{7,5},{8,10},{9,11},{10,... | collective-permute-start | bytes 786440 | tf_op jit(solution)/shard_map/b2/ppermute | solution.py:23
  143.2 24.4 %copy-start.4 = (f32[256]{0:T(256)S(1)}, f32[256]{0:T(256)}, u32[]{:S(2)}) copy-start(f32[256]{0:T(256)} %param.8) | copy-start | bytes 3076
  143.2 24.4 %copy-start.5 = (f32[256]{0:T(256)S(1)}, f32[256]{0:T(256)}, u32[]{:S(2)}) copy-start(f32[256]{0:T(256)} %param.9) | copy-start | bytes 3076
  143.2 18.3 %collective-permute-start.20 = (bf16[512,256]{1,0:T(8,128)(2,1)S(1)}, bf16[512,256]{1,0:T(8,128)(2,1)S(1)}, u32[]{:S(2)}, u32[]{:S(2)}) collective-permute-start(bf16[512,256]{1,0:T(8,128)(2,1)S(1)} %get-tuple-element.78), channel_id=1, source_target_pairs={{0,3},{1,2},{2,1},{3,0},{4,7},{5,6},{6,5},{7,4},{8,11},{9,10},{10,... | collective-permute-start | bytes 786440 | tf_op jit(solution)/shard_map/b3/ppermute | solution.py:23
  150.2 14.2 %collective-permute-start.11 = (bf16[336,256]{1,0:T(8,128)(2,1)S(1)}, bf16[336,256]{1,0:T(8,128)(2,1)S(1)}, u32[]{:S(2)}, u32[]{:S(2)}) collective-permute-start(bf16[336,256]{1,0:T(8,128)(2,1)S(1)} %get-tuple-element.68), channel_id=1, source_target_pairs={{0,1},{1,0},{2,3},{3,2},{4,5},{5,4},{6,7},{7,6},{8,9},{9,8},{10,11... | collective-permute-start | bytes 516104 | tf_op jit(solution)/shard_map/c1/ppermute | solution.py:23
  150.6 14.6 %collective-permute-start.12 = (bf16[336,256]{1,0:T(8,128)(2,1)S(1)}, bf16[336,256]{1,0:T(8,128)(2,1)S(1)}, u32[]{:S(2)}, u32[]{:S(2)}) collective-permute-start(bf16[336,256]{1,0:T(8,128)(2,1)S(1)} %get-tuple-element.69), channel_id=1, source_target_pairs={{0,2},{1,3},{2,0},{3,1},{4,6},{5,7},{6,4},{7,5},{8,10},{9,11},{10,... | collective-permute-start | bytes 516104 | tf_op jit(solution)/shard_map/c2/ppermute | solution.py:23
  152.0 23.2 %collective-permute-start.13 = (bf16[336,256]{1,0:T(8,128)(2,1)S(1)}, bf16[336,256]{1,0:T(8,128)(2,1)S(1)}, u32[]{:S(2)}, u32[]{:S(2)}) collective-permute-start(bf16[336,256]{1,0:T(8,128)(2,1)S(1)} %get-tuple-element.70), channel_id=1, source_target_pairs={{0,3},{1,2},{2,1},{3,0},{4,7},{5,6},{6,5},{7,4},{8,11},{9,10},{10,... | collective-permute-start | bytes 516104 | tf_op jit(solution)/shard_map/c3/ppermute | solution.py:23
  152.4 22.8 %collective-permute-start.14 = (bf16[336,256]{1,0:T(8,128)(2,1)S(1)}, bf16[336,256]{1,0:T(8,128)(2,1)S(1)}, u32[]{:S(2)}, u32[]{:S(2)}) collective-permute-start(bf16[336,256]{1,0:T(8,128)(2,1)S(1)} %get-tuple-element.71), channel_id=1, source_target_pairs={{0,4},{1,5},{2,6},{3,7},{4,0},{5,1},{6,2},{7,3},{8,12},{9,13},{10,... | collective-permute-start | bytes 516104 | tf_op jit(solution)/shard_map/c4/ppermute | solution.py:23
  161.5 18.8 %collective-permute-start.15 = (bf16[336,256]{1,0:T(8,128)(2,1)S(1)}, bf16[336,256]{1,0:T(8,128)(2,1)S(1)}, u32[]{:S(2)}, u32[]{:S(2)}) collective-permute-start(bf16[336,256]{1,0:T(8,128)(2,1)S(1)} %get-tuple-element.72), channel_id=1, source_target_pairs={{0,5},{1,4},{2,7},{3,6},{4,1},{5,0},{6,3},{7,2},{8,13},{9,12},{10,... | collective-permute-start | bytes 516104 | tf_op jit(solution)/shard_map/c5/ppermute | solution.py:23
  164.5 21.1 %collective-permute-start.16 = (bf16[336,256]{1,0:T(8,128)(2,1)S(1)}, bf16[336,256]{1,0:T(8,128)(2,1)S(1)}, u32[]{:S(2)}, u32[]{:S(2)}) collective-permute-start(bf16[336,256]{1,0:T(8,128)(2,1)S(1)} %get-tuple-element.73), channel_id=1, source_target_pairs={{0,6},{1,7},{2,4},{3,5},{4,2},{5,3},{6,0},{7,1},{8,14},{9,15},{10,... | collective-permute-start | bytes 516104 | tf_op jit(solution)/shard_map/c6/ppermute | solution.py:23
  165.2 24.0 %collective-permute-start.17 = (bf16[336,256]{1,0:T(8,128)(2,1)S(1)}, bf16[336,256]{1,0:T(8,128)(2,1)S(1)}, u32[]{:S(2)}, u32[]{:S(2)}) collective-permute-start(bf16[336,256]{1,0:T(8,128)(2,1)S(1)} %get-tuple-element.74), channel_id=1, source_target_pairs={{0,7},{1,6},{2,5},{3,4},{4,3},{5,2},{6,1},{7,0},{8,15},{9,14},{10,... | collective-permute-start | bytes 516104 | tf_op jit(solution)/shard_map/c7/ppermute | solution.py:23

commit v2 on v1

--- a/solution.py
+++ b/solution.py
@@ -9,7 +9,7 @@
 
 GROUPS = 32
 EPS = 1e-05
-VMEM_BYTES = 40 * 1024 * 1024
+VMEM_BYTES = 56 * 1024 * 1024
 
 
 def passed_along(array, axis, by):
@@ -64,10 +64,11 @@
     sums_refs = take(plan["sums_in"])
     out_refs = take(parts if parts else len(jobs))
     sums_out = take(1 if plan["sums_out"] else 0)
-    slab_ref, acc_ref, part_ref, stat_ref = refs
+    sources = x_ref.shape[0]
+    slab_refs, refs = refs[:sources], refs[sources:]
+    acc_refs, part_ref, stat_ref = refs[: len(jobs)], refs[-2], refs[-1]
     step = pl.program_id(0)
-    sources = x_ref.shape[0]
-    half = slab_ref.shape[2]
+    half = acc_refs[0].shape[0]
     above = lax.rem(step + 1, 2)
     below = lax.rem(step, 2)
     start = place_ref[0]
@@ -76,40 +77,36 @@
     @pl.when(step == 0)
     def _():
         for source in range(sources):
-            split_columns(above_ref.at[source, 0], slab_ref.at[source, 1])
+            split_columns(above_ref.at[source, 0], slab_refs[source].at[1])
         stat_ref[...] = jnp.zeros_like(stat_ref)
         for flip in range(parts if lead else 0):
             out_refs[flip][0:lead] = lead_refs[flip][...]
 
+    def product(source, tap):
+        slab_ref = slab_refs[source]
+        rows = jnp.concatenate([slab_ref[above], slab_ref[2], slab_ref[below]], axis=1)
+        return jnp.dot(rows, w_ref[tap], preferred_element_type=jnp.float32)
+
+    empty = [True] * len(jobs)
+    for at, (target, taps, addend) in enumerate(jobs):
+        if addend is not None:
+            acc_refs[at][...] = add_refs[addend][0].astype(jnp.float32)
+            empty[at] = False
     for source in range(sources):
-        split_columns(x_ref.at[source, 0], slab_ref.at[source, 2])
-        split_columns(x_ref.at[source, 1], slab_ref.at[source, below])
-
-    def product(source, tap):
-        rows = jnp.concatenate(
-            [slab_ref[source, above], slab_ref[source, 2], slab_ref[source, below]], axis=1)
-        return jnp.dot(rows, w_ref[tap], preferred_element_type=jnp.float32)
-
-    for at, (target, taps, addend) in enumerate(jobs):
-        empty = addend is None
-        if addend is not None:
-            acc_ref[...] = add_refs[addend][0].astype(jnp.float32)
-        for source, tap in taps:
-            frame = plan["first"] + source
-            if frame == target:
+        split_columns(x_ref.at[source, 0], slab_refs[source].at[2])
+        split_columns(x_ref.at[source, 1], slab_refs[source].at[below])
+        frame = plan["first"] + source
+        for at, (target, taps, _) in enumerate(jobs):
+            for tap in [tap for other, tap in taps if other == source]:
                 value = product(source, tap)
-                acc_ref[...] = value if empty else acc_ref[...] + value
-                empty = False
-                continue
-            if empty:
-                acc_ref[...] = jnp.zeros_like(acc_ref)
-                empty = False
-            same = clip_ref[start + frame] == clip_ref[jnp.minimum(start + target, last)]
-
-            @pl.when(same)
-            def _(source=source, tap=tap):
-                acc_ref[...] += product(source, tap)
-
+                if frame != target:
+                    same = clip_ref[start + frame] == clip_ref[jnp.minimum(start + target, last)]
+                    value = value * same.astype(jnp.float32)
+                acc_refs[at][...] = value if empty[at] else acc_refs[at][...] + value
+                empty[at] = False
+
+    for at in range(len(jobs)):
+        acc_ref = acc_refs[at]
         if not parts:
             out_refs[at][0] = acc_ref[...].astype(jnp.bfloat16)
             continue
@@ -119,11 +116,11 @@
         stat_ref[2 * at + 1] += jnp.sum(tiles * tiles, axis=0)
         for part in range(parts):
             piece = rounded[part * part_width : (part + 1) * part_width]
-            part_ref[part, 0:part_width] = piece.astype(jnp.bfloat16)
+            part_ref[at, part, 0:part_width] = piece.astype(jnp.bfloat16)
         mine = place_ref[1]
         for flip in range(parts):
             offset = pl.multiple_of(lead + (at * steps + step) * part_rows, 16)
-            out_refs[flip][pl.ds(offset, part_rows)] = part_ref[mine ^ flip]
+            out_refs[flip][pl.ds(offset, part_rows)] = part_ref[at, mine ^ flip]
 
     if sums_out or tail:
         @pl.when(step == steps - 1)
@@ -145,7 +142,8 @@
 
 
 def conv_frames(frames, halo, weight, clip_ids, place, first, sources, jobs, row=0, steps=None,
-                addends=(), parts=0, leads=(), sums=(), sums_out=False, tail=0):
+                addends=(), parts=0, leads=(), sums=(), sums_out=False, tail=0,
+                weigh=1):
     _, band, width, ci = frames.shape
     co = weight.shape[2]
     half = width // 2
@@ -187,15 +185,15 @@
             in_specs=in_specs,
             out_specs=out_specs,
             scratch_shapes=[
-                pltpu.VMEM((sources, 3, half, 3 * ci), jnp.bfloat16),
-                pltpu.VMEM((half, co), jnp.float32),
-                pltpu.VMEM((max(parts, 1), part_rows, co), jnp.bfloat16),
+                *[pltpu.VMEM((3, half, 3 * ci), jnp.bfloat16) for _ in range(sources)],
+                *[pltpu.VMEM((half, co), jnp.float32) for _ in jobs],
+                pltpu.VMEM((len(jobs), max(parts, 1), part_rows, co), jnp.bfloat16),
                 pltpu.VMEM((2 * len(jobs), 8, co), jnp.float32),
             ],
         ),
         cost_estimate=pl.CostEstimate(
-            flops=2 * products * steps * half * 9 * ci * co,
-            bytes_accessed=4 * sources * steps * width * ci + 2 * len(jobs) * steps * half * co,
+            flops=2 * weigh * products * steps * half * 9 * ci * co,
+            bytes_accessed=weigh * (4 * sources * steps * width * ci + 2 * len(jobs) * steps * half * co),
             transcendentals=0,
         ),
         compiler_params=pltpu.CompilerParams(vmem_limit_bytes=VMEM_BYTES),
@@ -325,19 +323,20 @@
     a_got = {flip: named(f"a{flip}", exchanged, a_sent[flip], "rows", flip) for flip in far}
 
     run = functools.partial(conv_frames, frames, after(halo, a_sums), weight, clip_ids, place)
-    onward = named("conv_hist", run, 2, 2, [(4, [(0, 0), (1, 1)], None), (5, [(1, 0)], None)])
+    onward = named("conv_hist", run, 2, 2, [(4, [(0, 0), (1, 1)], None), (5, [(1, 0)], None)], weigh=1)
     first_add = named("hist0", passed_along, onward[0], "tm", 1)
-    *top, top_sums = named("conv_top", run, 0, 4, later, row=0, steps=1, parts=parts, sums_out=True)
-    second_add = named("hist1", passed_along, onward[1], "tm", 1)
-
-    b_sent = named("conv_b", run, 0, 1, [(0, [(0, 2)], 0)], addends=(after(first_add, *[a_got[f] for f in far]),), parts=parts, leads=top,
-                   sums=(a_sums, top_sums), tail=32)
-    b_got = {flip: named(f"b{flip}", exchanged, b_sent[flip], "rows", flip) for flip in far}
-    c_sent = named("conv_c", run, 0, 2, [(1, [(0, 1), (1, 2)], 0)], addends=(after(second_add, *[b_got[f] for f in far]),), parts=parts, tail=16)
+    *top, top_sums = named("conv_top", run, 0, 4, later, row=0, steps=1, parts=parts, sums_out=True, weigh=20)
+    second_add = named("hist1", passed_along, after(onward[1], first_add), "tm", 1)
+
+    b_sent = named("conv_b", run, 0, 1, [(0, [(0, 2)], 0)], addends=(first_add,), parts=parts, leads=top,
+                   sums=(a_sums, top_sums), tail=32, weigh=20)
+    b_got = {flip: named(f"b{flip}", exchanged, after(b_sent[flip], a_got[flip]), "rows", flip) for flip in far}
+    c_sent = named("conv_c", run, 0, 2, [(1, [(0, 1), (1, 2)], 0)], addends=(second_add,), parts=parts, tail=16, weigh=20)
+    c_got = {flip: named(f"c{flip}", exchanged, after(c_sent[flip], b_got[flip]), "rows", flip) for flip in far}
     for flip in near:
-        a_got[flip] = named(f"a{flip}", exchanged, a_sent[flip], "rows", flip)
-        b_got[flip] = named(f"b{flip}", exchanged, b_sent[flip], "rows", flip)
-    c_got = {flip: named(f"c{flip}", exchanged, c_sent[flip], "rows", flip) for flip in far + near}
+        a_got[flip] = named(f"a{flip}", exchanged, after(a_sent[flip], c_sent[0]), "rows", flip)
+        b_got[flip] = named(f"b{flip}", exchanged, after(b_sent[flip], c_sent[0]), "rows", flip)
+        c_got[flip] = named(f"c{flip}", exchanged, after(c_sent[flip], b_got[flip]), "rows", flip)
 
     def whole(sent, got):
         return [sent[0]] + [got[flip] for flip in range(1, parts)]

time: 192 us -> 185 us (0.964)
  the two profiles are of different devices: /device:TPU:11 before, /device:TPU:4 now
where the time goes in v2:
time: 185 us; the launch traced here: 183 us
  waiting for transfers between devices  66.1 us (36%)
  Pallas kernels  65.6 us (35%)
  starting transfers between devices  44.6 us (24%)
  local copies, waits for them, and re-layouts  5.63 us (3%)
    pallas_call x5, Pallas kernels, conv_frames(): pl.pallas_call(functools.partial(conv_kernel, plan), out_shape=out_shape,...  48.7 us
    ppermute x3, waiting for transfers between devices, passed_along(): return lax.ppermute(array, axis, pairs)  40.5 us
    ppermute x21, starting transfers between devices, exchanged(): return lax.ppermute(array, axis, [(i, i ^ flip) for i in range(length)])  36.6 us
    ppermute x21, waiting for transfers between devices, exchanged(): return lax.ppermute(array, axis, [(i, i ^ flip) for i in range(length)])  25.6 us
    pallas_call x3, Pallas kernels, norm_frames(): pl.pallas_call(functools.partial(norm_kernel, plan), out_shape=jax.ShapeD...  16.9 us
    ppermute x3, starting transfers between devices, passed_along(): return lax.ppermute(array, axis, pairs)  8.01 us
    unnamed x62, local copies, waits for them, and re-layouts  4.22 us
  transfers between devices with their start and end apart: 24, of which 7 were waited for; matrix products, arithmetic and copies ran while one was open for 0% of the time, Pallas kernels for 33%

profile of v2, /device:TPU:4, one launch (start us, length us, event | category | flops | bytes accessed | tf_op | source)
XLA Modules:
  0.0 183.1 jit_solution(2118318087409816821)
XLA Ops:
  0.0 1.4 slice.3
  1.4 1.8 collective-permute-start
  3.3 0.7 pad_add_fusion.place_ref
  3.9 14.4 %conv_a.1 = (bf16[480,256]{1,0:T(8,128)(2,1)}, bf16[480,256]{1,0:T(8,128)(2,1)}, bf16[480,256]{1,0:T(8,128)(2,1)}, bf16[480,256]{1,0:T(8,128)(2,1)}, bf16[480,25...) custom-call(s32[16]{0:T(128)} %clip_ref.9, ...), custom_call_target="tpu_custom_call" | custom-call | flops 6794772480 | bytes 9830400 | tf_op jit(solution)/shard_map/conv_a/pallas_call | solution.py:179
  18.3 2.7 %collective-permute-start.9 = (bf16[480,256]{1,0:T(8,128)(2,1)}, bf16[480,256]{1,0:T(8,128)(2,1)S(1)}, u32[]{:S(2)}, u32[]{:S(2)}) collective-permute-start(bf16[480,256]{1,0:T(8,128)(2,1)} %get-tuple-element.89), channel_id=1, source_target_pairs={{0,4},{1,5},{2,6},{3,7},{4,0},{5,1},{6,2},{7,3},{8,12},{9,13},{10,... | collective-permute-start | bytes 737288 | tf_op jit(solution)/shard_map/a4/ppermute | solution.py:23
  21.0 1.3 collective-permute-start.12
  22.3 1.3 collective-permute-start.15
  23.7 1.8 %collective-permute-start.18 = (bf16[480,256]{1,0:T(8,128)(2,1)}, bf16[480,256]{1,0:T(8,128)(2,1)S(1)}, u32[]{:S(2)}, u32[]{:S(2)}) collective-permute-start(bf16[480,256]{1,0:T(8,128)(2,1)} %get-tuple-element.104), channel_id=1, source_target_pairs={{0,7},{1,6},{2,5},{3,4},{4,3},{5,2},{6,1},{7,0},{8,15},{9,14},{10,... | collective-permute-start | bytes 737288 | tf_op jit(solution)/shard_map/a7/ppermute | solution.py:23
  25.5 0.0 collective-permute-done.above_ref
  25.5 1.1 copy-done.21
  26.6 10.2 %conv_hist.1 = (bf16[1,4,640,256]{3,2,1,0:T(8,128)(2,1)}, bf16[1,4,640,256]{3,2,1,0:T(8,128)(2,1)}) custom-call(s32[16]{0:T(128)} %clip_ref.9, s32[2]{0:T(128)} %pad_add_fusion.place_ref, bf16[4,8,1280,128]{3,2,1,0:T(8,128)(2,1)} %x_ref.9, bf16[4,1,1280,128]{3,2,1,0:T(8,128)(2,1)} %copy-done.21, bf16[3,1152,256]{2,1,0:T(8,128)(2,1)} %bitcast.13), custom_call_target="tpu_custom_call" | custom-call | flops 4529848320 | bytes 7864320 | tf_op jit(solution)/shard_map/conv_hist/pallas_call | solution.py:179
  36.8 3.5 %collective-permute-start.1 = (bf16[1,4,640,256]{3,2,1,0:T(8,128)(2,1)}, bf16[1,4,640,256]{3,2,1,0:T(8,128)(2,1)S(1)}, u32[]{:S(2)}, u32[]{:S(2)}) collective-permute-start(bf16[1,4,640,256]{3,2,1,0:T(8,128)(2,1)} %get-tuple-element.63), channel_id=1, source_target_pairs={{0,8},{8,16},{16,24},{1,9},{9,17},{17,25},{2,10},{10,18},{18,26},{... | collective-permute-start | bytes 3932168 | tf_op jit(solution)/shard_map/hist0/ppermute | solution.py:18
  40.3 7.0 %conv_top.1 = (bf16[160,256]{1,0:T(8,128)(2,1)}, bf16[160,256]{1,0:T(8,128)(2,1)}, bf16[160,256]{1,0:T(8,128)(2,1)}, bf16[160,256]{1,0:T(8,128)(2,1)}, bf16[160,...) custom-call(s32[16]{0:T(128)} %clip_ref.9, ...), custom_call_target="tpu_custom_call" | custom-call | flops 45298483200 | bytes 65536000 | tf_op jit(solution)/shard_map/conv_top/pallas_call | solution.py:179
  47.3 24.1 %collective-permute-done.1.refs_0_ = bf16[1,4,640,256]{3,2,1,0:T(8,128)(2,1)S(1)} collective-permute-done((bf16[1,4,640,256]{3,2,1,0:T(8,128)(2,1)}, bf16[1,4,640,256]{3,2,1,0:T(8,128)(2,1)S(1)}, u32[]{:S(2)}, u32[]{:S(2)}) %collective-permute-start.1) | collective-permute-done | bytes 1310752 | tf_op jit(solution)/shard_map/hist0/ppermute | solution.py:18
  71.3 2.7 %collective-permute-start.2 = (bf16[1,4,640,256]{3,2,1,0:T(8,128)(2,1)S(1)}, bf16[1,4,640,256]{3,2,1,0:T(8,128)(2,1)S(1)}, u32[]{:S(2)}, u32[]{:S(2)}) collective-permute-start(bf16[1,4,640,256]{3,2,1,0:T(8,128)(2,1)S(1)} %copy-done.22), channel_id=1, source_target_pairs={{0,8},{8,16},{16,24},{1,9},{9,17},{17,25},{2,10},{10,18},{18,26},{... | collective-permute-start | bytes 3932168 | tf_op jit(solution)/shard_map/hist1/ppermute | solution.py:18
  74.0 7.8 %conv_b.1 = (bf16[512,256]{1,0:T(8,128)(2,1)}, bf16[512,256]{1,0:T(8,128)(2,1)}, bf16[512,256]{1,0:T(8,128)(2,1)}, bf16[512,256]{1,0:T(8,128)(2,1)}, bf16[512,25...) custom-call(s32[16]{0:T(128)} %clip_ref.9, ...), custom_call_target="tpu_custom_call" | custom-call | flops 30198988800 | bytes 78643200 | tf_op jit(solution)/shard_map/conv_b/pallas_call | solution.py:179
  81.8 0.0 collective-permute-done.9.refs_4_
  81.8 0.0 collective-permute-done.12.refs_5_
  81.9 0.0 collective-permute-done.15.refs_6_
  81.9 0.0 collective-permute-done.18.refs_7_
  82.0 0.1 collective-permute-start.19
  82.0 3.0 %collective-permute-start.16 = (bf16[512,256]{1,0:T(8,128)(2,1)}, bf16[512,256]{1,0:T(8,128)(2,1)S(1)}, u32[]{:S(2)}, u32[]{:S(2)}) collective-permute-start(bf16[512,256]{1,0:T(8,128)(2,1)} %get-tuple-element.100), channel_id=1, source_target_pairs={{0,6},{1,7},{2,4},{3,5},{4,2},{5,3},{6,0},{7,1},{8,14},{9,15},{10,... | collective-permute-start | bytes 786440 | tf_op jit(solution)/shard_map/b6/ppermute | solution.py:23
  85.1 0.0 collective-permute-start.13
  85.1 3.1 %collective-permute-start.10 = (bf16[512,256]{1,0:T(8,128)(2,1)}, bf16[512,256]{1,0:T(8,128)(2,1)S(1)}, u32[]{:S(2)}, u32[]{:S(2)}) collective-permute-start(bf16[512,256]{1,0:T(8,128)(2,1)} %get-tuple-element.90), channel_id=1, source_target_pairs={{0,4},{1,5},{2,6},{3,7},{4,0},{5,1},{6,2},{7,3},{8,12},{9,13},{10,... | collective-permute-start | bytes 786440 | tf_op jit(solution)/shard_map/b4/ppermute | solution.py:23
  88.2 16.4 %collective-permute-done.2.refs_0_ = bf16[1,4,640,256]{3,2,1,0:T(8,128)(2,1)S(1)} collective-permute-done((bf16[1,4,640,256]{3,2,1,0:T(8,128)(2,1)S(1)}, bf16[1,4,640,256]{3,2,1,0:T(8,128)(2,1)S(1)}, u32[]{:S(2)}, u32[]{:S(2)}) %collective-permute-start.2) | collective-permute-done | bytes 1310752 | tf_op jit(solution)/shard_map/hist1/ppermute | solution.py:18
  104.7 1.1 copy-done.23
  105.8 9.3 %conv_c.1 = (bf16[336,256]{1,0:T(8,128)(2,1)}, bf16[336,256]{1,0:T(8,128)(2,1)}, bf16[336,256]{1,0:T(8,128)(2,1)}, bf16[336,256]{1,0:T(8,128)(2,1)}, bf16[336,25...) custom-call(s32[16]{0:T(128)} %clip_ref.9, ...), custom_call_target="tpu_custom_call" | custom-call | flops 60397977600 | bytes 131072000 | tf_op jit(solution)/shard_map/conv_c/pallas_call | solution.py:179
  115.1 0.1 collective-permute-start.7
  115.2 0.0 collective-permute-done.19.refs_15_.refs_23_.refs_7_
  115.2 0.7 collective-permute-start.5
  115.9 0.0 collective-permute-done.16.refs_14_.refs_22_.refs_6_
  115.9 1.3 collective-permute-start.3
  117.2 6.7 %collective-permute-done.13.refs_13_.refs_21_.refs_5_ = bf16[512,256]{1,0:T(8,128)(2,1)S(1)} collective-permute-done((bf16[512,256]{1,0:T(8,128)(2,1)}, bf16[512,256]{1,0:T(8,128)(2,1)S(1)}, u32[]{:S(2)}, u32[]{:S(2)}) %collective-permute-start.13) | collective-permute-done | bytes 262176 | tf_op jit(solution)/shard_map/b5/ppermute | solution.py:23
  123.9 0.0 collective-permute-start.21
  123.9 4.9 %collective-permute-done.10.refs_12_.refs_20_.refs_4_ = bf16[512,256]{1,0:T(8,128)(2,1)S(1)} collective-permute-done((bf16[512,256]{1,0:T(8,128)(2,1)}, bf16[512,256]{1,0:T(8,128)(2,1)S(1)}, u32[]{:S(2)}, u32[]{:S(2)}) %collective-permute-start.10) | collective-permute-done | bytes 262176 | tf_op jit(solution)/shard_map/b4/ppermute | solution.py:23
  128.8 0.0 collective-permute-start.22
  128.8 5.8 %collective-permute-done.7.refs_11_.refs_19_.refs_3_ = bf16[512,256]{1,0:T(8,128)(2,1)S(1)} collective-permute-done((bf16[512,256]{1,0:T(8,128)(2,1)S(1)}, bf16[512,256]{1,0:T(8,128)(2,1)S(1)}, u32[]{:S(2)}, u32[]{:S(2)}) %collective-permute-start.7) | collective-permute-done | bytes 262176 | tf_op jit(solution)/shard_map/b3/ppermute | solution.py:23
  134.7 0.0 collective-permute-start.23
  134.7 4.8 %collective-permute-done.5.refs_10_.refs_18_.refs_2_ = bf16[512,256]{1,0:T(8,128)(2,1)S(1)} collective-permute-done((bf16[512,256]{1,0:T(8,128)(2,1)S(1)}, bf16[512,256]{1,0:T(8,128)(2,1)S(1)}, u32[]{:S(2)}, u32[]{:S(2)}) %collective-permute-start.5) | collective-permute-done | bytes 262176 | tf_op jit(solution)/shard_map/b2/ppermute | solution.py:23
  139.4 0.8 collective-permute-start.20
  140.2 0.0 collective-permute-done.3.refs_9_.refs_17_.refs_1_
  140.3 3.6 %collective-permute-start.17 = (bf16[336,256]{1,0:T(8,128)(2,1)}, bf16[336,256]{1,0:T(8,128)(2,1)S(1)}, u32[]{:S(2)}, u32[]{:S(2)}) collective-permute-start(bf16[336,256]{1,0:T(8,128)(2,1)} %get-tuple-element.101), channel_id=1, source_target_pairs={{0,6},{1,7},{2,4},{3,5},{4,2},{5,3},{6,0},{7,1},{8,14},{9,15},{10,... | collective-permute-start | bytes 516104 | tf_op jit(solution)/shard_map/c6/ppermute | solution.py:23
  143.8 3.3 %collective-permute-done.20.refs_7_.refs_15_ = bf16[336,256]{1,0:T(8,128)(2,1)S(1)} collective-permute-done((bf16[336,256]{1,0:T(8,128)(2,1)}, bf16[336,256]{1,0:T(8,128)(2,1)S(1)}, u32[]{:S(2)}, u32[]{:S(2)}) %collective-permute-start.20) | collective-permute-done | bytes 172064 | tf_op jit(solution)/shard_map/c7/ppermute | solution.py:23
  147.2 5.5 %collective-permute-start.14 = (bf16[336,256]{1,0:T(8,128)(2,1)}, bf16[336,256]{1,0:T(8,128)(2,1)S(1)}, u32[]{:S(2)}, u32[]{:S(2)}) collective-permute-start(bf16[336,256]{1,0:T(8,128)(2,1)} %get-tuple-element.96), channel_id=1, source_target_pairs={{0,5},{1,4},{2,7},{3,6},{4,1},{5,0},{6,3},{7,2},{8,13},{9,12},{10,... | collective-permute-start | bytes 516104 | tf_op jit(solution)/shard_map/c5/ppermute | solution.py:23
  152.7 0.0 collective-permute-done.17.refs_6_.refs_14_
  152.7 8.0 %collective-permute-start.11 = (bf16[336,256]{1,0:T(8,128)(2,1)}, bf16[336,256]{1,0:T(8,128)(2,1)S(1)}, u32[]{:S(2)}, u32[]{:S(2)}) collective-permute-start(bf16[336,256]{1,0:T(8,128)(2,1)} %get-tuple-element.91), channel_id=1, source_target_pairs={{0,4},{1,5},{2,6},{3,7},{4,0},{5,1},{6,2},{7,3},{8,12},{9,13},{10,... | collective-permute-start | bytes 516104 | tf_op jit(solution)/shard_map/c4/ppermute | solution.py:23
  160.7 0.0 collective-permute-done.21.refs_1_
  160.7 0.0 collective-permute-start.8
  160.7 0.0 collective-permute-done.22.refs_2_
  160.8 3.0 %collective-permute-start.6 = (bf16[336,256]{1,0:T(8,128)(2,1)}, bf16[336,256]{1,0:T(8,128)(2,1)S(1)}, u32[]{:S(2)}, u32[]{:S(2)}) collective-permute-start(bf16[336,256]{1,0:T(8,128)(2,1)} %get-tuple-element.82), channel_id=1, source_target_pairs={{0,2},{1,3},{2,0},{3,1},{4,6},{5,7},{6,4},{7,5},{8,10},{9,11},{10,... | collective-permute-start | bytes 516104 | tf_op jit(solution)/shard_map/c2/ppermute | solution.py:23
  163.8 0.0 collective-permute-done.23.refs_3_
  163.8 0.1 collective-permute-start.4
  164.0 0.5 copy-done.20
  164.5 7.5 %norm_a.1.refs_18_ = bf16[4,8,4,80,256]{4,3,2,1,0:T(8,128)(2,1)} custom-call(s32[2]{0:T(128)} %pad_add_fusion.place_ref, bf16[480,256]{1,0:T(8,128)(2,1)} %get-tuple-element.108.refs_0_, bf16[480,256]{1,0:T(8,128)(2,1)} %copy-done.18, bf16[480,256]{1,0:T(8,128)(2,1)} %copy-done.19, bf16[480,256]{1,0:T(8,128)(2,1)} %copy-done.20, ...), custom_call_target="tpu_custom_call" | custom-call | flops 10485760 | bytes 5242880 | tf_op jit(solution)/shard_map/norm_a/pallas_call | solution.py:280
  172.0 4.8 %norm_b.1.refs_18_ = bf16[4,8,4,80,256]{4,3,2,1,0:T(8,128)(2,1)} custom-call(s32[2]{0:T(128)} %pad_add_fusion.place_ref, bf16[512,256]{1,0:T(8,128)(2,1)} %get-tuple-element.107.refs_8_.refs_16_.refs_0_, bf16[512,256]{1,0:T(8,128)(2,1)} %copy-done.6, bf16[512,256]{1,0:T(8,128)(2,1)} %copy-done.5, ...), custom_call_target="tpu_custom_call", output_to_operand_aliasing={{}: (19, {})} | custom-call | flops 5242880 | bytes 2621440 | tf_op jit(solution)/shard_map/norm_b/pallas_call | solution.py:280
  176.7 0.0 collective-permute-done.14.refs_5_.refs_13_
  176.8 0.0 collective-permute-done.8.refs_3_.refs_11_
  176.8 0.0 collective-permute-done.6.refs_2_.refs_10_
  176.8 0.6 copy-done.9
  177.4 0.1 copy-done.10
  177.5 0.1 copy-done.11
  177.6 0.0 copy-done.12
  177.6 0.7 copy-done.13
  178.3 4.7 %norm_c.1 = bf16[4,8,4,80,256]{4,3,2,1,0:T(8,128)(2,1)} custom-call(s32[2]{0:T(128)} %pad_add_fusion.place_ref, bf16[336,256]{1,0:T(8,128)(2,1)} %get-tuple-element.65.refs_0_.refs_8_, bf16[336,256]{1,0:T(8,128)(2,1)} %copy-done.13, bf16[336,256]{1,0:T(8,128)(2,1)} %copy-done.12, bf16[336,256]{1,0:T(8,128)(2,1)} %copy-done.11, ...), custom_call_target="tpu_custom_call", output_to_operand_aliasing={{}: (19, {})} | custom-call | flops 5242880 | bytes 2621440 | tf_op jit(solution)/shard_map/norm_c/pallas_call | solution.py:280
  (56 shorter events, 0.1 us)
Async XLA Ops:
  1.4 24.1 %collective-permute-start = (bf16[4,1,1280,128]{3,2,1,0:T(8,128)(2,1)S(1)}, bf16[4,1,1280,128]{3,2,1,0:T(8,128)(2,1)S(1)}, u32[]{:S(2)}, u32[]{:S(2)}) collective-permute-start(bf16[4,1,1280,128]{3,2,1,0:T(8,128)(2,1)S(1)} %slice.3), channel_id=1, source_target_pairs={{0,1},{1,2},{2,3},{3,4},{4,5},{5,6},{6,7},{8,9},{9,10},{10,11},{11... | collective-permute-start | bytes 3932168 | tf_op jit(solution)/shard_map/halo/ppermute | solution.py:18
  18.3 63.5 %collective-permute-start.9 = (bf16[480,256]{1,0:T(8,128)(2,1)}, bf16[480,256]{1,0:T(8,128)(2,1)S(1)}, u32[]{:S(2)}, u32[]{:S(2)}) collective-permute-start(bf16[480,256]{1,0:T(8,128)(2,1)} %get-tuple-element.89), channel_id=1, source_target_pairs={{0,4},{1,5},{2,6},{3,7},{4,0},{5,1},{6,2},{7,3},{8,12},{9,13},{10,... | collective-permute-start | bytes 737288 | tf_op jit(solution)/shard_map/a4/ppermute | solution.py:23
  21.0 60.9 %collective-permute-start.12 = (bf16[480,256]{1,0:T(8,128)(2,1)}, bf16[480,256]{1,0:T(8,128)(2,1)S(1)}, u32[]{:S(2)}, u32[]{:S(2)}) collective-permute-start(bf16[480,256]{1,0:T(8,128)(2,1)} %get-tuple-element.94), channel_id=1, source_target_pairs={{0,5},{1,4},{2,7},{3,6},{4,1},{5,0},{6,3},{7,2},{8,13},{9,12},{10,... | collective-permute-start | bytes 737288 | tf_op jit(solution)/shard_map/a5/ppermute | solution.py:23
  22.3 59.5 %collective-permute-start.15 = (bf16[480,256]{1,0:T(8,128)(2,1)}, bf16[480,256]{1,0:T(8,128)(2,1)S(1)}, u32[]{:S(2)}, u32[]{:S(2)}) collective-permute-start(bf16[480,256]{1,0:T(8,128)(2,1)} %get-tuple-element.99), channel_id=1, source_target_pairs={{0,6},{1,7},{2,4},{3,5},{4,2},{5,3},{6,0},{7,1},{8,14},{9,15},{10,... | collective-permute-start | bytes 737288 | tf_op jit(solution)/shard_map/a6/ppermute | solution.py:23
  23.7 58.2 %collective-permute-start.18 = (bf16[480,256]{1,0:T(8,128)(2,1)}, bf16[480,256]{1,0:T(8,128)(2,1)S(1)}, u32[]{:S(2)}, u32[]{:S(2)}) collective-permute-start(bf16[480,256]{1,0:T(8,128)(2,1)} %get-tuple-element.104), channel_id=1, source_target_pairs={{0,7},{1,6},{2,5},{3,4},{4,3},{5,2},{6,1},{7,0},{8,15},{9,14},{10,... | collective-permute-start | bytes 737288 | tf_op jit(solution)/shard_map/a7/ppermute | solution.py:23
  25.5 1.1 copy-start.21
  36.8 34.6 %copy-start.22 = (bf16[1,4,640,256]{3,2,1,0:T(8,128)(2,1)S(1)}, bf16[1,4,640,256]{3,2,1,0:T(8,128)(2,1)}, u32[]{:S(2)}) copy-start(bf16[1,4,640,256]{3,2,1,0:T(8,128)(2,1)} %get-tuple-element.64) | copy-start | bytes 3932164
  36.8 34.6 %collective-permute-start.1 = (bf16[1,4,640,256]{3,2,1,0:T(8,128)(2,1)}, bf16[1,4,640,256]{3,2,1,0:T(8,128)(2,1)S(1)}, u32[]{:S(2)}, u32[]{:S(2)}) collective-permute-start(bf16[1,4,640,256]{3,2,1,0:T(8,128)(2,1)} %get-tuple-element.63), channel_id=1, source_target_pairs={{0,8},{8,16},{16,24},{1,9},{9,17},{17,25},{2,10},{10,18},{18,26},{... | collective-permute-start | bytes 3932168 | tf_op jit(solution)/shard_map/hist0/ppermute | solution.py:18
  71.3 2.7 %copy-start.24 = (bf16[1,4,640,256]{3,2,1,0:T(8,128)(2,1)}, bf16[1,4,640,256]{3,2,1,0:T(8,128)(2,1)S(1)}, u32[]{:S(2)}) copy-start(bf16[1,4,640,256]{3,2,1,0:T(8,128)(2,1)S(1)} %collective-permute-done.1.refs_0_) | copy-start | bytes 3932164
  71.3 33.4 %collective-permute-start.2 = (bf16[1,4,640,256]{3,2,1,0:T(8,128)(2,1)S(1)}, bf16[1,4,640,256]{3,2,1,0:T(8,128)(2,1)S(1)}, u32[]{:S(2)}, u32[]{:S(2)}) collective-permute-start(bf16[1,4,640,256]{3,2,1,0:T(8,128)(2,1)S(1)} %copy-done.22), channel_id=1, source_target_pairs={{0,8},{8,16},{16,24},{1,9},{9,17},{17,25},{2,10},{10,18},{18,26},{... | collective-permute-start | bytes 3932168 | tf_op jit(solution)/shard_map/hist1/ppermute | solution.py:18
  81.8 33.3 %copy-start.14 = (bf16[480,256]{1,0:T(8,128)(2,1)}, bf16[480,256]{1,0:T(8,128)(2,1)S(1)}, u32[]{:S(2)}) copy-start(bf16[480,256]{1,0:T(8,128)(2,1)S(1)} %collective-permute-done.9.refs_4_) | copy-start | bytes 737284
  81.9 33.2 %copy-start.15 = (bf16[480,256]{1,0:T(8,128)(2,1)}, bf16[480,256]{1,0:T(8,128)(2,1)S(1)}, u32[]{:S(2)}) copy-start(bf16[480,256]{1,0:T(8,128)(2,1)S(1)} %collective-permute-done.12.refs_5_) | copy-start | bytes 737284
  81.9 33.2 %copy-start.16 = (bf16[480,256]{1,0:T(8,128)(2,1)}, bf16[480,256]{1,0:T(8,128)(2,1)S(1)}, u32[]{:S(2)}) copy-start(bf16[480,256]{1,0:T(8,128)(2,1)S(1)} %collective-permute-done.15.refs_6_) | copy-start | bytes 737284
  81.9 33.2 %copy-start.17 = (bf16[480,256]{1,0:T(8,128)(2,1)}, bf16[480,256]{1,0:T(8,128)(2,1)S(1)}, u32[]{:S(2)}) copy-start(bf16[480,256]{1,0:T(8,128)(2,1)S(1)} %collective-permute-done.18.refs_7_) | copy-start | bytes 737284
  81.9 33.2 %copy-start.27 = (bf16[512,256]{1,0:T(8,128)(2,1)S(1)}, bf16[512,256]{1,0:T(8,128)(2,1)}, u32[]{:S(2)}) copy-start(bf16[512,256]{1,0:T(8,128)(2,1)} %get-tuple-element.85) | copy-start | bytes 786436
  81.9 33.3 %copy-start.26 = (bf16[512,256]{1,0:T(8,128)(2,1)S(1)}, bf16[512,256]{1,0:T(8,128)(2,1)}, u32[]{:S(2)}) copy-start(bf16[512,256]{1,0:T(8,128)(2,1)} %get-tuple-element.81) | copy-start | bytes 786436
  81.9 34.0 %copy-start.25 = (bf16[512,256]{1,0:T(8,128)(2,1)S(1)}, bf16[512,256]{1,0:T(8,128)(2,1)}, u32[]{:S(2)}) copy-start(bf16[512,256]{1,0:T(8,128)(2,1)} %get-tuple-element.77) | copy-start | bytes 786436
  81.9 41.9 %copy-start.30 = (bf16[480,256]{1,0:T(8,128)(2,1)S(1)}, bf16[480,256]{1,0:T(8,128)(2,1)}, u32[]{:S(2)}) copy-start(bf16[480,256]{1,0:T(8,128)(2,1)} %get-tuple-element.110) | copy-start | bytes 737284
  81.9 46.9 %copy-start.29 = (bf16[480,256]{1,0:T(8,128)(2,1)S(1)}, bf16[480,256]{1,0:T(8,128)(2,1)}, u32[]{:S(2)}) copy-start(bf16[480,256]{1,0:T(8,128)(2,1)} %get-tuple-element.112) | copy-start | bytes 737284
  82.0 52.7 %copy-start.28 = (bf16[480,256]{1,0:T(8,128)(2,1)S(1)}, bf16[480,256]{1,0:T(8,128)(2,1)}, u32[]{:S(2)}) copy-start(bf16[480,256]{1,0:T(8,128)(2,1)} %get-tuple-element.114) | copy-start | bytes 737284
  82.0 33.2 %collective-permute-start.19 = (bf16[512,256]{1,0:T(8,128)(2,1)}, bf16[512,256]{1,0:T(8,128)(2,1)S(1)}, u32[]{:S(2)}, u32[]{:S(2)}) collective-permute-start(bf16[512,256]{1,0:T(8,128)(2,1)} %get-tuple-element.105), channel_id=1, source_target_pairs={{0,7},{1,6},{2,5},{3,4},{4,3},{5,2},{6,1},{7,0},{8,15},{9,14},{10,... | collective-permute-start | bytes 786440 | tf_op jit(solution)/shard_map/b7/ppermute | solution.py:23
  82.0 33.9 %collective-permute-start.16 = (bf16[512,256]{1,0:T(8,128)(2,1)}, bf16[512,256]{1,0:T(8,128)(2,1)S(1)}, u32[]{:S(2)}, u32[]{:S(2)}) collective-permute-start(bf16[512,256]{1,0:T(8,128)(2,1)} %get-tuple-element.100), channel_id=1, source_target_pairs={{0,6},{1,7},{2,4},{3,5},{4,2},{5,3},{6,0},{7,1},{8,14},{9,15},{10,... | collective-permute-start | bytes 786440 | tf_op jit(solution)/shard_map/b6/ppermute | solution.py:23
  85.1 38.8 %collective-permute-start.13 = (bf16[512,256]{1,0:T(8,128)(2,1)}, bf16[512,256]{1,0:T(8,128)(2,1)S(1)}, u32[]{:S(2)}, u32[]{:S(2)}) collective-permute-start(bf16[512,256]{1,0:T(8,128)(2,1)} %get-tuple-element.95), channel_id=1, source_target_pairs={{0,5},{1,4},{2,7},{3,6},{4,1},{5,0},{6,3},{7,2},{8,13},{9,12},{10,... | collective-permute-start | bytes 786440 | tf_op jit(solution)/shard_map/b5/ppermute | solution.py:23
  85.1 43.7 %collective-permute-start.10 = (bf16[512,256]{1,0:T(8,128)(2,1)}, bf16[512,256]{1,0:T(8,128)(2,1)S(1)}, u32[]{:S(2)}, u32[]{:S(2)}) collective-permute-start(bf16[512,256]{1,0:T(8,128)(2,1)} %get-tuple-element.90), channel_id=1, source_target_pairs={{0,4},{1,5},{2,6},{3,7},{4,0},{5,1},{6,2},{7,3},{8,12},{9,13},{10,... | collective-permute-start | bytes 786440 | tf_op jit(solution)/shard_map/b4/ppermute | solution.py:23
  104.7 1.1 copy-start.23
  115.1 19.5 %collective-permute-start.7 = (bf16[512,256]{1,0:T(8,128)(2,1)S(1)}, bf16[512,256]{1,0:T(8,128)(2,1)S(1)}, u32[]{:S(2)}, u32[]{:S(2)}) collective-permute-start(bf16[512,256]{1,0:T(8,128)(2,1)S(1)} %copy-done.27), channel_id=1, source_target_pairs={{0,3},{1,2},{2,1},{3,0},{4,7},{5,6},{6,5},{7,4},{8,11},{9,10},{10,... | collective-permute-start | bytes 786440 | tf_op jit(solution)/shard_map/b3/ppermute | solution.py:23
  115.2 48.7 %copy-start = (bf16[512,256]{1,0:T(8,128)(2,1)}, bf16[512,256]{1,0:T(8,128)(2,1)S(1)}, u32[]{:S(2)}) copy-start(bf16[512,256]{1,0:T(8,128)(2,1)S(1)} %collective-permute-done.19.refs_15_.refs_23_.refs_7_) | copy-start | bytes 786436
  115.2 24.2 %collective-permute-start.5 = (bf16[512,256]{1,0:T(8,128)(2,1)S(1)}, bf16[512,256]{1,0:T(8,128)(2,1)S(1)}, u32[]{:S(2)}, u32[]{:S(2)}) collective-permute-start(bf16[512,256]{1,0:T(8,128)(2,1)S(1)} %copy-done.26), channel_id=1, source_target_pairs={{0,2},{1,3},{2,0},{3,1},{4,6},{5,7},{6,4},{7,5},{8,10},{9,11},{10,... | collective-permute-start | bytes 786440 | tf_op jit(solution)/shard_map/b2/ppermute | solution.py:23
  115.9 48.0 %copy-start.1 = (bf16[512,256]{1,0:T(8,128)(2,1)}, bf16[512,256]{1,0:T(8,128)(2,1)S(1)}, u32[]{:S(2)}) copy-start(bf16[512,256]{1,0:T(8,128)(2,1)S(1)} %collective-permute-done.16.refs_14_.refs_22_.refs_6_) | copy-start | bytes 786436
  115.9 24.3 %collective-permute-start.3 = (bf16[512,256]{1,0:T(8,128)(2,1)S(1)}, bf16[512,256]{1,0:T(8,128)(2,1)S(1)}, u32[]{:S(2)}, u32[]{:S(2)}) collective-permute-start(bf16[512,256]{1,0:T(8,128)(2,1)S(1)} %copy-done.25), channel_id=1, source_target_pairs={{0,1},{1,0},{2,3},{3,2},{4,5},{5,4},{6,7},{7,6},{8,9},{9,8},{10,11... | collective-permute-start | bytes 786440 | tf_op jit(solution)/shard_map/b1/ppermute | solution.py:23
  123.9 40.0 %copy-start.2 = (bf16[512,256]{1,0:T(8,128)(2,1)}, bf16[512,256]{1,0:T(8,128)(2,1)S(1)}, u32[]{:S(2)}) copy-start(bf16[512,256]{1,0:T(8,128)(2,1)S(1)} %collective-permute-done.13.refs_13_.refs_21_.refs_5_) | copy-start | bytes 786436
  123.9 36.9 %collective-permute-start.21 = (bf16[480,256]{1,0:T(8,128)(2,1)S(1)}, bf16[480,256]{1,0:T(8,128)(2,1)S(1)}, u32[]{:S(2)}, u32[]{:S(2)}) collective-permute-start(bf16[480,256]{1,0:T(8,128)(2,1)S(1)} %copy-done.30), channel_id=1, source_target_pairs={{0,1},{1,0},{2,3},{3,2},{4,5},{5,4},{6,7},{7,6},{8,9},{9,8},{10,11... | collective-permute-start | bytes 737288 | tf_op jit(solution)/shard_map/a1/ppermute | solution.py:23
  128.8 35.1 %copy-start.3 = (bf16[512,256]{1,0:T(8,128)(2,1)}, bf16[512,256]{1,0:T(8,128)(2,1)S(1)}, u32[]{:S(2)}) copy-start(bf16[512,256]{1,0:T(8,128)(2,1)S(1)} %collective-permute-done.10.refs_12_.refs_20_.refs_4_) | copy-start | bytes 786436
  128.8 31.9 %collective-permute-start.22 = (bf16[480,256]{1,0:T(8,128)(2,1)S(1)}, bf16[480,256]{1,0:T(8,128)(2,1)S(1)}, u32[]{:S(2)}, u32[]{:S(2)}) collective-permute-start(bf16[480,256]{1,0:T(8,128)(2,1)S(1)} %copy-done.29), channel_id=1, source_target_pairs={{0,2},{1,3},{2,0},{3,1},{4,6},{5,7},{6,4},{7,5},{8,10},{9,11},{10,... | collective-permute-start | bytes 737288 | tf_op jit(solution)/shard_map/a2/ppermute | solution.py:23
  134.6 29.3 %copy-start.4 = (bf16[512,256]{1,0:T(8,128)(2,1)}, bf16[512,256]{1,0:T(8,128)(2,1)S(1)}, u32[]{:S(2)}) copy-start(bf16[512,256]{1,0:T(8,128)(2,1)S(1)} %collective-permute-done.7.refs_11_.refs_19_.refs_3_) | copy-start | bytes 786436
  134.7 29.1 %collective-permute-start.23 = (bf16[480,256]{1,0:T(8,128)(2,1)S(1)}, bf16[480,256]{1,0:T(8,128)(2,1)S(1)}, u32[]{:S(2)}, u32[]{:S(2)}) collective-permute-start(bf16[480,256]{1,0:T(8,128)(2,1)S(1)} %copy-done.28), channel_id=1, source_target_pairs={{0,3},{1,2},{2,1},{3,0},{4,7},{5,6},{6,5},{7,4},{8,11},{9,10},{10,... | collective-permute-start | bytes 737288 | tf_op jit(solution)/shard_map/a3/ppermute | solution.py:23
  139.4 24.5 %copy-start.5 = (bf16[512,256]{1,0:T(8,128)(2,1)}, bf16[512,256]{1,0:T(8,128)(2,1)S(1)}, u32[]{:S(2)}) copy-start(bf16[512,256]{1,0:T(8,128)(2,1)S(1)} %collective-permute-done.5.refs_10_.refs_18_.refs_2_) | copy-start | bytes 786436
  139.4 7.7 %collective-permute-start.20 = (bf16[336,256]{1,0:T(8,128)(2,1)}, bf16[336,256]{1,0:T(8,128)(2,1)S(1)}, u32[]{:S(2)}, u32[]{:S(2)}) collective-permute-start(bf16[336,256]{1,0:T(8,128)(2,1)} %get-tuple-element.106), channel_id=1, source_target_pairs={{0,7},{1,6},{2,5},{3,4},{4,3},{5,2},{6,1},{7,0},{8,15},{9,14},{10,... | collective-permute-start | bytes 516104 | tf_op jit(solution)/shard_map/c7/ppermute | solution.py:23
  140.2 23.7 %copy-start.6 = (bf16[512,256]{1,0:T(8,128)(2,1)}, bf16[512,256]{1,0:T(8,128)(2,1)S(1)}, u32[]{:S(2)}) copy-start(bf16[512,256]{1,0:T(8,128)(2,1)S(1)} %collective-permute-done.3.refs_9_.refs_17_.refs_1_) | copy-start | bytes 786436
  140.3 12.5 %collective-permute-start.17 = (bf16[336,256]{1,0:T(8,128)(2,1)}, bf16[336,256]{1,0:T(8,128)(2,1)S(1)}, u32[]{:S(2)}, u32[]{:S(2)}) collective-permute-start(bf16[336,256]{1,0:T(8,128)(2,1)} %get-tuple-element.101), channel_id=1, source_target_pairs={{0,6},{1,7},{2,4},{3,5},{4,2},{5,3},{6,0},{7,1},{8,14},{9,15},{10,... | collective-permute-start | bytes 516104 | tf_op jit(solution)/shard_map/c6/ppermute | solution.py:23
  147.2 24.8 %copy-start.7 = (bf16[336,256]{1,0:T(8,128)(2,1)}, bf16[336,256]{1,0:T(8,128)(2,1)S(1)}, u32[]{:S(2)}) copy-start(bf16[336,256]{1,0:T(8,128)(2,1)S(1)} %collective-permute-done.20.refs_7_.refs_15_) | copy-start | bytes 516100
  147.2 29.6 %collective-permute-start.14 = (bf16[336,256]{1,0:T(8,128)(2,1)}, bf16[336,256]{1,0:T(8,128)(2,1)S(1)}, u32[]{:S(2)}, u32[]{:S(2)}) collective-permute-start(bf16[336,256]{1,0:T(8,128)(2,1)} %get-tuple-element.96), channel_id=1, source_target_pairs={{0,5},{1,4},{2,7},{3,6},{4,1},{5,0},{6,3},{7,2},{8,13},{9,12},{10,... | collective-permute-start | bytes 516104 | tf_op jit(solution)/shard_map/c5/ppermute | solution.py:23
  152.7 19.3 %copy-start.8 = (bf16[336,256]{1,0:T(8,128)(2,1)}, bf16[336,256]{1,0:T(8,128)(2,1)S(1)}, u32[]{:S(2)}) copy-start(bf16[336,256]{1,0:T(8,128)(2,1)S(1)} %collective-permute-done.17.refs_6_.refs_14_) | copy-start | bytes 516100
  152.7 24.1 %collective-permute-start.11 = (bf16[336,256]{1,0:T(8,128)(2,1)}, bf16[336,256]{1,0:T(8,128)(2,1)S(1)}, u32[]{:S(2)}, u32[]{:S(2)}) collective-permute-start(bf16[336,256]{1,0:T(8,128)(2,1)} %get-tuple-element.91), channel_id=1, source_target_pairs={{0,4},{1,5},{2,6},{3,7},{4,0},{5,1},{6,2},{7,3},{8,12},{9,13},{10,... | collective-permute-start | bytes 516104 | tf_op jit(solution)/shard_map/c4/ppermute | solution.py:23
  160.7 3.2 %copy-start.18 = (bf16[480,256]{1,0:T(8,128)(2,1)}, bf16[480,256]{1,0:T(8,128)(2,1)S(1)}, u32[]{:S(2)}) copy-start(bf16[480,256]{1,0:T(8,128)(2,1)S(1)} %collective-permute-done.21.refs_1_) | copy-start | bytes 737284
  160.7 16.1 %collective-permute-start.8 = (bf16[336,256]{1,0:T(8,128)(2,1)}, bf16[336,256]{1,0:T(8,128)(2,1)S(1)}, u32[]{:S(2)}, u32[]{:S(2)}) collective-permute-start(bf16[336,256]{1,0:T(8,128)(2,1)} %get-tuple-element.86), channel_id=1, source_target_pairs={{0,3},{1,2},{2,1},{3,0},{4,7},{5,6},{6,5},{7,4},{8,11},{9,10},{10,... | collective-permute-start | bytes 516104 | tf_op jit(solution)/shard_map/c3/ppermute | solution.py:23
  160.8 3.2 %copy-start.19 = (bf16[480,256]{1,0:T(8,128)(2,1)}, bf16[480,256]{1,0:T(8,128)(2,1)S(1)}, u32[]{:S(2)}) copy-start(bf16[480,256]{1,0:T(8,128)(2,1)S(1)} %collective-permute-done.22.refs_2_) | copy-start | bytes 737284
  160.8 16.0 %collective-permute-start.6 = (bf16[336,256]{1,0:T(8,128)(2,1)}, bf16[336,256]{1,0:T(8,128)(2,1)S(1)}, u32[]{:S(2)}, u32[]{:S(2)}) collective-permute-start(bf16[336,256]{1,0:T(8,128)(2,1)} %get-tuple-element.82), channel_id=1, source_target_pairs={{0,2},{1,3},{2,0},{3,1},{4,6},{5,7},{6,4},{7,5},{8,10},{9,11},{10,... | collective-permute-start | bytes 516104 | tf_op jit(solution)/shard_map/c2/ppermute | solution.py:23
  163.8 0.7 copy-start.20
  163.8 13.0 %collective-permute-start.4 = (bf16[336,256]{1,0:T(8,128)(2,1)}, bf16[336,256]{1,0:T(8,128)(2,1)S(1)}, u32[]{:S(2)}, u32[]{:S(2)}) collective-permute-start(bf16[336,256]{1,0:T(8,128)(2,1)} %get-tuple-element.78), channel_id=1, source_target_pairs={{0,1},{1,0},{2,3},{3,2},{4,5},{5,4},{6,7},{7,6},{8,9},{9,8},{10,11... | collective-permute-start | bytes 516104 | tf_op jit(solution)/shard_map/c1/ppermute | solution.py:23
  176.8 0.7 copy-start.9
  176.8 0.7 copy-start.10
  176.8 0.8 copy-start.11
  176.8 0.8 copy-start.12
  177.6 0.7 copy-start.13

commit v3 on v2

v3 whole, which is shorter than its diff:
```python
import functools

import jax
import jax.numpy as jnp
from jax import lax
from jax.experimental import pallas as pl
from jax.experimental.pallas import tpu as pltpu
from jax.sharding import PartitionSpec as P

GROUPS = 32
EPS = 1e-05
STAT_ROWS = 16
VMEM_BYTES = 60 * 1024 * 1024


def passed_along(array, axis, by):
    length = lax.axis_size(axis)
    pairs = [(i, i + by) for i in range(length) if 0 <= i + by < length]
    return lax.ppermute(array, axis, pairs)


def exchanged(array, axis, flip):
    length = lax.axis_size(axis)
    return lax.ppermute(array, axis, [(i, i ^ flip) for i in range(length)])


def after(array, *earlier):
    return lax.optimization_barrier((array, *earlier))[0]


def rounded_up(rows):
    return -(-rows // 16) * 16


def split_columns(row_ref, slab_ref):
    width, ci = row_ref.shape
    half = width // 2
    slab_ref[:, 0:ci] = row_ref[pl.ds(0, half, stride=2), :]
    slab_ref[:, ci:] = row_ref[pl.ds(1, half, stride=2), :]


def split_three(total):
    high = total.astype(jnp.bfloat16).astype(jnp.float32)
    rest = total - high
    middle = rest.astype(jnp.bfloat16).astype(jnp.float32)
    return [high, middle, rest - middle]


def conv_kernel(plan, clip_ref, place_ref, x_ref, above_ref, w_ref, *refs):
    jobs, parts, part_rows, part_width = (
        plan["jobs"], plan["parts"], plan["part_rows"], plan["part_width"])
    lead, steps, tap_first = plan["lead"], plan["steps"], plan["tap_first"]

    def take(number):
        nonlocal refs
        some, refs = refs[:number], refs[number:]
        return some

    add_refs = take(plan["addends"])
    sums_refs = take(plan["sums_in"])
    take(plan["kept"])
    out_refs = take(parts if parts else len(jobs))
    sums_out = take(1 if plan["sums_out"] else 0)
    sources, ci = x_ref.shape[0], x_ref.shape[3]
    slab_refs, main_refs, left_refs = take(sources), take(len(jobs)), take(len(jobs))
    part_ref, stat_ref = refs
    step = pl.program_id(0)
    half, co = main_refs[0].shape
    above = lax.rem(step + 1, 2)
    below = lax.rem(step, 2)
    start = place_ref[0]
    last = clip_ref.shape[0] - 1

    @pl.when(step == 0)
    def _():
        for source in range(sources):
            split_columns(above_ref.at[source, 0], slab_refs[source].at[1])
        for left_ref in left_refs:
            left_ref[0:8] = jnp.zeros((8, co), jnp.float32)
        stat_ref[...] = jnp.zeros_like(stat_ref)

    def products(source, tap):
        slab_ref, tap = slab_refs[source], tap - tap_first
        rows = [slab_ref[above], slab_ref[2], slab_ref[below]]
        main = jnp.dot(
            jnp.concatenate(rows, axis=1),
            jnp.concatenate([w_ref[tap, (3 * a + 1) * ci : (3 * a + 3) * ci] for a in range(3)], axis=0),
            preferred_element_type=jnp.float32)
        left = jnp.dot(
            jnp.concatenate([row[:, ci:] for row in rows], axis=1),
            jnp.concatenate([w_ref[tap, 3 * a * ci : (3 * a + 1) * ci] for a in range(3)], axis=0),
            preferred_element_type=jnp.float32)
        return main, left

    empty = [True] * len(jobs)
    for source in range(sources):
        split_columns(x_ref.at[source, 0], slab_refs[source].at[2])
        split_columns(x_ref.at[source, 1], slab_refs[source].at[below])
        frame = plan["first"] + source
        for at, (target, taps, addend) in enumerate(jobs):
            for tap in [tap for other, tap in taps if other == source]:
                main, left = products(source, tap)
                if frame != target:
                    same = clip_ref[start + frame] == clip_ref[jnp.minimum(start + target, last)]
                    same = same.astype(jnp.float32)
                    main, left = main * same, left * same
                if empty[at]:
                    if addend is not None:
                        main = main + add_refs[addend][0].astype(jnp.float32)
                    main_refs[at][...] = main
                    left_refs[at][8:] = left
                else:
                    main_refs[at][...] += main
                    left_refs[at][8:] += left
                empty[at] = False

    for at in range(len(jobs)):
        total = main_refs[at][...] + left_refs[at][7 : 7 + half]
        if not parts:
            out_refs[at][0] = total.astype(jnp.bfloat16)
            continue
        rounded = total.astype(jnp.bfloat16).astype(jnp.float32)
        tiles = rounded.reshape(half // 8, 8, co)
        stat_ref[2 * at] += jnp.sum(tiles, axis=0)
        stat_ref[2 * at + 1] += jnp.sum(tiles * tiles, axis=0)
        for part in range(parts):
            piece = rounded[part * part_width : (part + 1) * part_width]
            part_ref[at, part, 0:part_width] = piece.astype(jnp.bfloat16)
        mine = place_ref[1]
        for flip in range(parts):
            offset = pl.multiple_of(lead + (at * steps + step) * part_rows, 16)
            out_refs[flip][pl.ds(offset, part_rows)] = part_ref[at, mine ^ flip]

    if parts:
        @pl.when(step == steps - 1)
        def _():
            if sums_out:
                sums_out[0][...] = stat_ref[...]
                return
            rows = []
            for at in range(2 * len(jobs)):
                total = stat_ref[at]
                for ref in sums_refs:
                    total = total + ref[at]
                rows += split_three(jnp.sum(total, axis=0, keepdims=True))
            blank = jnp.zeros((STAT_ROWS - len(rows), co), jnp.float32)
            closing = jnp.concatenate(rows + [blank], axis=0).astype(jnp.bfloat16)
            for flip in range(parts):
                out_refs[flip][0:STAT_ROWS] = closing


def conv_frames(frames, halo, weight, clip_ids, place, first, sources, jobs, row=0, steps=None,
                addends=(), parts=0, sums=(), sums_out=False, lead=0, kept=(), weigh=1):
    _, band, width, ci = frames.shape
    co = weight.shape[2]
    half = width // 2
    steps = steps or band // 2
    part_width = half // parts if parts else half
    part_rows = rounded_up(part_width)
    taps = sorted({tap for _, some, _ in jobs for _, tap in some})
    tap_first, tap_count = 0, 3
    if len(taps) == 1 or taps == [0, 1]:
        tap_first, tap_count = taps[0], len(taps)
    plan = dict(jobs=jobs, addends=len(addends), parts=parts, part_rows=part_rows, lead=lead,
                part_width=part_width, first=first, steps=steps, kept=len(kept),
                sums_in=len(sums), sums_out=sums_out, tap_first=tap_first)
    block = first // sources
    above = (frames, 2 * row - 1) if row else (halo, 0)
    in_specs = [
        pl.BlockSpec((sources, 2, width, ci), lambda i, *_: (block, row + i, 0, 0)),
        pl.BlockSpec((sources, 1, width, ci), lambda i, *_: (block, above[1], 0, 0)),
        pl.BlockSpec((tap_count, 9 * ci, co), lambda i, *_: (tap_first // tap_count, 0, 0)),
    ]
    in_specs += [pl.BlockSpec((1, None, half, co), lambda i, *_: (0, i, 0, 0)) for _ in addends]
    in_specs += [pl.BlockSpec(a.shape, lambda i, *_: (0, 0, 0)) for a in sums]
    in_specs += [pl.BlockSpec(memory_space=pl.ANY) for _ in kept]
    operands = [clip_ids, place, frames, above[0], weight, *addends, *sums, *kept]
    aliases = {len(operands) - len(kept) + at: at for at in range(len(kept))}
    if parts:
        rows = lead + len(jobs) * steps * part_rows
        shape = kept[0].shape if kept else (rows, co)
        out_shape = [jax.ShapeDtypeStruct(shape, jnp.bfloat16) for _ in range(parts)]
        out_specs = [pl.BlockSpec((rows, co), lambda i, *_: (0, 0)) for _ in range(parts)]
    else:
        out_shape = [jax.ShapeDtypeStruct((1, steps, half, co), jnp.bfloat16) for _ in jobs]
        out_specs = [pl.BlockSpec((1, None, half, co), lambda i, *_: (0, i, 0, 0)) for _ in jobs]
    if sums_out:
        shape = (2 * len(jobs), 8, co)
        out_shape.append(jax.ShapeDtypeStruct(shape, jnp.float32))
        out_specs.append(pl.BlockSpec(shape, lambda i, *_: (0, 0, 0)))
    products = sum(len(some) for _, some, _ in jobs)
    return pl.pallas_call(
        functools.partial(conv_kernel, plan),
        out_shape=out_shape,
        grid_spec=pltpu.PrefetchScalarGridSpec(
            num_scalar_prefetch=2,
            grid=(steps,),
            in_specs=in_specs,
            out_specs=out_specs,
            scratch_shapes=[
                *[pltpu.VMEM((3, half, 2 * ci), jnp.bfloat16) for _ in range(sources)],
                *[pltpu.VMEM((half, co), jnp.float32) for _ in jobs],
                *[pltpu.VMEM((8 + half, co), jnp.float32) for _ in jobs],
                pltpu.VMEM((len(jobs), max(parts, 1), part_rows, co), jnp.bfloat16),
                pltpu.VMEM((2 * len(jobs), 8, co), jnp.float32),
            ],
        ),
        input_output_aliases=aliases,
        cost_estimate=pl.CostEstimate(
            flops=2 * weigh * products * steps * half * 9 * ci * co,
            bytes_accessed=weigh * (4 * sources * steps * width * ci + 2 * len(jobs) * steps * half * co),
            transcendentals=0,
        ),
        compiler_params=pltpu.CompilerParams(vmem_limit_bytes=VMEM_BYTES),
    )(*operands)


def norm_kernel(plan, place_ref, *refs):
    parts, jobs, steps, rows = plan["parts"], plan["jobs"], plan["steps"], plan["rows"]
    lead, part_rows = plan["lead"], plan["part_rows"]
    data_refs, (gain_ref, bias_ref) = refs[:parts], refs[parts : parts + 2]
    out_ref, scale_ref = refs[-2:]
    frame, step = pl.program_id(0), pl.program_id(1)
    part_width, co = out_ref.shape[-2:]

    @pl.when((frame == 0) & (step == 0))
    def _():
        total = data_refs[0][0:STAT_ROWS].astype(jnp.float32)
        for flip in range(1, parts):
            total = total + data_refs[flip][0:STAT_ROWS].astype(jnp.float32)
        size = co // GROUPS
        same = (lax.broadcasted_iota(jnp.int32, (co, co), 0) // size
                == lax.broadcasted_iota(jnp.int32, (co, co), 1) // size).astype(jnp.float32)
        grouped = jnp.dot(total, same, precision=lax.Precision.HIGHEST,
                          preferred_element_type=jnp.float32)
        for at in range(jobs):
            def taken(which):
                base = 6 * at + 3 * which
                return grouped[base : base + 1] + grouped[base + 1 : base + 2] + grouped[base + 2 : base + 3]
            mean = taken(0) / plan["entries"]
            variance = taken(1) / plan["entries"] - mean * mean
            scale_ref[at, 0:1] = mean
            scale_ref[at, 1:2] = lax.rsqrt(variance + EPS) * gain_ref[...]

    mean = scale_ref[frame, 0:1]
    scale = scale_ref[frame, 1:2]
    bias = bias_ref[...]
    mine = place_ref[1]
    for at in range(rows):
        row = step * rows + at
        if plan["top_first"]:
            place = jnp.where(row == 0, frame, jobs + frame * (steps - 1) + row - 1)
        else:
            place = frame * steps + row
        offset = pl.multiple_of(lead + place * part_rows, 16)
        for flip in range(parts):
            values = data_refs[flip][pl.ds(offset, part_rows)][0:part_width].astype(jnp.float32)
            value = 0.5 * ((values - mean) * scale + bias)
            out_ref[0, mine ^ flip, at] = (value + value * jnp.tanh(value)).astype(jnp.bfloat16)


def norm_frames(messages, gain, bias, place, first, jobs, shape, top_first=False, base=None):
    frames, parts, steps, part_width, co = shape
    rows = 2 if steps % 2 == 0 else 1
    plan = dict(parts=parts, jobs=jobs, steps=steps, rows=rows, lead=STAT_ROWS,
                part_rows=rounded_up(part_width), top_first=top_first,
                entries=float(parts * steps * part_width * parts * (co // GROUPS)))
    in_specs = (
        [pl.BlockSpec(message.shape, lambda f, i, *_: (0, 0)) for message in messages]
        + [pl.BlockSpec((1, co), lambda f, i, *_: (0, 0))] * 2
    )
    operands = [place, *messages, gain, bias]
    aliases = {}
    if base is not None:
        in_specs.append(pl.BlockSpec(memory_space=pl.ANY))
        aliases = {len(operands): 0}
        operands.append(base)
    return pl.pallas_call(
        functools.partial(norm_kernel, plan),
        out_shape=jax.ShapeDtypeStruct(shape, jnp.bfloat16),
        grid_spec=pltpu.PrefetchScalarGridSpec(
            num_scalar_prefetch=1,
            grid=(jobs, steps // rows),
            in_specs=in_specs,
            out_specs=pl.BlockSpec(
                (1, parts, rows, part_width, co), lambda f, i, *_: (first + f, 0, i, 0, 0)),
            scratch_shapes=[pltpu.VMEM((jobs, 8, co), jnp.float32)],
        ),
        input_output_aliases=aliases,
        cost_estimate=pl.CostEstimate(
            flops=8 * jobs * parts * steps * part_width * co,
            bytes_accessed=4 * jobs * parts * steps * part_width * co,
            transcendentals=jobs * parts * steps * part_width * co,
        ),
        compiler_params=pltpu.CompilerParams(vmem_limit_bytes=VMEM_BYTES),
    )(*operands)


def on_device(frames, clip_ids, conv_weight, norm_gain, norm_bias):
    count, band, width, ci = frames.shape
    co = conv_weight.shape[4]
    parts = lax.axis_size("rows")
    place = jnp.stack([lax.axis_index("tm") * count, lax.axis_index("rows")]).astype(jnp.int32)
    weight = conv_weight.reshape(3, 9 * ci, co)
    gain, bias = norm_gain.reshape(1, co), norm_bias.reshape(1, co)
    steps = band // 2
    shape = (count, parts, steps, width // 2 // parts, co)
    part_rows = rounded_up(shape[3])
    top_rows = STAT_ROWS + 2 * part_rows

    def named(name, function, *args, **keywords):
        with jax.named_scope(name):
            return function(*args, **keywords)

    halo = named("halo", passed_along, frames[:, -1:], "rows", 1)
    far = [flip for flip in range(parts - 1, 0, -1) if 2 * flip >= parts]
    near = [flip for flip in range(parts - 1, 0, -1) if 2 * flip < parts]

    later = [(2, [(0, 0), (1, 1), (2, 2)], None), (3, [(1, 0), (2, 1), (3, 2)], None)]
    run = functools.partial(conv_frames, frames, halo, weight, clip_ids, place)
    *a_sent, a_sums = named("conv_a", run, 0, 4, later, row=1, steps=steps - 1, parts=parts,
                            sums_out=True, lead=top_rows, weigh=1)
    a_sent = named("conv_top", run, 0, 4, later, steps=1, parts=parts, sums=(a_sums,),
                   lead=STAT_ROWS, kept=a_sent, weigh=1)
    run = functools.partial(conv_frames, frames, after(halo, a_sent[0]), weight, clip_ids, place)
    onward, = named("conv_hist0", run, 2, 2, [(4, [(0, 0), (1, 1)], None)])
    first_add = named("hist0", passed_along, onward, "tm", 1)
    run = functools.partial(conv_frames, frames, after(halo, onward), weight, clip_ids, place)
    onward, = named("conv_hist1", run, 3, 1, [(5, [(0, 0)], None)], weigh=40)
    second_add = named("hist1", passed_along, after(onward, first_add), "tm", 1)
    b_sent = named("conv_b", run, 0, 1, [(0, [(0, 2)], 0)], addends=(after(first_add, onward),), parts=parts,
                   lead=STAT_ROWS, weigh=20)
    c_sent = named("conv_c", run, 0, 2, [(1, [(0, 1), (1, 2)], 0)], addends=(second_add,), parts=parts,
                   lead=STAT_ROWS, weigh=20)

    a_got, b_got, c_got = {}, {}, {}
    chain = []
    for name, sent, got in (("a", a_sent, a_got), ("b", b_sent, b_got), ("c", c_sent, c_got)):
        for flip in far:
            earlier = chain[-4:][:1] if len(chain) >= 4 else []
            got[flip] = named(f"{name}{flip}", exchanged, after(sent[flip], *earlier), "rows", flip)
            chain.append(got[flip])
    for name, sent, got, earlier in (("a", a_sent, a_got, a_sums), ("b", b_sent, b_got, c_sent[0]), ("c", c_sent, c_got, c_sent[0])):
        for flip in near:
            got[flip] = named(f"{name}{flip}", exchanged, after(sent[flip], earlier), "rows", flip)

    def whole(sent, got):
        return [sent[0]] + [got[flip] for flip in range(1, parts)]

    a_all, b_all, c_all = whole(a_sent, a_got), whole(b_sent, b_got), whole(c_sent, c_got)
    out = named("norm_a", norm_frames, a_all, gain, bias, place, 2, 2, shape, top_first=True)
    out = named("norm_b", norm_frames, b_all, gain, bias, place, 0, 1, shape, base=out)
    out = named("norm_c", norm_frames, c_all, gain, bias, place, 1, 1, shape, base=out)
    return out.reshape(count, parts * steps, shape[3], co)


def solution(mesh):
    in_specs = (P("tm", "rows", None, None), P(), P(), P(), P())
    out_specs = P("tm", None, "rows", None)
    return jax.shard_map(
        on_device, mesh=mesh, in_specs=in_specs, out_specs=out_specs, check_vma=False
    )
```

time: 185 us -> 167 us (0.903)
  the two profiles are of different devices: /device:TPU:4 before, /device:TPU:15 now
where the time goes in v3:
time: 167 us; the launch traced here: 166 us
  Pallas kernels  66.8 us (40%)
  waiting for transfers between devices  66.7 us (40%)
  starting transfers between devices  27.9 us (17%)
  local copies, waits for them, and re-layouts  3.98 us (2%)
    pallas_call x6, Pallas kernels, conv_frames(): pl.pallas_call(functools.partial(conv_kernel, plan), out_shape=out_shape,...  52.4 us
    ppermute x21, waiting for transfers between devices, exchanged(): return lax.ppermute(array, axis, [(i, i ^ flip) for i in range(length)])  40.5 us
    ppermute x3, waiting for transfers between devices, passed_along(): return lax.ppermute(array, axis, pairs)  26.2 us
    ppermute x21, starting transfers between devices, exchanged(): return lax.ppermute(array, axis, [(i, i ^ flip) for i in range(length)])  21.4 us
    pallas_call x3, Pallas kernels, norm_frames(): pl.pallas_call(functools.partial(norm_kernel, plan), out_shape=jax.ShapeD...  14.4 us
    ppermute x3, starting transfers between devices, passed_along(): return lax.ppermute(array, axis, pairs)  6.51 us
  transfers between devices with their start and end apart: 24, of which 10 were waited for; matrix products, arithmetic and copies ran while one was open for 0% of the time, Pallas kernels for 33%

profile of v3, /device:TPU:15, one launch (start us, length us, event | category | flops | bytes accessed | tf_op | source)
XLA Modules:
  0.0 166.3 jit_solution(764556136468203337)
XLA Ops:
  0.0 1.4 slice.3
  1.4 3.8 %collective-permute-start = (bf16[4,1,1280,128]{3,2,1,0:T(8,128)(2,1)S(1)}, bf16[4,1,1280,128]{3,2,1,0:T(8,128)(2,1)S(1)}, u32[]{:S(2)}, u32[]{:S(2)}) collective-permute-start(bf16[4,1,1280,128]{3,2,1,0:T(8,128)(2,1)S(1)} %slice.3), channel_id=1, source_target_pairs={{0,1},{1,2},{2,3},{3,4},{4,5},{5,6},{6,7},{8,9},{9,10},{10,11},{11... | collective-permute-start | bytes 3932168 | tf_op jit(solution)/shard_map/halo/ppermute | solution.py:19
  5.2 0.6 pad_add_fusion.place_ref
  5.8 14.5 %conv_a.1 = (bf16[656,256]{1,0:T(8,128)(2,1)}, bf16[656,256]{1,0:T(8,128)(2,1)}, bf16[656,256]{1,0:T(8,128)(2,1)}, bf16[656,256]{1,0:T(8,128)(2,1)}, bf16[656,25...) custom-call(s32[16]{0:T(128)} %clip_ref.11, ...), custom_call_target="tpu_custom_call" | custom-call | flops 6794772480 | bytes 9830400 | tf_op jit(solution)/shard_map/conv_a/pallas_call | solution.py:192
  20.2 0.0 collective-permute-done.above_ref
  20.3 1.0 copy-done
  21.3 7.1 %conv_top.1 = (bf16[656,256]{1,0:T(8,128)(2,1)}, bf16[656,256]{1,0:T(8,128)(2,1)}, bf16[656,256]{1,0:T(8,128)(2,1)}, bf16[656,256]{1,0:T(8,128)(2,1)}, bf16[656,...) custom-call(s32[16]{0:T(128)} %clip_ref.11, ...), custom_call_target="tpu_custom_call", output_to_operand_aliasing={{0}: (6, {}), {1}: (7, {}), {2}: (8, {}), {3}: (9, {}), {4}... | custom-call | flops 2264924160 | bytes 3276800 | tf_op jit(solution)/shard_map/conv_top/pallas_call | solution.py:192
  28.4 3.0 %collective-permute-start.9 = (bf16[656,256]{1,0:T(8,128)(2,1)}, bf16[656,256]{1,0:T(8,128)(2,1)S(1)}, u32[]{:S(2)}, u32[]{:S(2)}) collective-permute-start(bf16[656,256]{1,0:T(8,128)(2,1)} %get-tuple-element.87), channel_id=1, source_target_pairs={{0,5},{1,4},{2,7},{3,6},{4,1},{5,0},{6,3},{7,2},{8,13},{9,12},{10,... | collective-permute-start | bytes 1007624 | tf_op jit(solution)/shard_map/a5/ppermute | solution.py:24
  31.3 0.1 collective-permute-start.6
  31.4 1.3 collective-permute-start.12
  32.7 0.7 collective-permute-start.15
  33.4 8.3 %conv_hist0.1 = bf16[1,4,640,256]{3,2,1,0:T(8,128)(2,1)} custom-call(s32[16]{0:T(128)} %clip_ref.11, s32[2]{0:T(128)} %pad_add_fusion.place_ref, bf16[4,8,1280,128]{3,2,1,0:T(8,128)(2,1)} %x_ref.11, bf16[4,1,1280,128]{3,2,1,0:T(8,128)(2,1)} %copy-done, bf16[3,1152,256]{2,1,0:T(8,128)(2,1)} %bitcast.8), custom_call_target="tpu_custom_call" | custom-call | flops 3019898880 | bytes 6553600 | tf_op jit(solution)/shard_map/conv_hist0/pallas_call | solution.py:192
  41.7 1.3 collective-permute-start.1
  43.0 6.2 %conv_hist1.1 = bf16[1,4,640,256]{3,2,1,0:T(8,128)(2,1)} custom-call(s32[16]{0:T(128)} %clip_ref.11, s32[2]{0:T(128)} %pad_add_fusion.place_ref, bf16[4,8,1280,128]{3,2,1,0:T(8,128)(2,1)} %x_ref.11, bf16[4,1,1280,128]{3,2,1,0:T(8,128)(2,1)} %copy-done, bf16[3,1152,256]{2,1,0:T(8,128)(2,1)} %bitcast.9), custom_call_target="tpu_custom_call" | custom-call | flops 60397977600 | bytes 157286400 | tf_op jit(solution)/shard_map/conv_hist1/pallas_call | solution.py:192
  49.2 25.2 %collective-permute-done.1.refs_0_ = bf16[1,4,640,256]{3,2,1,0:T(8,128)(2,1)} collective-permute-done((bf16[1,4,640,256]{3,2,1,0:T(8,128)(2,1)}, bf16[1,4,640,256]{3,2,1,0:T(8,128)(2,1)}, u32[]{:S(2)}, u32[]{:S(2)}) %collective-permute-start.1) | collective-permute-done | bytes 1310752 | tf_op jit(solution)/shard_map/hist0/ppermute | solution.py:19
  74.4 1.5 collective-permute-start.2
  75.9 7.2 %conv_b.1 = (bf16[336,256]{1,0:T(8,128)(2,1)}, bf16[336,256]{1,0:T(8,128)(2,1)}, bf16[336,256]{1,0:T(8,128)(2,1)}, bf16[336,256]{1,0:T(8,128)(2,1)}, bf16[336,25...) custom-call(s32[16]{0:T(128)} %clip_ref.11, ...), custom_call_target="tpu_custom_call" | custom-call | flops 30198988800 | bytes 78643200 | tf_op jit(solution)/shard_map/conv_b/pallas_call | solution.py:192
  83.1 13.0 %collective-permute-done.15.refs_7_ = bf16[656,256]{1,0:T(8,128)(2,1)S(1)} collective-permute-done((bf16[656,256]{1,0:T(8,128)(2,1)}, bf16[656,256]{1,0:T(8,128)(2,1)S(1)}, u32[]{:S(2)}, u32[]{:S(2)}) %collective-permute-start.15) | collective-permute-done | bytes 335904 | tf_op jit(solution)/shard_map/a7/ppermute | solution.py:24
  96.1 2.4 %collective-permute-start.16 = (bf16[336,256]{1,0:T(8,128)(2,1)}, bf16[336,256]{1,0:T(8,128)(2,1)S(1)}, u32[]{:S(2)}, u32[]{:S(2)}) collective-permute-start(bf16[336,256]{1,0:T(8,128)(2,1)} %get-tuple-element.98), channel_id=1, source_target_pairs={{0,7},{1,6},{2,5},{3,4},{4,3},{5,2},{6,1},{7,0},{8,15},{9,14},{10,... | collective-permute-start | bytes 516104 | tf_op jit(solution)/shard_map/b7/ppermute | solution.py:24
  98.5 0.0 collective-permute-done.12.refs_6_
  98.5 0.0 collective-permute-start.13
  98.5 0.0 collective-permute-done.6.refs_4_
  98.5 0.1 collective-permute-start.23
  98.6 0.0 collective-permute-done.9.refs_5_
  98.6 1.8 %collective-permute-start.22 = (bf16[656,256]{1,0:T(8,128)(2,1)S(1)}, bf16[656,256]{1,0:T(8,128)(2,1)S(1)}, u32[]{:S(2)}, u32[]{:S(2)}) collective-permute-start(bf16[656,256]{1,0:T(8,128)(2,1)S(1)} %copy-done.9), channel_id=1, source_target_pairs={{0,2},{1,3},{2,0},{3,1},{4,6},{5,7},{6,4},{7,5},{8,10},{9,11},{10,... | collective-permute-start | bytes 1007624 | tf_op jit(solution)/shard_map/a2/ppermute | solution.py:24
  100.4 2.4 %collective-permute-done.16.refs_7_ = bf16[336,256]{1,0:T(8,128)(2,1)S(1)} collective-permute-done((bf16[336,256]{1,0:T(8,128)(2,1)}, bf16[336,256]{1,0:T(8,128)(2,1)S(1)}, u32[]{:S(2)}, u32[]{:S(2)}) %collective-permute-start.16) | collective-permute-done | bytes 172064 | tf_op jit(solution)/shard_map/b7/ppermute | solution.py:24
  102.8 0.0 collective-permute-start.21
  102.8 2.4 %collective-permute-done.13.refs_6_ = bf16[336,256]{1,0:T(8,128)(2,1)S(1)} collective-permute-done((bf16[336,256]{1,0:T(8,128)(2,1)}, bf16[336,256]{1,0:T(8,128)(2,1)S(1)}, u32[]{:S(2)}, u32[]{:S(2)}) %collective-permute-start.13) | collective-permute-done | bytes 172064 | tf_op jit(solution)/shard_map/b6/ppermute | solution.py:24
  105.2 0.0 collective-permute-start.10
  105.2 1.0 collective-permute-done.2.refs_0_
  106.2 2.2 %collective-permute-start.7 = (bf16[336,256]{1,0:T(8,128)(2,1)}, bf16[336,256]{1,0:T(8,128)(2,1)S(1)}, u32[]{:S(2)}, u32[]{:S(2)}) collective-permute-start(bf16[336,256]{1,0:T(8,128)(2,1)} %get-tuple-element.83), channel_id=1, source_target_pairs={{0,4},{1,5},{2,6},{3,7},{4,0},{5,1},{6,2},{7,3},{8,12},{9,13},{10,... | collective-permute-start | bytes 516104 | tf_op jit(solution)/shard_map/b4/ppermute | solution.py:24
  108.4 9.2 %conv_c.1 = (bf16[336,256]{1,0:T(8,128)(2,1)}, bf16[336,256]{1,0:T(8,128)(2,1)}, bf16[336,256]{1,0:T(8,128)(2,1)}, bf16[336,256]{1,0:T(8,128)(2,1)}, bf16[336,25...) custom-call(s32[16]{0:T(128)} %clip_ref.11, ...), custom_call_target="tpu_custom_call" | custom-call | flops 60397977600 | bytes 131072000 | tf_op jit(solution)/shard_map/conv_c/pallas_call | solution.py:192
  117.6 0.0 collective-permute-done.23.refs_3_
  117.6 1.4 collective-permute-start.20
  119.1 1.2 collective-permute-done.22.refs_2_
  120.3 2.2 %collective-permute-start.19 = (bf16[336,256]{1,0:T(8,128)(2,1)}, bf16[336,256]{1,0:T(8,128)(2,1)S(1)}, u32[]{:S(2)}, u32[]{:S(2)}) collective-permute-start(bf16[336,256]{1,0:T(8,128)(2,1)} %get-tuple-element.104), channel_id=1, source_target_pairs={{0,2},{1,3},{2,0},{3,1},{4,6},{5,7},{6,4},{7,5},{8,10},{9,11},{10,... | collective-permute-start | bytes 516104 | tf_op jit(solution)/shard_map/b2/ppermute | solution.py:24
  122.5 0.0 collective-permute-done.21.refs_1_
  122.5 1.8 %collective-permute-start.18 = (bf16[336,256]{1,0:T(8,128)(2,1)}, bf16[336,256]{1,0:T(8,128)(2,1)S(1)}, u32[]{:S(2)}, u32[]{:S(2)}) collective-permute-start(bf16[336,256]{1,0:T(8,128)(2,1)} %get-tuple-element.102), channel_id=1, source_target_pairs={{0,1},{1,0},{2,3},{3,2},{4,5},{5,4},{6,7},{7,6},{8,9},{9,8},{10,11... | collective-permute-start | bytes 516104 | tf_op jit(solution)/shard_map/b1/ppermute | solution.py:24
  124.3 0.0 collective-permute-done.10.refs_5_
  124.3 0.0 collective-permute-start.17
  124.3 0.0 collective-permute-done.7.refs_4_
  124.3 1.4 collective-permute-start.14
  125.8 1.6 collective-permute-done.20.refs_3_
  127.3 0.0 collective-permute-start.11
  127.3 3.2 %collective-permute-done.19.refs_2_ = bf16[336,256]{1,0:T(8,128)(2,1)S(1)} collective-permute-done((bf16[336,256]{1,0:T(8,128)(2,1)}, bf16[336,256]{1,0:T(8,128)(2,1)S(1)}, u32[]{:S(2)}, u32[]{:S(2)}) %collective-permute-start.19) | collective-permute-done | bytes 172064 | tf_op jit(solution)/shard_map/b2/ppermute | solution.py:24
  130.5 0.0 collective-permute-start.8
  130.5 0.0 collective-permute-done.18.refs_1_
  130.5 1.5 collective-permute-start.5
  132.0 14.2 %collective-permute-done.17.refs_7_ = bf16[336,256]{1,0:T(8,128)(2,1)S(1)} collective-permute-done((bf16[336,256]{1,0:T(8,128)(2,1)}, bf16[336,256]{1,0:T(8,128)(2,1)S(1)}, u32[]{:S(2)}, u32[]{:S(2)}) %collective-permute-start.17) | collective-permute-done | bytes 172064 | tf_op jit(solution)/shard_map/c7/ppermute | solution.py:24
  146.2 0.0 collective-permute-start.4
  146.2 2.6 %collective-permute-done.14.refs_6_ = bf16[336,256]{1,0:T(8,128)(2,1)S(1)} collective-permute-done((bf16[336,256]{1,0:T(8,128)(2,1)}, bf16[336,256]{1,0:T(8,128)(2,1)S(1)}, u32[]{:S(2)}, u32[]{:S(2)}) %collective-permute-start.14) | collective-permute-done | bytes 172064 | tf_op jit(solution)/shard_map/c6/ppermute | solution.py:24
  148.8 1.5 collective-permute-start.3
  150.3 5.8 %norm_a.1.refs_10_ = bf16[4,8,4,80,256]{4,3,2,1,0:T(8,128)(2,1)} custom-call(s32[2]{0:T(128)} %pad_add_fusion.place_ref, bf16[656,256]{1,0:T(8,128)(2,1)} %get-tuple-element.68.refs_0_, bf16[656,256]{1,0:T(8,128)(2,1)} %copy-done.7, bf16[656,256]{1,0:T(8,128)(2,1)} %copy-done.6, bf16[656,256]{1,0:T(8,128)(2,1)} %copy-done.5, bf16[656,256]{1,0:T(8,128)(2,1)} %copy-done.2, ...), custom_call_target="tpu_custom_call" | custom-call | flops 10485760 | bytes 5242880 | tf_op jit(solution)/shard_map/norm_a/pallas_call | solution.py:278
  156.2 4.3 %norm_b.1.refs_10_ = bf16[4,8,4,80,256]{4,3,2,1,0:T(8,128)(2,1)} custom-call(s32[2]{0:T(128)} %pad_add_fusion.place_ref, bf16[336,256]{1,0:T(8,128)(2,1)} %get-tuple-element.100.refs_0_, bf16[336,256]{1,0:T(8,128)(2,1)} %copy-done.20, bf16[336,256]{1,0:T(8,128)(2,1)} %copy-done.18, bf16[336,256]{1,0:T(8,128)(2,1)} %copy-done.16, ...), custom_call_target="tpu_custom_call", output_to_operand_aliasing={{}: (11, {})} | custom-call | flops 5242880 | bytes 2621440 | tf_op jit(solution)/shard_map/norm_b/pallas_call | solution.py:278
  160.5 0.0 collective-permute-done.11.refs_5_
  160.5 0.0 collective-permute-done.8.refs_4_
  160.5 0.0 collective-permute-done.5.refs_3_
  160.5 0.0 collective-permute-done.3.refs_1_
  160.5 0.6 copy-done.19
  161.2 0.1 copy-done.21
  161.2 0.1 copy-done.22
  161.3 0.0 copy-done.23
  161.3 0.7 copy-done.24
  162.0 4.3 %norm_c.1 = bf16[4,8,4,80,256]{4,3,2,1,0:T(8,128)(2,1)} custom-call(s32[2]{0:T(128)} %pad_add_fusion.place_ref, bf16[336,256]{1,0:T(8,128)(2,1)} %get-tuple-element.72.refs_0_, bf16[336,256]{1,0:T(8,128)(2,1)} %copy-done.24, bf16[336,256]{1,0:T(8,128)(2,1)} %copy-done.23, bf16[336,256]{1,0:T(8,128)(2,1)} %copy-done.22, ...), custom_call_target="tpu_custom_call", output_to_operand_aliasing={{}: (11, {})} | custom-call | flops 5242880 | bytes 2621440 | tf_op jit(solution)/shard_map/norm_c/pallas_call | solution.py:278
  (45 shorter events, 0.1 us)
Async XLA Ops:
  1.4 18.8 %collective-permute-start = (bf16[4,1,1280,128]{3,2,1,0:T(8,128)(2,1)S(1)}, bf16[4,1,1280,128]{3,2,1,0:T(8,128)(2,1)S(1)}, u32[]{:S(2)}, u32[]{:S(2)}) collective-permute-start(bf16[4,1,1280,128]{3,2,1,0:T(8,128)(2,1)S(1)} %slice.3), channel_id=1, source_target_pairs={{0,1},{1,2},{2,3},{3,4},{4,5},{5,6},{6,7},{8,9},{9,10},{10,11},{11... | collective-permute-start | bytes 3932168 | tf_op jit(solution)/shard_map/halo/ppermute | solution.py:19
  20.3 1.1 copy-start
  28.4 70.2 %collective-permute-start.9 = (bf16[656,256]{1,0:T(8,128)(2,1)}, bf16[656,256]{1,0:T(8,128)(2,1)S(1)}, u32[]{:S(2)}, u32[]{:S(2)}) collective-permute-start(bf16[656,256]{1,0:T(8,128)(2,1)} %get-tuple-element.87), channel_id=1, source_target_pairs={{0,5},{1,4},{2,7},{3,6},{4,1},{5,0},{6,3},{7,2},{8,13},{9,12},{10,... | collective-permute-start | bytes 1007624 | tf_op jit(solution)/shard_map/a5/ppermute | solution.py:24
  31.3 67.2 %collective-permute-start.6 = (bf16[656,256]{1,0:T(8,128)(2,1)}, bf16[656,256]{1,0:T(8,128)(2,1)S(1)}, u32[]{:S(2)}, u32[]{:S(2)}) collective-permute-start(bf16[656,256]{1,0:T(8,128)(2,1)} %get-tuple-element.82), channel_id=1, source_target_pairs={{0,4},{1,5},{2,6},{3,7},{4,0},{5,1},{6,2},{7,3},{8,12},{9,13},{10,... | collective-permute-start | bytes 1007624 | tf_op jit(solution)/shard_map/a4/ppermute | solution.py:24
  31.4 67.1 %collective-permute-start.12 = (bf16[656,256]{1,0:T(8,128)(2,1)}, bf16[656,256]{1,0:T(8,128)(2,1)S(1)}, u32[]{:S(2)}, u32[]{:S(2)}) collective-permute-start(bf16[656,256]{1,0:T(8,128)(2,1)} %get-tuple-element.92), channel_id=1, source_target_pairs={{0,6},{1,7},{2,4},{3,5},{4,2},{5,3},{6,0},{7,1},{8,14},{9,15},{10,... | collective-permute-start | bytes 1007624 | tf_op jit(solution)/shard_map/a6/ppermute | solution.py:24
  32.7 63.4 %collective-permute-start.15 = (bf16[656,256]{1,0:T(8,128)(2,1)}, bf16[656,256]{1,0:T(8,128)(2,1)S(1)}, u32[]{:S(2)}, u32[]{:S(2)}) collective-permute-start(bf16[656,256]{1,0:T(8,128)(2,1)} %get-tuple-element.97), channel_id=1, source_target_pairs={{0,7},{1,6},{2,5},{3,4},{4,3},{5,2},{6,1},{7,0},{8,15},{9,14},{10,... | collective-permute-start | bytes 1007624 | tf_op jit(solution)/shard_map/a7/ppermute | solution.py:24
  41.7 32.7 %collective-permute-start.1 = (bf16[1,4,640,256]{3,2,1,0:T(8,128)(2,1)}, bf16[1,4,640,256]{3,2,1,0:T(8,128)(2,1)}, u32[]{:S(2)}, u32[]{:S(2)}) collective-permute-start(bf16[1,4,640,256]{3,2,1,0:T(8,128)(2,1)} %conv_hist0.1), channel_id=1, source_target_pairs={{0,8},{8,16},{16,24},{1,9},{9,17},{17,25},{2,10},{10,18},{18,26},{... | collective-permute-start | bytes 3932168 | tf_op jit(solution)/shard_map/hist0/ppermute | solution.py:19
  49.2 49.3 %copy-start.10 = (bf16[656,256]{1,0:T(8,128)(2,1)S(1)}, bf16[656,256]{1,0:T(8,128)(2,1)}, u32[]{:S(2)}) copy-start(bf16[656,256]{1,0:T(8,128)(2,1)} %get-tuple-element.112) | copy-start | bytes 1007620
  49.2 49.4 %copy-start.9 = (bf16[656,256]{1,0:T(8,128)(2,1)S(1)}, bf16[656,256]{1,0:T(8,128)(2,1)}, u32[]{:S(2)}) copy-start(bf16[656,256]{1,0:T(8,128)(2,1)} %get-tuple-element.110) | copy-start | bytes 1007620
  49.2 53.6 %copy-start.8 = (bf16[656,256]{1,0:T(8,128)(2,1)S(1)}, bf16[656,256]{1,0:T(8,128)(2,1)}, u32[]{:S(2)}) copy-start(bf16[656,256]{1,0:T(8,128)(2,1)} %get-tuple-element.108) | copy-start | bytes 1007620
  74.4 31.8 %collective-permute-start.2 = (bf16[1,4,640,256]{3,2,1,0:T(8,128)(2,1)}, bf16[1,4,640,256]{3,2,1,0:T(8,128)(2,1)}, u32[]{:S(2)}, u32[]{:S(2)}) collective-permute-start(bf16[1,4,640,256]{3,2,1,0:T(8,128)(2,1)} %conv_hist1.1), channel_id=1, source_target_pairs={{0,8},{8,16},{16,24},{1,9},{9,17},{17,25},{2,10},{10,18},{18,26},{... | collective-permute-start | bytes 3932168 | tf_op jit(solution)/shard_map/hist1/ppermute | solution.py:19
  96.1 21.5 %copy-start.4 = (bf16[656,256]{1,0:T(8,128)(2,1)}, bf16[656,256]{1,0:T(8,128)(2,1)S(1)}, u32[]{:S(2)}) copy-start(bf16[656,256]{1,0:T(8,128)(2,1)S(1)} %collective-permute-done.15.refs_7_) | copy-start | bytes 1007620
  96.1 6.7 %collective-permute-start.16 = (bf16[336,256]{1,0:T(8,128)(2,1)}, bf16[336,256]{1,0:T(8,128)(2,1)S(1)}, u32[]{:S(2)}, u32[]{:S(2)}) collective-permute-start(bf16[336,256]{1,0:T(8,128)(2,1)} %get-tuple-element.98), channel_id=1, source_target_pairs={{0,7},{1,6},{2,5},{3,4},{4,3},{5,2},{6,1},{7,0},{8,15},{9,14},{10,... | collective-permute-start | bytes 516104 | tf_op jit(solution)/shard_map/b7/ppermute | solution.py:24
  98.5 19.1 %copy-start.3 = (bf16[656,256]{1,0:T(8,128)(2,1)}, bf16[656,256]{1,0:T(8,128)(2,1)S(1)}, u32[]{:S(2)}) copy-start(bf16[656,256]{1,0:T(8,128)(2,1)S(1)} %collective-permute-done.12.refs_6_) | copy-start | bytes 1007620
  98.5 6.7 %collective-permute-start.13 = (bf16[336,256]{1,0:T(8,128)(2,1)}, bf16[336,256]{1,0:T(8,128)(2,1)S(1)}, u32[]{:S(2)}, u32[]{:S(2)}) collective-permute-start(bf16[336,256]{1,0:T(8,128)(2,1)} %get-tuple-element.93), channel_id=1, source_target_pairs={{0,6},{1,7},{2,4},{3,5},{4,2},{5,3},{6,0},{7,1},{8,14},{9,15},{10,... | collective-permute-start | bytes 516104 | tf_op jit(solution)/shard_map/b6/ppermute | solution.py:24
  98.5 19.1 %copy-start.2 = (bf16[656,256]{1,0:T(8,128)(2,1)}, bf16[656,256]{1,0:T(8,128)(2,1)S(1)}, u32[]{:S(2)}) copy-start(bf16[656,256]{1,0:T(8,128)(2,1)S(1)} %collective-permute-done.6.refs_4_) | copy-start | bytes 1007620
  98.5 19.1 %collective-permute-start.23 = (bf16[656,256]{1,0:T(8,128)(2,1)S(1)}, bf16[656,256]{1,0:T(8,128)(2,1)S(1)}, u32[]{:S(2)}, u32[]{:S(2)}) collective-permute-start(bf16[656,256]{1,0:T(8,128)(2,1)S(1)} %copy-done.10), channel_id=1, source_target_pairs={{0,3},{1,2},{2,1},{3,0},{4,7},{5,6},{6,5},{7,4},{8,11},{9,10},{10,... | collective-permute-start | bytes 1007624 | tf_op jit(solution)/shard_map/a3/ppermute | solution.py:24
  98.6 19.0 %copy-start.1 = (bf16[656,256]{1,0:T(8,128)(2,1)}, bf16[656,256]{1,0:T(8,128)(2,1)S(1)}, u32[]{:S(2)}) copy-start(bf16[656,256]{1,0:T(8,128)(2,1)S(1)} %collective-permute-done.9.refs_5_) | copy-start | bytes 1007620
  98.6 21.7 %collective-permute-start.22 = (bf16[656,256]{1,0:T(8,128)(2,1)S(1)}, bf16[656,256]{1,0:T(8,128)(2,1)S(1)}, u32[]{:S(2)}, u32[]{:S(2)}) collective-permute-start(bf16[656,256]{1,0:T(8,128)(2,1)S(1)} %copy-done.9), channel_id=1, source_target_pairs={{0,2},{1,3},{2,0},{3,1},{4,6},{5,7},{6,4},{7,5},{8,10},{9,11},{10,... | collective-permute-start | bytes 1007624 | tf_op jit(solution)/shard_map/a2/ppermute | solution.py:24
  102.8 14.8 %copy-start.11 = (bf16[336,256]{1,0:T(8,128)(2,1)}, bf16[336,256]{1,0:T(8,128)(2,1)S(1)}, u32[]{:S(2)}) copy-start(bf16[336,256]{1,0:T(8,128)(2,1)S(1)} %collective-permute-done.16.refs_7_) | copy-start | bytes 516100
  102.8 19.7 %collective-permute-start.21 = (bf16[656,256]{1,0:T(8,128)(2,1)S(1)}, bf16[656,256]{1,0:T(8,128)(2,1)S(1)}, u32[]{:S(2)}, u32[]{:S(2)}) collective-permute-start(bf16[656,256]{1,0:T(8,128)(2,1)S(1)} %copy-done.8), channel_id=1, source_target_pairs={{0,1},{1,0},{2,3},{3,2},{4,5},{5,4},{6,7},{7,6},{8,9},{9,8},{10,11... | collective-permute-start | bytes 1007624 | tf_op jit(solution)/shard_map/a1/ppermute | solution.py:24
  105.2 12.4 %copy-start.12 = (bf16[336,256]{1,0:T(8,128)(2,1)}, bf16[336,256]{1,0:T(8,128)(2,1)S(1)}, u32[]{:S(2)}) copy-start(bf16[336,256]{1,0:T(8,128)(2,1)S(1)} %collective-permute-done.13.refs_6_) | copy-start | bytes 516100
  105.2 19.1 %collective-permute-start.10 = (bf16[336,256]{1,0:T(8,128)(2,1)}, bf16[336,256]{1,0:T(8,128)(2,1)S(1)}, u32[]{:S(2)}, u32[]{:S(2)}) collective-permute-start(bf16[336,256]{1,0:T(8,128)(2,1)} %get-tuple-element.88), channel_id=1, source_target_pairs={{0,5},{1,4},{2,7},{3,6},{4,1},{5,0},{6,3},{7,2},{8,13},{9,12},{10,... | collective-permute-start | bytes 516104 | tf_op jit(solution)/shard_map/b5/ppermute | solution.py:24
  106.2 18.1 %collective-permute-start.7 = (bf16[336,256]{1,0:T(8,128)(2,1)}, bf16[336,256]{1,0:T(8,128)(2,1)S(1)}, u32[]{:S(2)}, u32[]{:S(2)}) collective-permute-start(bf16[336,256]{1,0:T(8,128)(2,1)} %get-tuple-element.83), channel_id=1, source_target_pairs={{0,4},{1,5},{2,6},{3,7},{4,0},{5,1},{6,2},{7,3},{8,12},{9,13},{10,... | collective-permute-start | bytes 516104 | tf_op jit(solution)/shard_map/b4/ppermute | solution.py:24
  117.6 32.7 %copy-start.5 = (bf16[656,256]{1,0:T(8,128)(2,1)}, bf16[656,256]{1,0:T(8,128)(2,1)S(1)}, u32[]{:S(2)}) copy-start(bf16[656,256]{1,0:T(8,128)(2,1)S(1)} %collective-permute-done.23.refs_3_) | copy-start | bytes 1007620
  117.6 9.7 %collective-permute-start.20 = (bf16[336,256]{1,0:T(8,128)(2,1)}, bf16[336,256]{1,0:T(8,128)(2,1)S(1)}, u32[]{:S(2)}, u32[]{:S(2)}) collective-permute-start(bf16[336,256]{1,0:T(8,128)(2,1)} %get-tuple-element.106), channel_id=1, source_target_pairs={{0,3},{1,2},{2,1},{3,0},{4,7},{5,6},{6,5},{7,4},{8,11},{9,10},{10,... | collective-permute-start | bytes 516104 | tf_op jit(solution)/shard_map/b3/ppermute | solution.py:24
  120.3 30.0 %copy-start.6 = (bf16[656,256]{1,0:T(8,128)(2,1)}, bf16[656,256]{1,0:T(8,128)(2,1)S(1)}, u32[]{:S(2)}) copy-start(bf16[656,256]{1,0:T(8,128)(2,1)S(1)} %collective-permute-done.22.refs_2_) | copy-start | bytes 1007620
  120.3 10.2 %collective-permute-start.19 = (bf16[336,256]{1,0:T(8,128)(2,1)}, bf16[336,256]{1,0:T(8,128)(2,1)S(1)}, u32[]{:S(2)}, u32[]{:S(2)}) collective-permute-start(bf16[336,256]{1,0:T(8,128)(2,1)} %get-tuple-element.104), channel_id=1, source_target_pairs={{0,2},{1,3},{2,0},{3,1},{4,6},{5,7},{6,4},{7,5},{8,10},{9,11},{10,... | collective-permute-start | bytes 516104 | tf_op jit(solution)/shard_map/b2/ppermute | solution.py:24
  122.5 27.8 %copy-start.7 = (bf16[656,256]{1,0:T(8,128)(2,1)}, bf16[656,256]{1,0:T(8,128)(2,1)S(1)}, u32[]{:S(2)}) copy-start(bf16[656,256]{1,0:T(8,128)(2,1)S(1)} %collective-permute-done.21.refs_1_) | copy-start | bytes 1007620
  122.5 8.0 %collective-permute-start.18 = (bf16[336,256]{1,0:T(8,128)(2,1)}, bf16[336,256]{1,0:T(8,128)(2,1)S(1)}, u32[]{:S(2)}, u32[]{:S(2)}) collective-permute-start(bf16[336,256]{1,0:T(8,128)(2,1)} %get-tuple-element.102), channel_id=1, source_target_pairs={{0,1},{1,0},{2,3},{3,2},{4,5},{5,4},{6,7},{7,6},{8,9},{9,8},{10,11... | collective-permute-start | bytes 516104 | tf_op jit(solution)/shard_map/b1/ppermute | solution.py:24
  124.3 31.8 %copy-start.13 = (bf16[336,256]{1,0:T(8,128)(2,1)}, bf16[336,256]{1,0:T(8,128)(2,1)S(1)}, u32[]{:S(2)}) copy-start(bf16[336,256]{1,0:T(8,128)(2,1)S(1)} %collective-permute-done.10.refs_5_) | copy-start | bytes 516100
  124.3 21.9 %collective-permute-start.17 = (bf16[336,256]{1,0:T(8,128)(2,1)}, bf16[336,256]{1,0:T(8,128)(2,1)S(1)}, u32[]{:S(2)}, u32[]{:S(2)}) collective-permute-start(bf16[336,256]{1,0:T(8,128)(2,1)} %get-tuple-element.99), channel_id=1, source_target_pairs={{0,7},{1,6},{2,5},{3,4},{4,3},{5,2},{6,1},{7,0},{8,15},{9,14},{10,... | collective-permute-start | bytes 516104 | tf_op jit(solution)/shard_map/c7/ppermute | solution.py:24
  124.3 31.8 %copy-start.14 = (bf16[336,256]{1,0:T(8,128)(2,1)}, bf16[336,256]{1,0:T(8,128)(2,1)S(1)}, u32[]{:S(2)}) copy-start(bf16[336,256]{1,0:T(8,128)(2,1)S(1)} %collective-permute-done.7.refs_4_) | copy-start | bytes 516100
  124.3 24.4 %collective-permute-start.14 = (bf16[336,256]{1,0:T(8,128)(2,1)}, bf16[336,256]{1,0:T(8,128)(2,1)S(1)}, u32[]{:S(2)}, u32[]{:S(2)}) collective-permute-start(bf16[336,256]{1,0:T(8,128)(2,1)} %get-tuple-element.94), channel_id=1, source_target_pairs={{0,6},{1,7},{2,4},{3,5},{4,2},{5,3},{6,0},{7,1},{8,14},{9,15},{10,... | collective-permute-start | bytes 516104 | tf_op jit(solution)/shard_map/c6/ppermute | solution.py:24
  127.3 28.8 %copy-start.16 = (bf16[336,256]{1,0:T(8,128)(2,1)}, bf16[336,256]{1,0:T(8,128)(2,1)S(1)}, u32[]{:S(2)}) copy-start(bf16[336,256]{1,0:T(8,128)(2,1)S(1)} %collective-permute-done.20.refs_3_) | copy-start | bytes 516100
  127.3 33.1 %collective-permute-start.11 = (bf16[336,256]{1,0:T(8,128)(2,1)}, bf16[336,256]{1,0:T(8,128)(2,1)S(1)}, u32[]{:S(2)}, u32[]{:S(2)}) collective-permute-start(bf16[336,256]{1,0:T(8,128)(2,1)} %get-tuple-element.89), channel_id=1, source_target_pairs={{0,5},{1,4},{2,7},{3,6},{4,1},{5,0},{6,3},{7,2},{8,13},{9,12},{10,... | collective-permute-start | bytes 516104 | tf_op jit(solution)/shard_map/c5/ppermute | solution.py:24
  130.5 25.6 %copy-start.18 = (bf16[336,256]{1,0:T(8,128)(2,1)}, bf16[336,256]{1,0:T(8,128)(2,1)S(1)}, u32[]{:S(2)}) copy-start(bf16[336,256]{1,0:T(8,128)(2,1)S(1)} %collective-permute-done.19.refs_2_) | copy-start | bytes 516100
  130.5 30.0 %collective-permute-start.8 = (bf16[336,256]{1,0:T(8,128)(2,1)}, bf16[336,256]{1,0:T(8,128)(2,1)S(1)}, u32[]{:S(2)}, u32[]{:S(2)}) collective-permute-start(bf16[336,256]{1,0:T(8,128)(2,1)} %get-tuple-element.84), channel_id=1, source_target_pairs={{0,4},{1,5},{2,6},{3,7},{4,0},{5,1},{6,2},{7,3},{8,12},{9,13},{10,... | collective-permute-start | bytes 516104 | tf_op jit(solution)/shard_map/c4/ppermute | solution.py:24
  130.5 25.6 %copy-start.20 = (bf16[336,256]{1,0:T(8,128)(2,1)}, bf16[336,256]{1,0:T(8,128)(2,1)S(1)}, u32[]{:S(2)}) copy-start(bf16[336,256]{1,0:T(8,128)(2,1)S(1)} %collective-permute-done.18.refs_1_) | copy-start | bytes 516100
  130.5 30.0 %collective-permute-start.5 = (bf16[336,256]{1,0:T(8,128)(2,1)}, bf16[336,256]{1,0:T(8,128)(2,1)S(1)}, u32[]{:S(2)}, u32[]{:S(2)}) collective-permute-start(bf16[336,256]{1,0:T(8,128)(2,1)} %get-tuple-element.78), channel_id=1, source_target_pairs={{0,3},{1,2},{2,1},{3,0},{4,7},{5,6},{6,5},{7,4},{8,11},{9,10},{10,... | collective-permute-start | bytes 516104 | tf_op jit(solution)/shard_map/c3/ppermute | solution.py:24
  146.2 10.0 %copy-start.15 = (bf16[336,256]{1,0:T(8,128)(2,1)}, bf16[336,256]{1,0:T(8,128)(2,1)S(1)}, u32[]{:S(2)}) copy-start(bf16[336,256]{1,0:T(8,128)(2,1)S(1)} %collective-permute-done.17.refs_7_) | copy-start | bytes 516100
  146.2 14.3 %collective-permute-start.4 = (bf16[336,256]{1,0:T(8,128)(2,1)}, bf16[336,256]{1,0:T(8,128)(2,1)S(1)}, u32[]{:S(2)}, u32[]{:S(2)}) collective-permute-start(bf16[336,256]{1,0:T(8,128)(2,1)} %get-tuple-element.76), channel_id=1, source_target_pairs={{0,2},{1,3},{2,0},{3,1},{4,6},{5,7},{6,4},{7,5},{8,10},{9,11},{10,... | collective-permute-start | bytes 516104 | tf_op jit(solution)/shard_map/c2/ppermute | solution.py:24
  148.8 7.4 %copy-start.17 = (bf16[336,256]{1,0:T(8,128)(2,1)}, bf16[336,256]{1,0:T(8,128)(2,1)S(1)}, u32[]{:S(2)}) copy-start(bf16[336,256]{1,0:T(8,128)(2,1)S(1)} %collective-permute-done.14.refs_6_) | copy-start | bytes 516100
  148.8 11.8 %collective-permute-start.3 = (bf16[336,256]{1,0:T(8,128)(2,1)}, bf16[336,256]{1,0:T(8,128)(2,1)S(1)}, u32[]{:S(2)}, u32[]{:S(2)}) collective-permute-start(bf16[336,256]{1,0:T(8,128)(2,1)} %get-tuple-element.74), channel_id=1, source_target_pairs={{0,1},{1,0},{2,3},{3,2},{4,5},{5,4},{6,7},{7,6},{8,9},{9,8},{10,11... | collective-permute-start | bytes 516104 | tf_op jit(solution)/shard_map/c1/ppermute | solution.py:24
  160.5 0.7 copy-start.19
  160.5 0.7 copy-start.21
  160.5 0.8 copy-start.22
  160.5 0.8 copy-start.23
  161.3 0.7 copy-start.24

commit v4 on v3

--- a/solution.py
+++ b/solution.py
@@ -10,7 +10,6 @@
 GROUPS = 32
 EPS = 1e-05
 STAT_ROWS = 16
-VMEM_BYTES = 60 * 1024 * 1024
 
 
 def passed_along(array, axis, by):
@@ -46,7 +45,7 @@
     return [high, middle, rest - middle]
 
 
-def conv_kernel(plan, clip_ref, place_ref, x_ref, above_ref, w_ref, *refs):
+def conv_kernel(plan, clip_ref, x_ref, above_ref, w_ref, *refs):
     jobs, parts, part_rows, part_width = (
         plan["jobs"], plan["parts"], plan["part_rows"], plan["part_width"])
     lead, steps, tap_first = plan["lead"], plan["steps"], plan["tap_first"]
@@ -63,12 +62,12 @@
     sums_out = take(1 if plan["sums_out"] else 0)
     sources, ci = x_ref.shape[0], x_ref.shape[3]
     slab_refs, main_refs, left_refs = take(sources), take(len(jobs)), take(len(jobs))
-    part_ref, stat_ref = refs
+    part_ref, stat_ref, closing_ref, part_sem, tail_sem = refs
     step = pl.program_id(0)
     half, co = main_refs[0].shape
     above = lax.rem(step + 1, 2)
     below = lax.rem(step, 2)
-    start = place_ref[0]
+    start = lax.axis_index("tm") * plan["count"]
     last = clip_ref.shape[0] - 1
 
     @pl.when(step == 0)
@@ -78,6 +77,15 @@
         for left_ref in left_refs:
             left_ref[0:8] = jnp.zeros((8, co), jnp.float32)
         stat_ref[...] = jnp.zeros_like(stat_ref)
+
+    def piece_copies(at, slot, step):
+        mine = lax.axis_index("rows")
+        offset = pl.multiple_of(lead + (at * steps + step) * part_rows, 16)
+        return [
+            pltpu.make_async_copy(part_ref.at[slot, at, mine ^ flip],
+                                  out.at[pl.ds(offset, part_rows)], part_sem.at[slot, at, flip])
+            for flip, out in enumerate(out_refs)
+        ]
 
     def products(source, tap):
         slab_ref, tap = slab_refs[source], tap - tap_first
@@ -123,34 +131,50 @@
         tiles = rounded.reshape(half // 8, 8, co)
         stat_ref[2 * at] += jnp.sum(tiles, axis=0)
         stat_ref[2 * at + 1] += jnp.sum(tiles * tiles, axis=0)
+        slot = lax.rem(step, 2)
+
+        @pl.when(step >= 2)
+        def _(at=at, slot=slot):
+            for copy in piece_copies(at, slot, step):
+                copy.wait()
+
         for part in range(parts):
             piece = rounded[part * part_width : (part + 1) * part_width]
-            part_ref[at, part, 0:part_width] = piece.astype(jnp.bfloat16)
-        mine = place_ref[1]
-        for flip in range(parts):
-            offset = pl.multiple_of(lead + (at * steps + step) * part_rows, 16)
-            out_refs[flip][pl.ds(offset, part_rows)] = part_ref[at, mine ^ flip]
+            part_ref[slot, at, part, 0:part_width] = piece.astype(jnp.bfloat16)
+        for copy in piece_copies(at, slot, step):
+            copy.start()
 
     if parts:
         @pl.when(step == steps - 1)
         def _():
+            closing = []
             if sums_out:
                 sums_out[0][...] = stat_ref[...]
-                return
-            rows = []
-            for at in range(2 * len(jobs)):
-                total = stat_ref[at]
-                for ref in sums_refs:
-                    total = total + ref[at]
-                rows += split_three(jnp.sum(total, axis=0, keepdims=True))
-            blank = jnp.zeros((STAT_ROWS - len(rows), co), jnp.float32)
-            closing = jnp.concatenate(rows + [blank], axis=0).astype(jnp.bfloat16)
-            for flip in range(parts):
-                out_refs[flip][0:STAT_ROWS] = closing
-
-
-def conv_frames(frames, halo, weight, clip_ids, place, first, sources, jobs, row=0, steps=None,
-                addends=(), parts=0, sums=(), sums_out=False, lead=0, kept=(), weigh=1):
+            else:
+                rows = []
+                for at in range(2 * len(jobs)):
+                    total = stat_ref[at]
+                    for ref in sums_refs:
+                        total = total + ref[at]
+                    rows += split_three(jnp.sum(total, axis=0, keepdims=True))
+                blank = jnp.zeros((STAT_ROWS - len(rows), co), jnp.float32)
+                closing_ref[...] = jnp.concatenate(rows + [blank], axis=0).astype(jnp.bfloat16)
+                closing = [
+                    pltpu.make_async_copy(closing_ref, out.at[0:STAT_ROWS], tail_sem.at[flip])
+                    for flip, out in enumerate(out_refs)
+                ]
+            for copy in closing:
+                copy.start()
+            for at in range(len(jobs)):
+                for back in range(min(steps, 2)):
+                    for copy in piece_copies(at, lax.rem(step - back, 2), step - back):
+                        copy.wait()
+            for copy in closing:
+                copy.wait()
+
+
+def conv_frames(frames, halo, weight, clip_ids, first, sources, jobs, row=0, steps=None,
+                addends=(), parts=0, sums=(), sums_out=False, lead=0, kept=(), weigh=1, vmem=60):
     _, band, width, ci = frames.shape
     co = weight.shape[2]
     half = width // 2
@@ -163,7 +187,7 @@
         tap_first, tap_count = taps[0], len(taps)
     plan = dict(jobs=jobs, addends=len(addends), parts=parts, part_rows=part_rows, lead=lead,
                 part_width=part_width, first=first, steps=steps, kept=len(kept),
-                sums_in=len(sums), sums_out=sums_out, tap_first=tap_first)
+                sums_in=len(sums), sums_out=sums_out, tap_first=tap_first, count=frames.shape[0])
     block = first // sources
     above = (frames, 2 * row - 1) if row else (halo, 0)
     in_specs = [
@@ -174,13 +198,13 @@
     in_specs += [pl.BlockSpec((1, None, half, co), lambda i, *_: (0, i, 0, 0)) for _ in addends]
     in_specs += [pl.BlockSpec(a.shape, lambda i, *_: (0, 0, 0)) for a in sums]
     in_specs += [pl.BlockSpec(memory_space=pl.ANY) for _ in kept]
-    operands = [clip_ids, place, frames, above[0], weight, *addends, *sums, *kept]
+    operands = [clip_ids, frames, above[0], weight, *addends, *sums, *kept]
     aliases = {len(operands) - len(kept) + at: at for at in range(len(kept))}
     if parts:
         rows = lead + len(jobs) * steps * part_rows
         shape = kept[0].shape if kept else (rows, co)
         out_shape = [jax.ShapeDtypeStruct(shape, jnp.bfloat16) for _ in range(parts)]
-        out_specs = [pl.BlockSpec((rows, co), lambda i, *_: (0, 0)) for _ in range(parts)]
+        out_specs = [pl.BlockSpec(memory_space=pl.ANY) for _ in range(parts)]
     else:
         out_shape = [jax.ShapeDtypeStruct((1, steps, half, co), jnp.bfloat16) for _ in jobs]
         out_specs = [pl.BlockSpec((1, None, half, co), lambda i, *_: (0, i, 0, 0)) for _ in jobs]
@@ -193,7 +217,7 @@
         functools.partial(conv_kernel, plan),
         out_shape=out_shape,
         grid_spec=pltpu.PrefetchScalarGridSpec(
-            num_scalar_prefetch=2,
+            num_scalar_prefetch=1,
             grid=(steps,),
             in_specs=in_specs,
             out_specs=out_specs,
@@ -201,8 +225,11 @@
                 *[pltpu.VMEM((3, half, 2 * ci), jnp.bfloat16) for _ in range(sources)],
                 *[pltpu.VMEM((half, co), jnp.float32) for _ in jobs],
                 *[pltpu.VMEM((8 + half, co), jnp.float32) for _ in jobs],
-                pltpu.VMEM((len(jobs), max(parts, 1), part_rows, co), jnp.bfloat16),
+                pltpu.VMEM((2, len(jobs), max(parts, 1), part_rows, co), jnp.bfloat16),
                 pltpu.VMEM((2 * len(jobs), 8, co), jnp.float32),
+                pltpu.VMEM((STAT_ROWS, co), jnp.bfloat16),
+                pltpu.SemaphoreType.DMA((2, len(jobs), max(parts, 1))),
+                pltpu.SemaphoreType.DMA((max(parts, 1),)),
             ],
         ),
         input_output_aliases=aliases,
@@ -211,20 +238,21 @@
             bytes_accessed=weigh * (4 * sources * steps * width * ci + 2 * len(jobs) * steps * half * co),
             transcendentals=0,
         ),
-        compiler_params=pltpu.CompilerParams(vmem_limit_bytes=VMEM_BYTES),
+        compiler_params=pltpu.CompilerParams(vmem_limit_bytes=vmem * 1024 * 1024),
     )(*operands)
 
 
-def norm_kernel(plan, place_ref, *refs):
+def norm_kernel(plan, *refs):
     parts, jobs, steps, rows = plan["parts"], plan["jobs"], plan["steps"], plan["rows"]
     lead, part_rows = plan["lead"], plan["part_rows"]
     data_refs, (gain_ref, bias_ref) = refs[:parts], refs[parts : parts + 2]
-    out_ref, scale_ref = refs[-2:]
+    out_ref, done_ref, scale_ref = refs[-3:]
     frame, step = pl.program_id(0), pl.program_id(1)
     part_width, co = out_ref.shape[-2:]
 
     @pl.when((frame == 0) & (step == 0))
     def _():
+        scale_ref[...] = jnp.zeros_like(scale_ref)
         total = data_refs[0][0:STAT_ROWS].astype(jnp.float32)
         for flip in range(1, parts):
             total = total + data_refs[flip][0:STAT_ROWS].astype(jnp.float32)
@@ -242,10 +270,11 @@
             scale_ref[at, 0:1] = mean
             scale_ref[at, 1:2] = lax.rsqrt(variance + EPS) * gain_ref[...]
 
+    done_ref[...] = scale_ref[0]
     mean = scale_ref[frame, 0:1]
     scale = scale_ref[frame, 1:2]
     bias = bias_ref[...]
-    mine = place_ref[1]
+    mine = lax.axis_index("rows")
     for at in range(rows):
         row = step * rows + at
         if plan["top_first"]:
@@ -259,7 +288,7 @@
             out_ref[0, mine ^ flip, at] = (value + value * jnp.tanh(value)).astype(jnp.bfloat16)
 
 
-def norm_frames(messages, gain, bias, place, first, jobs, shape, top_first=False, base=None):
+def norm_frames(messages, gain, bias, first, jobs, shape, top_first=False, base=None, vmem=20):
     frames, parts, steps, part_width, co = shape
     rows = 2 if steps % 2 == 0 else 1
     plan = dict(parts=parts, jobs=jobs, steps=steps, rows=rows, lead=STAT_ROWS,
@@ -269,7 +298,7 @@
         [pl.BlockSpec(message.shape, lambda f, i, *_: (0, 0)) for message in messages]
         + [pl.BlockSpec((1, co), lambda f, i, *_: (0, 0))] * 2
     )
-    operands = [place, *messages, gain, bias]
+    operands = [*messages, gain, bias]
     aliases = {}
     if base is not None:
         in_specs.append(pl.BlockSpec(memory_space=pl.ANY))
@@ -277,13 +306,15 @@
         operands.append(base)
     return pl.pallas_call(
         functools.partial(norm_kernel, plan),
-        out_shape=jax.ShapeDtypeStruct(shape, jnp.bfloat16),
+        out_shape=[jax.ShapeDtypeStruct(shape, jnp.bfloat16), jax.ShapeDtypeStruct((8, co), jnp.float32)],
         grid_spec=pltpu.PrefetchScalarGridSpec(
-            num_scalar_prefetch=1,
+            num_scalar_prefetch=0,
             grid=(jobs, steps // rows),
             in_specs=in_specs,
-            out_specs=pl.BlockSpec(
-                (1, parts, rows, part_width, co), lambda f, i, *_: (first + f, 0, i, 0, 0)),
+            out_specs=[
+                pl.BlockSpec((1, parts, rows, part_width, co), lambda f, i, *_: (first + f, 0, i, 0, 0)),
+                pl.BlockSpec((8, co), lambda f, i, *_: (0, 0)),
+            ],
             scratch_shapes=[pltpu.VMEM((jobs, 8, co), jnp.float32)],
         ),
         input_output_aliases=aliases,
@@ -292,7 +323,7 @@
             bytes_accessed=4 * jobs * parts * steps * part_width * co,
             transcendentals=jobs * parts * steps * part_width * co,
         ),
-        compiler_params=pltpu.CompilerParams(vmem_limit_bytes=VMEM_BYTES),
+        compiler_params=pltpu.CompilerParams(vmem_limit_bytes=vmem * 1024 * 1024),
     )(*operands)
 
 
@@ -300,7 +331,6 @@
     count, band, width, ci = frames.shape
     co = conv_weight.shape[4]
     parts = lax.axis_size("rows")
-    place = jnp.stack([lax.axis_index("tm") * count, lax.axis_index("rows")]).astype(jnp.int32)
     weight = conv_weight.reshape(3, 9 * ci, co)
     gain, bias = norm_gain.reshape(1, co), norm_bias.reshape(1, co)
     steps = band // 2
@@ -312,45 +342,56 @@
         with jax.named_scope(name):
             return function(*args, **keywords)
 
+    def whole(sent, got):
+        return [sent[0]] + [got[flip] for flip in range(1, parts)]
+
+    chain = []
+
+    def send_far(name, sent, *earlier):
+        got = {}
+        for flip in [flip for flip in range(parts - 1, 0, -1) if 2 * flip >= parts]:
+            before = chain[-4:][:1] if len(chain) >= 4 else []
+            got[flip] = named(f"{name}{flip}", exchanged, after(sent[flip], *before, *earlier), "rows", flip)
+            chain.append(got[flip])
+        return got
+
+    def send_near(name, sent, single, *earlier):
+        got = {}
+        for flip in near:
+            got[flip] = named(f"{name}{flip}", exchanged, after(sent[flip], *earlier), "rows", flip)
+            if single:
+                earlier = (got[flip],)
+        return got
+
+    near = [flip for flip in range(1, parts) if 2 * flip < parts]
     halo = named("halo", passed_along, frames[:, -1:], "rows", 1)
-    far = [flip for flip in range(parts - 1, 0, -1) if 2 * flip >= parts]
-    near = [flip for flip in range(parts - 1, 0, -1) if 2 * flip < parts]
 
     later = [(2, [(0, 0), (1, 1), (2, 2)], None), (3, [(1, 0), (2, 1), (3, 2)], None)]
-    run = functools.partial(conv_frames, frames, halo, weight, clip_ids, place)
+    run = functools.partial(conv_frames, frames, halo, weight, clip_ids)
     *a_sent, a_sums = named("conv_a", run, 0, 4, later, row=1, steps=steps - 1, parts=parts,
-                            sums_out=True, lead=top_rows, weigh=1)
+                            sums_out=True, lead=top_rows, vmem=63)
     a_sent = named("conv_top", run, 0, 4, later, steps=1, parts=parts, sums=(a_sums,),
-                   lead=STAT_ROWS, kept=a_sent, weigh=1)
-    run = functools.partial(conv_frames, frames, after(halo, a_sent[0]), weight, clip_ids, place)
-    onward, = named("conv_hist0", run, 2, 2, [(4, [(0, 0), (1, 1)], None)])
-    first_add = named("hist0", passed_along, onward, "tm", 1)
-    run = functools.partial(conv_frames, frames, after(halo, onward), weight, clip_ids, place)
+                   lead=STAT_ROWS, kept=a_sent, weigh=1, vmem=63)
+    a_got = send_far("a", a_sent)
+    run = functools.partial(conv_frames, frames, after(halo, a_sent[0]), weight, clip_ids)
+    ahead, = named("conv_hist0", run, 2, 2, [(4, [(0, 0), (1, 1)], None)])
+    first_add = named("hist0", passed_along, ahead, "tm", 1)
+    run = functools.partial(conv_frames, frames, after(halo, ahead), weight, clip_ids)
     onward, = named("conv_hist1", run, 3, 1, [(5, [(0, 0)], None)], weigh=40)
     second_add = named("hist1", passed_along, after(onward, first_add), "tm", 1)
-    b_sent = named("conv_b", run, 0, 1, [(0, [(0, 2)], 0)], addends=(after(first_add, onward),), parts=parts,
-                   lead=STAT_ROWS, weigh=20)
+    a_got.update(send_near("a", a_sent, True, a_sums))
+    b_sent = named("conv_b", run, 0, 1, [(0, [(0, 2)], 0)],
+                   addends=(after(first_add, onward, *[a_got[flip] for flip in near]),), parts=parts,
+                   lead=STAT_ROWS, weigh=20, vmem=24)
+    b_got = send_far("b", b_sent)
     c_sent = named("conv_c", run, 0, 2, [(1, [(0, 1), (1, 2)], 0)], addends=(second_add,), parts=parts,
-                   lead=STAT_ROWS, weigh=20)
-
-    a_got, b_got, c_got = {}, {}, {}
-    chain = []
-    for name, sent, got in (("a", a_sent, a_got), ("b", b_sent, b_got), ("c", c_sent, c_got)):
-        for flip in far:
-            earlier = chain[-4:][:1] if len(chain) >= 4 else []
-            got[flip] = named(f"{name}{flip}", exchanged, after(sent[flip], *earlier), "rows", flip)
-            chain.append(got[flip])
-    for name, sent, got, earlier in (("a", a_sent, a_got, a_sums), ("b", b_sent, b_got, c_sent[0]), ("c", c_sent, c_got, c_sent[0])):
-        for flip in near:
-            got[flip] = named(f"{name}{flip}", exchanged, after(sent[flip], earlier), "rows", flip)
-
-    def whole(sent, got):
-        return [sent[0]] + [got[flip] for flip in range(1, parts)]
-
-    a_all, b_all, c_all = whole(a_sent, a_got), whole(b_sent, b_got), whole(c_sent, c_got)
-    out = named("norm_a", norm_frames, a_all, gain, bias, place, 2, 2, shape, top_first=True)
-    out = named("norm_b", norm_frames, b_all, gain, bias, place, 0, 1, shape, base=out)
-    out = named("norm_c", norm_frames, c_all, gain, bias, place, 1, 1, shape, base=out)
+                   lead=STAT_ROWS, weigh=20, vmem=24)
+    out, a_done = named("norm_a", norm_frames, whole(a_sent, a_got), gain, bias, 2, 2, shape, top_first=True, vmem=20)
+    b_got.update(send_near("b", b_sent, False, c_sent[0]))
+    c_got = send_far("c", c_sent, a_done)
+    out, b_done = named("norm_b", norm_frames, whole(b_sent, b_got), gain, bias, 0, 1, shape, base=out, vmem=20)
+    c_got.update(send_near("c", c_sent, False, b_done))
+    out, _ = named("norm_c", norm_frames, whole(c_sent, c_got), gain, bias, 1, 1, shape, base=out, vmem=64)
     return out.reshape(count, parts * steps, shape[3], co)
 
 

time: 167 us -> 168 us (level)
  the two profiles are of different devices: /device:TPU:15 before, /device:TPU:4 now
where the time goes in v4:
time: 168 us; the launch traced here: 167 us
  Pallas kernels  62.8 us (37%)
  waiting for transfers between devices  48.1 us (29%)
  starting transfers between devices  47 us (28%)
  local copies, waits for them, and re-layouts  9.23 us (5%)
    pallas_call x6, Pallas kernels, conv_frames(): pl.pallas_call(functools.partial(conv_kernel, plan), out_shape=out_shape,...  53.7 us
    ppermute x21, starting transfers between devices, exchanged(): return lax.ppermute(array, axis, [(i, i ^ flip) for i in range(length)])  38 us
    ppermute x21, waiting for transfers between devices, exchanged(): return lax.ppermute(array, axis, [(i, i ^ flip) for i in range(length)])  27.9 us
    ppermute x3, waiting for transfers between devices, passed_along(): return lax.ppermute(array, axis, pairs)  20.2 us
    pallas_call x3, Pallas kernels, norm_frames(): pl.pallas_call(functools.partial(norm_kernel, plan), out_shape=[jax.Shape...  9.18 us
    ppermute x3, starting transfers between devices, passed_along(): return lax.ppermute(array, axis, pairs)  8.92 us
    unnamed x40, local copies, waits for them, and re-layouts  6.77 us
  transfers between devices with their start and end apart: 24, of which 7 were waited for; matrix products, arithmetic and copies ran while one was open for 0% of the time, Pallas kernels for 31%

profile of v4, /device:TPU:4, one launch (start us, length us, event | category | flops | bytes accessed | tf_op | source)
XLA Modules:
  0.0 167.4 jit_solution(6550787221822933106)
XLA Ops:
  0.0 2.5 %slice.3 = bf16[4,1,1280,128]{3,2,1,0:T(8,128)(2,1)} slice(bf16[4,8,1280,128]{3,2,1,0:T(8,128)(2,1)} %x_ref.11), slice={[0:4], [7:8], [0:1280], [0:128]} | slice | bytes 2621440 | tf_op jit(solution)/shard_map/slice | solution.py:367
  2.5 2.8 %collective-permute-start = (bf16[4,1,1280,128]{3,2,1,0:T(8,128)(2,1)}, bf16[4,1,1280,128]{3,2,1,0:T(8,128)(2,1)}, u32[]{:S(2)}, u32[]{:S(2)}) collective-permute-start(bf16[4,1,1280,128]{3,2,1,0:T(8,128)(2,1)} %slice.3), channel_id=1, source_target_pairs={{0,1},{1,2},{2,3},{3,4},{4,5},{5,6},{6,7},{8,9},{9,10},{10,11},{11... | collective-permute-start | bytes 3932168 | tf_op jit(solution)/shard_map/halo/ppermute | solution.py:18
  5.3 15.0 %conv_a.1 = (bf16[656,256]{1,0:T(8,128)(2,1)}, bf16[656,256]{1,0:T(8,128)(2,1)}, bf16[656,256]{1,0:T(8,128)(2,1)}, bf16[656,256]{1,0:T(8,128)(2,1)}, bf16[656,25...) custom-call(s32[16]{0:T(128)} %clip_ref.11, ...), custom_call_target="tpu_custom_call" | custom-call | flops 6794772480 | bytes 9830400 | tf_op jit(solution)/shard_map/conv_a/pallas_call | solution.py:216
  20.4 0.0 collective-permute-done.above_ref
  20.4 7.3 %conv_top.1 = (bf16[656,256]{1,0:T(8,128)(2,1)}, bf16[656,256]{1,0:T(8,128)(2,1)}, bf16[656,256]{1,0:T(8,128)(2,1)}, bf16[656,256]{1,0:T(8,128)(2,1)}, bf16[656,...) custom-call(s32[16]{0:T(128)} %clip_ref.11, ...), custom_call_target="tpu_custom_call", output_to_operand_aliasing={{0}: (5, {}), {1}: (6, {}), {2}: (7, {}), {3}: (8, {}), {4}... | custom-call | flops 2264924160 | bytes 3276800 | tf_op jit(solution)/shard_map/conv_top/pallas_call | solution.py:216
  27.7 0.8 collective-permute-start.3
  28.5 1.5 collective-permute-done.3.refs_1_
  30.0 0.7 copy-done.3
  30.7 2.5 %collective-permute-start.4 = (bf16[656,256]{1,0:T(8,128)(2,1)}, bf16[656,256]{1,0:T(8,128)(2,1)S(1)}, u32[]{:S(2)}, u32[]{:S(2)}) collective-permute-start(bf16[656,256]{1,0:T(8,128)(2,1)} %get-tuple-element.82), channel_id=1, source_target_pairs={{0,2},{1,3},{2,0},{3,1},{4,6},{5,7},{6,4},{7,5},{8,10},{9,11},{10,... | collective-permute-start | bytes 1007624 | tf_op jit(solution)/shard_map/a2/ppermute | solution.py:23
  33.2 2.0 %collective-permute-start.11 = (bf16[656,256]{1,0:T(8,128)(2,1)}, bf16[656,256]{1,0:T(8,128)(2,1)S(1)}, u32[]{:S(2)}, u32[]{:S(2)}) collective-permute-start(bf16[656,256]{1,0:T(8,128)(2,1)} %get-tuple-element.97), channel_id=1, source_target_pairs={{0,5},{1,4},{2,7},{3,6},{4,1},{5,0},{6,3},{7,2},{8,13},{9,12},{10,... | collective-permute-start | bytes 1007624 | tf_op jit(solution)/shard_map/a5/ppermute | solution.py:23
  35.3 0.4 collective-permute-start.13
  35.7 3.4 %collective-permute-start.15 = (bf16[656,256]{1,0:T(8,128)(2,1)}, bf16[656,256]{1,0:T(8,128)(2,1)S(1)}, u32[]{:S(2)}, u32[]{:S(2)}) collective-permute-start(bf16[656,256]{1,0:T(8,128)(2,1)} %get-tuple-element.103), channel_id=1, source_target_pairs={{0,7},{1,6},{2,5},{3,4},{4,3},{5,2},{6,1},{7,0},{8,15},{9,14},{10,... | collective-permute-start | bytes 1007624 | tf_op jit(solution)/shard_map/a7/ppermute | solution.py:23
  39.1 8.5 %conv_hist0.1 = bf16[1,4,640,256]{3,2,1,0:T(8,128)(2,1)} custom-call(s32[16]{0:T(128)} %clip_ref.11, bf16[4,8,1280,128]{3,2,1,0:T(8,128)(2,1)} %x_ref.11, bf16[4,1,1280,128]{3,2,1,0:T(8,128)(2,1)} %collective-permute-done.above_ref, bf16[3,1152,256]{2,1,0:T(8,128)(2,1)} %bitcast.6), custom_call_target="tpu_custom_call" | custom-call | flops 3019898880 | bytes 6553600 | tf_op jit(solution)/shard_map/conv_hist0/pallas_call | solution.py:216
  47.6 3.4 %collective-permute-start.1 = (bf16[1,4,640,256]{3,2,1,0:T(8,128)(2,1)}, bf16[1,4,640,256]{3,2,1,0:T(8,128)(2,1)}, u32[]{:S(2)}, u32[]{:S(2)}) collective-permute-start(bf16[1,4,640,256]{3,2,1,0:T(8,128)(2,1)} %conv_hist0.1), channel_id=1, source_target_pairs={{0,8},{8,16},{16,24},{1,9},{9,17},{17,25},{2,10},{10,18},{18,26},{... | collective-permute-start | bytes 3932168 | tf_op jit(solution)/shard_map/hist0/ppermute | solution.py:18
  51.0 0.0 collective-permute-done.4.refs_2_
  51.0 0.7 copy-done.5
  51.7 0.1 collective-permute-start.5
  51.8 6.4 %conv_hist1.1 = bf16[1,4,640,256]{3,2,1,0:T(8,128)(2,1)} custom-call(s32[16]{0:T(128)} %clip_ref.11, bf16[4,8,1280,128]{3,2,1,0:T(8,128)(2,1)} %x_ref.11, bf16[4,1,1280,128]{3,2,1,0:T(8,128)(2,1)} %collective-permute-done.above_ref, bf16[3,1152,256]{2,1,0:T(8,128)(2,1)} %bitcast.7), custom_call_target="tpu_custom_call" | custom-call | flops 60397977600 | bytes 157286400 | tf_op jit(solution)/shard_map/conv_hist1/pallas_call | solution.py:216
  58.2 15.2 %collective-permute-done.5.refs_3_ = bf16[656,256]{1,0:T(8,128)(2,1)S(1)} collective-permute-done((bf16[656,256]{1,0:T(8,128)(2,1)S(1)}, bf16[656,256]{1,0:T(8,128)(2,1)S(1)}, u32[]{:S(2)}, u32[]{:S(2)}) %collective-permute-start.5) | collective-permute-done | bytes 335904 | tf_op jit(solution)/shard_map/a3/ppermute | solution.py:23
  73.4 0.6 collective-permute-start.9
  73.9 7.6 %collective-permute-done.1.refs_0_ = bf16[1,4,640,256]{3,2,1,0:T(8,128)(2,1)} collective-permute-done((bf16[1,4,640,256]{3,2,1,0:T(8,128)(2,1)}, bf16[1,4,640,256]{3,2,1,0:T(8,128)(2,1)}, u32[]{:S(2)}, u32[]{:S(2)}) %collective-permute-start.1) | collective-permute-done | bytes 1310752 | tf_op jit(solution)/shard_map/hist0/ppermute | solution.py:18
  81.5 2.7 %collective-permute-start.2 = (bf16[1,4,640,256]{3,2,1,0:T(8,128)(2,1)}, bf16[1,4,640,256]{3,2,1,0:T(8,128)(2,1)S(1)}, u32[]{:S(2)}, u32[]{:S(2)}) collective-permute-start(bf16[1,4,640,256]{3,2,1,0:T(8,128)(2,1)} %conv_hist1.1), channel_id=1, source_target_pairs={{0,8},{8,16},{16,24},{1,9},{9,17},{17,25},{2,10},{10,18},{18,26},{... | collective-permute-start | bytes 3932168 | tf_op jit(solution)/shard_map/hist1/ppermute | solution.py:18
  84.2 0.0 copy-start
  84.2 4.0 %copy-done = bf16[4,8,1280,128]{3,2,1,0:T(8,128)(2,1)S(1)} copy-done((bf16[4,8,1280,128]{3,2,1,0:T(8,128)(2,1)S(1)}, bf16[4,8,1280,128]{3,2,1,0:T(8,128)(2,1)}, u32[]{:S(2)}) %copy-start) | copy-done | bytes 10485784
  88.2 7.3 %conv_b.1 = (bf16[336,256]{1,0:T(8,128)(2,1)S(1)}, bf16[336,256]{1,0:T(8,128)(2,1)S(1)}, bf16[336,256]{1,0:T(8,128)(2,1)S(1)}, bf16[336,256]{1,0:T(8,128)(2,1)S(...) custom-call(s32[16]{0:T(128)S(1)} %copy-done.10, ...), custom_call_target="tpu_custom_call" | custom-call | flops 30198988800 | bytes 78643200 | tf_op jit(solution)/shard_map/conv_b/pallas_call | solution.py:216
  95.5 0.0 collective-permute-done.15.refs_7_
  95.5 0.1 collective-permute-start.16
  95.6 0.0 collective-permute-done.13.refs_6_
  95.6 2.4 %collective-permute-start.14 = (bf16[336,256]{1,0:T(8,128)(2,1)S(1)}, bf16[336,256]{1,0:T(8,128)(2,1)S(1)}, u32[]{:S(2)}, u32[]{:S(2)}) collective-permute-start(bf16[336,256]{1,0:T(8,128)(2,1)S(1)} %get-tuple-element.101), channel_id=1, source_target_pairs={{0,6},{1,7},{2,4},{3,5},{4,2},{5,3},{6,0},{7,1},{8,14},{9,15},{10,... | collective-permute-start | bytes 516104 | tf_op jit(solution)/shard_map/b6/ppermute | solution.py:23
  98.1 0.0 collective-permute-done.11.refs_5_
  98.1 0.0 collective-permute-start.12
  98.1 0.0 collective-permute-done.9.refs_4_
  98.1 0.0 copy-start.8
  98.1 0.0 copy-start.9
  98.1 3.8 %collective-permute-start.10 = (bf16[336,256]{1,0:T(8,128)(2,1)S(1)}, bf16[336,256]{1,0:T(8,128)(2,1)S(1)}, u32[]{:S(2)}, u32[]{:S(2)}) collective-permute-start(bf16[336,256]{1,0:T(8,128)(2,1)S(1)} %get-tuple-element.95), channel_id=1, source_target_pairs={{0,4},{1,5},{2,6},{3,7},{4,0},{5,1},{6,2},{7,3},{8,12},{9,13},{10,... | collective-permute-start | bytes 516104 | tf_op jit(solution)/shard_map/b4/ppermute | solution.py:23
  101.9 12.6 %collective-permute-done.2.refs_0_ = bf16[1,4,640,256]{3,2,1,0:T(8,128)(2,1)S(1)} collective-permute-done((bf16[1,4,640,256]{3,2,1,0:T(8,128)(2,1)}, bf16[1,4,640,256]{3,2,1,0:T(8,128)(2,1)S(1)}, u32[]{:S(2)}, u32[]{:S(2)}) %collective-permute-start.2) | collective-permute-done | bytes 1310752 | tf_op jit(solution)/shard_map/hist1/ppermute | solution.py:18
  114.5 9.1 %conv_c.1 = (bf16[336,256]{1,0:T(8,128)(2,1)S(1)}, bf16[336,256]{1,0:T(8,128)(2,1)S(1)}, bf16[336,256]{1,0:T(8,128)(2,1)S(1)}, bf16[336,256]{1,0:T(8,128)(2,1)S(...) custom-call(s32[16]{0:T(128)S(1)} %copy-done.10, ...), custom_call_target="tpu_custom_call" | custom-call | flops 60397977600 | bytes 131072000 | tf_op jit(solution)/shard_map/conv_c/pallas_call | solution.py:216
  123.7 0.1 collective-permute-start.8
  123.7 0.0 collective-permute-done.16.refs_7_
  123.8 0.1 collective-permute-start.7
  123.8 0.0 collective-permute-done.14.refs_6_
  123.8 1.8 %collective-permute-start.6 = (bf16[336,256]{1,0:T(8,128)(2,1)S(1)}, bf16[336,256]{1,0:T(8,128)(2,1)S(1)}, u32[]{:S(2)}, u32[]{:S(2)}) collective-permute-start(bf16[336,256]{1,0:T(8,128)(2,1)S(1)} %get-tuple-element.88), channel_id=1, source_target_pairs={{0,1},{1,0},{2,3},{3,2},{4,5},{5,4},{6,7},{7,6},{8,9},{9,8},{10,11... | collective-permute-start | bytes 516104 | tf_op jit(solution)/shard_map/b1/ppermute | solution.py:23
  125.6 3.4 %norm_a.1 = (bf16[4,8,4,80,256]{4,3,2,1,0:T(8,128)(2,1)}, f32[8,256]{1,0:T(8,128)}) custom-call(bf16[656,256]{1,0:T(8,128)(2,1)S(1)} %copy-done.2, bf16[656,256]{1,0:T(8,128)(2,1)S(1)} %copy-done.4, bf16[656,256]{1,0:T(8,128)(2,1)S(1)} %copy-done.6, bf16[656,256]{1,0:T(8,128)(2,1)S(1)} %collective-permute-done.5.refs_3_, ...), custom_call_target="tpu_custom_call" | custom-call | flops 10485760 | bytes 5242880 | tf_op jit(solution)/shard_map/norm_a/pallas_call | solution.py:307
  129.1 0.0 collective-permute-done.12.refs_5_
  129.1 0.2 collective-permute-start.23
  129.3 0.0 collective-permute-done.10.refs_4_
  129.3 3.3 %collective-permute-start.22 = (bf16[336,256]{1,0:T(8,128)(2,1)S(1)}, bf16[336,256]{1,0:T(8,128)(2,1)S(1)}, u32[]{:S(2)}, u32[]{:S(2)}) collective-permute-start(bf16[336,256]{1,0:T(8,128)(2,1)S(1)} %get-tuple-element.118), channel_id=1, source_target_pairs={{0,6},{1,7},{2,4},{3,5},{4,2},{5,3},{6,0},{7,1},{8,14},{9,15},{10,... | collective-permute-start | bytes 516104 | tf_op jit(solution)/shard_map/c6/ppermute | solution.py:23
  132.6 0.0 collective-permute-done.8.refs_3_
  132.6 0.0 collective-permute-start.21
  132.6 0.0 collective-permute-done.7.refs_2_
  132.6 2.7 %collective-permute-start.20 = (bf16[336,256]{1,0:T(8,128)(2,1)S(1)}, bf16[336,256]{1,0:T(8,128)(2,1)S(1)}, u32[]{:S(2)}, u32[]{:S(2)}) collective-permute-start(bf16[336,256]{1,0:T(8,128)(2,1)S(1)} %get-tuple-element.114), channel_id=1, source_target_pairs={{0,4},{1,5},{2,6},{3,7},{4,0},{5,1},{6,2},{7,3},{8,12},{9,13},{10,... | collective-permute-start | bytes 516104 | tf_op jit(solution)/shard_map/c4/ppermute | solution.py:23
  135.3 0.0 collective-permute-done.6.refs_1_
  135.3 2.1 %norm_b.1 = (bf16[4,8,4,80,256]{4,3,2,1,0:T(8,128)(2,1)}, f32[8,256]{1,0:T(8,128)}) custom-call(bf16[336,256]{1,0:T(8,128)(2,1)S(1)} %get-tuple-element.86.refs_0_, bf16[336,256]{1,0:T(8,128)(2,1)S(1)} %collective-permute-done.6.refs_1_, bf16[336,256]{1,0:T(8,128)(2,1)S(1)} %collective-permute-done.7.refs_2_, ...), custom_call_target="tpu_custom_call", output_to_operand_aliasing={{0}: (10, {})} | custom-call | flops 5242880 | bytes 2621440 | tf_op jit(solution)/shard_map/norm_b/pallas_call | solution.py:307
  137.5 7.0 %collective-permute-start.19 = (bf16[336,256]{1,0:T(8,128)(2,1)S(1)}, bf16[336,256]{1,0:T(8,128)(2,1)S(1)}, u32[]{:S(2)}, u32[]{:S(2)}) collective-permute-start(bf16[336,256]{1,0:T(8,128)(2,1)S(1)} %get-tuple-element.111), channel_id=1, source_target_pairs={{0,3},{1,2},{2,1},{3,0},{4,7},{5,6},{6,5},{7,4},{8,11},{9,10},{10,... | collective-permute-start | bytes 516104 | tf_op jit(solution)/shard_map/c3/ppermute | solution.py:23
  144.4 0.0 collective-permute-done.23.refs_7_
  144.4 5.9 %collective-permute-start.18 = (bf16[336,256]{1,0:T(8,128)(2,1)S(1)}, bf16[336,256]{1,0:T(8,128)(2,1)S(1)}, u32[]{:S(2)}, u32[]{:S(2)}) collective-permute-start(bf16[336,256]{1,0:T(8,128)(2,1)S(1)} %get-tuple-element.109), channel_id=1, source_target_pairs={{0,2},{1,3},{2,0},{3,1},{4,6},{5,7},{6,4},{7,5},{8,10},{9,11},{10,... | collective-permute-start | bytes 516104 | tf_op jit(solution)/shard_map/c2/ppermute | solution.py:23
  150.3 0.0 collective-permute-done.22.refs_6_
  150.4 0.9 collective-permute-start.17
  151.3 6.0 %collective-permute-done.21.refs_5_ = bf16[336,256]{1,0:T(8,128)(2,1)S(1)} collective-permute-done((bf16[336,256]{1,0:T(8,128)(2,1)S(1)}, bf16[336,256]{1,0:T(8,128)(2,1)S(1)}, u32[]{:S(2)}, u32[]{:S(2)}) %collective-permute-start.21) | collective-permute-done | bytes 172064 | tf_op jit(solution)/shard_map/c5/ppermute | solution.py:23
  157.3 4.2 %collective-permute-done.20.refs_4_ = bf16[336,256]{1,0:T(8,128)(2,1)S(1)} collective-permute-done((bf16[336,256]{1,0:T(8,128)(2,1)S(1)}, bf16[336,256]{1,0:T(8,128)(2,1)S(1)}, u32[]{:S(2)}, u32[]{:S(2)}) %collective-permute-start.20) | collective-permute-done | bytes 172064 | tf_op jit(solution)/shard_map/c4/ppermute | solution.py:23
  161.5 1.0 collective-permute-done.18.refs_2_
  162.5 0.6 copy-done.18
  163.2 0.7 copy-done.19
  163.8 3.6 %norm_c.1 = (bf16[4,8,4,80,256]{4,3,2,1,0:T(8,128)(2,1)}, f32[8,256]{1,0:T(8,128)}) custom-call(bf16[336,256]{1,0:T(8,128)(2,1)} %copy-done.7, bf16[336,256]{1,0:T(8,128)(2,1)} %copy-done.19, bf16[336,256]{1,0:T(8,128)(2,1)} %copy-done.18, bf16[336,256]{1,0:T(8,128)(2,1)} %copy-done.17, ...), custom_call_target="tpu_custom_call", output_to_operand_aliasing={{0}: (10, {})} | custom-call | flops 5242880 | bytes 2621440 | tf_op jit(solution)/shard_map/norm_c/pallas_call | solution.py:307
  (34 shorter events, 0.1 us)
Async XLA Ops:
  2.5 17.9 %collective-permute-start = (bf16[4,1,1280,128]{3,2,1,0:T(8,128)(2,1)}, bf16[4,1,1280,128]{3,2,1,0:T(8,128)(2,1)}, u32[]{:S(2)}, u32[]{:S(2)}) collective-permute-start(bf16[4,1,1280,128]{3,2,1,0:T(8,128)(2,1)} %slice.3), channel_id=1, source_target_pairs={{0,1},{1,2},{2,3},{3,4},{4,5},{5,6},{6,7},{8,9},{9,10},{10,11},{11... | collective-permute-start | bytes 3932168 | tf_op jit(solution)/shard_map/halo/ppermute | solution.py:18
  27.7 2.3 %collective-permute-start.3 = (bf16[656,256]{1,0:T(8,128)(2,1)}, bf16[656,256]{1,0:T(8,128)(2,1)S(1)}, u32[]{:S(2)}, u32[]{:S(2)}) collective-permute-start(bf16[656,256]{1,0:T(8,128)(2,1)} %get-tuple-element.80), channel_id=1, source_target_pairs={{0,1},{1,0},{2,3},{3,2},{4,5},{5,4},{6,7},{7,6},{8,9},{9,8},{10,11... | collective-permute-start | bytes 1007624 | tf_op jit(solution)/shard_map/a1/ppermute | solution.py:23
  30.0 0.7 copy-start.3
  30.7 20.3 %collective-permute-start.4 = (bf16[656,256]{1,0:T(8,128)(2,1)}, bf16[656,256]{1,0:T(8,128)(2,1)S(1)}, u32[]{:S(2)}, u32[]{:S(2)}) collective-permute-start(bf16[656,256]{1,0:T(8,128)(2,1)} %get-tuple-element.82), channel_id=1, source_target_pairs={{0,2},{1,3},{2,0},{3,1},{4,6},{5,7},{6,4},{7,5},{8,10},{9,11},{10,... | collective-permute-start | bytes 1007624 | tf_op jit(solution)/shard_map/a2/ppermute | solution.py:23
  33.2 64.8 %collective-permute-start.11 = (bf16[656,256]{1,0:T(8,128)(2,1)}, bf16[656,256]{1,0:T(8,128)(2,1)S(1)}, u32[]{:S(2)}, u32[]{:S(2)}) collective-permute-start(bf16[656,256]{1,0:T(8,128)(2,1)} %get-tuple-element.97), channel_id=1, source_target_pairs={{0,5},{1,4},{2,7},{3,6},{4,1},{5,0},{6,3},{7,2},{8,13},{9,12},{10,... | collective-permute-start | bytes 1007624 | tf_op jit(solution)/shard_map/a5/ppermute | solution.py:23
  35.3 60.3 %collective-permute-start.13 = (bf16[656,256]{1,0:T(8,128)(2,1)}, bf16[656,256]{1,0:T(8,128)(2,1)S(1)}, u32[]{:S(2)}, u32[]{:S(2)}) collective-permute-start(bf16[656,256]{1,0:T(8,128)(2,1)} %get-tuple-element.100), channel_id=1, source_target_pairs={{0,6},{1,7},{2,4},{3,5},{4,2},{5,3},{6,0},{7,1},{8,14},{9,15},{10,... | collective-permute-start | bytes 1007624 | tf_op jit(solution)/shard_map/a6/ppermute | solution.py:23
  35.7 59.8 %collective-permute-start.15 = (bf16[656,256]{1,0:T(8,128)(2,1)}, bf16[656,256]{1,0:T(8,128)(2,1)S(1)}, u32[]{:S(2)}, u32[]{:S(2)}) collective-permute-start(bf16[656,256]{1,0:T(8,128)(2,1)} %get-tuple-element.103), channel_id=1, source_target_pairs={{0,7},{1,6},{2,5},{3,4},{4,3},{5,2},{6,1},{7,0},{8,15},{9,14},{10,... | collective-permute-start | bytes 1007624 | tf_op jit(solution)/shard_map/a7/ppermute | solution.py:23
  39.1 12.6 %copy-start.11 = (bf16[656,256]{1,0:T(8,128)(2,1)S(1)}, bf16[656,256]{1,0:T(8,128)(2,1)}, u32[]{:S(2)}) copy-start(bf16[656,256]{1,0:T(8,128)(2,1)} %get-tuple-element.84) | copy-start | bytes 1007620
  47.6 33.9 %collective-permute-start.1 = (bf16[1,4,640,256]{3,2,1,0:T(8,128)(2,1)}, bf16[1,4,640,256]{3,2,1,0:T(8,128)(2,1)}, u32[]{:S(2)}, u32[]{:S(2)}) collective-permute-start(bf16[1,4,640,256]{3,2,1,0:T(8,128)(2,1)} %conv_hist0.1), channel_id=1, source_target_pairs={{0,8},{8,16},{16,24},{1,9},{9,17},{17,25},{2,10},{10,18},{18,26},{... | collective-permute-start | bytes 3932168 | tf_op jit(solution)/shard_map/hist0/ppermute | solution.py:18
  51.0 0.7 copy-start.5
  51.7 21.6 %copy-start.12 = (bf16[656,256]{1,0:T(8,128)(2,1)S(1)}, bf16[656,256]{1,0:T(8,128)(2,1)}, u32[]{:S(2)}) copy-start(bf16[656,256]{1,0:T(8,128)(2,1)} %get-tuple-element.94) | copy-start | bytes 1007620
  51.7 32.5 %copy-start.1 = (bf16[3,3,3,128,256]{4,3,2,1,0:T(8,128)(2,1)S(1)}, bf16[3,3,3,128,256]{4,3,2,1,0:T(8,128)(2,1)}, u32[]{:S(2)}) copy-start(bf16[3,3,3,128,256]{4,3,2,1,0:T(8,128)(2,1)} %param.7) | copy-start | bytes 5308420
  51.7 32.5 %copy-start.10 = (s32[16]{0:T(128)S(1)}, s32[16]{0:T(128)}, u32[]{:S(2)}) copy-start(s32[16]{0:T(128)} %clip_ref.11) | copy-start | bytes 196
  51.7 21.6 %collective-permute-start.5 = (bf16[656,256]{1,0:T(8,128)(2,1)S(1)}, bf16[656,256]{1,0:T(8,128)(2,1)S(1)}, u32[]{:S(2)}, u32[]{:S(2)}) collective-permute-start(bf16[656,256]{1,0:T(8,128)(2,1)S(1)} %copy-done.11), channel_id=1, source_target_pairs={{0,3},{1,2},{2,1},{3,0},{4,7},{5,6},{6,5},{7,4},{8,11},{9,10},{10,... | collective-permute-start | bytes 1007624 | tf_op jit(solution)/shard_map/a3/ppermute | solution.py:23
  73.4 24.7 %collective-permute-start.9 = (bf16[656,256]{1,0:T(8,128)(2,1)S(1)}, bf16[656,256]{1,0:T(8,128)(2,1)S(1)}, u32[]{:S(2)}, u32[]{:S(2)}) collective-permute-start(bf16[656,256]{1,0:T(8,128)(2,1)S(1)} %copy-done.12), channel_id=1, source_target_pairs={{0,4},{1,5},{2,6},{3,7},{4,0},{5,1},{6,2},{7,3},{8,12},{9,13},{10,... | collective-permute-start | bytes 1007624 | tf_op jit(solution)/shard_map/a4/ppermute | solution.py:23
  81.5 33.0 %collective-permute-start.2 = (bf16[1,4,640,256]{3,2,1,0:T(8,128)(2,1)}, bf16[1,4,640,256]{3,2,1,0:T(8,128)(2,1)S(1)}, u32[]{:S(2)}, u32[]{:S(2)}) collective-permute-start(bf16[1,4,640,256]{3,2,1,0:T(8,128)(2,1)} %conv_hist1.1), channel_id=1, source_target_pairs={{0,8},{8,16},{16,24},{1,9},{9,17},{17,25},{2,10},{10,18},{18,26},{... | collective-permute-start | bytes 3932168 | tf_op jit(solution)/shard_map/hist1/ppermute | solution.py:18
  84.2 4.0 %copy-start = (bf16[4,8,1280,128]{3,2,1,0:T(8,128)(2,1)S(1)}, bf16[4,8,1280,128]{3,2,1,0:T(8,128)(2,1)}, u32[]{:S(2)}) copy-start(bf16[4,8,1280,128]{3,2,1,0:T(8,128)(2,1)} %x_ref.11) | copy-start | bytes 31457284
  95.5 28.2 %collective-permute-start.16 = (bf16[336,256]{1,0:T(8,128)(2,1)S(1)}, bf16[336,256]{1,0:T(8,128)(2,1)S(1)}, u32[]{:S(2)}, u32[]{:S(2)}) collective-permute-start(bf16[336,256]{1,0:T(8,128)(2,1)S(1)} %get-tuple-element.104), channel_id=1, source_target_pairs={{0,7},{1,6},{2,5},{3,4},{4,3},{5,2},{6,1},{7,0},{8,15},{9,14},{10,... | collective-permute-start | bytes 516104 | tf_op jit(solution)/shard_map/b7/ppermute | solution.py:23
  95.6 28.2 %collective-permute-start.14 = (bf16[336,256]{1,0:T(8,128)(2,1)S(1)}, bf16[336,256]{1,0:T(8,128)(2,1)S(1)}, u32[]{:S(2)}, u32[]{:S(2)}) collective-permute-start(bf16[336,256]{1,0:T(8,128)(2,1)S(1)} %get-tuple-element.101), channel_id=1, source_target_pairs={{0,6},{1,7},{2,4},{3,5},{4,2},{5,3},{6,0},{7,1},{8,14},{9,15},{10,... | collective-permute-start | bytes 516104 | tf_op jit(solution)/shard_map/b6/ppermute | solution.py:23
  98.1 31.0 %collective-permute-start.12 = (bf16[336,256]{1,0:T(8,128)(2,1)S(1)}, bf16[336,256]{1,0:T(8,128)(2,1)S(1)}, u32[]{:S(2)}, u32[]{:S(2)}) collective-permute-start(bf16[336,256]{1,0:T(8,128)(2,1)S(1)} %get-tuple-element.98), channel_id=1, source_target_pairs={{0,5},{1,4},{2,7},{3,6},{4,1},{5,0},{6,3},{7,2},{8,13},{9,12},{10,... | collective-permute-start | bytes 516104 | tf_op jit(solution)/shard_map/b5/ppermute | solution.py:23
  98.1 27.5 %copy-start.2 = (bf16[656,256]{1,0:T(8,128)(2,1)S(1)}, bf16[656,256]{1,0:T(8,128)(2,1)}, u32[]{:S(2)}) copy-start(bf16[656,256]{1,0:T(8,128)(2,1)} %get-tuple-element.73.refs_0_) | copy-start | bytes 1007620
  98.1 27.5 %copy-start.4 = (bf16[656,256]{1,0:T(8,128)(2,1)S(1)}, bf16[656,256]{1,0:T(8,128)(2,1)}, u32[]{:S(2)}) copy-start(bf16[656,256]{1,0:T(8,128)(2,1)} %copy-done.3) | copy-start | bytes 1007620
  98.1 27.5 %copy-start.6 = (bf16[656,256]{1,0:T(8,128)(2,1)S(1)}, bf16[656,256]{1,0:T(8,128)(2,1)}, u32[]{:S(2)}) copy-start(bf16[656,256]{1,0:T(8,128)(2,1)} %copy-done.5) | copy-start | bytes 1007620
  98.1 27.5 %copy-start.8 = (f32[256]{0:T(256)S(1)}, f32[256]{0:T(256)}, u32[]{:S(2)}) copy-start(f32[256]{0:T(256)} %param.8) | copy-start | bytes 3076
  98.1 27.5 %copy-start.9 = (f32[256]{0:T(256)S(1)}, f32[256]{0:T(256)}, u32[]{:S(2)}) copy-start(f32[256]{0:T(256)} %param.9) | copy-start | bytes 3076
  98.1 31.2 %collective-permute-start.10 = (bf16[336,256]{1,0:T(8,128)(2,1)S(1)}, bf16[336,256]{1,0:T(8,128)(2,1)S(1)}, u32[]{:S(2)}, u32[]{:S(2)}) collective-permute-start(bf16[336,256]{1,0:T(8,128)(2,1)S(1)} %get-tuple-element.95), channel_id=1, source_target_pairs={{0,4},{1,5},{2,6},{3,7},{4,0},{5,1},{6,2},{7,3},{8,12},{9,13},{10,... | collective-permute-start | bytes 516104 | tf_op jit(solution)/shard_map/b4/ppermute | solution.py:23
  123.7 5.4 %copy-start.7 = (bf16[336,256]{1,0:T(8,128)(2,1)}, bf16[336,256]{1,0:T(8,128)(2,1)S(1)}, u32[]{:S(2)}) copy-start(bf16[336,256]{1,0:T(8,128)(2,1)S(1)} %get-tuple-element.77.refs_0_) | copy-start | bytes 516100
  123.7 8.9 %collective-permute-start.8 = (bf16[336,256]{1,0:T(8,128)(2,1)S(1)}, bf16[336,256]{1,0:T(8,128)(2,1)S(1)}, u32[]{:S(2)}, u32[]{:S(2)}) collective-permute-start(bf16[336,256]{1,0:T(8,128)(2,1)S(1)} %get-tuple-element.92), channel_id=1, source_target_pairs={{0,3},{1,2},{2,1},{3,0},{4,7},{5,6},{6,5},{7,4},{8,11},{9,10},{10,... | collective-permute-start | bytes 516104 | tf_op jit(solution)/shard_map/b3/ppermute | solution.py:23
  123.8 8.8 %collective-permute-start.7 = (bf16[336,256]{1,0:T(8,128)(2,1)S(1)}, bf16[336,256]{1,0:T(8,128)(2,1)S(1)}, u32[]{:S(2)}, u32[]{:S(2)}) collective-permute-start(bf16[336,256]{1,0:T(8,128)(2,1)S(1)} %get-tuple-element.90), channel_id=1, source_target_pairs={{0,2},{1,3},{2,0},{3,1},{4,6},{5,7},{6,4},{7,5},{8,10},{9,11},{10,... | collective-permute-start | bytes 516104 | tf_op jit(solution)/shard_map/b2/ppermute | solution.py:23
  123.8 11.5 %collective-permute-start.6 = (bf16[336,256]{1,0:T(8,128)(2,1)S(1)}, bf16[336,256]{1,0:T(8,128)(2,1)S(1)}, u32[]{:S(2)}, u32[]{:S(2)}) collective-permute-start(bf16[336,256]{1,0:T(8,128)(2,1)S(1)} %get-tuple-element.88), channel_id=1, source_target_pairs={{0,1},{1,0},{2,3},{3,2},{4,5},{5,4},{6,7},{7,6},{8,9},{9,8},{10,11... | collective-permute-start | bytes 516104 | tf_op jit(solution)/shard_map/b1/ppermute | solution.py:23
  129.1 15.4 %collective-permute-start.23 = (bf16[336,256]{1,0:T(8,128)(2,1)S(1)}, bf16[336,256]{1,0:T(8,128)(2,1)S(1)}, u32[]{:S(2)}, u32[]{:S(2)}) collective-permute-start(bf16[336,256]{1,0:T(8,128)(2,1)S(1)} %get-tuple-element.120), channel_id=1, source_target_pairs={{0,7},{1,6},{2,5},{3,4},{4,3},{5,2},{6,1},{7,0},{8,15},{9,14},{10,... | collective-permute-start | bytes 516104 | tf_op jit(solution)/shard_map/c7/ppermute | solution.py:23
  129.3 21.1 %collective-permute-start.22 = (bf16[336,256]{1,0:T(8,128)(2,1)S(1)}, bf16[336,256]{1,0:T(8,128)(2,1)S(1)}, u32[]{:S(2)}, u32[]{:S(2)}) collective-permute-start(bf16[336,256]{1,0:T(8,128)(2,1)S(1)} %get-tuple-element.118), channel_id=1, source_target_pairs={{0,6},{1,7},{2,4},{3,5},{4,2},{5,3},{6,0},{7,1},{8,14},{9,15},{10,... | collective-permute-start | bytes 516104 | tf_op jit(solution)/shard_map/c6/ppermute | solution.py:23
  132.6 24.7 %collective-permute-start.21 = (bf16[336,256]{1,0:T(8,128)(2,1)S(1)}, bf16[336,256]{1,0:T(8,128)(2,1)S(1)}, u32[]{:S(2)}, u32[]{:S(2)}) collective-permute-start(bf16[336,256]{1,0:T(8,128)(2,1)S(1)} %get-tuple-element.116), channel_id=1, source_target_pairs={{0,5},{1,4},{2,7},{3,6},{4,1},{5,0},{6,3},{7,2},{8,13},{9,12},{10,... | collective-permute-start | bytes 516104 | tf_op jit(solution)/shard_map/c5/ppermute | solution.py:23
  132.6 28.9 %collective-permute-start.20 = (bf16[336,256]{1,0:T(8,128)(2,1)S(1)}, bf16[336,256]{1,0:T(8,128)(2,1)S(1)}, u32[]{:S(2)}, u32[]{:S(2)}) collective-permute-start(bf16[336,256]{1,0:T(8,128)(2,1)S(1)} %get-tuple-element.114), channel_id=1, source_target_pairs={{0,4},{1,5},{2,6},{3,7},{4,0},{5,1},{6,2},{7,3},{8,12},{9,13},{10,... | collective-permute-start | bytes 516104 | tf_op jit(solution)/shard_map/c4/ppermute | solution.py:23
  137.5 24.0 %collective-permute-start.19 = (bf16[336,256]{1,0:T(8,128)(2,1)S(1)}, bf16[336,256]{1,0:T(8,128)(2,1)S(1)}, u32[]{:S(2)}, u32[]{:S(2)}) collective-permute-start(bf16[336,256]{1,0:T(8,128)(2,1)S(1)} %get-tuple-element.111), channel_id=1, source_target_pairs={{0,3},{1,2},{2,1},{3,0},{4,7},{5,6},{6,5},{7,4},{8,11},{9,10},{10,... | collective-permute-start | bytes 516104 | tf_op jit(solution)/shard_map/c3/ppermute | solution.py:23
  144.4 18.0 %copy-start.13 = (bf16[336,256]{1,0:T(8,128)(2,1)}, bf16[336,256]{1,0:T(8,128)(2,1)S(1)}, u32[]{:S(2)}) copy-start(bf16[336,256]{1,0:T(8,128)(2,1)S(1)} %collective-permute-done.23.refs_7_) | copy-start | bytes 516100
  144.4 18.0 %collective-permute-start.18 = (bf16[336,256]{1,0:T(8,128)(2,1)S(1)}, bf16[336,256]{1,0:T(8,128)(2,1)S(1)}, u32[]{:S(2)}, u32[]{:S(2)}) collective-permute-start(bf16[336,256]{1,0:T(8,128)(2,1)S(1)} %get-tuple-element.109), channel_id=1, source_target_pairs={{0,2},{1,3},{2,0},{3,1},{4,6},{5,7},{6,4},{7,5},{8,10},{9,11},{10,... | collective-permute-start | bytes 516104 | tf_op jit(solution)/shard_map/c2/ppermute | solution.py:23
  150.4 12.1 %copy-start.14 = (bf16[336,256]{1,0:T(8,128)(2,1)}, bf16[336,256]{1,0:T(8,128)(2,1)S(1)}, u32[]{:S(2)}) copy-start(bf16[336,256]{1,0:T(8,128)(2,1)S(1)} %collective-permute-done.22.refs_6_) | copy-start | bytes 516100
  150.4 12.1 %collective-permute-start.17 = (bf16[336,256]{1,0:T(8,128)(2,1)S(1)}, bf16[336,256]{1,0:T(8,128)(2,1)S(1)}, u32[]{:S(2)}, u32[]{:S(2)}) collective-permute-start(bf16[336,256]{1,0:T(8,128)(2,1)S(1)} %get-tuple-element.107), channel_id=1, source_target_pairs={{0,1},{1,0},{2,3},{3,2},{4,5},{5,4},{6,7},{7,6},{8,9},{9,8},{10,11... | collective-permute-start | bytes 516104 | tf_op jit(solution)/shard_map/c1/ppermute | solution.py:23
  157.3 5.3 %copy-start.15 = (bf16[336,256]{1,0:T(8,128)(2,1)}, bf16[336,256]{1,0:T(8,128)(2,1)S(1)}, u32[]{:S(2)}) copy-start(bf16[336,256]{1,0:T(8,128)(2,1)S(1)} %collective-permute-done.21.refs_5_) | copy-start | bytes 516100
  161.5 1.0 copy-start.16
  161.5 1.0 copy-start.17
  162.5 0.7 copy-start.18
  163.2 0.7 copy-start.19

commit v5 on v4

--- a/solution.py
+++ b/solution.py
@@ -45,25 +45,28 @@
     return [high, middle, rest - middle]
 
 
-def conv_kernel(plan, clip_ref, x_ref, above_ref, w_ref, *refs):
-    jobs, parts, part_rows, part_width = (
-        plan["jobs"], plan["parts"], plan["part_rows"], plan["part_width"])
-    lead, steps, tap_first = plan["lead"], plan["steps"], plan["tap_first"]
+def conv_kernel(plan, clip_ref, *refs):
+    jobs, plains, parts, part_rows, part_width = (
+        plan["jobs"], plan["plains"], plan["parts"], plan["part_rows"], plan["part_width"])
+    lead, steps, sources, taps = plan["lead"], plan["steps"], plan["sources"], plan["taps"]
 
     def take(number):
         nonlocal refs
         some, refs = refs[:number], refs[number:]
         return some
 
+    x_refs, above_refs, w_refs = take(sources), take(sources), take(len(taps))
     add_refs = take(plan["addends"])
     sums_refs = take(plan["sums_in"])
     take(plan["kept"])
-    out_refs = take(parts if parts else len(jobs))
+    out_refs = take(parts)
+    plain_refs = take(len(plains))
     sums_out = take(1 if plan["sums_out"] else 0)
-    sources, ci = x_ref.shape[0], x_ref.shape[3]
-    slab_refs, main_refs, left_refs = take(sources), take(len(jobs)), take(len(jobs))
+    works = jobs + plains
+    slab_refs, main_refs, left_refs = take(sources), take(len(works)), take(len(works))
     part_ref, stat_ref, closing_ref, part_sem, tail_sem = refs
     step = pl.program_id(0)
+    ci = x_refs[0].shape[3]
     half, co = main_refs[0].shape
     above = lax.rem(step + 1, 2)
     below = lax.rem(step, 2)
@@ -73,7 +76,7 @@
     @pl.when(step == 0)
     def _():
         for source in range(sources):
-            split_columns(above_ref.at[source, 0], slab_refs[source].at[1])
+            split_columns(above_refs[source].at[0, 0], slab_refs[source].at[1])
         for left_ref in left_refs:
             left_ref[0:8] = jnp.zeros((8, co), jnp.float32)
         stat_ref[...] = jnp.zeros_like(stat_ref)
@@ -88,25 +91,25 @@
         ]
 
     def products(source, tap):
-        slab_ref, tap = slab_refs[source], tap - tap_first
+        slab_ref, w_ref = slab_refs[source], w_refs[taps.index(tap)]
         rows = [slab_ref[above], slab_ref[2], slab_ref[below]]
         main = jnp.dot(
             jnp.concatenate(rows, axis=1),
-            jnp.concatenate([w_ref[tap, (3 * a + 1) * ci : (3 * a + 3) * ci] for a in range(3)], axis=0),
+            jnp.concatenate([w_ref[0, (3 * a + 1) * ci : (3 * a + 3) * ci] for a in range(3)], axis=0),
             preferred_element_type=jnp.float32)
         left = jnp.dot(
             jnp.concatenate([row[:, ci:] for row in rows], axis=1),
-            jnp.concatenate([w_ref[tap, 3 * a * ci : (3 * a + 1) * ci] for a in range(3)], axis=0),
+            jnp.concatenate([w_ref[0, 3 * a * ci : (3 * a + 1) * ci] for a in range(3)], axis=0),
             preferred_element_type=jnp.float32)
         return main, left
 
-    empty = [True] * len(jobs)
+    empty = [True] * len(works)
     for source in range(sources):
-        split_columns(x_ref.at[source, 0], slab_refs[source].at[2])
-        split_columns(x_ref.at[source, 1], slab_refs[source].at[below])
+        split_columns(x_refs[source].at[0, 0], slab_refs[source].at[2])
+        split_columns(x_refs[source].at[0, 1], slab_refs[source].at[below])
         frame = plan["first"] + source
-        for at, (target, taps, addend) in enumerate(jobs):
-            for tap in [tap for other, tap in taps if other == source]:
+        for at, (target, pairs, addend) in enumerate(works):
+            for tap in [tap for other, tap in pairs if other == source]:
                 main, left = products(source, tap)
                 if frame != target:
                     same = clip_ref[start + frame] == clip_ref[jnp.minimum(start + target, last)]
@@ -122,10 +125,10 @@
                     left_refs[at][8:] += left
                 empty[at] = False
 
-    for at in range(len(jobs)):
+    for at in range(len(works)):
         total = main_refs[at][...] + left_refs[at][7 : 7 + half]
-        if not parts:
-            out_refs[at][0] = total.astype(jnp.bfloat16)
+        if at >= len(jobs):
+            plain_refs[at - len(jobs)][0] = total.astype(jnp.bfloat16)
             continue
         rounded = total.astype(jnp.bfloat16).astype(jnp.float32)
         tiles = rounded.reshape(half // 8, 8, co)
@@ -144,75 +147,73 @@
         for copy in piece_copies(at, slot, step):
             copy.start()
 
-    if parts:
-        @pl.when(step == steps - 1)
-        def _():
-            closing = []
-            if sums_out:
-                sums_out[0][...] = stat_ref[...]
-            else:
-                rows = []
-                for at in range(2 * len(jobs)):
-                    total = stat_ref[at]
-                    for ref in sums_refs:
-                        total = total + ref[at]
-                    rows += split_three(jnp.sum(total, axis=0, keepdims=True))
-                blank = jnp.zeros((STAT_ROWS - len(rows), co), jnp.float32)
-                closing_ref[...] = jnp.concatenate(rows + [blank], axis=0).astype(jnp.bfloat16)
-                closing = [
-                    pltpu.make_async_copy(closing_ref, out.at[0:STAT_ROWS], tail_sem.at[flip])
-                    for flip, out in enumerate(out_refs)
-                ]
-            for copy in closing:
-                copy.start()
-            for at in range(len(jobs)):
-                for back in range(min(steps, 2)):
-                    for copy in piece_copies(at, lax.rem(step - back, 2), step - back):
-                        copy.wait()
-            for copy in closing:
-                copy.wait()
-
-
-def conv_frames(frames, halo, weight, clip_ids, first, sources, jobs, row=0, steps=None,
-                addends=(), parts=0, sums=(), sums_out=False, lead=0, kept=(), weigh=1, vmem=60):
+    @pl.when(step == steps - 1)
+    def _():
+        closing = []
+        if sums_out:
+            sums_out[0][...] = stat_ref[...]
+        else:
+            rows = []
+            for at in range(2 * len(jobs)):
+                total = stat_ref[at]
+                for ref in sums_refs:
+                    total = total + ref[at]
+                rows += split_three(jnp.sum(total, axis=0, keepdims=True))
+            blank = jnp.zeros((STAT_ROWS - len(rows), co), jnp.float32)
+            closing_ref[...] = jnp.concatenate(rows + [blank], axis=0).astype(jnp.bfloat16)
+            closing = [
+                pltpu.make_async_copy(closing_ref, out.at[0:STAT_ROWS], tail_sem.at[flip])
+                for flip, out in enumerate(out_refs)
+            ]
+        for copy in closing:
+            copy.start()
+        for at in range(len(jobs)):
+            for back in range(min(steps, 2)):
+                for copy in piece_copies(at, lax.rem(step - back, 2), step - back):
+                    copy.wait()
+        for copy in closing:
+            copy.wait()
+
+
+def conv_frames(frames, halo, weight, clip_ids, parts, first, sources, jobs, plains=(), row=0,
+                steps=None, addends=(), sums=(), sums_out=False, lead=0, kept=(), weigh=1, vmem=56):
     _, band, width, ci = frames.shape
     co = weight.shape[2]
     half = width // 2
     steps = steps or band // 2
-    part_width = half // parts if parts else half
+    part_width = half // parts
     part_rows = rounded_up(part_width)
-    taps = sorted({tap for _, some, _ in jobs for _, tap in some})
-    tap_first, tap_count = 0, 3
-    if len(taps) == 1 or taps == [0, 1]:
-        tap_first, tap_count = taps[0], len(taps)
-    plan = dict(jobs=jobs, addends=len(addends), parts=parts, part_rows=part_rows, lead=lead,
-                part_width=part_width, first=first, steps=steps, kept=len(kept),
-                sums_in=len(sums), sums_out=sums_out, tap_first=tap_first, count=frames.shape[0])
-    block = first // sources
-    above = (frames, 2 * row - 1) if row else (halo, 0)
-    in_specs = [
-        pl.BlockSpec((sources, 2, width, ci), lambda i, *_: (block, row + i, 0, 0)),
-        pl.BlockSpec((sources, 1, width, ci), lambda i, *_: (block, above[1], 0, 0)),
-        pl.BlockSpec((tap_count, 9 * ci, co), lambda i, *_: (tap_first // tap_count, 0, 0)),
-    ]
-    in_specs += [pl.BlockSpec((1, None, half, co), lambda i, *_: (0, i, 0, 0)) for _ in addends]
+    works = list(jobs) + list(plains)
+    taps = sorted({tap for _, pairs, _ in works for _, tap in pairs})
+    plan = dict(jobs=list(jobs), plains=list(plains), addends=len(addends), parts=parts,
+                part_rows=part_rows, lead=lead, part_width=part_width, first=first, steps=steps,
+                kept=len(kept), sums_in=len(sums), sums_out=sums_out, sources=sources, taps=taps,
+                count=frames.shape[0])
+    above, above_row = (frames, 2 * row - 1) if row else (halo, 0)
+    plain_spec = pl.BlockSpec((1, None, half, co), lambda i, *_: (0, row + i, 0, 0))
+    frame_spec = lambda source: pl.BlockSpec((1, 2, width, ci), lambda i, *_: (source, row + i, 0, 0))
+    above_spec = lambda source: pl.BlockSpec((1, 1, width, ci), lambda i, *_: (source, above_row, 0, 0))
+    tap_spec = lambda tap: pl.BlockSpec((1, 9 * ci, co), lambda i, *_: (tap, 0, 0))
+    in_specs = [frame_spec(first + source) for source in range(sources)]
+    in_specs += [above_spec(first + source) for source in range(sources)]
+    in_specs += [tap_spec(tap) for tap in taps]
+    in_specs += [plain_spec for _ in addends]
     in_specs += [pl.BlockSpec(a.shape, lambda i, *_: (0, 0, 0)) for a in sums]
     in_specs += [pl.BlockSpec(memory_space=pl.ANY) for _ in kept]
-    operands = [clip_ids, frames, above[0], weight, *addends, *sums, *kept]
+    operands = [clip_ids, *[frames] * sources, *[above] * sources, *[weight] * len(taps),
+                *addends, *sums, *kept]
     aliases = {len(operands) - len(kept) + at: at for at in range(len(kept))}
-    if parts:
-        rows = lead + len(jobs) * steps * part_rows
-        shape = kept[0].shape if kept else (rows, co)
-        out_shape = [jax.ShapeDtypeStruct(shape, jnp.bfloat16) for _ in range(parts)]
-        out_specs = [pl.BlockSpec(memory_space=pl.ANY) for _ in range(parts)]
-    else:
-        out_shape = [jax.ShapeDtypeStruct((1, steps, half, co), jnp.bfloat16) for _ in jobs]
-        out_specs = [pl.BlockSpec((1, None, half, co), lambda i, *_: (0, i, 0, 0)) for _ in jobs]
+    rows = lead + len(jobs) * steps * part_rows
+    shape = kept[0].shape if kept else (rows, co)
+    out_shape = [jax.ShapeDtypeStruct(shape, jnp.bfloat16) for _ in range(parts)]
+    out_specs = [pl.BlockSpec(memory_space=pl.ANY) for _ in range(parts)]
+    out_shape += [jax.ShapeDtypeStruct((1, band // 2, half, co), jnp.bfloat16) for _ in plains]
+    out_specs += [plain_spec for _ in plains]
     if sums_out:
         shape = (2 * len(jobs), 8, co)
         out_shape.append(jax.ShapeDtypeStruct(shape, jnp.float32))
         out_specs.append(pl.BlockSpec(shape, lambda i, *_: (0, 0, 0)))
-    products = sum(len(some) for _, some, _ in jobs)
+    products = sum(len(pairs) for _, pairs, _ in works)
     return pl.pallas_call(
         functools.partial(conv_kernel, plan),
         out_shape=out_shape,
@@ -223,19 +224,19 @@
             out_specs=out_specs,
             scratch_shapes=[
                 *[pltpu.VMEM((3, half, 2 * ci), jnp.bfloat16) for _ in range(sources)],
-                *[pltpu.VMEM((half, co), jnp.float32) for _ in jobs],
-                *[pltpu.VMEM((8 + half, co), jnp.float32) for _ in jobs],
-                pltpu.VMEM((2, len(jobs), max(parts, 1), part_rows, co), jnp.bfloat16),
+                *[pltpu.VMEM((half, co), jnp.float32) for _ in works],
+                *[pltpu.VMEM((8 + half, co), jnp.float32) for _ in works],
+                pltpu.VMEM((2, len(jobs), parts, part_rows, co), jnp.bfloat16),
                 pltpu.VMEM((2 * len(jobs), 8, co), jnp.float32),
                 pltpu.VMEM((STAT_ROWS, co), jnp.bfloat16),
-                pltpu.SemaphoreType.DMA((2, len(jobs), max(parts, 1))),
-                pltpu.SemaphoreType.DMA((max(parts, 1),)),
+                pltpu.SemaphoreType.DMA((2, len(jobs), parts)),
+                pltpu.SemaphoreType.DMA((parts,)),
             ],
         ),
         input_output_aliases=aliases,
         cost_estimate=pl.CostEstimate(
             flops=2 * weigh * products * steps * half * 9 * ci * co,
-            bytes_accessed=weigh * (4 * sources * steps * width * ci + 2 * len(jobs) * steps * half * co),
+            bytes_accessed=weigh * (4 * sources * steps * width * ci + 2 * len(works) * steps * half * co),
             transcendentals=0,
         ),
         compiler_params=pltpu.CompilerParams(vmem_limit_bytes=vmem * 1024 * 1024),
@@ -345,6 +346,7 @@
     def whole(sent, got):
         return [sent[0]] + [got[flip] for flip in range(1, parts)]
 
+    near = [flip for flip in range(1, parts) if 2 * flip < parts]
     chain = []
 
     def send_far(name, sent, *earlier):
@@ -363,35 +365,29 @@
                 earlier = (got[flip],)
         return got
 
-    near = [flip for flip in range(1, parts) if 2 * flip < parts]
     halo = named("halo", passed_along, frames[:, -1:], "rows", 1)
-
     later = [(2, [(0, 0), (1, 1), (2, 2)], None), (3, [(1, 0), (2, 1), (3, 2)], None)]
-    run = functools.partial(conv_frames, frames, halo, weight, clip_ids)
-    *a_sent, a_sums = named("conv_a", run, 0, 4, later, row=1, steps=steps - 1, parts=parts,
-                            sums_out=True, lead=top_rows, vmem=63)
-    a_sent = named("conv_top", run, 0, 4, later, steps=1, parts=parts, sums=(a_sums,),
-                   lead=STAT_ROWS, kept=a_sent, weigh=1, vmem=63)
+    onward = [(4, [(2, 0), (3, 1)], None), (5, [(3, 0)], None)]
+    run = functools.partial(conv_frames, frames, halo, weight, clip_ids, parts)
+    *kept, a_sums = named("conv_a", run, 0, 4, later, onward, row=1, steps=steps - 1,
+                          sums_out=True, lead=top_rows, weigh=1, vmem=56)
+    *a_sent, first_on, second_on = named("conv_top", run, 0, 4, later, onward, steps=1, sums=(a_sums,),
+                                         lead=STAT_ROWS, kept=kept, weigh=1, vmem=56)
+    first_add = named("hist0", passed_along, first_on, "tm", 1)
+    second_add = named("hist1", passed_along, after(second_on, first_add), "tm", 1)
     a_got = send_far("a", a_sent)
-    run = functools.partial(conv_frames, frames, after(halo, a_sent[0]), weight, clip_ids)
-    ahead, = named("conv_hist0", run, 2, 2, [(4, [(0, 0), (1, 1)], None)])
-    first_add = named("hist0", passed_along, ahead, "tm", 1)
-    run = functools.partial(conv_frames, frames, after(halo, ahead), weight, clip_ids)
-    onward, = named("conv_hist1", run, 3, 1, [(5, [(0, 0)], None)], weigh=40)
-    second_add = named("hist1", passed_along, after(onward, first_add), "tm", 1)
     a_got.update(send_near("a", a_sent, True, a_sums))
-    b_sent = named("conv_b", run, 0, 1, [(0, [(0, 2)], 0)],
-                   addends=(after(first_add, onward, *[a_got[flip] for flip in near]),), parts=parts,
-                   lead=STAT_ROWS, weigh=20, vmem=24)
+    b_sent = named("conv_b", run, 0, 1, [(0, [(0, 2)], 0)], addends=(after(first_add, a_sums),),
+                   lead=STAT_ROWS, weigh=20, vmem=56)
     b_got = send_far("b", b_sent)
-    c_sent = named("conv_c", run, 0, 2, [(1, [(0, 1), (1, 2)], 0)], addends=(second_add,), parts=parts,
-                   lead=STAT_ROWS, weigh=20, vmem=24)
+    c_sent = named("conv_c", run, 0, 2, [(1, [(0, 1), (1, 2)], 0)], addends=(after(second_add, a_sums),),
+                   lead=STAT_ROWS, weigh=20, vmem=56)
     out, a_done = named("norm_a", norm_frames, whole(a_sent, a_got), gain, bias, 2, 2, shape, top_first=True, vmem=20)
     b_got.update(send_near("b", b_sent, False, c_sent[0]))
-    c_got = send_far("c", c_sent, a_done)
+    c_got = send_near("c", c_sent, False, c_sent[0])
+    c_got.update(send_far("c", c_sent, c_sent[0]))
     out, b_done = named("norm_b", norm_frames, whole(b_sent, b_got), gain, bias, 0, 1, shape, base=out, vmem=20)
-    c_got.update(send_near("c", c_sent, False, b_done))
-    out, _ = named("norm_c", norm_frames, whole(c_sent, c_got), gain, bias, 1, 1, shape, base=out, vmem=64)
+    out, _ = named("norm_c", norm_frames, whole(c_sent, c_got), gain, bias, 1, 1, shape, base=out, vmem=20)
     return out.reshape(count, parts * steps, shape[3], co)
 
 

time: 168 us -> 169 us (level)
  starting transfers between devices: 47 us -> 61.3 us
  Pallas kernels: 62.8 us -> 52.8 us
  local copies, waits for them, and re-layouts: 9.23 us -> 2.63 us
  waiting for transfers between devices: 48.1 us -> 50.4 us
    ppermute x21, starting transfers between devices: 38 us -> 53.3 us  [exchanged(): return lax.ppermute(array, axis, [(i, i ^ flip) for i in range(length)])]
    ppermute x21, waiting for transfers between devices: 27.9 us -> 40.6 us  [exchanged(): return lax.ppermute(array, axis, [(i, i ^ flip) for i in range(length)])]
    ppermute x3, waiting for transfers between devices: 20.2 us -> 9.84 us  [passed_along(): return lax.ppermute(array, axis, pairs)]
    pallas_call x6 -> x4, Pallas kernels: 53.7 us -> 45 us  [conv_frames(): pl.pallas_call(functools.partial(conv_kernel, plan), out_shape=out_shape,...]
    unnamed x40 -> x24, local copies, waits for them, and re-layouts: 6.77 us -> 1.23 us
  transfers between devices with their start and end apart: 24 -> 24, of which waited for: 7 -> 11; matrix products, arithmetic and copies ran while one was open for 0% -> 0% of each run, Pallas kernels for 31% -> 25%
where the time goes in v5:
time: 169 us; the launch traced here: 167 us
  starting transfers between devices  61.3 us (36%)
  Pallas kernels  52.8 us (31%)
  waiting for transfers between devices  50.4 us (30%)
  local copies, waits for them, and re-layouts  2.63 us (2%)
    ppermute x21, starting transfers between devices, exchanged(): return lax.ppermute(array, axis, [(i, i ^ flip) for i in range(length)])  53.3 us
    pallas_call x4, Pallas kernels, conv_frames(): pl.pallas_call(functools.partial(conv_kernel, plan), out_shape=out_shape,...  45 us
    ppermute x21, waiting for transfers between devices, exchanged(): return lax.ppermute(array, axis, [(i, i ^ flip) for i in range(length)])  40.6 us
    ppermute x3, waiting for transfers between devices, passed_along(): return lax.ppermute(array, axis, pairs)  9.84 us
    ppermute x3, starting transfers between devices, passed_along(): return lax.ppermute(array, axis, pairs)  8.02 us
    pallas_call x3, Pallas kernels, norm_frames(): pl.pallas_call(functools.partial(norm_kernel, plan), out_shape=[jax.Shape...  7.78 us
  transfers between devices with their start and end apart: 24, of which 11 were waited for; matrix products, arithmetic and copies ran while one was open for 0% of the time, Pallas kernels for 25%

profile of v5, /device:TPU:4, one launch (start us, length us, event | category | flops | bytes accessed | tf_op | source)
XLA Modules:
  0.0 167.4 jit_solution(18185391353012856383)
XLA Ops:
  0.0 1.4 slice.3
  1.4 1.8 %collective-permute-start = (bf16[4,1,1280,128]{3,2,1,0:T(8,128)(2,1)S(1)}, bf16[4,1,1280,128]{3,2,1,0:T(8,128)(2,1)S(1)}, u32[]{:S(2)}, u32[]{:S(2)}) collective-permute-start(bf16[4,1,1280,128]{3,2,1,0:T(8,128)(2,1)S(1)} %slice.3), channel_id=1, source_target_pairs={{0,1},{1,2},{2,3},{3,4},{4,5},{5,6},{6,7},{8,9},{9,10},{10,11},{11... | collective-permute-start | bytes 3932168 | tf_op jit(solution)/shard_map/halo/ppermute | solution.py:18
  3.2 19.8 %conv_a.1 = (bf16[656,256]{1,0:T(8,128)(2,1)}, bf16[656,256]{1,0:T(8,128)(2,1)}, bf16[656,256]{1,0:T(8,128)(2,1)}, bf16[656,256]{1,0:T(8,128)(2,1)}, bf16[656,25...) custom-call(s32[16]{0:T(128)} %clip_ref.7, ...), custom_call_target="tpu_custom_call" | custom-call | flops 10192158720 | bytes 11796480 | tf_op jit(solution)/shard_map/conv_a/pallas_call | solution.py:217
  23.0 0.0 collective-permute-done.refs_4_.refs_5_.refs_6_.refs_7_.refs_2_.refs_3_.refs_1_
  23.1 0.0 copy-start.5
  23.1 1.0 copy-done.5
  24.1 8.9 %conv_top.1 = (bf16[656,256]{1,0:T(8,128)(2,1)}, bf16[656,256]{1,0:T(8,128)(2,1)}, bf16[656,256]{1,0:T(8,128)(2,1)}, bf16[656,256]{1,0:T(8,128)(2,1)}, bf16[656,...) custom-call(s32[16]{0:T(128)} %clip_ref.7, ...), custom_call_target="tpu_custom_call", output_to_operand_aliasing={{0}: (13, {}), {1}: (14, {}), {2}: (15, {}), {3}: (16, {}),... | custom-call | flops 3397386240 | bytes 3932160 | tf_op jit(solution)/shard_map/conv_top/pallas_call | solution.py:217
  33.0 3.4 %collective-permute-start.1 = (bf16[1,4,640,256]{3,2,1,0:T(8,128)(2,1)}, bf16[1,4,640,256]{3,2,1,0:T(8,128)(2,1)S(1)}, u32[]{:S(2)}, u32[]{:S(2)}) collective-permute-start(bf16[1,4,640,256]{3,2,1,0:T(8,128)(2,1)} %get-tuple-element.77), channel_id=1, source_target_pairs={{0,8},{8,16},{16,24},{1,9},{9,17},{17,25},{2,10},{10,18},{18,26},{... | collective-permute-start | bytes 3932168 | tf_op jit(solution)/shard_map/hist0/ppermute | solution.py:18
  36.4 1.6 collective-permute-start.21
  38.0 1.5 collective-permute-done.21.refs_1_
  39.5 1.6 collective-permute-start.22
  41.1 1.5 collective-permute-start.6
  42.6 0.8 collective-permute-start.9
  43.4 2.5 %collective-permute-start.12 = (bf16[656,256]{1,0:T(8,128)(2,1)}, bf16[656,256]{1,0:T(8,128)(2,1)S(1)}, u32[]{:S(2)}, u32[]{:S(2)}) collective-permute-start(bf16[656,256]{1,0:T(8,128)(2,1)} %get-tuple-element.100), channel_id=1, source_target_pairs={{0,6},{1,7},{2,4},{3,5},{4,2},{5,3},{6,0},{7,1},{8,14},{9,15},{10,... | collective-permute-start | bytes 1007624 | tf_op jit(solution)/shard_map/a6/ppermute | solution.py:23
  45.9 11.1 %collective-permute-done.22.refs_2_ = bf16[656,256]{1,0:T(8,128)(2,1)S(1)} collective-permute-done((bf16[656,256]{1,0:T(8,128)(2,1)}, bf16[656,256]{1,0:T(8,128)(2,1)S(1)}, u32[]{:S(2)}, u32[]{:S(2)}) %collective-permute-start.22) | collective-permute-done | bytes 335904 | tf_op jit(solution)/shard_map/a2/ppermute | solution.py:23
  56.9 0.1 collective-permute-start.15
  57.1 9.8 %collective-permute-done.1.refs_3_ = bf16[1,4,640,256]{3,2,1,0:T(8,128)(2,1)S(1)} collective-permute-done((bf16[1,4,640,256]{3,2,1,0:T(8,128)(2,1)}, bf16[1,4,640,256]{3,2,1,0:T(8,128)(2,1)S(1)}, u32[]{:S(2)}, u32[]{:S(2)}) %collective-permute-start.1) | collective-permute-done | bytes 1310752 | tf_op jit(solution)/shard_map/hist0/ppermute | solution.py:18
  66.9 2.8 %collective-permute-start.2 = (bf16[1,4,640,256]{3,2,1,0:T(8,128)(2,1)}, bf16[1,4,640,256]{3,2,1,0:T(8,128)(2,1)S(1)}, u32[]{:S(2)}, u32[]{:S(2)}) collective-permute-start(bf16[1,4,640,256]{3,2,1,0:T(8,128)(2,1)} %get-tuple-element.78), channel_id=1, source_target_pairs={{0,8},{8,16},{16,24},{1,9},{9,17},{17,25},{2,10},{10,18},{18,26},{... | collective-permute-start | bytes 3932168 | tf_op jit(solution)/shard_map/hist1/ppermute | solution.py:18
  69.7 7.2 %conv_b.1 = (bf16[336,256]{1,0:T(8,128)(2,1)}, bf16[336,256]{1,0:T(8,128)(2,1)}, bf16[336,256]{1,0:T(8,128)(2,1)}, bf16[336,256]{1,0:T(8,128)(2,1)}, bf16[336,25...) custom-call(s32[16]{0:T(128)} %clip_ref.7, ...), custom_call_target="tpu_custom_call" | custom-call | flops 30198988800 | bytes 78643200 | tf_op jit(solution)/shard_map/conv_b/pallas_call | solution.py:217
  76.9 4.9 %collective-permute-done.6.refs_4_ = bf16[656,256]{1,0:T(8,128)(2,1)S(1)} collective-permute-done((bf16[656,256]{1,0:T(8,128)(2,1)}, bf16[656,256]{1,0:T(8,128)(2,1)S(1)}, u32[]{:S(2)}, u32[]{:S(2)}) %collective-permute-start.6) | collective-permute-done | bytes 335904 | tf_op jit(solution)/shard_map/a4/ppermute | solution.py:23
  81.8 0.0 collective-permute-start.23
  81.8 5.5 %collective-permute-done.9.refs_5_ = bf16[656,256]{1,0:T(8,128)(2,1)S(1)} collective-permute-done((bf16[656,256]{1,0:T(8,128)(2,1)}, bf16[656,256]{1,0:T(8,128)(2,1)S(1)}, u32[]{:S(2)}, u32[]{:S(2)}) %collective-permute-start.9) | collective-permute-done | bytes 335904 | tf_op jit(solution)/shard_map/a5/ppermute | solution.py:23
  87.3 0.0 collective-permute-done.12.refs_6_
  87.3 0.0 collective-permute-done.15.refs_7_
  87.3 0.0 copy-start.3
  87.4 0.0 copy-start.4
  87.4 4.0 %collective-permute-start.16 = (bf16[336,256]{1,0:T(8,128)(2,1)}, bf16[336,256]{1,0:T(8,128)(2,1)S(1)}, u32[]{:S(2)}, u32[]{:S(2)}) collective-permute-start(bf16[336,256]{1,0:T(8,128)(2,1)} %get-tuple-element.106), channel_id=1, source_target_pairs={{0,7},{1,6},{2,5},{3,4},{4,3},{5,2},{6,1},{7,0},{8,15},{9,14},{10,... | collective-permute-start | bytes 516104 | tf_op jit(solution)/shard_map/b7/ppermute | solution.py:23
  91.3 1.3 collective-permute-start.13
  92.7 19.5 %collective-permute-start.10 = (bf16[336,256]{1,0:T(8,128)(2,1)}, bf16[336,256]{1,0:T(8,128)(2,1)S(1)}, u32[]{:S(2)}, u32[]{:S(2)}) collective-permute-start(bf16[336,256]{1,0:T(8,128)(2,1)} %get-tuple-element.96), channel_id=1, source_target_pairs={{0,5},{1,4},{2,7},{3,6},{4,1},{5,0},{6,3},{7,2},{8,13},{9,12},{10,... | collective-permute-start | bytes 516104 | tf_op jit(solution)/shard_map/b5/ppermute | solution.py:23
  112.2 0.0 collective-permute-done.2.refs_6_
  112.2 0.9 collective-permute-start.7
  113.1 0.1 copy-done.7
  113.2 9.2 %conv_c.1 = (bf16[336,256]{1,0:T(8,128)(2,1)}, bf16[336,256]{1,0:T(8,128)(2,1)}, bf16[336,256]{1,0:T(8,128)(2,1)}, bf16[336,256]{1,0:T(8,128)(2,1)}, bf16[336,25...) custom-call(s32[16]{0:T(128)} %clip_ref.7, ...), custom_call_target="tpu_custom_call" | custom-call | flops 60397977600 | bytes 131072000 | tf_op jit(solution)/shard_map/conv_c/pallas_call | solution.py:217
  122.4 0.0 collective-permute-done.16.refs_7_
  122.4 0.0 copy-done.11
  122.4 1.8 %collective-permute-start.20 = (bf16[336,256]{1,0:T(8,128)(2,1)S(1)}, bf16[336,256]{1,0:T(8,128)(2,1)S(1)}, u32[]{:S(2)}, u32[]{:S(2)}) collective-permute-start(bf16[336,256]{1,0:T(8,128)(2,1)S(1)} %copy-done.11), channel_id=1, source_target_pairs={{0,3},{1,2},{2,1},{3,0},{4,7},{5,6},{6,5},{7,4},{8,11},{9,10},{10,... | collective-permute-start | bytes 516104 | tf_op jit(solution)/shard_map/b3/ppermute | solution.py:23
  124.2 0.0 collective-permute-done.13.refs_6_
  124.2 4.3 %collective-permute-start.19 = (bf16[336,256]{1,0:T(8,128)(2,1)S(1)}, bf16[336,256]{1,0:T(8,128)(2,1)S(1)}, u32[]{:S(2)}, u32[]{:S(2)}) collective-permute-start(bf16[336,256]{1,0:T(8,128)(2,1)S(1)} %copy-done.10), channel_id=1, source_target_pairs={{0,2},{1,3},{2,0},{3,1},{4,6},{5,7},{6,4},{7,5},{8,10},{9,11},{10,... | collective-permute-start | bytes 516104 | tf_op jit(solution)/shard_map/b2/ppermute | solution.py:23
  128.5 0.0 collective-permute-done.23.refs_3_
  128.5 0.0 collective-permute-start.18
  128.5 1.8 %collective-permute-done.10.refs_5_ = bf16[336,256]{1,0:T(8,128)(2,1)S(1)} collective-permute-done((bf16[336,256]{1,0:T(8,128)(2,1)}, bf16[336,256]{1,0:T(8,128)(2,1)S(1)}, u32[]{:S(2)}, u32[]{:S(2)}) %collective-permute-start.10) | collective-permute-done | bytes 172064 | tf_op jit(solution)/shard_map/b5/ppermute | solution.py:23
  130.3 3.3 %collective-permute-start.17 = (bf16[336,256]{1,0:T(8,128)(2,1)}, bf16[336,256]{1,0:T(8,128)(2,1)S(1)}, u32[]{:S(2)}, u32[]{:S(2)}) collective-permute-start(bf16[336,256]{1,0:T(8,128)(2,1)} %get-tuple-element.107), channel_id=1, source_target_pairs={{0,7},{1,6},{2,5},{3,4},{4,3},{5,2},{6,1},{7,0},{8,15},{9,14},{10,... | collective-permute-start | bytes 516104 | tf_op jit(solution)/shard_map/c7/ppermute | solution.py:23
  133.6 1.5 collective-permute-done.7.refs_4_
  135.1 8.2 %collective-permute-start.14 = (bf16[336,256]{1,0:T(8,128)(2,1)}, bf16[336,256]{1,0:T(8,128)(2,1)S(1)}, u32[]{:S(2)}, u32[]{:S(2)}) collective-permute-start(bf16[336,256]{1,0:T(8,128)(2,1)} %get-tuple-element.102), channel_id=1, source_target_pairs={{0,6},{1,7},{2,4},{3,5},{4,2},{5,3},{6,0},{7,1},{8,14},{9,15},{10,... | collective-permute-start | bytes 516104 | tf_op jit(solution)/shard_map/c6/ppermute | solution.py:23
  143.3 0.0 collective-permute-done.20.refs_3_
  143.4 0.0 collective-permute-start.11
  143.4 4.1 %collective-permute-done.19.refs_2_ = bf16[336,256]{1,0:T(8,128)(2,1)S(1)} collective-permute-done((bf16[336,256]{1,0:T(8,128)(2,1)S(1)}, bf16[336,256]{1,0:T(8,128)(2,1)S(1)}, u32[]{:S(2)}, u32[]{:S(2)}) %collective-permute-start.19) | collective-permute-done | bytes 172064 | tf_op jit(solution)/shard_map/b2/ppermute | solution.py:23
  147.4 0.0 collective-permute-start.8
  147.4 0.0 collective-permute-done.18.refs_1_
  147.4 0.7 collective-permute-start.5
  148.2 0.0 collective-permute-done.17.refs_7_
  148.2 0.7 collective-permute-start.4
  148.9 0.0 collective-permute-done.14.refs_6_
  148.9 0.5 collective-permute-start.3
  149.3 0.0 copy-done.4
  149.3 3.4 %norm_a.1 = (bf16[4,8,4,80,256]{4,3,2,1,0:T(8,128)(2,1)}, f32[8,256]{1,0:T(8,128)}) custom-call(bf16[656,256]{1,0:T(8,128)(2,1)S(1)} %copy-done, bf16[656,256]{1,0:T(8,128)(2,1)S(1)} %collective-permute-done.21.refs_1_, bf16[656,256]{1,0:T(8,128)(2,1)S(1)} %collective-permute-done.22.refs_2_, bf16[656,256]{1,0:T(8,128)(2,1)S(1)} %collective-permute-done.23.refs_3_, ...), custom_call_target="tpu_custom_call" | custom-call | flops 10485760 | bytes 5242880 | tf_op jit(solution)/shard_map/norm_a/pallas_call | solution.py:308
  152.8 2.2 %norm_b.1 = (bf16[4,8,4,80,256]{4,3,2,1,0:T(8,128)(2,1)}, f32[8,256]{1,0:T(8,128)}) custom-call(bf16[336,256]{1,0:T(8,128)(2,1)S(1)} %copy-done.1, bf16[336,256]{1,0:T(8,128)(2,1)S(1)} %collective-permute-done.18.refs_1_, bf16[336,256]{1,0:T(8,128)(2,1)S(1)} %collective-permute-done.19.refs_2_, ...), custom_call_target="tpu_custom_call", output_to_operand_aliasing={{0}: (10, {})} | custom-call | flops 5242880 | bytes 2621440 | tf_op jit(solution)/shard_map/norm_b/pallas_call | solution.py:308
  154.9 5.1 %collective-permute-done.11.refs_5_ = bf16[336,256]{1,0:T(8,128)(2,1)S(1)} collective-permute-done((bf16[336,256]{1,0:T(8,128)(2,1)}, bf16[336,256]{1,0:T(8,128)(2,1)S(1)}, u32[]{:S(2)}, u32[]{:S(2)}) %collective-permute-start.11) | collective-permute-done | bytes 172064 | tf_op jit(solution)/shard_map/c5/ppermute | solution.py:23
  160.0 4.2 %collective-permute-done.8.refs_4_ = bf16[336,256]{1,0:T(8,128)(2,1)S(1)} collective-permute-done((bf16[336,256]{1,0:T(8,128)(2,1)}, bf16[336,256]{1,0:T(8,128)(2,1)S(1)}, u32[]{:S(2)}, u32[]{:S(2)}) %collective-permute-start.8) | collective-permute-done | bytes 172064 | tf_op jit(solution)/shard_map/c4/ppermute | solution.py:23
  164.2 0.0 collective-permute-done.5.refs_3_
  164.2 1.0 collective-permute-done.4.refs_2_
  165.2 0.0 collective-permute-done.3.refs_1_
  165.2 0.0 copy-done.2
  165.2 2.2 %norm_c.1 = (bf16[4,8,4,80,256]{4,3,2,1,0:T(8,128)(2,1)}, f32[8,256]{1,0:T(8,128)}) custom-call(bf16[336,256]{1,0:T(8,128)(2,1)S(1)} %copy-done.2, bf16[336,256]{1,0:T(8,128)(2,1)S(1)} %collective-permute-done.3.refs_1_, bf16[336,256]{1,0:T(8,128)(2,1)S(1)} %collective-permute-done.4.refs_2_, ...), custom_call_target="tpu_custom_call", output_to_operand_aliasing={{0}: (10, {})} | custom-call | flops 5242880 | bytes 2621440 | tf_op jit(solution)/shard_map/norm_c/pallas_call | solution.py:308
  (16 shorter events, 0.0 us)
Async XLA Ops:
  1.4 21.6 %collective-permute-start = (bf16[4,1,1280,128]{3,2,1,0:T(8,128)(2,1)S(1)}, bf16[4,1,1280,128]{3,2,1,0:T(8,128)(2,1)S(1)}, u32[]{:S(2)}, u32[]{:S(2)}) collective-permute-start(bf16[4,1,1280,128]{3,2,1,0:T(8,128)(2,1)S(1)} %slice.3), channel_id=1, source_target_pairs={{0,1},{1,2},{2,3},{3,4},{4,5},{5,6},{6,7},{8,9},{9,10},{10,11},{11... | collective-permute-start | bytes 3932168 | tf_op jit(solution)/shard_map/halo/ppermute | solution.py:18
  23.1 1.1 copy-start.5
  33.0 33.9 %collective-permute-start.1 = (bf16[1,4,640,256]{3,2,1,0:T(8,128)(2,1)}, bf16[1,4,640,256]{3,2,1,0:T(8,128)(2,1)S(1)}, u32[]{:S(2)}, u32[]{:S(2)}) collective-permute-start(bf16[1,4,640,256]{3,2,1,0:T(8,128)(2,1)} %get-tuple-element.77), channel_id=1, source_target_pairs={{0,8},{8,16},{16,24},{1,9},{9,17},{17,25},{2,10},{10,18},{18,26},{... | collective-permute-start | bytes 3932168 | tf_op jit(solution)/shard_map/hist0/ppermute | solution.py:18
  36.4 3.0 %collective-permute-start.21 = (bf16[656,256]{1,0:T(8,128)(2,1)}, bf16[656,256]{1,0:T(8,128)(2,1)S(1)}, u32[]{:S(2)}, u32[]{:S(2)}) collective-permute-start(bf16[656,256]{1,0:T(8,128)(2,1)} %get-tuple-element.117), channel_id=1, source_target_pairs={{0,1},{1,0},{2,3},{3,2},{4,5},{5,4},{6,7},{7,6},{8,9},{9,8},{10,11... | collective-permute-start | bytes 1007624 | tf_op jit(solution)/shard_map/a1/ppermute | solution.py:23
  39.5 17.5 %collective-permute-start.22 = (bf16[656,256]{1,0:T(8,128)(2,1)}, bf16[656,256]{1,0:T(8,128)(2,1)S(1)}, u32[]{:S(2)}, u32[]{:S(2)}) collective-permute-start(bf16[656,256]{1,0:T(8,128)(2,1)} %get-tuple-element.119), channel_id=1, source_target_pairs={{0,2},{1,3},{2,0},{3,1},{4,6},{5,7},{6,4},{7,5},{8,10},{9,11},{10,... | collective-permute-start | bytes 1007624 | tf_op jit(solution)/shard_map/a2/ppermute | solution.py:23
  41.1 40.7 %collective-permute-start.6 = (bf16[656,256]{1,0:T(8,128)(2,1)}, bf16[656,256]{1,0:T(8,128)(2,1)S(1)}, u32[]{:S(2)}, u32[]{:S(2)}) collective-permute-start(bf16[656,256]{1,0:T(8,128)(2,1)} %get-tuple-element.90), channel_id=1, source_target_pairs={{0,4},{1,5},{2,6},{3,7},{4,0},{5,1},{6,2},{7,3},{8,12},{9,13},{10,... | collective-permute-start | bytes 1007624 | tf_op jit(solution)/shard_map/a4/ppermute | solution.py:23
  42.6 44.7 %collective-permute-start.9 = (bf16[656,256]{1,0:T(8,128)(2,1)}, bf16[656,256]{1,0:T(8,128)(2,1)S(1)}, u32[]{:S(2)}, u32[]{:S(2)}) collective-permute-start(bf16[656,256]{1,0:T(8,128)(2,1)} %get-tuple-element.95), channel_id=1, source_target_pairs={{0,5},{1,4},{2,7},{3,6},{4,1},{5,0},{6,3},{7,2},{8,13},{9,12},{10,... | collective-permute-start | bytes 1007624 | tf_op jit(solution)/shard_map/a5/ppermute | solution.py:23
  43.4 43.9 %collective-permute-start.12 = (bf16[656,256]{1,0:T(8,128)(2,1)}, bf16[656,256]{1,0:T(8,128)(2,1)S(1)}, u32[]{:S(2)}, u32[]{:S(2)}) collective-permute-start(bf16[656,256]{1,0:T(8,128)(2,1)} %get-tuple-element.100), channel_id=1, source_target_pairs={{0,6},{1,7},{2,4},{3,5},{4,2},{5,3},{6,0},{7,1},{8,14},{9,15},{10,... | collective-permute-start | bytes 1007624 | tf_op jit(solution)/shard_map/a6/ppermute | solution.py:23
  56.9 30.4 %collective-permute-start.15 = (bf16[656,256]{1,0:T(8,128)(2,1)}, bf16[656,256]{1,0:T(8,128)(2,1)S(1)}, u32[]{:S(2)}, u32[]{:S(2)}) collective-permute-start(bf16[656,256]{1,0:T(8,128)(2,1)} %get-tuple-element.105), channel_id=1, source_target_pairs={{0,7},{1,6},{2,5},{3,4},{4,3},{5,2},{6,1},{7,0},{8,15},{9,14},{10,... | collective-permute-start | bytes 1007624 | tf_op jit(solution)/shard_map/a7/ppermute | solution.py:23
  66.9 2.8 %copy-start.8 = (bf16[1,4,640,256]{3,2,1,0:T(8,128)(2,1)}, bf16[1,4,640,256]{3,2,1,0:T(8,128)(2,1)S(1)}, u32[]{:S(2)}) copy-start(bf16[1,4,640,256]{3,2,1,0:T(8,128)(2,1)S(1)} %collective-permute-done.1.refs_3_) | copy-start | bytes 3932164
  66.9 14.9 %copy-start.6 = (bf16[656,256]{1,0:T(8,128)(2,1)S(1)}, bf16[656,256]{1,0:T(8,128)(2,1)}, u32[]{:S(2)}) copy-start(bf16[656,256]{1,0:T(8,128)(2,1)} %get-tuple-element.121) | copy-start | bytes 1007620
  66.9 45.3 %collective-permute-start.2 = (bf16[1,4,640,256]{3,2,1,0:T(8,128)(2,1)}, bf16[1,4,640,256]{3,2,1,0:T(8,128)(2,1)S(1)}, u32[]{:S(2)}, u32[]{:S(2)}) collective-permute-start(bf16[1,4,640,256]{3,2,1,0:T(8,128)(2,1)} %get-tuple-element.78), channel_id=1, source_target_pairs={{0,8},{8,16},{16,24},{1,9},{9,17},{17,25},{2,10},{10,18},{18,26},{... | collective-permute-start | bytes 3932168 | tf_op jit(solution)/shard_map/hist1/ppermute | solution.py:18
  81.8 46.7 %collective-permute-start.23 = (bf16[656,256]{1,0:T(8,128)(2,1)S(1)}, bf16[656,256]{1,0:T(8,128)(2,1)S(1)}, u32[]{:S(2)}, u32[]{:S(2)}) collective-permute-start(bf16[656,256]{1,0:T(8,128)(2,1)S(1)} %copy-done.6), channel_id=1, source_target_pairs={{0,3},{1,2},{2,1},{3,0},{4,7},{5,6},{6,5},{7,4},{8,11},{9,10},{10,... | collective-permute-start | bytes 1007624 | tf_op jit(solution)/shard_map/a3/ppermute | solution.py:23
  87.3 35.1 %copy-start.11 = (bf16[336,256]{1,0:T(8,128)(2,1)S(1)}, bf16[336,256]{1,0:T(8,128)(2,1)}, u32[]{:S(2)}) copy-start(bf16[336,256]{1,0:T(8,128)(2,1)} %get-tuple-element.114) | copy-start | bytes 516100
  87.3 36.9 %copy-start.10 = (bf16[336,256]{1,0:T(8,128)(2,1)S(1)}, bf16[336,256]{1,0:T(8,128)(2,1)}, u32[]{:S(2)}) copy-start(bf16[336,256]{1,0:T(8,128)(2,1)} %get-tuple-element.112) | copy-start | bytes 516100
  87.3 41.1 %copy-start.9 = (bf16[336,256]{1,0:T(8,128)(2,1)S(1)}, bf16[336,256]{1,0:T(8,128)(2,1)}, u32[]{:S(2)}) copy-start(bf16[336,256]{1,0:T(8,128)(2,1)} %get-tuple-element.110) | copy-start | bytes 516100
  87.3 62.0 %copy-start = (bf16[656,256]{1,0:T(8,128)(2,1)S(1)}, bf16[656,256]{1,0:T(8,128)(2,1)}, u32[]{:S(2)}) copy-start(bf16[656,256]{1,0:T(8,128)(2,1)} %get-tuple-element.115.refs_0_) | copy-start | bytes 1007620
  87.3 62.0 %copy-start.3 = (f32[256]{0:T(256)S(1)}, f32[256]{0:T(256)}, u32[]{:S(2)}) copy-start(f32[256]{0:T(256)} %param.8) | copy-start | bytes 3076
  87.4 62.0 %copy-start.4 = (f32[256]{0:T(256)S(1)}, f32[256]{0:T(256)}, u32[]{:S(2)}) copy-start(f32[256]{0:T(256)} %param.9) | copy-start | bytes 3076
  87.4 35.0 %collective-permute-start.16 = (bf16[336,256]{1,0:T(8,128)(2,1)}, bf16[336,256]{1,0:T(8,128)(2,1)S(1)}, u32[]{:S(2)}, u32[]{:S(2)}) collective-permute-start(bf16[336,256]{1,0:T(8,128)(2,1)} %get-tuple-element.106), channel_id=1, source_target_pairs={{0,7},{1,6},{2,5},{3,4},{4,3},{5,2},{6,1},{7,0},{8,15},{9,14},{10,... | collective-permute-start | bytes 516104 | tf_op jit(solution)/shard_map/b7/ppermute | solution.py:23
  91.3 32.9 %collective-permute-start.13 = (bf16[336,256]{1,0:T(8,128)(2,1)}, bf16[336,256]{1,0:T(8,128)(2,1)S(1)}, u32[]{:S(2)}, u32[]{:S(2)}) collective-permute-start(bf16[336,256]{1,0:T(8,128)(2,1)} %get-tuple-element.101), channel_id=1, source_target_pairs={{0,6},{1,7},{2,4},{3,5},{4,2},{5,3},{6,0},{7,1},{8,14},{9,15},{10,... | collective-permute-start | bytes 516104 | tf_op jit(solution)/shard_map/b6/ppermute | solution.py:23
  92.7 37.6 %collective-permute-start.10 = (bf16[336,256]{1,0:T(8,128)(2,1)}, bf16[336,256]{1,0:T(8,128)(2,1)S(1)}, u32[]{:S(2)}, u32[]{:S(2)}) collective-permute-start(bf16[336,256]{1,0:T(8,128)(2,1)} %get-tuple-element.96), channel_id=1, source_target_pairs={{0,5},{1,4},{2,7},{3,6},{4,1},{5,0},{6,3},{7,2},{8,13},{9,12},{10,... | collective-permute-start | bytes 516104 | tf_op jit(solution)/shard_map/b5/ppermute | solution.py:23
  112.2 1.1 copy-start.7
  112.2 23.0 %collective-permute-start.7 = (bf16[336,256]{1,0:T(8,128)(2,1)}, bf16[336,256]{1,0:T(8,128)(2,1)S(1)}, u32[]{:S(2)}, u32[]{:S(2)}) collective-permute-start(bf16[336,256]{1,0:T(8,128)(2,1)} %get-tuple-element.91), channel_id=1, source_target_pairs={{0,4},{1,5},{2,6},{3,7},{4,0},{5,1},{6,2},{7,3},{8,12},{9,13},{10,... | collective-permute-start | bytes 516104 | tf_op jit(solution)/shard_map/b4/ppermute | solution.py:23
  122.4 20.9 %collective-permute-start.20 = (bf16[336,256]{1,0:T(8,128)(2,1)S(1)}, bf16[336,256]{1,0:T(8,128)(2,1)S(1)}, u32[]{:S(2)}, u32[]{:S(2)}) collective-permute-start(bf16[336,256]{1,0:T(8,128)(2,1)S(1)} %copy-done.11), channel_id=1, source_target_pairs={{0,3},{1,2},{2,1},{3,0},{4,7},{5,6},{6,5},{7,4},{8,11},{9,10},{10,... | collective-permute-start | bytes 516104 | tf_op jit(solution)/shard_map/b3/ppermute | solution.py:23
  124.2 23.2 %collective-permute-start.19 = (bf16[336,256]{1,0:T(8,128)(2,1)S(1)}, bf16[336,256]{1,0:T(8,128)(2,1)S(1)}, u32[]{:S(2)}, u32[]{:S(2)}) collective-permute-start(bf16[336,256]{1,0:T(8,128)(2,1)S(1)} %copy-done.10), channel_id=1, source_target_pairs={{0,2},{1,3},{2,0},{3,1},{4,6},{5,7},{6,4},{7,5},{8,10},{9,11},{10,... | collective-permute-start | bytes 516104 | tf_op jit(solution)/shard_map/b2/ppermute | solution.py:23
  128.5 19.0 %collective-permute-start.18 = (bf16[336,256]{1,0:T(8,128)(2,1)S(1)}, bf16[336,256]{1,0:T(8,128)(2,1)S(1)}, u32[]{:S(2)}, u32[]{:S(2)}) collective-permute-start(bf16[336,256]{1,0:T(8,128)(2,1)S(1)} %copy-done.9), channel_id=1, source_target_pairs={{0,1},{1,0},{2,3},{3,2},{4,5},{5,4},{6,7},{7,6},{8,9},{9,8},{10,11... | collective-permute-start | bytes 516104 | tf_op jit(solution)/shard_map/b1/ppermute | solution.py:23
  130.3 17.9 %collective-permute-start.17 = (bf16[336,256]{1,0:T(8,128)(2,1)}, bf16[336,256]{1,0:T(8,128)(2,1)S(1)}, u32[]{:S(2)}, u32[]{:S(2)}) collective-permute-start(bf16[336,256]{1,0:T(8,128)(2,1)} %get-tuple-element.107), channel_id=1, source_target_pairs={{0,7},{1,6},{2,5},{3,4},{4,3},{5,2},{6,1},{7,0},{8,15},{9,14},{10,... | collective-permute-start | bytes 516104 | tf_op jit(solution)/shard_map/c7/ppermute | solution.py:23
  135.1 13.7 %collective-permute-start.14 = (bf16[336,256]{1,0:T(8,128)(2,1)}, bf16[336,256]{1,0:T(8,128)(2,1)S(1)}, u32[]{:S(2)}, u32[]{:S(2)}) collective-permute-start(bf16[336,256]{1,0:T(8,128)(2,1)} %get-tuple-element.102), channel_id=1, source_target_pairs={{0,6},{1,7},{2,4},{3,5},{4,2},{5,3},{6,0},{7,1},{8,14},{9,15},{10,... | collective-permute-start | bytes 516104 | tf_op jit(solution)/shard_map/c6/ppermute | solution.py:23
  143.4 16.7 %collective-permute-start.11 = (bf16[336,256]{1,0:T(8,128)(2,1)}, bf16[336,256]{1,0:T(8,128)(2,1)S(1)}, u32[]{:S(2)}, u32[]{:S(2)}) collective-permute-start(bf16[336,256]{1,0:T(8,128)(2,1)} %get-tuple-element.97), channel_id=1, source_target_pairs={{0,5},{1,4},{2,7},{3,6},{4,1},{5,0},{6,3},{7,2},{8,13},{9,12},{10,... | collective-permute-start | bytes 516104 | tf_op jit(solution)/shard_map/c5/ppermute | solution.py:23
  147.4 16.8 %collective-permute-start.8 = (bf16[336,256]{1,0:T(8,128)(2,1)}, bf16[336,256]{1,0:T(8,128)(2,1)S(1)}, u32[]{:S(2)}, u32[]{:S(2)}) collective-permute-start(bf16[336,256]{1,0:T(8,128)(2,1)} %get-tuple-element.92), channel_id=1, source_target_pairs={{0,4},{1,5},{2,6},{3,7},{4,0},{5,1},{6,2},{7,3},{8,12},{9,13},{10,... | collective-permute-start | bytes 516104 | tf_op jit(solution)/shard_map/c4/ppermute | solution.py:23
  147.4 16.8 %collective-permute-start.5 = (bf16[336,256]{1,0:T(8,128)(2,1)}, bf16[336,256]{1,0:T(8,128)(2,1)S(1)}, u32[]{:S(2)}, u32[]{:S(2)}) collective-permute-start(bf16[336,256]{1,0:T(8,128)(2,1)} %get-tuple-element.86), channel_id=1, source_target_pairs={{0,3},{1,2},{2,1},{3,0},{4,7},{5,6},{6,5},{7,4},{8,11},{9,10},{10,... | collective-permute-start | bytes 516104 | tf_op jit(solution)/shard_map/c3/ppermute | solution.py:23
  148.2 17.0 %collective-permute-start.4 = (bf16[336,256]{1,0:T(8,128)(2,1)}, bf16[336,256]{1,0:T(8,128)(2,1)S(1)}, u32[]{:S(2)}, u32[]{:S(2)}) collective-permute-start(bf16[336,256]{1,0:T(8,128)(2,1)} %get-tuple-element.84), channel_id=1, source_target_pairs={{0,2},{1,3},{2,0},{3,1},{4,6},{5,7},{6,4},{7,5},{8,10},{9,11},{10,... | collective-permute-start | bytes 516104 | tf_op jit(solution)/shard_map/c2/ppermute | solution.py:23
  148.9 16.3 %collective-permute-start.3 = (bf16[336,256]{1,0:T(8,128)(2,1)}, bf16[336,256]{1,0:T(8,128)(2,1)S(1)}, u32[]{:S(2)}, u32[]{:S(2)}) collective-permute-start(bf16[336,256]{1,0:T(8,128)(2,1)} %get-tuple-element.82), channel_id=1, source_target_pairs={{0,1},{1,0},{2,3},{3,2},{4,5},{5,4},{6,7},{7,6},{8,9},{9,8},{10,11... | collective-permute-start | bytes 516104 | tf_op jit(solution)/shard_map/c1/ppermute | solution.py:23
  149.3 3.5 %copy-start.1 = (bf16[336,256]{1,0:T(8,128)(2,1)S(1)}, bf16[336,256]{1,0:T(8,128)(2,1)}, u32[]{:S(2)}) copy-start(bf16[336,256]{1,0:T(8,128)(2,1)} %get-tuple-element.108.refs_0_) | copy-start | bytes 516100
  152.8 12.4 %copy-start.2 = (bf16[336,256]{1,0:T(8,128)(2,1)S(1)}, bf16[336,256]{1,0:T(8,128)(2,1)}, u32[]{:S(2)}) copy-start(bf16[336,256]{1,0:T(8,128)(2,1)} %get-tuple-element.80.refs_0_) | copy-start | bytes 516100

commit v6 on v5

--- a/solution.py
+++ b/solution.py
@@ -48,7 +48,7 @@
 def conv_kernel(plan, clip_ref, *refs):
     jobs, plains, parts, part_rows, part_width = (
         plan["jobs"], plan["plains"], plan["parts"], plan["part_rows"], plan["part_width"])
-    lead, steps, sources, taps = plan["lead"], plan["steps"], plan["sources"], plan["taps"]
+    leads, steps, sources, taps = plan["leads"], plan["steps"], plan["sources"], plan["taps"]
 
     def take(number):
         nonlocal refs
@@ -83,10 +83,12 @@
 
     def piece_copies(at, slot, step):
         mine = lax.axis_index("rows")
-        offset = pl.multiple_of(lead + (at * steps + step) * part_rows, 16)
+        place = (at * steps + step) * part_rows
         return [
-            pltpu.make_async_copy(part_ref.at[slot, at, mine ^ flip],
-                                  out.at[pl.ds(offset, part_rows)], part_sem.at[slot, at, flip])
+            pltpu.make_async_copy(
+                part_ref.at[slot, at, mine ^ flip],
+                out.at[pl.ds(pl.multiple_of(leads[flip] + place, 16), part_rows)],
+                part_sem.at[slot, at, flip])
             for flip, out in enumerate(out_refs)
         ]
 
@@ -146,6 +148,9 @@
             part_ref[slot, at, part, 0:part_width] = piece.astype(jnp.bfloat16)
         for copy in piece_copies(at, slot, step):
             copy.start()
+
+    if not jobs:
+        return
 
     @pl.when(step == steps - 1)
     def _():
@@ -176,7 +181,7 @@
 
 
 def conv_frames(frames, halo, weight, clip_ids, parts, first, sources, jobs, plains=(), row=0,
-                steps=None, addends=(), sums=(), sums_out=False, lead=0, kept=(), weigh=1, vmem=56):
+                steps=None, addends=(), sums=(), sums_out=False, leads=(), kept=None, weigh=1, vmem=56):
     _, band, width, ci = frames.shape
     co = weight.shape[2]
     half = width // 2
@@ -184,10 +189,13 @@
     part_width = half // parts
     part_rows = rounded_up(part_width)
     works = list(jobs) + list(plains)
+    kept = kept or {}
+    leads = leads or [STAT_ROWS] * parts
+    messages = parts if jobs else 0
     taps = sorted({tap for _, pairs, _ in works for _, tap in pairs})
-    plan = dict(jobs=list(jobs), plains=list(plains), addends=len(addends), parts=parts,
-                part_rows=part_rows, lead=lead, part_width=part_width, first=first, steps=steps,
-                kept=len(kept), sums_in=len(sums), sums_out=sums_out, sources=sources, taps=taps,
+    plan = dict(jobs=list(jobs), plains=list(plains), addends=len(addends), parts=messages,
+                part_rows=part_rows, leads=list(leads), part_width=part_width, first=first,
+                steps=steps, kept=len(kept), sums_in=len(sums), sums_out=sums_out, sources=sources, taps=taps,
                 count=frames.shape[0])
     above, above_row = (frames, 2 * row - 1) if row else (halo, 0)
     plain_spec = pl.BlockSpec((1, None, half, co), lambda i, *_: (0, row + i, 0, 0))
@@ -201,12 +209,12 @@
     in_specs += [pl.BlockSpec(a.shape, lambda i, *_: (0, 0, 0)) for a in sums]
     in_specs += [pl.BlockSpec(memory_space=pl.ANY) for _ in kept]
     operands = [clip_ids, *[frames] * sources, *[above] * sources, *[weight] * len(taps),
-                *addends, *sums, *kept]
-    aliases = {len(operands) - len(kept) + at: at for at in range(len(kept))}
-    rows = lead + len(jobs) * steps * part_rows
-    shape = kept[0].shape if kept else (rows, co)
-    out_shape = [jax.ShapeDtypeStruct(shape, jnp.bfloat16) for _ in range(parts)]
-    out_specs = [pl.BlockSpec(memory_space=pl.ANY) for _ in range(parts)]
+                *addends, *sums, *kept.values()]
+    aliases = {len(operands) - len(kept) + at: flip for at, flip in enumerate(kept)}
+    rows = len(jobs) * steps * part_rows
+    out_shape = [jax.ShapeDtypeStruct(kept[flip].shape if flip in kept else (leads[flip] + rows, co),
+                                      jnp.bfloat16) for flip in range(messages)]
+    out_specs = [pl.BlockSpec(memory_space=pl.ANY) for _ in range(messages)]
     out_shape += [jax.ShapeDtypeStruct((1, band // 2, half, co), jnp.bfloat16) for _ in plains]
     out_specs += [plain_spec for _ in plains]
     if sums_out:
@@ -226,10 +234,10 @@
                 *[pltpu.VMEM((3, half, 2 * ci), jnp.bfloat16) for _ in range(sources)],
                 *[pltpu.VMEM((half, co), jnp.float32) for _ in works],
                 *[pltpu.VMEM((8 + half, co), jnp.float32) for _ in works],
-                pltpu.VMEM((2, len(jobs), parts, part_rows, co), jnp.bfloat16),
-                pltpu.VMEM((2 * len(jobs), 8, co), jnp.float32),
+                pltpu.VMEM((2, max(len(jobs), 1), parts, part_rows, co), jnp.bfloat16),
+                pltpu.VMEM((2 * max(len(jobs), 1), 8, co), jnp.float32),
                 pltpu.VMEM((STAT_ROWS, co), jnp.bfloat16),
-                pltpu.SemaphoreType.DMA((2, len(jobs), parts)),
+                pltpu.SemaphoreType.DMA((2, max(len(jobs), 1), parts)),
                 pltpu.SemaphoreType.DMA((parts,)),
             ],
         ),
@@ -245,8 +253,9 @@
 
 def norm_kernel(plan, *refs):
     parts, jobs, steps, rows = plan["parts"], plan["jobs"], plan["steps"], plan["rows"]
-    lead, part_rows = plan["lead"], plan["part_rows"]
-    data_refs, (gain_ref, bias_ref) = refs[:parts], refs[parts : parts + 2]
+    part_rows, apart = plan["part_rows"], plan["apart"]
+    data_refs, rest_refs = refs[:parts], refs[parts : parts + len(apart)]
+    gain_ref, bias_ref = refs[parts + len(apart) : parts + len(apart) + 2]
     out_ref, done_ref, scale_ref = refs[-3:]
     frame, step = pl.program_id(0), pl.program_id(1)
     part_width, co = out_ref.shape[-2:]
@@ -276,30 +285,49 @@
     scale = scale_ref[frame, 1:2]
     bias = bias_ref[...]
     mine = lax.axis_index("rows")
+    top_rows = STAT_ROWS + jobs * part_rows
+
+    def write(flip, at, ref, offset):
+        values = ref[pl.ds(pl.multiple_of(offset, 16), part_rows)][0:part_width].astype(jnp.float32)
+        value = 0.5 * ((values - mean) * scale + bias)
+        out_ref[0, mine ^ flip, at] = (value + value * jnp.tanh(value)).astype(jnp.bfloat16)
+
     for at in range(rows):
         row = step * rows + at
-        if plan["top_first"]:
-            place = jnp.where(row == 0, frame, jobs + frame * (steps - 1) + row - 1)
-        else:
-            place = frame * steps + row
-        offset = pl.multiple_of(lead + place * part_rows, 16)
         for flip in range(parts):
-            values = data_refs[flip][pl.ds(offset, part_rows)][0:part_width].astype(jnp.float32)
-            value = 0.5 * ((values - mean) * scale + bias)
-            out_ref[0, mine ^ flip, at] = (value + value * jnp.tanh(value)).astype(jnp.bfloat16)
-
-
-def norm_frames(messages, gain, bias, first, jobs, shape, top_first=False, base=None, vmem=20):
+            if not plan["top_first"]:
+                write(flip, at, data_refs[flip], STAT_ROWS + (frame * steps + row) * part_rows)
+                continue
+            rest, base = data_refs[flip], top_rows
+            if flip in apart:
+                rest, base = rest_refs[apart.index(flip)], 0
+            below = base + (frame * (steps - 1) + row - 1) * part_rows
+            if at > 0:
+                write(flip, at, rest, below)
+                continue
+
+            @pl.when(row == 0)
+            def _(flip=flip):
+                write(flip, 0, data_refs[flip], STAT_ROWS + frame * part_rows)
+
+            @pl.when(row > 0)
+            def _(flip=flip, rest=rest, below=below):
+                write(flip, 0, rest, below)
+
+
+def norm_frames(messages, gain, bias, first, jobs, shape, top_first=False, rest=None, base=None,
+                vmem=20):
     frames, parts, steps, part_width, co = shape
     rows = 2 if steps % 2 == 0 else 1
-    plan = dict(parts=parts, jobs=jobs, steps=steps, rows=rows, lead=STAT_ROWS,
+    rest = rest or {}
+    plan = dict(parts=parts, jobs=jobs, steps=steps, rows=rows, apart=list(rest),
                 part_rows=rounded_up(part_width), top_first=top_first,
                 entries=float(parts * steps * part_width * parts * (co // GROUPS)))
     in_specs = (
-        [pl.BlockSpec(message.shape, lambda f, i, *_: (0, 0)) for message in messages]
+        [pl.BlockSpec(message.shape, lambda f, i, *_: (0, 0)) for message in [*messages, *rest.values()]]
         + [pl.BlockSpec((1, co), lambda f, i, *_: (0, 0))] * 2
     )
-    operands = [*messages, gain, bias]
+    operands = [*messages, *rest.values(), gain, bias]
     aliases = {}
     if base is not None:
         in_specs.append(pl.BlockSpec(memory_space=pl.ANY))
@@ -347,46 +375,50 @@
         return [sent[0]] + [got[flip] for flip in range(1, parts)]
 
     near = [flip for flip in range(1, parts) if 2 * flip < parts]
+    far = [flip for flip in range(parts - 1, 0, -1) if 2 * flip >= parts]
     chain = []
 
-    def send_far(name, sent, *earlier):
+    def send_far(name, sent):
         got = {}
-        for flip in [flip for flip in range(parts - 1, 0, -1) if 2 * flip >= parts]:
+        for flip in far:
             before = chain[-4:][:1] if len(chain) >= 4 else []
-            got[flip] = named(f"{name}{flip}", exchanged, after(sent[flip], *before, *earlier), "rows", flip)
+            got[flip] = named(f"{name}{flip}", exchanged, after(sent[flip], *before), "rows", flip)
             chain.append(got[flip])
         return got
 
-    def send_near(name, sent, single, *earlier):
-        got = {}
-        for flip in near:
-            got[flip] = named(f"{name}{flip}", exchanged, after(sent[flip], *earlier), "rows", flip)
-            if single:
-                earlier = (got[flip],)
-        return got
+    def send_near(name, sent, *earlier):
+        return {flip: named(f"{name}{flip}", exchanged, after(sent[flip], *earlier), "rows", flip)
+                for flip in near}
 
     halo = named("halo", passed_along, frames[:, -1:], "rows", 1)
+    run = functools.partial(conv_frames, frames, halo, weight, clip_ids, parts)
     later = [(2, [(0, 0), (1, 1), (2, 2)], None), (3, [(1, 0), (2, 1), (3, 2)], None)]
-    onward = [(4, [(2, 0), (3, 1)], None), (5, [(3, 0)], None)]
-    run = functools.partial(conv_frames, frames, halo, weight, clip_ids, parts)
-    *kept, a_sums = named("conv_a", run, 0, 4, later, onward, row=1, steps=steps - 1,
-                          sums_out=True, lead=top_rows, weigh=1, vmem=56)
-    *a_sent, first_on, second_on = named("conv_top", run, 0, 4, later, onward, steps=1, sums=(a_sums,),
-                                         lead=STAT_ROWS, kept=kept, weigh=1, vmem=56)
-    first_add = named("hist0", passed_along, first_on, "tm", 1)
-    second_add = named("hist1", passed_along, after(second_on, first_add), "tm", 1)
+    leads = [0 if flip in far else top_rows for flip in range(parts)]
+    *a_sent, a_sums = named("conv_a", run, 0, 4, later, row=1, steps=steps - 1, sums_out=True,
+                            leads=leads, vmem=56)
     a_got = send_far("a", a_sent)
-    a_got.update(send_near("a", a_sent, True, a_sums))
+    run = functools.partial(conv_frames, frames, after(halo, a_sums), weight, clip_ids, parts)
+    ahead, = named("conv_hist0", run, 2, 2, [], [(4, [(0, 0), (1, 1)], None)], vmem=56)
+    first_add = named("hist0", passed_along, ahead, "tm", 1)
+    run = functools.partial(conv_frames, frames, after(halo, ahead), weight, clip_ids, parts)
+    kept = {flip: a_sent[flip] for flip in range(parts) if flip not in far}
+    t_sent = named("conv_top", run, 0, 4, later, steps=1, sums=(a_sums,), kept=kept, weigh=20, vmem=56)
+    t_got = send_far("t", t_sent)
+    run = functools.partial(conv_frames, frames, after(halo, ahead), weight, clip_ids, parts)
+    onward, = named("conv_hist1", run, 3, 1, [], [(5, [(0, 0)], None)], weigh=20, vmem=56)
+    second_add = named("hist1", passed_along, after(onward, first_add), "tm", 1)
     b_sent = named("conv_b", run, 0, 1, [(0, [(0, 2)], 0)], addends=(after(first_add, a_sums),),
-                   lead=STAT_ROWS, weigh=20, vmem=56)
+                   weigh=20, vmem=56)
     b_got = send_far("b", b_sent)
-    c_sent = named("conv_c", run, 0, 2, [(1, [(0, 1), (1, 2)], 0)], addends=(after(second_add, a_sums),),
-                   lead=STAT_ROWS, weigh=20, vmem=56)
-    out, a_done = named("norm_a", norm_frames, whole(a_sent, a_got), gain, bias, 2, 2, shape, top_first=True, vmem=20)
-    b_got.update(send_near("b", b_sent, False, c_sent[0]))
-    c_got = send_near("c", c_sent, False, c_sent[0])
-    c_got.update(send_far("c", c_sent, c_sent[0]))
-    out, b_done = named("norm_b", norm_frames, whole(b_sent, b_got), gain, bias, 0, 1, shape, base=out, vmem=20)
+    c_sent = named("conv_c", run, 0, 2, [(1, [(0, 1), (1, 2)], 0)], addends=(second_add,),
+                   weigh=20, vmem=56)
+    c_got = send_far("c", c_sent)
+    t_got.update(send_near("t", t_sent, t_got[far[0]]))
+    b_got.update(send_near("b", b_sent, c_sent[0]))
+    c_got.update(send_near("c", c_sent, c_sent[0]))
+    out, _ = named("norm_a", norm_frames, whole(t_sent, t_got), gain, bias, 2, 2, shape, top_first=True,
+                   rest=a_got, vmem=20)
+    out, _ = named("norm_b", norm_frames, whole(b_sent, b_got), gain, bias, 0, 1, shape, base=out, vmem=20)
     out, _ = named("norm_c", norm_frames, whole(c_sent, c_got), gain, bias, 1, 1, shape, base=out, vmem=20)
     return out.reshape(count, parts * steps, shape[3], co)
 

time: 169 us -> 168 us (level)
  starting transfers between devices: 61.3 us -> 42.7 us
  Pallas kernels: 52.8 us -> 61.7 us
  waiting for transfers between devices: 50.4 us -> 58.6 us
    ppermute x21 -> x25, starting transfers between devices: 53.3 us -> 34.8 us  [exchanged(): return lax.ppermute(array, axis, [(i, i ^ flip) for i in range(length)])]
    pallas_call x4 -> x6, Pallas kernels: 45 us -> 53.7 us  [conv_frames(): pl.pallas_call(functools.partial(conv_kernel, plan), out_shape=out_shape,...]
    ppermute x21 -> x25, waiting for transfers between devices: 40.6 us -> 45.4 us  [exchanged(): return lax.ppermute(array, axis, [(i, i ^ flip) for i in range(length)])]
    ppermute x3, waiting for transfers between devices: 9.84 us -> 13.2 us  [passed_along(): return lax.ppermute(array, axis, pairs)]
  transfers between devices with their start and end apart: 24 -> 28, of which waited for: 11 -> 9; matrix products, arithmetic and copies ran while one was open for 0% -> 0% of each run, Pallas kernels for 25% -> 36%
where the time goes in v6:
time: 168 us; the launch traced here: 166 us
  Pallas kernels  61.7 us (37%)
  waiting for transfers between devices  58.6 us (35%)
  starting transfers between devices  42.7 us (25%)
  local copies, waits for them, and re-layouts  2.53 us (2%)
    pallas_call x6, Pallas kernels, conv_frames(): pl.pallas_call(functools.partial(conv_kernel, plan), out_shape=out_shape,...  53.7 us
    ppermute x25, waiting for transfers between devices, exchanged(): return lax.ppermute(array, axis, [(i, i ^ flip) for i in range(length)])  45.4 us
    ppermute x25, starting transfers between devices, exchanged(): return lax.ppermute(array, axis, [(i, i ^ flip) for i in range(length)])  34.8 us
    ppermute x3, waiting for transfers between devices, passed_along(): return lax.ppermute(array, axis, pairs)  13.2 us
    pallas_call x3, Pallas kernels, norm_frames(): pl.pallas_call(functools.partial(norm_kernel, plan), out_shape=[jax.Shape...  7.97 us
    ppermute x3, starting transfers between devices, passed_along(): return lax.ppermute(array, axis, pairs)  7.89 us
  transfers between devices with their start and end apart: 28, of which 9 were waited for; matrix products, arithmetic and copies ran while one was open for 0% of the time, Pallas kernels for 36%

profile of v6, /device:TPU:4, one launch (start us, length us, event | category | flops | bytes accessed | tf_op | source)
XLA Modules:
  0.0 165.9 jit_solution(14393234606684838680)
XLA Ops:
  0.0 1.4 slice.3
  1.4 1.8 %collective-permute-start = (bf16[4,1,1280,128]{3,2,1,0:T(8,128)(2,1)S(1)}, bf16[4,1,1280,128]{3,2,1,0:T(8,128)(2,1)S(1)}, u32[]{:S(2)}, u32[]{:S(2)}) collective-permute-start(bf16[4,1,1280,128]{3,2,1,0:T(8,128)(2,1)S(1)} %slice.3), channel_id=1, source_target_pairs={{0,1},{1,2},{2,3},{3,4},{4,5},{5,6},{6,7},{8,9},{9,10},{10,11},{11... | collective-permute-start | bytes 3932168 | tf_op jit(solution)/shard_map/halo/ppermute | solution.py:18
  3.2 15.2 %conv_a.1 = (bf16[656,256]{1,0:T(8,128)(2,1)}, bf16[656,256]{1,0:T(8,128)(2,1)}, bf16[656,256]{1,0:T(8,128)(2,1)}, bf16[656,256]{1,0:T(8,128)(2,1)}, bf16[480,25...) custom-call(s32[16]{0:T(128)} %clip_ref.11, ...), custom_call_target="tpu_custom_call" | custom-call | flops 6794772480 | bytes 9830400 | tf_op jit(solution)/shard_map/conv_a/pallas_call | solution.py:225
  18.5 2.8 %collective-permute-start.6 = (bf16[480,256]{1,0:T(8,128)(2,1)}, bf16[480,256]{1,0:T(8,128)(2,1)S(1)}, u32[]{:S(2)}, u32[]{:S(2)}) collective-permute-start(bf16[480,256]{1,0:T(8,128)(2,1)} %get-tuple-element.85), channel_id=1, source_target_pairs={{0,4},{1,5},{2,6},{3,7},{4,0},{5,1},{6,2},{7,3},{8,12},{9,13},{10,... | collective-permute-start | bytes 737288 | tf_op jit(solution)/shard_map/a4/ppermute | solution.py:23
  21.2 1.4 collective-permute-start.10
  22.6 1.3 collective-permute-start.14
  23.9 1.8 %collective-permute-start.18 = (bf16[480,256]{1,0:T(8,128)(2,1)}, bf16[480,256]{1,0:T(8,128)(2,1)S(1)}, u32[]{:S(2)}, u32[]{:S(2)}) collective-permute-start(bf16[480,256]{1,0:T(8,128)(2,1)} %get-tuple-element.106), channel_id=1, source_target_pairs={{0,7},{1,6},{2,5},{3,4},{4,3},{5,2},{6,1},{7,0},{8,15},{9,14},{10,... | collective-permute-start | bytes 737288 | tf_op jit(solution)/shard_map/a7/ppermute | solution.py:23
  25.8 0.0 collective-permute-done.refs_2_.refs_3_.refs_1_.refs_4_.refs_5_.refs_6_.refs_7_
  25.8 1.1 copy-done.5
  26.8 8.5 %conv_hist0.1 = bf16[1,4,640,256]{3,2,1,0:T(8,128)(2,1)} custom-call(s32[16]{0:T(128)} %clip_ref.11, bf16[4,8,1280,128]{3,2,1,0:T(8,128)(2,1)} %refs_3_.3, bf16[4,8,1280,128]{3,2,1,0:T(8,128)(2,1)} %refs_3_.3, bf16[4,1,1280,128]{3,2,1,0:T(8,128)(2,1)} %copy-done.5, bf16[4,1,1280,128]{3,2,1,0:T(8,128)(2,1)} %copy-done.5, bf16[3,1152,256]{2,1,0:T(8,128)(2,1)} %bitcast.13, ...), custom_call_target="tpu_custom_call" | custom-call | flops 3019898880 | bytes 6553600 | tf_op jit(solution)/shard_map/conv_hist0/pallas_call | solution.py:225
  35.3 3.4 %collective-permute-start.1 = (bf16[1,4,640,256]{3,2,1,0:T(8,128)(2,1)}, bf16[1,4,640,256]{3,2,1,0:T(8,128)(2,1)S(1)}, u32[]{:S(2)}, u32[]{:S(2)}) collective-permute-start(bf16[1,4,640,256]{3,2,1,0:T(8,128)(2,1)} %conv_hist0.1), channel_id=1, source_target_pairs={{0,8},{8,16},{16,24},{1,9},{9,17},{17,25},{2,10},{10,18},{18,26},{... | collective-permute-start | bytes 3932168 | tf_op jit(solution)/shard_map/hist0/ppermute | solution.py:18
  38.7 7.2 %conv_top.1 = (bf16[656,256]{1,0:T(8,128)(2,1)}, bf16[656,256]{1,0:T(8,128)(2,1)}, bf16[656,256]{1,0:T(8,128)(2,1)}, bf16[656,256]{1,0:T(8,128)(2,1)}, bf16[176,...) custom-call(s32[16]{0:T(128)} %clip_ref.11, ...), custom_call_target="tpu_custom_call", output_to_operand_aliasing={{0}: (13, {}), {1}: (14, {}), {2}: (15, {}), {3}: (16, {})} | custom-call | flops 45298483200 | bytes 65536000 | tf_op jit(solution)/shard_map/conv_top/pallas_call | solution.py:225
  46.0 6.5 %conv_hist1.1 = bf16[1,4,640,256]{3,2,1,0:T(8,128)(2,1)} custom-call(s32[16]{0:T(128)} %clip_ref.11, bf16[4,8,1280,128]{3,2,1,0:T(8,128)(2,1)} %refs_3_.3, bf16[4,1,1280,128]{3,2,1,0:T(8,128)(2,1)} %copy-done.5, bf16[3,1152,256]{2,1,0:T(8,128)(2,1)} %bitcast.18), custom_call_target="tpu_custom_call" | custom-call | flops 30198988800 | bytes 78643200 | tf_op jit(solution)/shard_map/conv_hist1/pallas_call | solution.py:225
  52.5 0.0 collective-permute-done.14.refs_9_
  52.5 0.0 collective-permute-done.18.refs_8_
  52.5 1.5 collective-permute-start.19
  54.0 2.5 %collective-permute-start.15 = (bf16[176,256]{1,0:T(8,128)(2,1)S(1)}, bf16[176,256]{1,0:T(8,128)(2,1)S(1)}, u32[]{:S(2)}, u32[]{:S(2)}) collective-permute-start(bf16[176,256]{1,0:T(8,128)(2,1)S(1)} %copy-done.16), channel_id=1, source_target_pairs={{0,6},{1,7},{2,4},{3,5},{4,2},{5,3},{6,0},{7,1},{8,14},{9,15},{10,... | collective-permute-start | bytes 270344 | tf_op jit(solution)/shard_map/t6/ppermute | solution.py:23
  56.5 13.2 %collective-permute-done.1.refs_3_ = bf16[1,4,640,256]{3,2,1,0:T(8,128)(2,1)S(1)} collective-permute-done((bf16[1,4,640,256]{3,2,1,0:T(8,128)(2,1)}, bf16[1,4,640,256]{3,2,1,0:T(8,128)(2,1)S(1)}, u32[]{:S(2)}, u32[]{:S(2)}) %collective-permute-start.1) | collective-permute-done | bytes 1310752 | tf_op jit(solution)/shard_map/hist0/ppermute | solution.py:18
  69.7 2.7 %collective-permute-start.2 = (bf16[1,4,640,256]{3,2,1,0:T(8,128)(2,1)}, bf16[1,4,640,256]{3,2,1,0:T(8,128)(2,1)S(1)}, u32[]{:S(2)}, u32[]{:S(2)}) collective-permute-start(bf16[1,4,640,256]{3,2,1,0:T(8,128)(2,1)} %conv_hist1.1), channel_id=1, source_target_pairs={{0,8},{8,16},{16,24},{1,9},{9,17},{17,25},{2,10},{10,18},{18,26},{... | collective-permute-start | bytes 3932168 | tf_op jit(solution)/shard_map/hist1/ppermute | solution.py:18
  72.4 7.2 %conv_b.1 = (bf16[336,256]{1,0:T(8,128)(2,1)}, bf16[336,256]{1,0:T(8,128)(2,1)}, bf16[336,256]{1,0:T(8,128)(2,1)}, bf16[336,256]{1,0:T(8,128)(2,1)}, bf16[336,25...) custom-call(s32[16]{0:T(128)} %clip_ref.11, ...), custom_call_target="tpu_custom_call" | custom-call | flops 30198988800 | bytes 78643200 | tf_op jit(solution)/shard_map/conv_b/pallas_call | solution.py:225
  79.6 0.0 collective-permute-done.19.refs_7_
  79.6 0.1 collective-permute-start.20
  79.7 0.0 collective-permute-done.15.refs_6_
  79.7 3.0 %collective-permute-start.16 = (bf16[336,256]{1,0:T(8,128)(2,1)}, bf16[336,256]{1,0:T(8,128)(2,1)S(1)}, u32[]{:S(2)}, u32[]{:S(2)}) collective-permute-start(bf16[336,256]{1,0:T(8,128)(2,1)} %get-tuple-element.101), channel_id=1, source_target_pairs={{0,6},{1,7},{2,4},{3,5},{4,2},{5,3},{6,0},{7,1},{8,14},{9,15},{10,... | collective-permute-start | bytes 516104 | tf_op jit(solution)/shard_map/b6/ppermute | solution.py:23
  82.7 0.0 collective-permute-done.6.refs_11_
  82.7 0.9 collective-permute-start.7
  83.7 0.0 collective-permute-done.10.refs_10_
  83.7 1.9 %collective-permute-start.11 = (bf16[176,256]{1,0:T(8,128)(2,1)S(1)}, bf16[176,256]{1,0:T(8,128)(2,1)S(1)}, u32[]{:S(2)}, u32[]{:S(2)}) collective-permute-start(bf16[176,256]{1,0:T(8,128)(2,1)S(1)} %copy-done.14), channel_id=1, source_target_pairs={{0,5},{1,4},{2,7},{3,6},{4,1},{5,0},{6,3},{7,2},{8,13},{9,12},{10,... | collective-permute-start | bytes 270344 | tf_op jit(solution)/shard_map/t5/ppermute | solution.py:23
  85.6 19.5 %collective-permute-done.7.refs_4_ = bf16[176,256]{1,0:T(8,128)(2,1)S(1)} collective-permute-done((bf16[176,256]{1,0:T(8,128)(2,1)S(1)}, bf16[176,256]{1,0:T(8,128)(2,1)S(1)}, u32[]{:S(2)}, u32[]{:S(2)}) %collective-permute-start.7) | collective-permute-done | bytes 90144 | tf_op jit(solution)/shard_map/t4/ppermute | solution.py:23
  105.1 0.0 collective-permute-start.25
  105.1 1.4 collective-permute-done.11.refs_5_
  106.5 0.0 collective-permute-start.26
  106.5 0.0 copy-start.3
  106.5 0.0 copy-start.4
  106.6 0.0 collective-permute-done.20.refs_7_
  106.6 1.5 collective-permute-start.27
  108.1 0.0 collective-permute-done.16.refs_6_
  108.1 0.1 collective-permute-start.12
  108.2 0.0 collective-permute-done.2.refs_6_
  108.2 3.1 %collective-permute-start.8 = (bf16[336,256]{1,0:T(8,128)(2,1)}, bf16[336,256]{1,0:T(8,128)(2,1)S(1)}, u32[]{:S(2)}, u32[]{:S(2)}) collective-permute-start(bf16[336,256]{1,0:T(8,128)(2,1)} %get-tuple-element.87), channel_id=1, source_target_pairs={{0,4},{1,5},{2,6},{3,7},{4,0},{5,1},{6,2},{7,3},{8,12},{9,13},{10,... | collective-permute-start | bytes 516104 | tf_op jit(solution)/shard_map/b4/ppermute | solution.py:23
  111.3 9.2 %conv_c.1 = (bf16[336,256]{1,0:T(8,128)(2,1)}, bf16[336,256]{1,0:T(8,128)(2,1)}, bf16[336,256]{1,0:T(8,128)(2,1)}, bf16[336,256]{1,0:T(8,128)(2,1)}, bf16[336,25...) custom-call(s32[16]{0:T(128)} %clip_ref.11, ...), custom_call_target="tpu_custom_call" | custom-call | flops 60397977600 | bytes 131072000 | tf_op jit(solution)/shard_map/conv_c/pallas_call | solution.py:225
  120.5 0.0 collective-permute-done.25.refs_1_
  120.5 0.1 collective-permute-start.24
  120.6 4.0 %collective-permute-done.26.refs_2_ = bf16[656,256]{1,0:T(8,128)(2,1)S(1)} collective-permute-done((bf16[656,256]{1,0:T(8,128)(2,1)S(1)}, bf16[656,256]{1,0:T(8,128)(2,1)S(1)}, u32[]{:S(2)}, u32[]{:S(2)}) %collective-permute-start.26) | collective-permute-done | bytes 335904 | tf_op jit(solution)/shard_map/t2/ppermute | solution.py:23
  124.6 0.0 collective-permute-start.23
  124.6 5.5 %collective-permute-done.27.refs_3_ = bf16[656,256]{1,0:T(8,128)(2,1)S(1)} collective-permute-done((bf16[656,256]{1,0:T(8,128)(2,1)S(1)}, bf16[656,256]{1,0:T(8,128)(2,1)S(1)}, u32[]{:S(2)}, u32[]{:S(2)}) %collective-permute-start.27) | collective-permute-done | bytes 335904 | tf_op jit(solution)/shard_map/t3/ppermute | solution.py:23
  130.1 1.8 %collective-permute-start.22 = (bf16[336,256]{1,0:T(8,128)(2,1)S(1)}, bf16[336,256]{1,0:T(8,128)(2,1)S(1)}, u32[]{:S(2)}, u32[]{:S(2)}) collective-permute-start(bf16[336,256]{1,0:T(8,128)(2,1)S(1)} %copy-done.11), channel_id=1, source_target_pairs={{0,1},{1,0},{2,3},{3,2},{4,5},{5,4},{6,7},{7,6},{8,9},{9,8},{10,11... | collective-permute-start | bytes 516104 | tf_op jit(solution)/shard_map/b1/ppermute | solution.py:23
  131.9 0.0 collective-permute-done.12.refs_5_
  131.9 0.9 collective-permute-start.21
  132.8 0.0 collective-permute-done.8.refs_4_
  132.8 2.6 %collective-permute-start.17 = (bf16[336,256]{1,0:T(8,128)(2,1)}, bf16[336,256]{1,0:T(8,128)(2,1)S(1)}, u32[]{:S(2)}, u32[]{:S(2)}) collective-permute-start(bf16[336,256]{1,0:T(8,128)(2,1)} %get-tuple-element.102), channel_id=1, source_target_pairs={{0,6},{1,7},{2,4},{3,5},{4,2},{5,3},{6,0},{7,1},{8,14},{9,15},{10,... | collective-permute-start | bytes 516104 | tf_op jit(solution)/shard_map/c6/ppermute | solution.py:23
  135.4 0.0 collective-permute-done.24.refs_3_
  135.4 0.0 collective-permute-start.13
  135.4 10.1 %collective-permute-done.23.refs_2_ = bf16[336,256]{1,0:T(8,128)(2,1)S(1)} collective-permute-done((bf16[336,256]{1,0:T(8,128)(2,1)S(1)}, bf16[336,256]{1,0:T(8,128)(2,1)S(1)}, u32[]{:S(2)}, u32[]{:S(2)}) %collective-permute-start.23) | collective-permute-done | bytes 172064 | tf_op jit(solution)/shard_map/b2/ppermute | solution.py:23
  145.6 0.0 collective-permute-start.5
  145.6 0.1 collective-permute-start.4
  145.7 0.2 collective-permute-done.17.refs_6_
  145.9 7.4 %collective-permute-start.3 = (bf16[336,256]{1,0:T(8,128)(2,1)}, bf16[336,256]{1,0:T(8,128)(2,1)S(1)}, u32[]{:S(2)}, u32[]{:S(2)}) collective-permute-start(bf16[336,256]{1,0:T(8,128)(2,1)} %get-tuple-element.72), channel_id=1, source_target_pairs={{0,1},{1,0},{2,3},{3,2},{4,5},{5,4},{6,7},{7,6},{8,9},{9,8},{10,11... | collective-permute-start | bytes 516104 | tf_op jit(solution)/shard_map/c1/ppermute | solution.py:23
  153.3 3.6 %norm_a.1 = (bf16[4,8,4,80,256]{4,3,2,1,0:T(8,128)(2,1)}, f32[8,256]{1,0:T(8,128)}) custom-call(bf16[656,256]{1,0:T(8,128)(2,1)S(1)} %copy-done, bf16[656,256]{1,0:T(8,128)(2,1)S(1)} %collective-permute-done.25.refs_1_, bf16[656,256]{1,0:T(8,128)(2,1)S(1)} %collective-permute-done.26.refs_2_, bf16[656,256]{1,0:T(8,128)(2,1)S(1)} %collective-permute-done.27.refs_3_, ...), custom_call_target="tpu_custom_call" | custom-call | flops 10485760 | bytes 5242880 | tf_op jit(solution)/shard_map/norm_a/pallas_call | solution.py:336
  157.0 2.2 %norm_b.1 = (bf16[4,8,4,80,256]{4,3,2,1,0:T(8,128)(2,1)}, f32[8,256]{1,0:T(8,128)}) custom-call(bf16[336,256]{1,0:T(8,128)(2,1)S(1)} %copy-done.1, bf16[336,256]{1,0:T(8,128)(2,1)S(1)} %collective-permute-done.22.refs_1_, bf16[336,256]{1,0:T(8,128)(2,1)S(1)} %collective-permute-done.23.refs_2_, ...), custom_call_target="tpu_custom_call", output_to_operand_aliasing={{0}: (10, {})} | custom-call | flops 5242880 | bytes 2621440 | tf_op jit(solution)/shard_map/norm_b/pallas_call | solution.py:336
  159.1 0.3 collective-permute-done.13.refs_5_
  159.4 4.3 %collective-permute-done.9.refs_4_ = bf16[336,256]{1,0:T(8,128)(2,1)S(1)} collective-permute-done((bf16[336,256]{1,0:T(8,128)(2,1)}, bf16[336,256]{1,0:T(8,128)(2,1)S(1)}, u32[]{:S(2)}, u32[]{:S(2)}) %collective-permute-start.9) | collective-permute-done | bytes 172064 | tf_op jit(solution)/shard_map/c4/ppermute | solution.py:23
  163.7 0.0 collective-permute-done.5.refs_3_
  163.7 2.2 %norm_c.1 = (bf16[4,8,4,80,256]{4,3,2,1,0:T(8,128)(2,1)}, f32[8,256]{1,0:T(8,128)}) custom-call(bf16[336,256]{1,0:T(8,128)(2,1)S(1)} %copy-done.2, bf16[336,256]{1,0:T(8,128)(2,1)S(1)} %collective-permute-done.3.refs_1_, bf16[336,256]{1,0:T(8,128)(2,1)S(1)} %collective-permute-done.4.refs_2_, ...), custom_call_target="tpu_custom_call", output_to_operand_aliasing={{0}: (10, {})} | custom-call | flops 5242880 | bytes 2621440 | tf_op jit(solution)/shard_map/norm_c/pallas_call | solution.py:336
  (38 shorter events, 0.1 us)
Async XLA Ops:
  1.4 24.4 %collective-permute-start = (bf16[4,1,1280,128]{3,2,1,0:T(8,128)(2,1)S(1)}, bf16[4,1,1280,128]{3,2,1,0:T(8,128)(2,1)S(1)}, u32[]{:S(2)}, u32[]{:S(2)}) collective-permute-start(bf16[4,1,1280,128]{3,2,1,0:T(8,128)(2,1)S(1)} %slice.3), channel_id=1, source_target_pairs={{0,1},{1,2},{2,3},{3,4},{4,5},{5,6},{6,7},{8,9},{9,10},{10,11},{11... | collective-permute-start | bytes 3932168 | tf_op jit(solution)/shard_map/halo/ppermute | solution.py:18
  18.5 64.3 %collective-permute-start.6 = (bf16[480,256]{1,0:T(8,128)(2,1)}, bf16[480,256]{1,0:T(8,128)(2,1)S(1)}, u32[]{:S(2)}, u32[]{:S(2)}) collective-permute-start(bf16[480,256]{1,0:T(8,128)(2,1)} %get-tuple-element.85), channel_id=1, source_target_pairs={{0,4},{1,5},{2,6},{3,7},{4,0},{5,1},{6,2},{7,3},{8,12},{9,13},{10,... | collective-permute-start | bytes 737288 | tf_op jit(solution)/shard_map/a4/ppermute | solution.py:23
  21.2 62.5 %collective-permute-start.10 = (bf16[480,256]{1,0:T(8,128)(2,1)}, bf16[480,256]{1,0:T(8,128)(2,1)S(1)}, u32[]{:S(2)}, u32[]{:S(2)}) collective-permute-start(bf16[480,256]{1,0:T(8,128)(2,1)} %get-tuple-element.92), channel_id=1, source_target_pairs={{0,5},{1,4},{2,7},{3,6},{4,1},{5,0},{6,3},{7,2},{8,13},{9,12},{10,... | collective-permute-start | bytes 737288 | tf_op jit(solution)/shard_map/a5/ppermute | solution.py:23
  22.6 29.9 %collective-permute-start.14 = (bf16[480,256]{1,0:T(8,128)(2,1)}, bf16[480,256]{1,0:T(8,128)(2,1)S(1)}, u32[]{:S(2)}, u32[]{:S(2)}) collective-permute-start(bf16[480,256]{1,0:T(8,128)(2,1)} %get-tuple-element.99), channel_id=1, source_target_pairs={{0,6},{1,7},{2,4},{3,5},{4,2},{5,3},{6,0},{7,1},{8,14},{9,15},{10,... | collective-permute-start | bytes 737288 | tf_op jit(solution)/shard_map/a6/ppermute | solution.py:23
  23.9 28.5 %collective-permute-start.18 = (bf16[480,256]{1,0:T(8,128)(2,1)}, bf16[480,256]{1,0:T(8,128)(2,1)S(1)}, u32[]{:S(2)}, u32[]{:S(2)}) collective-permute-start(bf16[480,256]{1,0:T(8,128)(2,1)} %get-tuple-element.106), channel_id=1, source_target_pairs={{0,7},{1,6},{2,5},{3,4},{4,3},{5,2},{6,1},{7,0},{8,15},{9,14},{10,... | collective-permute-start | bytes 737288 | tf_op jit(solution)/shard_map/a7/ppermute | solution.py:23
  25.8 1.1 copy-start.5
  35.3 34.4 %collective-permute-start.1 = (bf16[1,4,640,256]{3,2,1,0:T(8,128)(2,1)}, bf16[1,4,640,256]{3,2,1,0:T(8,128)(2,1)S(1)}, u32[]{:S(2)}, u32[]{:S(2)}) collective-permute-start(bf16[1,4,640,256]{3,2,1,0:T(8,128)(2,1)} %conv_hist0.1), channel_id=1, source_target_pairs={{0,8},{8,16},{16,24},{1,9},{9,17},{17,25},{2,10},{10,18},{18,26},{... | collective-permute-start | bytes 3932168 | tf_op jit(solution)/shard_map/hist0/ppermute | solution.py:18
  45.9 6.5 %copy-start.17 = (bf16[176,256]{1,0:T(8,128)(2,1)S(1)}, bf16[176,256]{1,0:T(8,128)(2,1)}, u32[]{:S(2)}) copy-start(bf16[176,256]{1,0:T(8,128)(2,1)} %get-tuple-element.107) | copy-start | bytes 270340
  45.9 8.1 %copy-start.16 = (bf16[176,256]{1,0:T(8,128)(2,1)S(1)}, bf16[176,256]{1,0:T(8,128)(2,1)}, u32[]{:S(2)}) copy-start(bf16[176,256]{1,0:T(8,128)(2,1)} %get-tuple-element.100) | copy-start | bytes 270340
  52.5 30.2 %copy-start.15 = (bf16[176,256]{1,0:T(8,128)(2,1)S(1)}, bf16[176,256]{1,0:T(8,128)(2,1)}, u32[]{:S(2)}) copy-start(bf16[176,256]{1,0:T(8,128)(2,1)} %get-tuple-element.86) | copy-start | bytes 270340
  52.5 31.2 %copy-start.14 = (bf16[176,256]{1,0:T(8,128)(2,1)S(1)}, bf16[176,256]{1,0:T(8,128)(2,1)}, u32[]{:S(2)}) copy-start(bf16[176,256]{1,0:T(8,128)(2,1)} %get-tuple-element.93) | copy-start | bytes 270340
  52.5 52.6 %copy-start.8 = (bf16[656,256]{1,0:T(8,128)(2,1)S(1)}, bf16[656,256]{1,0:T(8,128)(2,1)}, u32[]{:S(2)}) copy-start(bf16[656,256]{1,0:T(8,128)(2,1)} %get-tuple-element.119) | copy-start | bytes 1007620
  52.5 54.0 %copy-start.9 = (bf16[656,256]{1,0:T(8,128)(2,1)S(1)}, bf16[656,256]{1,0:T(8,128)(2,1)}, u32[]{:S(2)}) copy-start(bf16[656,256]{1,0:T(8,128)(2,1)} %get-tuple-element.121) | copy-start | bytes 1007620
  52.5 54.0 %copy-start.10 = (bf16[656,256]{1,0:T(8,128)(2,1)S(1)}, bf16[656,256]{1,0:T(8,128)(2,1)}, u32[]{:S(2)}) copy-start(bf16[656,256]{1,0:T(8,128)(2,1)} %get-tuple-element.123) | copy-start | bytes 1007620
  52.5 27.1 %collective-permute-start.19 = (bf16[176,256]{1,0:T(8,128)(2,1)S(1)}, bf16[176,256]{1,0:T(8,128)(2,1)S(1)}, u32[]{:S(2)}, u32[]{:S(2)}) collective-permute-start(bf16[176,256]{1,0:T(8,128)(2,1)S(1)} %copy-done.17), channel_id=1, source_target_pairs={{0,7},{1,6},{2,5},{3,4},{4,3},{5,2},{6,1},{7,0},{8,15},{9,14},{10,... | collective-permute-start | bytes 270344 | tf_op jit(solution)/shard_map/t7/ppermute | solution.py:23
  54.0 25.7 %collective-permute-start.15 = (bf16[176,256]{1,0:T(8,128)(2,1)S(1)}, bf16[176,256]{1,0:T(8,128)(2,1)S(1)}, u32[]{:S(2)}, u32[]{:S(2)}) collective-permute-start(bf16[176,256]{1,0:T(8,128)(2,1)S(1)} %copy-done.16), channel_id=1, source_target_pairs={{0,6},{1,7},{2,4},{3,5},{4,2},{5,3},{6,0},{7,1},{8,14},{9,15},{10,... | collective-permute-start | bytes 270344 | tf_op jit(solution)/shard_map/t6/ppermute | solution.py:23
  69.7 2.7 %copy-start.7 = (bf16[1,4,640,256]{3,2,1,0:T(8,128)(2,1)}, bf16[1,4,640,256]{3,2,1,0:T(8,128)(2,1)S(1)}, u32[]{:S(2)}) copy-start(bf16[1,4,640,256]{3,2,1,0:T(8,128)(2,1)S(1)} %collective-permute-done.1.refs_3_) | copy-start | bytes 3932164
  69.7 38.5 %collective-permute-start.2 = (bf16[1,4,640,256]{3,2,1,0:T(8,128)(2,1)}, bf16[1,4,640,256]{3,2,1,0:T(8,128)(2,1)S(1)}, u32[]{:S(2)}, u32[]{:S(2)}) collective-permute-start(bf16[1,4,640,256]{3,2,1,0:T(8,128)(2,1)} %conv_hist1.1), channel_id=1, source_target_pairs={{0,8},{8,16},{16,24},{1,9},{9,17},{17,25},{2,10},{10,18},{18,26},{... | collective-permute-start | bytes 3932168 | tf_op jit(solution)/shard_map/hist1/ppermute | solution.py:18
  79.6 27.0 %collective-permute-start.20 = (bf16[336,256]{1,0:T(8,128)(2,1)}, bf16[336,256]{1,0:T(8,128)(2,1)S(1)}, u32[]{:S(2)}, u32[]{:S(2)}) collective-permute-start(bf16[336,256]{1,0:T(8,128)(2,1)} %get-tuple-element.108), channel_id=1, source_target_pairs={{0,7},{1,6},{2,5},{3,4},{4,3},{5,2},{6,1},{7,0},{8,15},{9,14},{10,... | collective-permute-start | bytes 516104 | tf_op jit(solution)/shard_map/b7/ppermute | solution.py:23
  79.7 28.4 %collective-permute-start.16 = (bf16[336,256]{1,0:T(8,128)(2,1)}, bf16[336,256]{1,0:T(8,128)(2,1)S(1)}, u32[]{:S(2)}, u32[]{:S(2)}) collective-permute-start(bf16[336,256]{1,0:T(8,128)(2,1)} %get-tuple-element.101), channel_id=1, source_target_pairs={{0,6},{1,7},{2,4},{3,5},{4,2},{5,3},{6,0},{7,1},{8,14},{9,15},{10,... | collective-permute-start | bytes 516104 | tf_op jit(solution)/shard_map/b6/ppermute | solution.py:23
  82.7 22.4 %collective-permute-start.7 = (bf16[176,256]{1,0:T(8,128)(2,1)S(1)}, bf16[176,256]{1,0:T(8,128)(2,1)S(1)}, u32[]{:S(2)}, u32[]{:S(2)}) collective-permute-start(bf16[176,256]{1,0:T(8,128)(2,1)S(1)} %copy-done.15), channel_id=1, source_target_pairs={{0,4},{1,5},{2,6},{3,7},{4,0},{5,1},{6,2},{7,3},{8,12},{9,13},{10,... | collective-permute-start | bytes 270344 | tf_op jit(solution)/shard_map/t4/ppermute | solution.py:23
  83.7 22.8 %collective-permute-start.11 = (bf16[176,256]{1,0:T(8,128)(2,1)S(1)}, bf16[176,256]{1,0:T(8,128)(2,1)S(1)}, u32[]{:S(2)}, u32[]{:S(2)}) collective-permute-start(bf16[176,256]{1,0:T(8,128)(2,1)S(1)} %copy-done.14), channel_id=1, source_target_pairs={{0,5},{1,4},{2,7},{3,6},{4,1},{5,0},{6,3},{7,2},{8,13},{9,12},{10,... | collective-permute-start | bytes 270344 | tf_op jit(solution)/shard_map/t5/ppermute | solution.py:23
  105.1 15.4 %collective-permute-start.25 = (bf16[656,256]{1,0:T(8,128)(2,1)S(1)}, bf16[656,256]{1,0:T(8,128)(2,1)S(1)}, u32[]{:S(2)}, u32[]{:S(2)}) collective-permute-start(bf16[656,256]{1,0:T(8,128)(2,1)S(1)} %copy-done.8), channel_id=1, source_target_pairs={{0,1},{1,0},{2,3},{3,2},{4,5},{5,4},{6,7},{7,6},{8,9},{9,8},{10,11... | collective-permute-start | bytes 1007624 | tf_op jit(solution)/shard_map/t1/ppermute | solution.py:23
  106.5 18.1 %collective-permute-start.26 = (bf16[656,256]{1,0:T(8,128)(2,1)S(1)}, bf16[656,256]{1,0:T(8,128)(2,1)S(1)}, u32[]{:S(2)}, u32[]{:S(2)}) collective-permute-start(bf16[656,256]{1,0:T(8,128)(2,1)S(1)} %copy-done.9), channel_id=1, source_target_pairs={{0,2},{1,3},{2,0},{3,1},{4,6},{5,7},{6,4},{7,5},{8,10},{9,11},{10,... | collective-permute-start | bytes 1007624 | tf_op jit(solution)/shard_map/t2/ppermute | solution.py:23
  106.5 14.0 %copy-start.13 = (bf16[336,256]{1,0:T(8,128)(2,1)S(1)}, bf16[336,256]{1,0:T(8,128)(2,1)}, u32[]{:S(2)}) copy-start(bf16[336,256]{1,0:T(8,128)(2,1)} %get-tuple-element.116) | copy-start | bytes 516100
  106.5 18.1 %copy-start.12 = (bf16[336,256]{1,0:T(8,128)(2,1)S(1)}, bf16[336,256]{1,0:T(8,128)(2,1)}, u32[]{:S(2)}) copy-start(bf16[336,256]{1,0:T(8,128)(2,1)} %get-tuple-element.114) | copy-start | bytes 516100
  106.5 23.6 %copy-start.11 = (bf16[336,256]{1,0:T(8,128)(2,1)S(1)}, bf16[336,256]{1,0:T(8,128)(2,1)}, u32[]{:S(2)}) copy-start(bf16[336,256]{1,0:T(8,128)(2,1)} %get-tuple-element.112) | copy-start | bytes 516100
  106.5 46.8 %copy-start = (bf16[656,256]{1,0:T(8,128)(2,1)S(1)}, bf16[656,256]{1,0:T(8,128)(2,1)}, u32[]{:S(2)}) copy-start(bf16[656,256]{1,0:T(8,128)(2,1)} %get-tuple-element.117.refs_0_) | copy-start | bytes 1007620
  106.5 46.8 %copy-start.3 = (f32[256]{0:T(256)S(1)}, f32[256]{0:T(256)}, u32[]{:S(2)}) copy-start(f32[256]{0:T(256)} %param.8) | copy-start | bytes 3076
  106.5 46.8 %copy-start.4 = (f32[256]{0:T(256)S(1)}, f32[256]{0:T(256)}, u32[]{:S(2)}) copy-start(f32[256]{0:T(256)} %param.9) | copy-start | bytes 3076
  106.6 23.6 %collective-permute-start.27 = (bf16[656,256]{1,0:T(8,128)(2,1)S(1)}, bf16[656,256]{1,0:T(8,128)(2,1)S(1)}, u32[]{:S(2)}, u32[]{:S(2)}) collective-permute-start(bf16[656,256]{1,0:T(8,128)(2,1)S(1)} %copy-done.10), channel_id=1, source_target_pairs={{0,3},{1,2},{2,1},{3,0},{4,7},{5,6},{6,5},{7,4},{8,11},{9,10},{10,... | collective-permute-start | bytes 1007624 | tf_op jit(solution)/shard_map/t3/ppermute | solution.py:23
  108.1 23.8 %collective-permute-start.12 = (bf16[336,256]{1,0:T(8,128)(2,1)}, bf16[336,256]{1,0:T(8,128)(2,1)S(1)}, u32[]{:S(2)}, u32[]{:S(2)}) collective-permute-start(bf16[336,256]{1,0:T(8,128)(2,1)} %get-tuple-element.94), channel_id=1, source_target_pairs={{0,5},{1,4},{2,7},{3,6},{4,1},{5,0},{6,3},{7,2},{8,13},{9,12},{10,... | collective-permute-start | bytes 516104 | tf_op jit(solution)/shard_map/b5/ppermute | solution.py:23
  108.2 3.1 %copy-start.6 = (bf16[1,4,640,256]{3,2,1,0:T(8,128)(2,1)}, bf16[1,4,640,256]{3,2,1,0:T(8,128)(2,1)S(1)}, u32[]{:S(2)}) copy-start(bf16[1,4,640,256]{3,2,1,0:T(8,128)(2,1)S(1)} %collective-permute-done.2.refs_6_) | copy-start | bytes 3932164
  108.2 24.6 %collective-permute-start.8 = (bf16[336,256]{1,0:T(8,128)(2,1)}, bf16[336,256]{1,0:T(8,128)(2,1)S(1)}, u32[]{:S(2)}, u32[]{:S(2)}) collective-permute-start(bf16[336,256]{1,0:T(8,128)(2,1)} %get-tuple-element.87), channel_id=1, source_target_pairs={{0,4},{1,5},{2,6},{3,7},{4,0},{5,1},{6,2},{7,3},{8,12},{9,13},{10,... | collective-permute-start | bytes 516104 | tf_op jit(solution)/shard_map/b4/ppermute | solution.py:23
  120.5 14.9 %collective-permute-start.24 = (bf16[336,256]{1,0:T(8,128)(2,1)S(1)}, bf16[336,256]{1,0:T(8,128)(2,1)S(1)}, u32[]{:S(2)}, u32[]{:S(2)}) collective-permute-start(bf16[336,256]{1,0:T(8,128)(2,1)S(1)} %copy-done.13), channel_id=1, source_target_pairs={{0,3},{1,2},{2,1},{3,0},{4,7},{5,6},{6,5},{7,4},{8,11},{9,10},{10,... | collective-permute-start | bytes 516104 | tf_op jit(solution)/shard_map/b3/ppermute | solution.py:23
  124.6 20.9 %collective-permute-start.23 = (bf16[336,256]{1,0:T(8,128)(2,1)S(1)}, bf16[336,256]{1,0:T(8,128)(2,1)S(1)}, u32[]{:S(2)}, u32[]{:S(2)}) collective-permute-start(bf16[336,256]{1,0:T(8,128)(2,1)S(1)} %copy-done.12), channel_id=1, source_target_pairs={{0,2},{1,3},{2,0},{3,1},{4,6},{5,7},{6,4},{7,5},{8,10},{9,11},{10,... | collective-permute-start | bytes 516104 | tf_op jit(solution)/shard_map/b2/ppermute | solution.py:23
  130.1 15.4 %collective-permute-start.22 = (bf16[336,256]{1,0:T(8,128)(2,1)S(1)}, bf16[336,256]{1,0:T(8,128)(2,1)S(1)}, u32[]{:S(2)}, u32[]{:S(2)}) collective-permute-start(bf16[336,256]{1,0:T(8,128)(2,1)S(1)} %copy-done.11), channel_id=1, source_target_pairs={{0,1},{1,0},{2,3},{3,2},{4,5},{5,4},{6,7},{7,6},{8,9},{9,8},{10,11... | collective-permute-start | bytes 516104 | tf_op jit(solution)/shard_map/b1/ppermute | solution.py:23
  131.9 13.6 %collective-permute-start.21 = (bf16[336,256]{1,0:T(8,128)(2,1)}, bf16[336,256]{1,0:T(8,128)(2,1)S(1)}, u32[]{:S(2)}, u32[]{:S(2)}) collective-permute-start(bf16[336,256]{1,0:T(8,128)(2,1)} %get-tuple-element.109), channel_id=1, source_target_pairs={{0,7},{1,6},{2,5},{3,4},{4,3},{5,2},{6,1},{7,0},{8,15},{9,14},{10,... | collective-permute-start | bytes 516104 | tf_op jit(solution)/shard_map/c7/ppermute | solution.py:23
  132.8 13.0 %collective-permute-start.17 = (bf16[336,256]{1,0:T(8,128)(2,1)}, bf16[336,256]{1,0:T(8,128)(2,1)S(1)}, u32[]{:S(2)}, u32[]{:S(2)}) collective-permute-start(bf16[336,256]{1,0:T(8,128)(2,1)} %get-tuple-element.102), channel_id=1, source_target_pairs={{0,6},{1,7},{2,4},{3,5},{4,2},{5,3},{6,0},{7,1},{8,14},{9,15},{10,... | collective-permute-start | bytes 516104 | tf_op jit(solution)/shard_map/c6/ppermute | solution.py:23
  135.4 24.0 %collective-permute-start.13 = (bf16[336,256]{1,0:T(8,128)(2,1)}, bf16[336,256]{1,0:T(8,128)(2,1)S(1)}, u32[]{:S(2)}, u32[]{:S(2)}) collective-permute-start(bf16[336,256]{1,0:T(8,128)(2,1)} %get-tuple-element.95), channel_id=1, source_target_pairs={{0,5},{1,4},{2,7},{3,6},{4,1},{5,0},{6,3},{7,2},{8,13},{9,12},{10,... | collective-permute-start | bytes 516104 | tf_op jit(solution)/shard_map/c5/ppermute | solution.py:23
  145.6 18.1 %collective-permute-start.9 = (bf16[336,256]{1,0:T(8,128)(2,1)}, bf16[336,256]{1,0:T(8,128)(2,1)S(1)}, u32[]{:S(2)}, u32[]{:S(2)}) collective-permute-start(bf16[336,256]{1,0:T(8,128)(2,1)} %get-tuple-element.88), channel_id=1, source_target_pairs={{0,4},{1,5},{2,6},{3,7},{4,0},{5,1},{6,2},{7,3},{8,12},{9,13},{10,... | collective-permute-start | bytes 516104 | tf_op jit(solution)/shard_map/c4/ppermute | solution.py:23
  145.6 18.1 %collective-permute-start.5 = (bf16[336,256]{1,0:T(8,128)(2,1)}, bf16[336,256]{1,0:T(8,128)(2,1)S(1)}, u32[]{:S(2)}, u32[]{:S(2)}) collective-permute-start(bf16[336,256]{1,0:T(8,128)(2,1)} %get-tuple-element.76), channel_id=1, source_target_pairs={{0,3},{1,2},{2,1},{3,0},{4,7},{5,6},{6,5},{7,4},{8,11},{9,10},{10,... | collective-permute-start | bytes 516104 | tf_op jit(solution)/shard_map/c3/ppermute | solution.py:23
  145.6 18.1 %collective-permute-start.4 = (bf16[336,256]{1,0:T(8,128)(2,1)}, bf16[336,256]{1,0:T(8,128)(2,1)S(1)}, u32[]{:S(2)}, u32[]{:S(2)}) collective-permute-start(bf16[336,256]{1,0:T(8,128)(2,1)} %get-tuple-element.74), channel_id=1, source_target_pairs={{0,2},{1,3},{2,0},{3,1},{4,6},{5,7},{6,4},{7,5},{8,10},{9,11},{10,... | collective-permute-start | bytes 516104 | tf_op jit(solution)/shard_map/c2/ppermute | solution.py:23
  145.9 17.8 %collective-permute-start.3 = (bf16[336,256]{1,0:T(8,128)(2,1)}, bf16[336,256]{1,0:T(8,128)(2,1)S(1)}, u32[]{:S(2)}, u32[]{:S(2)}) collective-permute-start(bf16[336,256]{1,0:T(8,128)(2,1)} %get-tuple-element.72), channel_id=1, source_target_pairs={{0,1},{1,0},{2,3},{3,2},{4,5},{5,4},{6,7},{7,6},{8,9},{9,8},{10,11... | collective-permute-start | bytes 516104 | tf_op jit(solution)/shard_map/c1/ppermute | solution.py:23
  153.3 3.6 %copy-start.1 = (bf16[336,256]{1,0:T(8,128)(2,1)S(1)}, bf16[336,256]{1,0:T(8,128)(2,1)}, u32[]{:S(2)}) copy-start(bf16[336,256]{1,0:T(8,128)(2,1)} %get-tuple-element.110.refs_0_) | copy-start | bytes 516100
  156.9 6.7 %copy-start.2 = (bf16[336,256]{1,0:T(8,128)(2,1)S(1)}, bf16[336,256]{1,0:T(8,128)(2,1)}, u32[]{:S(2)}) copy-start(bf16[336,256]{1,0:T(8,128)(2,1)} %get-tuple-element.70.refs_0_) | copy-start | bytes 516100

commit v7 on v6

--- a/solution.py
+++ b/solution.py
@@ -48,7 +48,7 @@
 def conv_kernel(plan, clip_ref, *refs):
     jobs, plains, parts, part_rows, part_width = (
         plan["jobs"], plan["plains"], plan["parts"], plan["part_rows"], plan["part_width"])
-    leads, steps, sources, taps = plan["leads"], plan["steps"], plan["sources"], plan["taps"]
+    layout, steps, sources, taps = plan["layout"], plan["steps"], plan["sources"], plan["taps"]
 
     def take(number):
         nonlocal refs
@@ -66,8 +66,8 @@
     slab_refs, main_refs, left_refs = take(sources), take(len(works)), take(len(works))
     part_ref, stat_ref, closing_ref, part_sem, tail_sem = refs
     step = pl.program_id(0)
-    ci = x_refs[0].shape[3]
-    half, co = main_refs[0].shape
+    ci = plan["ci"]
+    half, co = plan["half"], plan["co"]
     above = lax.rem(step + 1, 2)
     below = lax.rem(step, 2)
     start = lax.axis_index("tm") * plan["count"]
@@ -87,7 +87,7 @@
         return [
             pltpu.make_async_copy(
                 part_ref.at[slot, at, mine ^ flip],
-                out.at[pl.ds(pl.multiple_of(leads[flip] + place, 16), part_rows)],
+                out.at[pl.ds(pl.multiple_of(layout[flip][1] + place, 16), part_rows)],
                 part_sem.at[slot, at, flip])
             for flip, out in enumerate(out_refs)
         ]
@@ -110,7 +110,7 @@
         split_columns(x_refs[source].at[0, 0], slab_refs[source].at[2])
         split_columns(x_refs[source].at[0, 1], slab_refs[source].at[below])
         frame = plan["first"] + source
-        for at, (target, pairs, addend) in enumerate(works):
+        for at, (target, pairs, _) in enumerate(works):
             for tap in [tap for other, tap in pairs if other == source]:
                 main, left = products(source, tap)
                 if frame != target:
@@ -118,8 +118,6 @@
                     same = same.astype(jnp.float32)
                     main, left = main * same, left * same
                 if empty[at]:
-                    if addend is not None:
-                        main = main + add_refs[addend][0].astype(jnp.float32)
                     main_refs[at][...] = main
                     left_refs[at][8:] = left
                 else:
@@ -127,10 +125,12 @@
                     left_refs[at][8:] += left
                 empty[at] = False
 
-    for at in range(len(works)):
-        total = main_refs[at][...] + left_refs[at][7 : 7 + half]
+    for at, (_, pairs, added) in enumerate(works):
+        total = main_refs[at][...] + left_refs[at][7 : 7 + half] if pairs else 0.0
+        for addend in added:
+            total = total + add_refs[addend][0].astype(jnp.float32)
         if at >= len(jobs):
-            plain_refs[at - len(jobs)][0] = total.astype(jnp.bfloat16)
+            plain_refs[at - len(jobs)][0] = total.astype(plain_refs[0].dtype)
             continue
         rounded = total.astype(jnp.bfloat16).astype(jnp.float32)
         tiles = rounded.reshape(half // 8, 8, co)
@@ -167,7 +167,8 @@
             blank = jnp.zeros((STAT_ROWS - len(rows), co), jnp.float32)
             closing_ref[...] = jnp.concatenate(rows + [blank], axis=0).astype(jnp.bfloat16)
             closing = [
-                pltpu.make_async_copy(closing_ref, out.at[0:STAT_ROWS], tail_sem.at[flip])
+                pltpu.make_async_copy(
+                    closing_ref, out.at[layout[flip][0] : layout[flip][0] + STAT_ROWS], tail_sem.at[flip])
                 for flip, out in enumerate(out_refs)
             ]
         for copy in closing:
@@ -181,7 +182,8 @@
 
 
 def conv_frames(frames, halo, weight, clip_ids, parts, first, sources, jobs, plains=(), row=0,
-                steps=None, addends=(), sums=(), sums_out=False, leads=(), kept=None, weigh=1, vmem=56):
+                steps=None, addends=(), sums=(), sums_out=False, layout=None, kept=None, exact=False,
+                weigh=1, vmem=56):
     _, band, width, ci = frames.shape
     co = weight.shape[2]
     half = width // 2
@@ -190,13 +192,13 @@
     part_rows = rounded_up(part_width)
     works = list(jobs) + list(plains)
     kept = kept or {}
-    leads = leads or [STAT_ROWS] * parts
     messages = parts if jobs else 0
     taps = sorted({tap for _, pairs, _ in works for _, tap in pairs})
     plan = dict(jobs=list(jobs), plains=list(plains), addends=len(addends), parts=messages,
-                part_rows=part_rows, leads=list(leads), part_width=part_width, first=first,
+                part_rows=part_rows, layout=layout, part_width=part_width, first=first,
                 steps=steps, kept=len(kept), sums_in=len(sums), sums_out=sums_out, sources=sources, taps=taps,
-                count=frames.shape[0])
+                count=frames.shape[0],
+                half=half, co=co, ci=ci)
     above, above_row = (frames, 2 * row - 1) if row else (halo, 0)
     plain_spec = pl.BlockSpec((1, None, half, co), lambda i, *_: (0, row + i, 0, 0))
     frame_spec = lambda source: pl.BlockSpec((1, 2, width, ci), lambda i, *_: (source, row + i, 0, 0))
@@ -211,11 +213,10 @@
     operands = [clip_ids, *[frames] * sources, *[above] * sources, *[weight] * len(taps),
                 *addends, *sums, *kept.values()]
     aliases = {len(operands) - len(kept) + at: flip for at, flip in enumerate(kept)}
-    rows = len(jobs) * steps * part_rows
-    out_shape = [jax.ShapeDtypeStruct(kept[flip].shape if flip in kept else (leads[flip] + rows, co),
-                                      jnp.bfloat16) for flip in range(messages)]
+    out_shape = [jax.ShapeDtypeStruct((layout[flip][2], co), jnp.bfloat16) for flip in range(messages)]
     out_specs = [pl.BlockSpec(memory_space=pl.ANY) for _ in range(messages)]
-    out_shape += [jax.ShapeDtypeStruct((1, band // 2, half, co), jnp.bfloat16) for _ in plains]
+    plain_type = jnp.float32 if exact else jnp.bfloat16
+    out_shape += [jax.ShapeDtypeStruct((1, band // 2, half, co), plain_type) for _ in plains]
     out_specs += [plain_spec for _ in plains]
     if sums_out:
         shape = (2 * len(jobs), 8, co)
@@ -253,7 +254,7 @@
 
 def norm_kernel(plan, *refs):
     parts, jobs, steps, rows = plan["parts"], plan["jobs"], plan["steps"], plan["rows"]
-    part_rows, apart = plan["part_rows"], plan["apart"]
+    part_rows, apart, bases = plan["part_rows"], plan["apart"], plan["bases"]
     data_refs, rest_refs = refs[:parts], refs[parts : parts + len(apart)]
     gain_ref, bias_ref = refs[parts + len(apart) : parts + len(apart) + 2]
     out_ref, done_ref, scale_ref = refs[-3:]
@@ -263,9 +264,9 @@
     @pl.when((frame == 0) & (step == 0))
     def _():
         scale_ref[...] = jnp.zeros_like(scale_ref)
-        total = data_refs[0][0:STAT_ROWS].astype(jnp.float32)
-        for flip in range(1, parts):
-            total = total + data_refs[flip][0:STAT_ROWS].astype(jnp.float32)
+        total = 0.0
+        for flip, base in enumerate(bases):
+            total = total + data_refs[flip][base : base + STAT_ROWS].astype(jnp.float32)
         size = co // GROUPS
         same = (lax.broadcasted_iota(jnp.int32, (co, co), 0) // size
                 == lax.broadcasted_iota(jnp.int32, (co, co), 1) // size).astype(jnp.float32)
@@ -296,7 +297,7 @@
         row = step * rows + at
         for flip in range(parts):
             if not plan["top_first"]:
-                write(flip, at, data_refs[flip], STAT_ROWS + (frame * steps + row) * part_rows)
+                write(flip, at, data_refs[flip], bases[flip] + STAT_ROWS + (frame * steps + row) * part_rows)
                 continue
             rest, base = data_refs[flip], top_rows
             if flip in apart:
@@ -315,12 +316,13 @@
                 write(flip, 0, rest, below)
 
 
-def norm_frames(messages, gain, bias, first, jobs, shape, top_first=False, rest=None, base=None,
-                vmem=20):
+def norm_frames(messages, gain, bias, first, jobs, shape, top_first=False, rest=None, bases=None,
+                base=None, vmem=20):
     frames, parts, steps, part_width, co = shape
     rows = 2 if steps % 2 == 0 else 1
     rest = rest or {}
     plan = dict(parts=parts, jobs=jobs, steps=steps, rows=rows, apart=list(rest),
+                bases=bases or [0] * parts,
                 part_rows=rounded_up(part_width), top_first=top_first,
                 entries=float(parts * steps * part_width * parts * (co // GROUPS)))
     in_specs = (
@@ -366,6 +368,8 @@
     shape = (count, parts, steps, width // 2 // parts, co)
     part_rows = rounded_up(shape[3])
     top_rows = STAT_ROWS + 2 * part_rows
+    all_rows = top_rows + 2 * (steps - 1) * part_rows
+    one_rows = STAT_ROWS + steps * part_rows
 
     def named(name, function, *args, **keywords):
         with jax.named_scope(name):
@@ -386,39 +390,57 @@
             chain.append(got[flip])
         return got
 
-    def send_near(name, sent, *earlier):
-        return {flip: named(f"{name}{flip}", exchanged, after(sent[flip], *earlier), "rows", flip)
-                for flip in near}
+    def send_near(name, sent, single, *earlier):
+        got = {}
+        for flip in near:
+            got[flip] = named(f"{name}{flip}", exchanged, after(sent[flip], *earlier), "rows", flip)
+            if single:
+                earlier = (got[flip],)
+        return got
+
+    def layout(far_one, near_one):
+        return [far_one if flip in far else near_one for flip in range(parts)]
 
     halo = named("halo", passed_along, frames[:, -1:], "rows", 1)
     run = functools.partial(conv_frames, frames, halo, weight, clip_ids, parts)
-    later = [(2, [(0, 0), (1, 1), (2, 2)], None), (3, [(1, 0), (2, 1), (3, 2)], None)]
-    leads = [0 if flip in far else top_rows for flip in range(parts)]
-    *a_sent, a_sums = named("conv_a", run, 0, 4, later, row=1, steps=steps - 1, sums_out=True,
-                            leads=leads, vmem=56)
+    later = [(2, [(0, 0), (1, 1), (2, 2)], ()), (3, [(1, 0), (2, 1), (3, 2)], ())]
+    near_rows = all_rows + one_rows
+    *a_sent, a_sums = named(
+        "conv_a", run, 0, 4, later, row=1, steps=steps - 1, sums_out=True, vmem=56,
+        layout=layout((0, 0, all_rows - top_rows), (0, top_rows, near_rows)))
     a_got = send_far("a", a_sent)
     run = functools.partial(conv_frames, frames, after(halo, a_sums), weight, clip_ids, parts)
-    ahead, = named("conv_hist0", run, 2, 2, [], [(4, [(0, 0), (1, 1)], None)], vmem=56)
+    ahead, = named("conv_hist0", run, 2, 2, [], [(4, [(0, 0), (1, 1)], ())], vmem=56)
     first_add = named("hist0", passed_along, ahead, "tm", 1)
     run = functools.partial(conv_frames, frames, after(halo, ahead), weight, clip_ids, parts)
+    own = named("conv_own", run, 0, 2, [], [(0, [(0, 2)], ()), (1, [(0, 1), (1, 2)], ())],
+                exact=True, weigh=20, vmem=56)
+    run = functools.partial(conv_frames, frames, after(halo, ahead, *own), weight, clip_ids, parts)
     kept = {flip: a_sent[flip] for flip in range(parts) if flip not in far}
-    t_sent = named("conv_top", run, 0, 4, later, steps=1, sums=(a_sums,), kept=kept, weigh=20, vmem=56)
+    t_sent = named(
+        "conv_top", run, 0, 4, later, steps=1, sums=(a_sums,), kept=kept, weigh=20, vmem=56,
+        layout=layout((0, STAT_ROWS, top_rows), (0, STAT_ROWS, near_rows)))
     t_got = send_far("t", t_sent)
-    run = functools.partial(conv_frames, frames, after(halo, ahead), weight, clip_ids, parts)
-    onward, = named("conv_hist1", run, 3, 1, [], [(5, [(0, 0)], None)], weigh=20, vmem=56)
-    second_add = named("hist1", passed_along, after(onward, first_add), "tm", 1)
-    b_sent = named("conv_b", run, 0, 1, [(0, [(0, 2)], 0)], addends=(after(first_add, a_sums),),
-                   weigh=20, vmem=56)
+    run = functools.partial(conv_frames, frames, after(halo, t_sent[0]), weight, clip_ids, parts)
+    onward, = named("conv_hist1", run, 3, 1, [], [(5, [(0, 0)], ())], weigh=20, vmem=56)
+    second_add = named("hist1", passed_along, after(onward, first_add, *a_got.values()), "tm", 1)
+    kept = {flip: t_sent[flip] for flip in range(parts) if flip not in far}
+    b_sent = named(
+        "add_b", run, 0, 0, [(0, [], (0, 1))], addends=(own[0], after(first_add, a_sums)), kept=kept,
+        weigh=20, vmem=56,
+        layout=layout((0, STAT_ROWS, one_rows), (all_rows, all_rows + STAT_ROWS, near_rows)))
     b_got = send_far("b", b_sent)
-    c_sent = named("conv_c", run, 0, 2, [(1, [(0, 1), (1, 2)], 0)], addends=(second_add,),
-                   weigh=20, vmem=56)
+    b_got.update(send_near("tb", b_sent, False, b_sent[0]))
+    c_sent = named(
+        "add_c", run, 0, 0, [(1, [], (0, 1))], addends=(own[1], after(second_add, a_sums)),
+        weigh=20, vmem=56, layout=[(0, STAT_ROWS, one_rows)] * parts)
     c_got = send_far("c", c_sent)
-    t_got.update(send_near("t", t_sent, t_got[far[0]]))
-    b_got.update(send_near("b", b_sent, c_sent[0]))
-    c_got.update(send_near("c", c_sent, c_sent[0]))
-    out, _ = named("norm_a", norm_frames, whole(t_sent, t_got), gain, bias, 2, 2, shape, top_first=True,
-                   rest=a_got, vmem=20)
-    out, _ = named("norm_b", norm_frames, whole(b_sent, b_got), gain, bias, 0, 1, shape, base=out, vmem=20)
+    c_got.update(send_near("c", c_sent, False))
+    both = whole(b_sent, b_got)
+    tops = [t_got[flip] if flip in far else both[flip] for flip in range(parts)]
+    out, _ = named("norm_a", norm_frames, tops, gain, bias, 2, 2, shape, top_first=True, rest=a_got, vmem=20)
+    out, _ = named("norm_b", norm_frames, both, gain, bias, 0, 1, shape, base=out, vmem=20,
+                   bases=layout(0, all_rows))
     out, _ = named("norm_c", norm_frames, whole(c_sent, c_got), gain, bias, 1, 1, shape, base=out, vmem=20)
     return out.reshape(count, parts * steps, shape[3], co)
 

time: 168 us -> 172 us (1.024)
  waiting for transfers between devices: 58.6 us -> 40.9 us
  starting transfers between devices: 42.7 us -> 58.1 us
  Pallas kernels: 61.7 us -> 67 us
    ppermute x25 -> x22, starting transfers between devices: 34.8 us -> 50.2 us  [exchanged(): return lax.ppermute(array, axis, [(i, i ^ flip) for i in range(length)])]
    ppermute x3, waiting for transfers between devices: 13.2 us -> 2.86 us  [passed_along(): return lax.ppermute(array, axis, pairs)]
    ppermute x25 -> x22, waiting for transfers between devices: 45.4 us -> 38 us  [exchanged(): return lax.ppermute(array, axis, [(i, i ^ flip) for i in range(length)])]
    pallas_call x6 -> x7, Pallas kernels: 53.7 us -> 57.8 us  [conv_frames(): pl.pallas_call(functools.partial(conv_kernel, plan), out_shape=out_shape,...]
  transfers between devices with their start and end apart: 28 -> 25, of which waited for: 9 -> 12; matrix products, arithmetic and copies ran while one was open for 0% -> 0% of each run, Pallas kernels for 36% -> 38%
where the time goes in v7:
time: 172 us; the launch traced here: 170 us
  Pallas kernels  67 us (39%)
  starting transfers between devices  58.1 us (34%)
  waiting for transfers between devices  40.9 us (24%)
  local copies, waits for them, and re-layouts  3.38 us (2%)
    pallas_call x7, Pallas kernels, conv_frames(): pl.pallas_call(functools.partial(conv_kernel, plan), out_shape=out_shape,...  57.8 us
    ppermute x22, starting transfers between devices, exchanged(): return lax.ppermute(array, axis, [(i, i ^ flip) for i in range(length)])  50.2 us
    ppermute x22, waiting for transfers between devices, exchanged(): return lax.ppermute(array, axis, [(i, i ^ flip) for i in range(length)])  38 us
    pallas_call x3, Pallas kernels, norm_frames(): pl.pallas_call(functools.partial(norm_kernel, plan), out_shape=[jax.Shape...  9.23 us
    ppermute x3, starting transfers between devices, passed_along(): return lax.ppermute(array, axis, pairs)  7.9 us
  transfers between devices with their start and end apart: 25, of which 12 were waited for; matrix products, arithmetic and copies ran while one was open for 0% of the time, Pallas kernels for 38%

profile of v7, /device:TPU:4, one launch (start us, length us, event | category | flops | bytes accessed | tf_op | source)
XLA Modules:
  0.0 169.5 jit_solution(17008470710018659016)
XLA Ops:
  0.0 1.4 slice.3
  1.4 1.8 %collective-permute-start = (bf16[4,1,1280,128]{3,2,1,0:T(8,128)(2,1)S(1)}, bf16[4,1,1280,128]{3,2,1,0:T(8,128)(2,1)S(1)}, u32[]{:S(2)}, u32[]{:S(2)}) collective-permute-start(bf16[4,1,1280,128]{3,2,1,0:T(8,128)(2,1)S(1)} %slice.3), channel_id=1, source_target_pairs={{0,1},{1,2},{2,3},{3,4},{4,5},{5,6},{6,7},{8,9},{9,10},{10,11},{11... | collective-permute-start | bytes 3932168 | tf_op jit(solution)/shard_map/halo/ppermute | solution.py:18
  3.2 15.2 %conv_a.1 = (bf16[992,256]{1,0:T(8,128)(2,1)}, bf16[992,256]{1,0:T(8,128)(2,1)}, bf16[992,256]{1,0:T(8,128)(2,1)}, bf16[992,256]{1,0:T(8,128)(2,1)}, bf16[480,25...) custom-call(s32[16]{0:T(128)} %clip_ref.13, ...), custom_call_target="tpu_custom_call" | custom-call | flops 6794772480 | bytes 9830400 | tf_op jit(solution)/shard_map/conv_a/pallas_call | solution.py:226
  18.5 2.6 %collective-permute-start.2 = (bf16[480,256]{1,0:T(8,128)(2,1)}, bf16[480,256]{1,0:T(8,128)(2,1)}, u32[]{:S(2)}, u32[]{:S(2)}) collective-permute-start(bf16[480,256]{1,0:T(8,128)(2,1)} %get-tuple-element.77), channel_id=1, source_target_pairs={{0,7},{1,6},{2,5},{3,4},{4,3},{5,2},{6,1},{7,0},{8,15},{9,14},{10,... | collective-permute-start | bytes 737288 | tf_op jit(solution)/shard_map/a7/ppermute | solution.py:23
  21.1 2.7 %collective-permute-start.3 = (bf16[480,256]{1,0:T(8,128)(2,1)}, bf16[480,256]{1,0:T(8,128)(2,1)}, u32[]{:S(2)}, u32[]{:S(2)}) collective-permute-start(bf16[480,256]{1,0:T(8,128)(2,1)} %get-tuple-element.78), channel_id=1, source_target_pairs={{0,6},{1,7},{2,4},{3,5},{4,2},{5,3},{6,0},{7,1},{8,14},{9,15},{10,... | collective-permute-start | bytes 737288 | tf_op jit(solution)/shard_map/a6/ppermute | solution.py:23
  23.8 0.0 collective-permute-start.4
  23.8 1.1 collective-permute-start.5
  24.9 0.0 collective-permute-done.refs_2_.refs_3_.refs_4_.refs_5_.refs_6_.refs_7_.refs_1_
  24.9 1.1 copy-done.4
  26.0 8.5 %conv_hist0.1 = bf16[1,4,640,256]{3,2,1,0:T(8,128)(2,1)} custom-call(s32[16]{0:T(128)} %clip_ref.13, bf16[4,8,1280,128]{3,2,1,0:T(8,128)(2,1)} %refs_0_.9, bf16[4,8,1280,128]{3,2,1,0:T(8,128)(2,1)} %refs_0_.9, bf16[4,1,1280,128]{3,2,1,0:T(8,128)(2,1)} %copy-done.4, bf16[4,1,1280,128]{3,2,1,0:T(8,128)(2,1)} %copy-done.4, bf16[3,1152,256]{2,1,0:T(8,128)(2,1)} %bitcast.13, ...), custom_call_target="tpu_custom_call" | custom-call | flops 3019898880 | bytes 6553600 | tf_op jit(solution)/shard_map/conv_hist0/pallas_call | solution.py:226
  34.5 3.4 %collective-permute-start.1 = (bf16[1,4,640,256]{3,2,1,0:T(8,128)(2,1)}, bf16[1,4,640,256]{3,2,1,0:T(8,128)(2,1)}, u32[]{:S(2)}, u32[]{:S(2)}) collective-permute-start(bf16[1,4,640,256]{3,2,1,0:T(8,128)(2,1)} %conv_hist0.1), channel_id=1, source_target_pairs={{0,8},{8,16},{16,24},{1,9},{9,17},{17,25},{2,10},{10,18},{18,26},{... | collective-permute-start | bytes 3932168 | tf_op jit(solution)/shard_map/hist0/ppermute | solution.py:18
  37.9 10.1 %conv_own.1 = (f32[1,4,640,256]{3,2,1,0:T(8,128)}, f32[1,4,640,256]{3,2,1,0:T(8,128)}) custom-call(s32[16]{0:T(128)} %clip_ref.13, bf16[4,8,1280,128]{3,2,1,0:T(8,128)(2,1)} %refs_0_.9, bf16[4,8,1280,128]{3,2,1,0:T(8,128)(2,1)} %refs_0_.9, bf16[4,1,1280,128]{3,2,1,0:T(8,128)(2,1)} %copy-done.4, bf16[4,1,1280,128]{3,2,1,0:T(8,128)(2,1)} %copy-done.4, ...), custom_call_target="tpu_custom_call" | custom-call | flops 90596966400 | bytes 157286400 | tf_op jit(solution)/shard_map/conv_own/pallas_call | solution.py:226
  48.0 7.2 %conv_top.1 = (bf16[992,256]{1,0:T(8,128)(2,1)}, bf16[992,256]{1,0:T(8,128)(2,1)}, bf16[992,256]{1,0:T(8,128)(2,1)}, bf16[992,256]{1,0:T(8,128)(2,1)}, bf16[176,...) custom-call(s32[16]{0:T(128)} %clip_ref.13, ...), custom_call_target="tpu_custom_call", output_to_operand_aliasing={{0}: (13, {}), {1}: (14, {}), {2}: (15, {}), {3}: (16, {})} | custom-call | flops 45298483200 | bytes 65536000 | tf_op jit(solution)/shard_map/conv_top/pallas_call | solution.py:226
  55.2 6.5 %conv_hist1.1 = bf16[1,4,640,256]{3,2,1,0:T(8,128)(2,1)} custom-call(s32[16]{0:T(128)} %clip_ref.13, bf16[4,8,1280,128]{3,2,1,0:T(8,128)(2,1)} %refs_0_.9, bf16[4,1,1280,128]{3,2,1,0:T(8,128)(2,1)} %copy-done.4, bf16[3,1152,256]{2,1,0:T(8,128)(2,1)} %bitcast.20), custom_call_target="tpu_custom_call" | custom-call | flops 30198988800 | bytes 78643200 | tf_op jit(solution)/shard_map/conv_hist1/pallas_call | solution.py:226
  61.7 0.0 collective-permute-done.2.refs_8_
  61.8 0.0 collective-permute-done.3.refs_9_
  61.8 0.0 collective-permute-done.4.refs_10_
  61.8 4.0 %collective-permute-done.5.refs_11_ = bf16[480,256]{1,0:T(8,128)(2,1)} collective-permute-done((bf16[480,256]{1,0:T(8,128)(2,1)}, bf16[480,256]{1,0:T(8,128)(2,1)}, u32[]{:S(2)}, u32[]{:S(2)}) %collective-permute-start.5) | collective-permute-done | bytes 245792 | tf_op jit(solution)/shard_map/a4/ppermute | solution.py:23
  65.8 2.9 %collective-permute-done.1.refs_1_ = bf16[1,4,640,256]{3,2,1,0:T(8,128)(2,1)} collective-permute-done((bf16[1,4,640,256]{3,2,1,0:T(8,128)(2,1)}, bf16[1,4,640,256]{3,2,1,0:T(8,128)(2,1)}, u32[]{:S(2)}, u32[]{:S(2)}) %collective-permute-start.1) | collective-permute-done | bytes 1310752 | tf_op jit(solution)/shard_map/hist0/ppermute | solution.py:18
  68.6 2.7 %collective-permute-start.6 = (bf16[1,4,640,256]{3,2,1,0:T(8,128)(2,1)}, bf16[1,4,640,256]{3,2,1,0:T(8,128)(2,1)S(1)}, u32[]{:S(2)}, u32[]{:S(2)}) collective-permute-start(bf16[1,4,640,256]{3,2,1,0:T(8,128)(2,1)} %conv_hist1.1), channel_id=1, source_target_pairs={{0,8},{8,16},{16,24},{1,9},{9,17},{17,25},{2,10},{10,18},{18,26},{... | collective-permute-start | bytes 3932168 | tf_op jit(solution)/shard_map/hist1/ppermute | solution.py:18
  71.3 2.4 %collective-permute-start.16 = (bf16[176,256]{1,0:T(8,128)(2,1)S(1)}, bf16[176,256]{1,0:T(8,128)(2,1)S(1)}, u32[]{:S(2)}, u32[]{:S(2)}) collective-permute-start(bf16[176,256]{1,0:T(8,128)(2,1)S(1)} %copy-done.9), channel_id=1, source_target_pairs={{0,6},{1,7},{2,4},{3,5},{4,2},{5,3},{6,0},{7,1},{8,14},{9,15},{10,... | collective-permute-start | bytes 270344 | tf_op jit(solution)/shard_map/t6/ppermute | solution.py:23
  73.8 5.2 %add_b.1 = (bf16[992,256]{1,0:T(8,128)(2,1)}, bf16[992,256]{1,0:T(8,128)(2,1)}, bf16[992,256]{1,0:T(8,128)(2,1)}, bf16[992,256]{1,0:T(8,128)(2,1)}, bf16[336,256...) custom-call(s32[16]{0:T(128)} %clip_ref.13, ...), custom_call_target="tpu_custom_call", output_to_operand_aliasing={{0}: (3, {}), {1}: (4, {}), {2}: (5, {}), {3}: (6, {})} | custom-call | bytes 26214400 | tf_op jit(solution)/shard_map/add_b/pallas_call | solution.py:226
  78.9 0.0 collective-permute-done.16.refs_6_
  79.0 1.5 collective-permute-start.17
  80.5 0.0 collective-permute-start.19
  80.5 0.4 collective-permute-start.13
  80.9 4.6 %collective-permute-start.10 = (bf16[176,256]{1,0:T(8,128)(2,1)S(1)}, bf16[176,256]{1,0:T(8,128)(2,1)S(1)}, u32[]{:S(2)}, u32[]{:S(2)}) collective-permute-start(bf16[176,256]{1,0:T(8,128)(2,1)S(1)} %copy-done.6), channel_id=1, source_target_pairs={{0,4},{1,5},{2,6},{3,7},{4,0},{5,1},{6,2},{7,3},{8,12},{9,13},{10,... | collective-permute-start | bytes 270344 | tf_op jit(solution)/shard_map/t4/ppermute | solution.py:23
  85.5 1.8 %collective-permute-done.19.refs_7_ = bf16[176,256]{1,0:T(8,128)(2,1)S(1)} collective-permute-done((bf16[176,256]{1,0:T(8,128)(2,1)S(1)}, bf16[176,256]{1,0:T(8,128)(2,1)S(1)}, u32[]{:S(2)}, u32[]{:S(2)}) %collective-permute-start.19) | collective-permute-done | bytes 90144 | tf_op jit(solution)/shard_map/t7/ppermute | solution.py:23
  87.3 3.8 %collective-permute-start.20 = (bf16[336,256]{1,0:T(8,128)(2,1)}, bf16[336,256]{1,0:T(8,128)(2,1)S(1)}, u32[]{:S(2)}, u32[]{:S(2)}) collective-permute-start(bf16[336,256]{1,0:T(8,128)(2,1)} %get-tuple-element.113), channel_id=1, source_target_pairs={{0,7},{1,6},{2,5},{3,4},{4,3},{5,2},{6,1},{7,0},{8,15},{9,14},{10,... | collective-permute-start | bytes 516104 | tf_op jit(solution)/shard_map/b7/ppermute | solution.py:23
  91.1 9.1 %collective-permute-done.13.refs_5_ = bf16[176,256]{1,0:T(8,128)(2,1)S(1)} collective-permute-done((bf16[176,256]{1,0:T(8,128)(2,1)S(1)}, bf16[176,256]{1,0:T(8,128)(2,1)S(1)}, u32[]{:S(2)}, u32[]{:S(2)}) %collective-permute-start.13) | collective-permute-done | bytes 90144 | tf_op jit(solution)/shard_map/t5/ppermute | solution.py:23
  100.2 0.9 collective-permute-start.24
  101.1 3.6 %collective-permute-done.10.refs_4_ = bf16[176,256]{1,0:T(8,128)(2,1)S(1)} collective-permute-done((bf16[176,256]{1,0:T(8,128)(2,1)S(1)}, bf16[176,256]{1,0:T(8,128)(2,1)S(1)}, u32[]{:S(2)}, u32[]{:S(2)}) %collective-permute-start.10) | collective-permute-done | bytes 90144 | tf_op jit(solution)/shard_map/t4/ppermute | solution.py:23
  104.7 0.0 collective-permute-start.23
  104.7 0.0 collective-permute-done.17.refs_6_
  104.7 0.0 collective-permute-start.22
  104.7 0.0 copy-start.2
  104.7 0.0 copy-start.3
  104.7 0.0 collective-permute-done.20.refs_7_
  104.7 2.6 %collective-permute-start.11 = (bf16[336,256]{1,0:T(8,128)(2,1)}, bf16[336,256]{1,0:T(8,128)(2,1)S(1)}, u32[]{:S(2)}, u32[]{:S(2)}) collective-permute-start(bf16[336,256]{1,0:T(8,128)(2,1)} %get-tuple-element.95), channel_id=1, source_target_pairs={{0,4},{1,5},{2,6},{3,7},{4,0},{5,1},{6,2},{7,3},{8,12},{9,13},{10,... | collective-permute-start | bytes 516104 | tf_op jit(solution)/shard_map/b4/ppermute | solution.py:23
  107.3 0.0 collective-permute-done.6.refs_1_
  107.3 0.2 collective-permute-start.14
  107.5 0.8 copy-done.5
  108.4 5.1 %add_c.1 = (bf16[336,256]{1,0:T(8,128)(2,1)}, bf16[336,256]{1,0:T(8,128)(2,1)}, bf16[336,256]{1,0:T(8,128)(2,1)}, bf16[336,256]{1,0:T(8,128)(2,1)}, bf16[336,256...) custom-call(s32[16]{0:T(128)} %clip_ref.13, ...), custom_call_target="tpu_custom_call" | custom-call | bytes 26214400 | tf_op jit(solution)/shard_map/add_c/pallas_call | solution.py:226
  113.4 13.4 %collective-permute-done.11.refs_4_ = bf16[336,256]{1,0:T(8,128)(2,1)S(1)} collective-permute-done((bf16[336,256]{1,0:T(8,128)(2,1)}, bf16[336,256]{1,0:T(8,128)(2,1)S(1)}, u32[]{:S(2)}, u32[]{:S(2)}) %collective-permute-start.11) | collective-permute-done | bytes 172064 | tf_op jit(solution)/shard_map/b4/ppermute | solution.py:23
  126.9 3.2 %collective-permute-start.21 = (bf16[336,256]{1,0:T(8,128)(2,1)}, bf16[336,256]{1,0:T(8,128)(2,1)S(1)}, u32[]{:S(2)}, u32[]{:S(2)}) collective-permute-start(bf16[336,256]{1,0:T(8,128)(2,1)} %get-tuple-element.114), channel_id=1, source_target_pairs={{0,7},{1,6},{2,5},{3,4},{4,3},{5,2},{6,1},{7,0},{8,15},{9,14},{10,... | collective-permute-start | bytes 516104 | tf_op jit(solution)/shard_map/c7/ppermute | solution.py:23
  130.0 0.5 collective-permute-done.14.refs_5_
  130.6 2.0 %collective-permute-start.18 = (bf16[336,256]{1,0:T(8,128)(2,1)}, bf16[336,256]{1,0:T(8,128)(2,1)S(1)}, u32[]{:S(2)}, u32[]{:S(2)}) collective-permute-start(bf16[336,256]{1,0:T(8,128)(2,1)} %get-tuple-element.108), channel_id=1, source_target_pairs={{0,6},{1,7},{2,4},{3,5},{4,2},{5,3},{6,0},{7,1},{8,14},{9,15},{10,... | collective-permute-start | bytes 516104 | tf_op jit(solution)/shard_map/c6/ppermute | solution.py:23
  132.6 0.0 collective-permute-done.24.refs_3_
  132.6 1.0 collective-permute-start.15
  133.6 0.4 collective-permute-done.23.refs_2_
  134.0 1.2 collective-permute-start.12
  135.2 0.1 collective-permute-start.7
  135.4 0.2 collective-permute-done.21.refs_7_
  135.5 16.4 %collective-permute-start.8 = (bf16[336,256]{1,0:T(8,128)(2,1)}, bf16[336,256]{1,0:T(8,128)(2,1)S(1)}, u32[]{:S(2)}, u32[]{:S(2)}) collective-permute-start(bf16[336,256]{1,0:T(8,128)(2,1)} %get-tuple-element.85), channel_id=1, source_target_pairs={{0,2},{1,3},{2,0},{3,1},{4,6},{5,7},{6,4},{7,5},{8,10},{9,11},{10,... | collective-permute-start | bytes 516104 | tf_op jit(solution)/shard_map/c2/ppermute | solution.py:23
  152.0 0.0 collective-permute-done.18.refs_6_
  152.0 3.4 %collective-permute-start.9 = (bf16[336,256]{1,0:T(8,128)(2,1)}, bf16[336,256]{1,0:T(8,128)(2,1)S(1)}, u32[]{:S(2)}, u32[]{:S(2)}) collective-permute-start(bf16[336,256]{1,0:T(8,128)(2,1)} %get-tuple-element.86), channel_id=1, source_target_pairs={{0,3},{1,2},{2,1},{3,0},{4,7},{5,6},{6,5},{7,4},{8,11},{9,10},{10,... | collective-permute-start | bytes 516104 | tf_op jit(solution)/shard_map/c3/ppermute | solution.py:23
  155.4 4.9 %norm_a.1 = (bf16[4,8,4,80,256]{4,3,2,1,0:T(8,128)(2,1)}, f32[8,256]{1,0:T(8,128)}) custom-call(bf16[992,256]{1,0:T(8,128)(2,1)S(1)} %copy-done, bf16[992,256]{1,0:T(8,128)(2,1)S(1)} %collective-permute-done.22.refs_1_, bf16[992,256]{1,0:T(8,128)(2,1)S(1)} %collective-permute-done.23.refs_2_, bf16[992,256]{1,0:T(8,128)(2,1)S(1)} %collective-permute-done.24.refs_3_, ...), custom_call_target="tpu_custom_call" | custom-call | flops 10485760 | bytes 5242880 | tf_op jit(solution)/shard_map/norm_a/pallas_call | solution.py:338
  160.3 2.1 %norm_b.1 = (bf16[4,8,4,80,256]{4,3,2,1,0:T(8,128)(2,1)}, f32[8,256]{1,0:T(8,128)}) custom-call(bf16[992,256]{1,0:T(8,128)(2,1)S(1)} %copy-done, bf16[992,256]{1,0:T(8,128)(2,1)S(1)} %collective-permute-done.22.refs_1_, bf16[992,256]{1,0:T(8,128)(2,1)S(1)} %collective-permute-done.23.refs_2_, ...), custom_call_target="tpu_custom_call", output_to_operand_aliasing={{0}: (10, {})} | custom-call | flops 5242880 | bytes 2621440 | tf_op jit(solution)/shard_map/norm_b/pallas_call | solution.py:338
  162.5 0.0 collective-permute-done.15.refs_5_
  162.5 0.2 collective-permute-done.12.refs_4_
  162.6 0.0 collective-permute-done.7.refs_1_
  162.7 2.1 %collective-permute-done.8.refs_2_ = bf16[336,256]{1,0:T(8,128)(2,1)S(1)} collective-permute-done((bf16[336,256]{1,0:T(8,128)(2,1)}, bf16[336,256]{1,0:T(8,128)(2,1)S(1)}, u32[]{:S(2)}, u32[]{:S(2)}) %collective-permute-start.8) | collective-permute-done | bytes 172064 | tf_op jit(solution)/shard_map/c2/ppermute | solution.py:23
  164.7 2.7 %collective-permute-done.9.refs_3_ = bf16[336,256]{1,0:T(8,128)(2,1)S(1)} collective-permute-done((bf16[336,256]{1,0:T(8,128)(2,1)}, bf16[336,256]{1,0:T(8,128)(2,1)S(1)}, u32[]{:S(2)}, u32[]{:S(2)}) %collective-permute-start.9) | collective-permute-done | bytes 172064 | tf_op jit(solution)/shard_map/c3/ppermute | solution.py:23
  167.4 2.1 %norm_c.1 = (bf16[4,8,4,80,256]{4,3,2,1,0:T(8,128)(2,1)}, f32[8,256]{1,0:T(8,128)}) custom-call(bf16[336,256]{1,0:T(8,128)(2,1)S(1)} %copy-done.1, bf16[336,256]{1,0:T(8,128)(2,1)S(1)} %collective-permute-done.7.refs_1_, bf16[336,256]{1,0:T(8,128)(2,1)S(1)} %collective-permute-done.8.refs_2_, ...), custom_call_target="tpu_custom_call", output_to_operand_aliasing={{0}: (10, {})} | custom-call | flops 5242880 | bytes 2621440 | tf_op jit(solution)/shard_map/norm_c/pallas_call | solution.py:338
  (17 shorter events, 0.0 us)
Async XLA Ops:
  1.4 23.5 %collective-permute-start = (bf16[4,1,1280,128]{3,2,1,0:T(8,128)(2,1)S(1)}, bf16[4,1,1280,128]{3,2,1,0:T(8,128)(2,1)S(1)}, u32[]{:S(2)}, u32[]{:S(2)}) collective-permute-start(bf16[4,1,1280,128]{3,2,1,0:T(8,128)(2,1)S(1)} %slice.3), channel_id=1, source_target_pairs={{0,1},{1,2},{2,3},{3,4},{4,5},{5,6},{6,7},{8,9},{9,10},{10,11},{11... | collective-permute-start | bytes 3932168 | tf_op jit(solution)/shard_map/halo/ppermute | solution.py:18
  18.5 43.3 %collective-permute-start.2 = (bf16[480,256]{1,0:T(8,128)(2,1)}, bf16[480,256]{1,0:T(8,128)(2,1)}, u32[]{:S(2)}, u32[]{:S(2)}) collective-permute-start(bf16[480,256]{1,0:T(8,128)(2,1)} %get-tuple-element.77), channel_id=1, source_target_pairs={{0,7},{1,6},{2,5},{3,4},{4,3},{5,2},{6,1},{7,0},{8,15},{9,14},{10,... | collective-permute-start | bytes 737288 | tf_op jit(solution)/shard_map/a7/ppermute | solution.py:23
  21.1 40.7 %collective-permute-start.3 = (bf16[480,256]{1,0:T(8,128)(2,1)}, bf16[480,256]{1,0:T(8,128)(2,1)}, u32[]{:S(2)}, u32[]{:S(2)}) collective-permute-start(bf16[480,256]{1,0:T(8,128)(2,1)} %get-tuple-element.78), channel_id=1, source_target_pairs={{0,6},{1,7},{2,4},{3,5},{4,2},{5,3},{6,0},{7,1},{8,14},{9,15},{10,... | collective-permute-start | bytes 737288 | tf_op jit(solution)/shard_map/a6/ppermute | solution.py:23
  23.8 38.0 %collective-permute-start.4 = (bf16[480,256]{1,0:T(8,128)(2,1)}, bf16[480,256]{1,0:T(8,128)(2,1)}, u32[]{:S(2)}, u32[]{:S(2)}) collective-permute-start(bf16[480,256]{1,0:T(8,128)(2,1)} %get-tuple-element.79), channel_id=1, source_target_pairs={{0,5},{1,4},{2,7},{3,6},{4,1},{5,0},{6,3},{7,2},{8,13},{9,12},{10,... | collective-permute-start | bytes 737288 | tf_op jit(solution)/shard_map/a5/ppermute | solution.py:23
  23.8 42.0 %collective-permute-start.5 = (bf16[480,256]{1,0:T(8,128)(2,1)}, bf16[480,256]{1,0:T(8,128)(2,1)}, u32[]{:S(2)}, u32[]{:S(2)}) collective-permute-start(bf16[480,256]{1,0:T(8,128)(2,1)} %get-tuple-element.80), channel_id=1, source_target_pairs={{0,4},{1,5},{2,6},{3,7},{4,0},{5,1},{6,2},{7,3},{8,12},{9,13},{10,... | collective-permute-start | bytes 737288 | tf_op jit(solution)/shard_map/a4/ppermute | solution.py:23
  24.9 1.1 copy-start.4
  34.5 34.2 %collective-permute-start.1 = (bf16[1,4,640,256]{3,2,1,0:T(8,128)(2,1)}, bf16[1,4,640,256]{3,2,1,0:T(8,128)(2,1)}, u32[]{:S(2)}, u32[]{:S(2)}) collective-permute-start(bf16[1,4,640,256]{3,2,1,0:T(8,128)(2,1)} %conv_hist0.1), channel_id=1, source_target_pairs={{0,8},{8,16},{16,24},{1,9},{9,17},{17,25},{2,10},{10,18},{18,26},{... | collective-permute-start | bytes 3932168 | tf_op jit(solution)/shard_map/hist0/ppermute | solution.py:18
  55.2 16.1 %copy-start.9 = (bf16[176,256]{1,0:T(8,128)(2,1)S(1)}, bf16[176,256]{1,0:T(8,128)(2,1)}, u32[]{:S(2)}) copy-start(bf16[176,256]{1,0:T(8,128)(2,1)} %get-tuple-element.106) | copy-start | bytes 270340
  68.6 38.7 %collective-permute-start.6 = (bf16[1,4,640,256]{3,2,1,0:T(8,128)(2,1)}, bf16[1,4,640,256]{3,2,1,0:T(8,128)(2,1)S(1)}, u32[]{:S(2)}, u32[]{:S(2)}) collective-permute-start(bf16[1,4,640,256]{3,2,1,0:T(8,128)(2,1)} %conv_hist1.1), channel_id=1, source_target_pairs={{0,8},{8,16},{16,24},{1,9},{9,17},{17,25},{2,10},{10,18},{18,26},{... | collective-permute-start | bytes 3932168 | tf_op jit(solution)/shard_map/hist1/ppermute | solution.py:18
  71.3 7.6 %collective-permute-start.16 = (bf16[176,256]{1,0:T(8,128)(2,1)S(1)}, bf16[176,256]{1,0:T(8,128)(2,1)S(1)}, u32[]{:S(2)}, u32[]{:S(2)}) collective-permute-start(bf16[176,256]{1,0:T(8,128)(2,1)S(1)} %copy-done.9), channel_id=1, source_target_pairs={{0,6},{1,7},{2,4},{3,5},{4,2},{5,3},{6,0},{7,1},{8,14},{9,15},{10,... | collective-permute-start | bytes 270344 | tf_op jit(solution)/shard_map/t6/ppermute | solution.py:23
  73.8 6.7 %copy-start.8 = (bf16[176,256]{1,0:T(8,128)(2,1)S(1)}, bf16[176,256]{1,0:T(8,128)(2,1)}, u32[]{:S(2)}) copy-start(bf16[176,256]{1,0:T(8,128)(2,1)} %get-tuple-element.112) | copy-start | bytes 270340
  73.8 6.7 %copy-start.7 = (bf16[176,256]{1,0:T(8,128)(2,1)S(1)}, bf16[176,256]{1,0:T(8,128)(2,1)}, u32[]{:S(2)}) copy-start(bf16[176,256]{1,0:T(8,128)(2,1)} %get-tuple-element.100) | copy-start | bytes 270340
  73.8 7.1 %copy-start.6 = (bf16[176,256]{1,0:T(8,128)(2,1)S(1)}, bf16[176,256]{1,0:T(8,128)(2,1)}, u32[]{:S(2)}) copy-start(bf16[176,256]{1,0:T(8,128)(2,1)} %get-tuple-element.94) | copy-start | bytes 270340
  79.0 25.7 %collective-permute-start.17 = (bf16[336,256]{1,0:T(8,128)(2,1)}, bf16[336,256]{1,0:T(8,128)(2,1)S(1)}, u32[]{:S(2)}, u32[]{:S(2)}) collective-permute-start(bf16[336,256]{1,0:T(8,128)(2,1)} %get-tuple-element.107), channel_id=1, source_target_pairs={{0,6},{1,7},{2,4},{3,5},{4,2},{5,3},{6,0},{7,1},{8,14},{9,15},{10,... | collective-permute-start | bytes 516104 | tf_op jit(solution)/shard_map/b6/ppermute | solution.py:23
  80.5 6.8 %collective-permute-start.19 = (bf16[176,256]{1,0:T(8,128)(2,1)S(1)}, bf16[176,256]{1,0:T(8,128)(2,1)S(1)}, u32[]{:S(2)}, u32[]{:S(2)}) collective-permute-start(bf16[176,256]{1,0:T(8,128)(2,1)S(1)} %copy-done.8), channel_id=1, source_target_pairs={{0,7},{1,6},{2,5},{3,4},{4,3},{5,2},{6,1},{7,0},{8,15},{9,14},{10,... | collective-permute-start | bytes 270344 | tf_op jit(solution)/shard_map/t7/ppermute | solution.py:23
  80.5 19.7 %collective-permute-start.13 = (bf16[176,256]{1,0:T(8,128)(2,1)S(1)}, bf16[176,256]{1,0:T(8,128)(2,1)S(1)}, u32[]{:S(2)}, u32[]{:S(2)}) collective-permute-start(bf16[176,256]{1,0:T(8,128)(2,1)S(1)} %copy-done.7), channel_id=1, source_target_pairs={{0,5},{1,4},{2,7},{3,6},{4,1},{5,0},{6,3},{7,2},{8,13},{9,12},{10,... | collective-permute-start | bytes 270344 | tf_op jit(solution)/shard_map/t5/ppermute | solution.py:23
  80.9 23.8 %collective-permute-start.10 = (bf16[176,256]{1,0:T(8,128)(2,1)S(1)}, bf16[176,256]{1,0:T(8,128)(2,1)S(1)}, u32[]{:S(2)}, u32[]{:S(2)}) collective-permute-start(bf16[176,256]{1,0:T(8,128)(2,1)S(1)} %copy-done.6), channel_id=1, source_target_pairs={{0,4},{1,5},{2,6},{3,7},{4,0},{5,1},{6,2},{7,3},{8,12},{9,13},{10,... | collective-permute-start | bytes 270344 | tf_op jit(solution)/shard_map/t4/ppermute | solution.py:23
  87.3 17.4 %collective-permute-start.20 = (bf16[336,256]{1,0:T(8,128)(2,1)}, bf16[336,256]{1,0:T(8,128)(2,1)S(1)}, u32[]{:S(2)}, u32[]{:S(2)}) collective-permute-start(bf16[336,256]{1,0:T(8,128)(2,1)} %get-tuple-element.113), channel_id=1, source_target_pairs={{0,7},{1,6},{2,5},{3,4},{4,3},{5,2},{6,1},{7,0},{8,15},{9,14},{10,... | collective-permute-start | bytes 516104 | tf_op jit(solution)/shard_map/b7/ppermute | solution.py:23
  100.2 32.3 %collective-permute-start.24 = (bf16[992,256]{1,0:T(8,128)(2,1)}, bf16[992,256]{1,0:T(8,128)(2,1)S(1)}, u32[]{:S(2)}, u32[]{:S(2)}) collective-permute-start(bf16[992,256]{1,0:T(8,128)(2,1)} %get-tuple-element.121), channel_id=1, source_target_pairs={{0,3},{1,2},{2,1},{3,0},{4,7},{5,6},{6,5},{7,4},{8,11},{9,10},{10,... | collective-permute-start | bytes 1523720 | tf_op jit(solution)/shard_map/tb3/ppermute | solution.py:23
  104.7 29.3 %collective-permute-start.23 = (bf16[992,256]{1,0:T(8,128)(2,1)}, bf16[992,256]{1,0:T(8,128)(2,1)S(1)}, u32[]{:S(2)}, u32[]{:S(2)}) collective-permute-start(bf16[992,256]{1,0:T(8,128)(2,1)} %get-tuple-element.119), channel_id=1, source_target_pairs={{0,2},{1,3},{2,0},{3,1},{4,6},{5,7},{6,4},{7,5},{8,10},{9,11},{10,... | collective-permute-start | bytes 1523720 | tf_op jit(solution)/shard_map/tb2/ppermute | solution.py:23
  104.7 30.5 %collective-permute-start.22 = (bf16[992,256]{1,0:T(8,128)(2,1)}, bf16[992,256]{1,0:T(8,128)(2,1)S(1)}, u32[]{:S(2)}, u32[]{:S(2)}) collective-permute-start(bf16[992,256]{1,0:T(8,128)(2,1)} %get-tuple-element.117), channel_id=1, source_target_pairs={{0,1},{1,0},{2,3},{3,2},{4,5},{5,4},{6,7},{7,6},{8,9},{9,8},{10,11... | collective-permute-start | bytes 1523720 | tf_op jit(solution)/shard_map/tb1/ppermute | solution.py:23
  104.7 50.7 %copy-start = (bf16[992,256]{1,0:T(8,128)(2,1)S(1)}, bf16[992,256]{1,0:T(8,128)(2,1)}, u32[]{:S(2)}) copy-start(bf16[992,256]{1,0:T(8,128)(2,1)} %get-tuple-element.115.refs_0_) | copy-start | bytes 1523716
  104.7 50.7 %copy-start.2 = (f32[256]{0:T(256)S(1)}, f32[256]{0:T(256)}, u32[]{:S(2)}) copy-start(f32[256]{0:T(256)} %param.8) | copy-start | bytes 3076
  104.7 50.7 %copy-start.3 = (f32[256]{0:T(256)S(1)}, f32[256]{0:T(256)}, u32[]{:S(2)}) copy-start(f32[256]{0:T(256)} %param.9) | copy-start | bytes 3076
  104.7 22.1 %collective-permute-start.11 = (bf16[336,256]{1,0:T(8,128)(2,1)}, bf16[336,256]{1,0:T(8,128)(2,1)S(1)}, u32[]{:S(2)}, u32[]{:S(2)}) collective-permute-start(bf16[336,256]{1,0:T(8,128)(2,1)} %get-tuple-element.95), channel_id=1, source_target_pairs={{0,4},{1,5},{2,6},{3,7},{4,0},{5,1},{6,2},{7,3},{8,12},{9,13},{10,... | collective-permute-start | bytes 516104 | tf_op jit(solution)/shard_map/b4/ppermute | solution.py:23
  107.3 1.1 copy-start.5
  107.3 23.3 %collective-permute-start.14 = (bf16[336,256]{1,0:T(8,128)(2,1)}, bf16[336,256]{1,0:T(8,128)(2,1)S(1)}, u32[]{:S(2)}, u32[]{:S(2)}) collective-permute-start(bf16[336,256]{1,0:T(8,128)(2,1)} %get-tuple-element.101), channel_id=1, source_target_pairs={{0,5},{1,4},{2,7},{3,6},{4,1},{5,0},{6,3},{7,2},{8,13},{9,12},{10,... | collective-permute-start | bytes 516104 | tf_op jit(solution)/shard_map/b5/ppermute | solution.py:23
  126.9 8.7 %collective-permute-start.21 = (bf16[336,256]{1,0:T(8,128)(2,1)}, bf16[336,256]{1,0:T(8,128)(2,1)S(1)}, u32[]{:S(2)}, u32[]{:S(2)}) collective-permute-start(bf16[336,256]{1,0:T(8,128)(2,1)} %get-tuple-element.114), channel_id=1, source_target_pairs={{0,7},{1,6},{2,5},{3,4},{4,3},{5,2},{6,1},{7,0},{8,15},{9,14},{10,... | collective-permute-start | bytes 516104 | tf_op jit(solution)/shard_map/c7/ppermute | solution.py:23
  130.6 21.4 %collective-permute-start.18 = (bf16[336,256]{1,0:T(8,128)(2,1)}, bf16[336,256]{1,0:T(8,128)(2,1)S(1)}, u32[]{:S(2)}, u32[]{:S(2)}) collective-permute-start(bf16[336,256]{1,0:T(8,128)(2,1)} %get-tuple-element.108), channel_id=1, source_target_pairs={{0,6},{1,7},{2,4},{3,5},{4,2},{5,3},{6,0},{7,1},{8,14},{9,15},{10,... | collective-permute-start | bytes 516104 | tf_op jit(solution)/shard_map/c6/ppermute | solution.py:23
  132.6 29.9 %collective-permute-start.15 = (bf16[336,256]{1,0:T(8,128)(2,1)}, bf16[336,256]{1,0:T(8,128)(2,1)S(1)}, u32[]{:S(2)}, u32[]{:S(2)}) collective-permute-start(bf16[336,256]{1,0:T(8,128)(2,1)} %get-tuple-element.102), channel_id=1, source_target_pairs={{0,5},{1,4},{2,7},{3,6},{4,1},{5,0},{6,3},{7,2},{8,13},{9,12},{10,... | collective-permute-start | bytes 516104 | tf_op jit(solution)/shard_map/c5/ppermute | solution.py:23
  134.0 28.7 %collective-permute-start.12 = (bf16[336,256]{1,0:T(8,128)(2,1)}, bf16[336,256]{1,0:T(8,128)(2,1)S(1)}, u32[]{:S(2)}, u32[]{:S(2)}) collective-permute-start(bf16[336,256]{1,0:T(8,128)(2,1)} %get-tuple-element.96), channel_id=1, source_target_pairs={{0,4},{1,5},{2,6},{3,7},{4,0},{5,1},{6,2},{7,3},{8,12},{9,13},{10,... | collective-permute-start | bytes 516104 | tf_op jit(solution)/shard_map/c4/ppermute | solution.py:23
  135.2 27.4 %collective-permute-start.7 = (bf16[336,256]{1,0:T(8,128)(2,1)}, bf16[336,256]{1,0:T(8,128)(2,1)S(1)}, u32[]{:S(2)}, u32[]{:S(2)}) collective-permute-start(bf16[336,256]{1,0:T(8,128)(2,1)} %get-tuple-element.84), channel_id=1, source_target_pairs={{0,1},{1,0},{2,3},{3,2},{4,5},{5,4},{6,7},{7,6},{8,9},{9,8},{10,11... | collective-permute-start | bytes 516104 | tf_op jit(solution)/shard_map/c1/ppermute | solution.py:23
  135.5 29.2 %collective-permute-start.8 = (bf16[336,256]{1,0:T(8,128)(2,1)}, bf16[336,256]{1,0:T(8,128)(2,1)S(1)}, u32[]{:S(2)}, u32[]{:S(2)}) collective-permute-start(bf16[336,256]{1,0:T(8,128)(2,1)} %get-tuple-element.85), channel_id=1, source_target_pairs={{0,2},{1,3},{2,0},{3,1},{4,6},{5,7},{6,4},{7,5},{8,10},{9,11},{10,... | collective-permute-start | bytes 516104 | tf_op jit(solution)/shard_map/c2/ppermute | solution.py:23
  152.0 15.4 %collective-permute-start.9 = (bf16[336,256]{1,0:T(8,128)(2,1)}, bf16[336,256]{1,0:T(8,128)(2,1)S(1)}, u32[]{:S(2)}, u32[]{:S(2)}) collective-permute-start(bf16[336,256]{1,0:T(8,128)(2,1)} %get-tuple-element.86), channel_id=1, source_target_pairs={{0,3},{1,2},{2,1},{3,0},{4,7},{5,6},{6,5},{7,4},{8,11},{9,10},{10,... | collective-permute-start | bytes 516104 | tf_op jit(solution)/shard_map/c3/ppermute | solution.py:23
  160.3 7.0 %copy-start.1 = (bf16[336,256]{1,0:T(8,128)(2,1)S(1)}, bf16[336,256]{1,0:T(8,128)(2,1)}, u32[]{:S(2)}) copy-start(bf16[336,256]{1,0:T(8,128)(2,1)} %get-tuple-element.83.refs_0_) | copy-start | bytes 516100

commit v8 on v7

--- a/solution.py
+++ b/solution.py
@@ -385,7 +385,7 @@
     def send_far(name, sent):
         got = {}
         for flip in far:
-            before = chain[-4:][:1] if len(chain) >= 4 else []
+            before = chain[-3:][:1] if len(chain) >= 3 else []
             got[flip] = named(f"{name}{flip}", exchanged, after(sent[flip], *before), "rows", flip)
             chain.append(got[flip])
         return got
@@ -404,43 +404,56 @@
     halo = named("halo", passed_along, frames[:, -1:], "rows", 1)
     run = functools.partial(conv_frames, frames, halo, weight, clip_ids, parts)
     later = [(2, [(0, 0), (1, 1), (2, 2)], ()), (3, [(1, 0), (2, 1), (3, 2)], ())]
-    near_rows = all_rows + one_rows
+    near_rows = top_rows + one_rows
     *a_sent, a_sums = named(
         "conv_a", run, 0, 4, later, row=1, steps=steps - 1, sums_out=True, vmem=56,
-        layout=layout((0, 0, all_rows - top_rows), (0, top_rows, near_rows)))
-    a_got = send_far("a", a_sent)
+        layout=[(0, 0, all_rows - top_rows)] * parts)
+    held = {}
+    a_got = {}
+
+    def send_one(got, name, sent, flip, *earlier):
+        got[flip] = named(f"{name}{flip}", exchanged, after(sent[flip], *earlier), "rows", flip)
+
+    for flip in far[:3]:
+        send_one(a_got, "a", a_sent, flip)
+    send_one(a_got, "a", a_sent, near[0])
     run = functools.partial(conv_frames, frames, after(halo, a_sums), weight, clip_ids, parts)
-    ahead, = named("conv_hist0", run, 2, 2, [], [(4, [(0, 0), (1, 1)], ())], vmem=56)
+    ahead, = named("conv_hist0", run, 2, 2, [], [(4, [(0, 0), (1, 1)], ())], weigh=1, vmem=56)
+    send_one(a_got, "a", a_sent, near[1], ahead, a_got[near[0]])
     first_add = named("hist0", passed_along, ahead, "tm", 1)
-    run = functools.partial(conv_frames, frames, after(halo, ahead), weight, clip_ids, parts)
+    run = functools.partial(conv_frames, frames, after(halo, ahead, a_got[near[0]]), weight, clip_ids, parts)
     own = named("conv_own", run, 0, 2, [], [(0, [(0, 2)], ()), (1, [(0, 1), (1, 2)], ())],
                 exact=True, weigh=20, vmem=56)
-    run = functools.partial(conv_frames, frames, after(halo, ahead, *own), weight, clip_ids, parts)
-    kept = {flip: a_sent[flip] for flip in range(parts) if flip not in far}
+    for at, flip in enumerate(near[2:]):
+        send_one(a_got, "a", a_sent, flip, own[0], a_got[near[at + 1]])
+    for at, flip in enumerate(far[3:]):
+        send_one(a_got, "a", a_sent, flip, own[0], a_got[far[at]])
+    chain += [a_got[flip] for flip in far]
+    run = functools.partial(conv_frames, frames, after(halo, *own, a_got[near[1]]), weight, clip_ids, parts)
     t_sent = named(
-        "conv_top", run, 0, 4, later, steps=1, sums=(a_sums,), kept=kept, weigh=20, vmem=56,
+        "conv_top", run, 0, 4, later, steps=1, sums=(a_sums,), weigh=20, vmem=56,
         layout=layout((0, STAT_ROWS, top_rows), (0, STAT_ROWS, near_rows)))
     t_got = send_far("t", t_sent)
-    run = functools.partial(conv_frames, frames, after(halo, t_sent[0]), weight, clip_ids, parts)
+    run = functools.partial(conv_frames, frames, after(halo, t_sent[0], a_got[near[2]]), weight, clip_ids, parts)
     onward, = named("conv_hist1", run, 3, 1, [], [(5, [(0, 0)], ())], weigh=20, vmem=56)
-    second_add = named("hist1", passed_along, after(onward, first_add, *a_got.values()), "tm", 1)
+    second_add = named("hist1", passed_along, after(onward, first_add, *[a_got[flip] for flip in far]), "tm", 1)
     kept = {flip: t_sent[flip] for flip in range(parts) if flip not in far}
     b_sent = named(
-        "add_b", run, 0, 0, [(0, [], (0, 1))], addends=(own[0], after(first_add, a_sums)), kept=kept,
+        "add_b", run, 0, 0, [(0, [], (0, 1))], addends=(own[0], after(first_add, t_got[far[0]], t_got[far[1]], t_got[far[2]])), kept=kept,
         weigh=20, vmem=56,
-        layout=layout((0, STAT_ROWS, one_rows), (all_rows, all_rows + STAT_ROWS, near_rows)))
+        layout=layout((0, STAT_ROWS, one_rows), (top_rows, top_rows + STAT_ROWS, near_rows)))
     b_got = send_far("b", b_sent)
-    b_got.update(send_near("tb", b_sent, False, b_sent[0]))
+    b_got.update(send_near("tb", b_sent, False, t_got[far[-1]]))
     c_sent = named(
-        "add_c", run, 0, 0, [(1, [], (0, 1))], addends=(own[1], after(second_add, a_sums)),
+        "add_c", run, 0, 0, [(1, [], (0, 1))], addends=(own[1], after(second_add, b_got[near[0]], b_got[near[1]])),
         weigh=20, vmem=56, layout=[(0, STAT_ROWS, one_rows)] * parts)
     c_got = send_far("c", c_sent)
     c_got.update(send_near("c", c_sent, False))
     both = whole(b_sent, b_got)
     tops = [t_got[flip] if flip in far else both[flip] for flip in range(parts)]
-    out, _ = named("norm_a", norm_frames, tops, gain, bias, 2, 2, shape, top_first=True, rest=a_got, vmem=20)
+    out, _ = named("norm_a", norm_frames, tops, gain, bias, 2, 2, shape, top_first=True, rest=dict(enumerate(whole(a_sent, a_got))), vmem=20)
     out, _ = named("norm_b", norm_frames, both, gain, bias, 0, 1, shape, base=out, vmem=20,
-                   bases=layout(0, all_rows))
+                   bases=layout(0, top_rows))
     out, _ = named("norm_c", norm_frames, whole(c_sent, c_got), gain, bias, 1, 1, shape, base=out, vmem=20)
     return out.reshape(count, parts * steps, shape[3], co)
 

time: 172 us -> 165 us (0.959)
  waiting for transfers between devices: 40.9 us -> 33.3 us
    ppermute x22 -> x25, waiting for transfers between devices: 38 us -> 32.4 us  [exchanged(): return lax.ppermute(array, axis, [(i, i ^ flip) for i in range(length)])]
    ppermute x3, waiting for transfers between devices: 2.86 us -> 0.86 us  [passed_along(): return lax.ppermute(array, axis, pairs)]
    ppermute x22 -> x25, starting transfers between devices: 50.2 us -> 49.7 us  [exchanged(): return lax.ppermute(array, axis, [(i, i ^ flip) for i in range(length)])]
  transfers between devices with their start and end apart: 25 -> 28, of which waited for: 12 -> 10; matrix products, arithmetic and copies ran while one was open for 0% -> 0% of each run, Pallas kernels for 38% -> 40%
where the time goes in v8:
time: 165 us; the launch traced here: 161 us
  Pallas kernels  66.6 us (40%)
  starting transfers between devices  57.6 us (35%)
  waiting for transfers between devices  33.3 us (20%)
  local copies, waits for them, and re-layouts  3.64 us (2%)
    pallas_call x7, Pallas kernels, conv_frames(): pl.pallas_call(functools.partial(conv_kernel, plan), out_shape=out_shape,...  57.6 us
    ppermute x25, starting transfers between devices, exchanged(): return lax.ppermute(array, axis, [(i, i ^ flip) for i in range(length)])  49.7 us
    ppermute x25, waiting for transfers between devices, exchanged(): return lax.ppermute(array, axis, [(i, i ^ flip) for i in range(length)])  32.4 us
    pallas_call x3, Pallas kernels, norm_frames(): pl.pallas_call(functools.partial(norm_kernel, plan), out_shape=[jax.Shape...  9 us
    ppermute x3, starting transfers between devices, passed_along(): return lax.ppermute(array, axis, pairs)  7.89 us
  transfers between devices with their start and end apart: 28, of which 10 were waited for; matrix products, arithmetic and copies ran while one was open for 0% of the time, Pallas kernels for 40%

profile of v8, /device:TPU:4, one launch (start us, length us, event | category | flops | bytes accessed | tf_op | source)
XLA Modules:
  0.0 161.4 jit_solution(6229690502644069177)
XLA Ops:
  0.0 1.4 slice.3
  1.4 1.8 %collective-permute-start = (bf16[4,1,1280,128]{3,2,1,0:T(8,128)(2,1)S(1)}, bf16[4,1,1280,128]{3,2,1,0:T(8,128)(2,1)S(1)}, u32[]{:S(2)}, u32[]{:S(2)}) collective-permute-start(bf16[4,1,1280,128]{3,2,1,0:T(8,128)(2,1)S(1)} %slice.3), channel_id=1, source_target_pairs={{0,1},{1,2},{2,3},{3,4},{4,5},{5,6},{6,7},{8,9},{9,10},{10,11},{11... | collective-permute-start | bytes 3932168 | tf_op jit(solution)/shard_map/halo/ppermute | solution.py:18
  3.2 15.2 %conv_a.1 = (bf16[480,256]{1,0:T(8,128)(2,1)}, bf16[480,256]{1,0:T(8,128)(2,1)}, bf16[480,256]{1,0:T(8,128)(2,1)}, bf16[480,256]{1,0:T(8,128)(2,1)}, bf16[480,25...) custom-call(s32[16]{0:T(128)} %clip_ref.13, ...), custom_call_target="tpu_custom_call" | custom-call | flops 6794772480 | bytes 9830400 | tf_op jit(solution)/shard_map/conv_a/pallas_call | solution.py:226
  18.4 1.8 %collective-permute-start.1 = (bf16[480,256]{1,0:T(8,128)(2,1)}, bf16[480,256]{1,0:T(8,128)(2,1)S(1)}, u32[]{:S(2)}, u32[]{:S(2)}) collective-permute-start(bf16[480,256]{1,0:T(8,128)(2,1)} %get-tuple-element.70), channel_id=1, source_target_pairs={{0,1},{1,0},{2,3},{3,2},{4,5},{5,4},{6,7},{7,6},{8,9},{9,8},{10,11... | collective-permute-start | bytes 737288 | tf_op jit(solution)/shard_map/a1/ppermute | solution.py:23
  20.3 2.1 %collective-permute-start.5 = (bf16[480,256]{1,0:T(8,128)(2,1)}, bf16[480,256]{1,0:T(8,128)(2,1)S(1)}, u32[]{:S(2)}, u32[]{:S(2)}) collective-permute-start(bf16[480,256]{1,0:T(8,128)(2,1)} %get-tuple-element.81), channel_id=1, source_target_pairs={{0,7},{1,6},{2,5},{3,4},{4,3},{5,2},{6,1},{7,0},{8,15},{9,14},{10,... | collective-permute-start | bytes 737288 | tf_op jit(solution)/shard_map/a7/ppermute | solution.py:23
  22.3 1.5 collective-permute-start.6
  23.8 0.6 collective-permute-start.7
  24.3 0.0 collective-permute-done.refs_2_.refs_3_.refs_4_.refs_5_.refs_6_.refs_7_.refs_1_
  24.3 1.1 copy-done.7
  25.5 8.6 %conv_hist0.1 = bf16[1,4,640,256]{3,2,1,0:T(8,128)(2,1)} custom-call(s32[16]{0:T(128)} %clip_ref.13, bf16[4,8,1280,128]{3,2,1,0:T(8,128)(2,1)} %refs_0_.9, bf16[4,8,1280,128]{3,2,1,0:T(8,128)(2,1)} %refs_0_.9, bf16[4,1,1280,128]{3,2,1,0:T(8,128)(2,1)} %copy-done.7, bf16[4,1,1280,128]{3,2,1,0:T(8,128)(2,1)} %copy-done.7, bf16[3,1152,256]{2,1,0:T(8,128)(2,1)} %bitcast.13, ...), custom_call_target="tpu_custom_call" | custom-call | flops 3019898880 | bytes 6553600 | tf_op jit(solution)/shard_map/conv_hist0/pallas_call | solution.py:226
  34.1 3.4 %collective-permute-start.4 = (bf16[1,4,640,256]{3,2,1,0:T(8,128)(2,1)}, bf16[1,4,640,256]{3,2,1,0:T(8,128)(2,1)}, u32[]{:S(2)}, u32[]{:S(2)}) collective-permute-start(bf16[1,4,640,256]{3,2,1,0:T(8,128)(2,1)} %conv_hist0.1), channel_id=1, source_target_pairs={{0,8},{8,16},{16,24},{1,9},{9,17},{17,25},{2,10},{10,18},{18,26},{... | collective-permute-start | bytes 3932168 | tf_op jit(solution)/shard_map/hist0/ppermute | solution.py:18
  37.5 0.0 collective-permute-done.1.refs_9_
  37.6 1.8 %collective-permute-start.2 = (bf16[480,256]{1,0:T(8,128)(2,1)S(1)}, bf16[480,256]{1,0:T(8,128)(2,1)S(1)}, u32[]{:S(2)}, u32[]{:S(2)}) collective-permute-start(bf16[480,256]{1,0:T(8,128)(2,1)S(1)} %copy-done.11), channel_id=1, source_target_pairs={{0,2},{1,3},{2,0},{3,1},{4,6},{5,7},{6,4},{7,5},{8,10},{9,11},{10,... | collective-permute-start | bytes 737288 | tf_op jit(solution)/shard_map/a2/ppermute | solution.py:23
  39.4 10.1 %conv_own.1 = (f32[1,4,640,256]{3,2,1,0:T(8,128)}, f32[1,4,640,256]{3,2,1,0:T(8,128)}) custom-call(s32[16]{0:T(128)} %clip_ref.13, bf16[4,8,1280,128]{3,2,1,0:T(8,128)(2,1)} %refs_0_.9, bf16[4,8,1280,128]{3,2,1,0:T(8,128)(2,1)} %refs_0_.9, bf16[4,1,1280,128]{3,2,1,0:T(8,128)(2,1)} %copy-done.7, bf16[4,1,1280,128]{3,2,1,0:T(8,128)(2,1)} %copy-done.7, ...), custom_call_target="tpu_custom_call" | custom-call | flops 90596966400 | bytes 157286400 | tf_op jit(solution)/shard_map/conv_own/pallas_call | solution.py:226
  49.5 0.0 collective-permute-done.5.refs_15_
  49.5 0.7 collective-permute-start.8
  50.2 0.0 collective-permute-done.2.refs_10_
  50.2 0.9 collective-permute-start.3
  51.1 7.2 %conv_top.1 = (bf16[512,256]{1,0:T(8,128)(2,1)}, bf16[512,256]{1,0:T(8,128)(2,1)}, bf16[512,256]{1,0:T(8,128)(2,1)}, bf16[512,256]{1,0:T(8,128)(2,1)}, bf16[176,...) custom-call(s32[16]{0:T(128)} %clip_ref.13, ...), custom_call_target="tpu_custom_call" | custom-call | flops 45298483200 | bytes 65536000 | tf_op jit(solution)/shard_map/conv_top/pallas_call | solution.py:226
  58.3 2.6 %collective-permute-done.3.refs_11_ = bf16[480,256]{1,0:T(8,128)(2,1)S(1)} collective-permute-done((bf16[480,256]{1,0:T(8,128)(2,1)S(1)}, bf16[480,256]{1,0:T(8,128)(2,1)S(1)}, u32[]{:S(2)}, u32[]{:S(2)}) %collective-permute-start.3) | collective-permute-done | bytes 245792 | tf_op jit(solution)/shard_map/a3/ppermute | solution.py:23
  60.8 6.5 %conv_hist1.1 = bf16[1,4,640,256]{3,2,1,0:T(8,128)(2,1)} custom-call(s32[16]{0:T(128)} %clip_ref.13, bf16[4,8,1280,128]{3,2,1,0:T(8,128)(2,1)} %refs_0_.9, bf16[4,1,1280,128]{3,2,1,0:T(8,128)(2,1)} %copy-done.7, bf16[3,1152,256]{2,1,0:T(8,128)(2,1)} %bitcast.20), custom_call_target="tpu_custom_call" | custom-call | flops 30198988800 | bytes 78643200 | tf_op jit(solution)/shard_map/conv_hist1/pallas_call | solution.py:226
  67.3 0.0 collective-permute-done.6.refs_14_
  67.4 0.0 collective-permute-done.7.refs_13_
  67.4 0.0 collective-permute-done.8.refs_12_
  67.4 0.9 collective-permute-done.4.refs_1_
  68.2 2.7 %collective-permute-start.9 = (bf16[1,4,640,256]{3,2,1,0:T(8,128)(2,1)}, bf16[1,4,640,256]{3,2,1,0:T(8,128)(2,1)S(1)}, u32[]{:S(2)}, u32[]{:S(2)}) collective-permute-start(bf16[1,4,640,256]{3,2,1,0:T(8,128)(2,1)} %conv_hist1.1), channel_id=1, source_target_pairs={{0,8},{8,16},{16,24},{1,9},{9,17},{17,25},{2,10},{10,18},{18,26},{... | collective-permute-start | bytes 3932168 | tf_op jit(solution)/shard_map/hist1/ppermute | solution.py:18
  70.9 7.1 %collective-permute-start.10 = (bf16[176,256]{1,0:T(8,128)(2,1)S(1)}, bf16[176,256]{1,0:T(8,128)(2,1)S(1)}, u32[]{:S(2)}, u32[]{:S(2)}) collective-permute-start(bf16[176,256]{1,0:T(8,128)(2,1)S(1)} %copy-done.15), channel_id=1, source_target_pairs={{0,7},{1,6},{2,5},{3,4},{4,3},{5,2},{6,1},{7,0},{8,15},{9,14},{10,... | collective-permute-start | bytes 270344 | tf_op jit(solution)/shard_map/t7/ppermute | solution.py:23
  78.1 0.0 collective-permute-start.12
  78.1 1.1 collective-permute-start.11
  79.1 1.9 %collective-permute-done.10.refs_7_ = bf16[176,256]{1,0:T(8,128)(2,1)S(1)} collective-permute-done((bf16[176,256]{1,0:T(8,128)(2,1)S(1)}, bf16[176,256]{1,0:T(8,128)(2,1)S(1)}, u32[]{:S(2)}, u32[]{:S(2)}) %collective-permute-start.10) | collective-permute-done | bytes 90144 | tf_op jit(solution)/shard_map/t7/ppermute | solution.py:23
  81.1 0.0 collective-permute-start.13
  81.1 7.9 %collective-permute-done.12.refs_5_ = bf16[176,256]{1,0:T(8,128)(2,1)S(1)} collective-permute-done((bf16[176,256]{1,0:T(8,128)(2,1)S(1)}, bf16[176,256]{1,0:T(8,128)(2,1)S(1)}, u32[]{:S(2)}, u32[]{:S(2)}) %collective-permute-start.12) | collective-permute-done | bytes 90144 | tf_op jit(solution)/shard_map/t5/ppermute | solution.py:23
  88.9 0.0 collective-permute-done.11.refs_6_
  88.9 5.0 %add_b.1 = (bf16[512,256]{1,0:T(8,128)(2,1)}, bf16[512,256]{1,0:T(8,128)(2,1)}, bf16[512,256]{1,0:T(8,128)(2,1)}, bf16[512,256]{1,0:T(8,128)(2,1)}, bf16[336,256...) custom-call(s32[16]{0:T(128)} %clip_ref.13, ...), custom_call_target="tpu_custom_call", output_to_operand_aliasing={{0}: (3, {}), {1}: (4, {}), {2}: (5, {}), {3}: (6, {})} | custom-call | bytes 26214400 | tf_op jit(solution)/shard_map/add_b/pallas_call | solution.py:226
  94.0 0.0 collective-permute-done.13.refs_4_
  94.0 0.2 collective-permute-start.14
  94.2 2.9 %collective-permute-start.22 = (bf16[336,256]{1,0:T(8,128)(2,1)}, bf16[336,256]{1,0:T(8,128)(2,1)S(1)}, u32[]{:S(2)}, u32[]{:S(2)}) collective-permute-start(bf16[336,256]{1,0:T(8,128)(2,1)} %get-tuple-element.117), channel_id=1, source_target_pairs={{0,7},{1,6},{2,5},{3,4},{4,3},{5,2},{6,1},{7,0},{8,15},{9,14},{10,... | collective-permute-start | bytes 516104 | tf_op jit(solution)/shard_map/b7/ppermute | solution.py:23
  97.1 1.9 %collective-permute-start.15 = (bf16[512,256]{1,0:T(8,128)(2,1)}, bf16[512,256]{1,0:T(8,128)(2,1)S(1)}, u32[]{:S(2)}, u32[]{:S(2)}) collective-permute-start(bf16[512,256]{1,0:T(8,128)(2,1)} %get-tuple-element.102), channel_id=1, source_target_pairs={{0,2},{1,3},{2,0},{3,1},{4,6},{5,7},{6,4},{7,5},{8,10},{9,11},{10,... | collective-permute-start | bytes 786440 | tf_op jit(solution)/shard_map/tb2/ppermute | solution.py:23
  99.0 0.9 collective-permute-start.19
  100.0 2.6 %collective-permute-done.22.refs_7_ = bf16[336,256]{1,0:T(8,128)(2,1)S(1)} collective-permute-done((bf16[336,256]{1,0:T(8,128)(2,1)}, bf16[336,256]{1,0:T(8,128)(2,1)S(1)}, u32[]{:S(2)}, u32[]{:S(2)}) %collective-permute-start.22) | collective-permute-done | bytes 172064 | tf_op jit(solution)/shard_map/b7/ppermute | solution.py:23
  102.6 6.1 %collective-permute-start.25 = (bf16[336,256]{1,0:T(8,128)(2,1)}, bf16[336,256]{1,0:T(8,128)(2,1)S(1)}, u32[]{:S(2)}, u32[]{:S(2)}) collective-permute-start(bf16[336,256]{1,0:T(8,128)(2,1)} %get-tuple-element.122), channel_id=1, source_target_pairs={{0,5},{1,4},{2,7},{3,6},{4,1},{5,0},{6,3},{7,2},{8,13},{9,12},{10,... | collective-permute-start | bytes 516104 | tf_op jit(solution)/shard_map/b5/ppermute | solution.py:23
  108.7 0.0 collective-permute-done.14.refs_1_
  108.7 0.0 collective-permute-start.27
  108.7 0.0 copy-start.5
  108.7 0.0 copy-start.6
  108.7 0.3 collective-permute-done.15.refs_2_
  109.0 0.9 collective-permute-start.23
  109.9 0.0 collective-permute-done.9.refs_1_
  109.9 1.1 copy-done.8
  111.0 5.0 %add_c.1 = (bf16[336,256]{1,0:T(8,128)(2,1)}, bf16[336,256]{1,0:T(8,128)(2,1)}, bf16[336,256]{1,0:T(8,128)(2,1)}, bf16[336,256]{1,0:T(8,128)(2,1)}, bf16[336,256...) custom-call(s32[16]{0:T(128)} %clip_ref.13, ...), custom_call_target="tpu_custom_call" | custom-call | bytes 26214400 | tf_op jit(solution)/shard_map/add_c/pallas_call | solution.py:226
  116.0 0.0 collective-permute-done.19.refs_6_
  116.0 2.8 %collective-permute-start.20 = (bf16[336,256]{1,0:T(8,128)(2,1)}, bf16[336,256]{1,0:T(8,128)(2,1)S(1)}, u32[]{:S(2)}, u32[]{:S(2)}) collective-permute-start(bf16[336,256]{1,0:T(8,128)(2,1)} %get-tuple-element.112), channel_id=1, source_target_pairs={{0,7},{1,6},{2,5},{3,4},{4,3},{5,2},{6,1},{7,0},{8,15},{9,14},{10,... | collective-permute-start | bytes 516104 | tf_op jit(solution)/shard_map/c7/ppermute | solution.py:23
  118.8 2.8 %collective-permute-done.25.refs_5_ = bf16[336,256]{1,0:T(8,128)(2,1)S(1)} collective-permute-done((bf16[336,256]{1,0:T(8,128)(2,1)}, bf16[336,256]{1,0:T(8,128)(2,1)S(1)}, u32[]{:S(2)}, u32[]{:S(2)}) %collective-permute-start.25) | collective-permute-done | bytes 172064 | tf_op jit(solution)/shard_map/b5/ppermute | solution.py:23
  121.6 3.0 %collective-permute-start.26 = (bf16[336,256]{1,0:T(8,128)(2,1)}, bf16[336,256]{1,0:T(8,128)(2,1)S(1)}, u32[]{:S(2)}, u32[]{:S(2)}) collective-permute-start(bf16[336,256]{1,0:T(8,128)(2,1)} %get-tuple-element.123), channel_id=1, source_target_pairs={{0,6},{1,7},{2,4},{3,5},{4,2},{5,3},{6,0},{7,1},{8,14},{9,15},{10,... | collective-permute-start | bytes 516104 | tf_op jit(solution)/shard_map/c6/ppermute | solution.py:23
  124.6 11.6 %collective-permute-done.23.refs_4_ = bf16[336,256]{1,0:T(8,128)(2,1)S(1)} collective-permute-done((bf16[336,256]{1,0:T(8,128)(2,1)}, bf16[336,256]{1,0:T(8,128)(2,1)S(1)}, u32[]{:S(2)}, u32[]{:S(2)}) %collective-permute-start.23) | collective-permute-done | bytes 172064 | tf_op jit(solution)/shard_map/b4/ppermute | solution.py:23
  136.1 0.0 collective-permute-start.24
  136.1 0.1 collective-permute-start.16
  136.2 7.8 %collective-permute-start.17 = (bf16[336,256]{1,0:T(8,128)(2,1)}, bf16[336,256]{1,0:T(8,128)(2,1)S(1)}, u32[]{:S(2)}, u32[]{:S(2)}) collective-permute-start(bf16[336,256]{1,0:T(8,128)(2,1)} %get-tuple-element.106), channel_id=1, source_target_pairs={{0,2},{1,3},{2,0},{3,1},{4,6},{5,7},{6,4},{7,5},{8,10},{9,11},{10,... | collective-permute-start | bytes 516104 | tf_op jit(solution)/shard_map/c2/ppermute | solution.py:23
  144.1 5.5 %collective-permute-start.21 = (bf16[336,256]{1,0:T(8,128)(2,1)}, bf16[336,256]{1,0:T(8,128)(2,1)S(1)}, u32[]{:S(2)}, u32[]{:S(2)}) collective-permute-start(bf16[336,256]{1,0:T(8,128)(2,1)} %get-tuple-element.113), channel_id=1, source_target_pairs={{0,4},{1,5},{2,6},{3,7},{4,0},{5,1},{6,2},{7,3},{8,12},{9,13},{10,... | collective-permute-start | bytes 516104 | tf_op jit(solution)/shard_map/c4/ppermute | solution.py:23
  149.6 4.7 %norm_a.1 = (bf16[4,8,4,80,256]{4,3,2,1,0:T(8,128)(2,1)}, f32[8,256]{1,0:T(8,128)}) custom-call(bf16[512,256]{1,0:T(8,128)(2,1)S(1)} %copy-done, bf16[512,256]{1,0:T(8,128)(2,1)S(1)} %collective-permute-done.14.refs_1_, bf16[512,256]{1,0:T(8,128)(2,1)S(1)} %collective-permute-done.15.refs_2_, bf16[512,256]{1,0:T(8,128)(2,1)S(1)} %collective-permute-done.27.refs_3_, ...), custom_call_target="tpu_custom_call" | custom-call | flops 10485760 | bytes 5242880 | tf_op jit(solution)/shard_map/norm_a/pallas_call | solution.py:338
  154.3 2.1 %norm_b.1 = (bf16[4,8,4,80,256]{4,3,2,1,0:T(8,128)(2,1)}, f32[8,256]{1,0:T(8,128)}) custom-call(bf16[512,256]{1,0:T(8,128)(2,1)S(1)} %copy-done, bf16[512,256]{1,0:T(8,128)(2,1)S(1)} %collective-permute-done.14.refs_1_, bf16[512,256]{1,0:T(8,128)(2,1)S(1)} %collective-permute-done.15.refs_2_, ...), custom_call_target="tpu_custom_call", output_to_operand_aliasing={{0}: (10, {})} | custom-call | flops 5242880 | bytes 2621440 | tf_op jit(solution)/shard_map/norm_b/pallas_call | solution.py:338
  156.4 0.4 collective-permute-done.17.refs_2_
  156.8 2.4 %collective-permute-done.18.refs_3_ = bf16[336,256]{1,0:T(8,128)(2,1)S(1)} collective-permute-done((bf16[336,256]{1,0:T(8,128)(2,1)}, bf16[336,256]{1,0:T(8,128)(2,1)S(1)}, u32[]{:S(2)}, u32[]{:S(2)}) %collective-permute-start.18) | collective-permute-done | bytes 172064 | tf_op jit(solution)/shard_map/c3/ppermute | solution.py:23
  159.2 2.2 %norm_c.1 = (bf16[4,8,4,80,256]{4,3,2,1,0:T(8,128)(2,1)}, f32[8,256]{1,0:T(8,128)}) custom-call(bf16[336,256]{1,0:T(8,128)(2,1)S(1)} %copy-done.4, bf16[336,256]{1,0:T(8,128)(2,1)S(1)} %collective-permute-done.16.refs_1_, bf16[336,256]{1,0:T(8,128)(2,1)S(1)} %collective-permute-done.17.refs_2_, ...), custom_call_target="tpu_custom_call", output_to_operand_aliasing={{0}: (10, {})} | custom-call | flops 5242880 | bytes 2621440 | tf_op jit(solution)/shard_map/norm_c/pallas_call | solution.py:338
  (35 shorter events, 0.1 us)
Async XLA Ops:
  1.4 22.9 %collective-permute-start = (bf16[4,1,1280,128]{3,2,1,0:T(8,128)(2,1)S(1)}, bf16[4,1,1280,128]{3,2,1,0:T(8,128)(2,1)S(1)}, u32[]{:S(2)}, u32[]{:S(2)}) collective-permute-start(bf16[4,1,1280,128]{3,2,1,0:T(8,128)(2,1)S(1)} %slice.3), channel_id=1, source_target_pairs={{0,1},{1,2},{2,3},{3,4},{4,5},{5,6},{6,7},{8,9},{9,10},{10,11},{11... | collective-permute-start | bytes 3932168 | tf_op jit(solution)/shard_map/halo/ppermute | solution.py:18
  18.4 19.1 %collective-permute-start.1 = (bf16[480,256]{1,0:T(8,128)(2,1)}, bf16[480,256]{1,0:T(8,128)(2,1)S(1)}, u32[]{:S(2)}, u32[]{:S(2)}) collective-permute-start(bf16[480,256]{1,0:T(8,128)(2,1)} %get-tuple-element.70), channel_id=1, source_target_pairs={{0,1},{1,0},{2,3},{3,2},{4,5},{5,4},{6,7},{7,6},{8,9},{9,8},{10,11... | collective-permute-start | bytes 737288 | tf_op jit(solution)/shard_map/a1/ppermute | solution.py:23
  20.3 29.2 %collective-permute-start.5 = (bf16[480,256]{1,0:T(8,128)(2,1)}, bf16[480,256]{1,0:T(8,128)(2,1)S(1)}, u32[]{:S(2)}, u32[]{:S(2)}) collective-permute-start(bf16[480,256]{1,0:T(8,128)(2,1)} %get-tuple-element.81), channel_id=1, source_target_pairs={{0,7},{1,6},{2,5},{3,4},{4,3},{5,2},{6,1},{7,0},{8,15},{9,14},{10,... | collective-permute-start | bytes 737288 | tf_op jit(solution)/shard_map/a7/ppermute | solution.py:23
  22.3 45.0 %collective-permute-start.6 = (bf16[480,256]{1,0:T(8,128)(2,1)}, bf16[480,256]{1,0:T(8,128)(2,1)}, u32[]{:S(2)}, u32[]{:S(2)}) collective-permute-start(bf16[480,256]{1,0:T(8,128)(2,1)} %get-tuple-element.82), channel_id=1, source_target_pairs={{0,6},{1,7},{2,4},{3,5},{4,2},{5,3},{6,0},{7,1},{8,14},{9,15},{10,... | collective-permute-start | bytes 737288 | tf_op jit(solution)/shard_map/a6/ppermute | solution.py:23
  23.8 43.6 %collective-permute-start.7 = (bf16[480,256]{1,0:T(8,128)(2,1)}, bf16[480,256]{1,0:T(8,128)(2,1)}, u32[]{:S(2)}, u32[]{:S(2)}) collective-permute-start(bf16[480,256]{1,0:T(8,128)(2,1)} %get-tuple-element.83), channel_id=1, source_target_pairs={{0,5},{1,4},{2,7},{3,6},{4,1},{5,0},{6,3},{7,2},{8,13},{9,12},{10,... | collective-permute-start | bytes 737288 | tf_op jit(solution)/shard_map/a5/ppermute | solution.py:23
  24.3 1.1 copy-start.7
  25.5 12.1 %copy-start.11 = (bf16[480,256]{1,0:T(8,128)(2,1)S(1)}, bf16[480,256]{1,0:T(8,128)(2,1)}, u32[]{:S(2)}) copy-start(bf16[480,256]{1,0:T(8,128)(2,1)} %get-tuple-element.75) | copy-start | bytes 737284
  34.1 34.1 %collective-permute-start.4 = (bf16[1,4,640,256]{3,2,1,0:T(8,128)(2,1)}, bf16[1,4,640,256]{3,2,1,0:T(8,128)(2,1)}, u32[]{:S(2)}, u32[]{:S(2)}) collective-permute-start(bf16[1,4,640,256]{3,2,1,0:T(8,128)(2,1)} %conv_hist0.1), channel_id=1, source_target_pairs={{0,8},{8,16},{16,24},{1,9},{9,17},{17,25},{2,10},{10,18},{18,26},{... | collective-permute-start | bytes 3932168 | tf_op jit(solution)/shard_map/hist0/ppermute | solution.py:18
  37.5 11.9 %copy-start.2 = (bf16[480,256]{1,0:T(8,128)(2,1)}, bf16[480,256]{1,0:T(8,128)(2,1)S(1)}, u32[]{:S(2)}) copy-start(bf16[480,256]{1,0:T(8,128)(2,1)S(1)} %collective-permute-done.1.refs_9_) | copy-start | bytes 737284
  37.5 11.9 %copy-start.9 = (bf16[480,256]{1,0:T(8,128)(2,1)S(1)}, bf16[480,256]{1,0:T(8,128)(2,1)}, u32[]{:S(2)}) copy-start(bf16[480,256]{1,0:T(8,128)(2,1)} %get-tuple-element.85) | copy-start | bytes 737284
  37.5 12.6 %copy-start.10 = (bf16[480,256]{1,0:T(8,128)(2,1)S(1)}, bf16[480,256]{1,0:T(8,128)(2,1)}, u32[]{:S(2)}) copy-start(bf16[480,256]{1,0:T(8,128)(2,1)} %get-tuple-element.79) | copy-start | bytes 737284
  37.6 12.6 %collective-permute-start.2 = (bf16[480,256]{1,0:T(8,128)(2,1)S(1)}, bf16[480,256]{1,0:T(8,128)(2,1)S(1)}, u32[]{:S(2)}, u32[]{:S(2)}) collective-permute-start(bf16[480,256]{1,0:T(8,128)(2,1)S(1)} %copy-done.11), channel_id=1, source_target_pairs={{0,2},{1,3},{2,0},{3,1},{4,6},{5,7},{6,4},{7,5},{8,10},{9,11},{10,... | collective-permute-start | bytes 737288 | tf_op jit(solution)/shard_map/a2/ppermute | solution.py:23
  49.5 17.9 %collective-permute-start.8 = (bf16[480,256]{1,0:T(8,128)(2,1)S(1)}, bf16[480,256]{1,0:T(8,128)(2,1)S(1)}, u32[]{:S(2)}, u32[]{:S(2)}) collective-permute-start(bf16[480,256]{1,0:T(8,128)(2,1)S(1)} %copy-done.9), channel_id=1, source_target_pairs={{0,4},{1,5},{2,6},{3,7},{4,0},{5,1},{6,2},{7,3},{8,12},{9,13},{10,... | collective-permute-start | bytes 737288 | tf_op jit(solution)/shard_map/a4/ppermute | solution.py:23
  50.2 10.7 %collective-permute-start.3 = (bf16[480,256]{1,0:T(8,128)(2,1)S(1)}, bf16[480,256]{1,0:T(8,128)(2,1)S(1)}, u32[]{:S(2)}, u32[]{:S(2)}) collective-permute-start(bf16[480,256]{1,0:T(8,128)(2,1)S(1)} %copy-done.10), channel_id=1, source_target_pairs={{0,3},{1,2},{2,1},{3,0},{4,7},{5,6},{6,5},{7,4},{8,11},{9,10},{10,... | collective-permute-start | bytes 737288 | tf_op jit(solution)/shard_map/a3/ppermute | solution.py:23
  60.8 10.1 %copy-start.15 = (bf16[176,256]{1,0:T(8,128)(2,1)S(1)}, bf16[176,256]{1,0:T(8,128)(2,1)}, u32[]{:S(2)}) copy-start(bf16[176,256]{1,0:T(8,128)(2,1)} %get-tuple-element.88) | copy-start | bytes 270340
  60.8 17.2 %copy-start.14 = (bf16[176,256]{1,0:T(8,128)(2,1)S(1)}, bf16[176,256]{1,0:T(8,128)(2,1)}, u32[]{:S(2)}) copy-start(bf16[176,256]{1,0:T(8,128)(2,1)} %get-tuple-element.92) | copy-start | bytes 270340
  60.8 17.2 %copy-start.13 = (bf16[176,256]{1,0:T(8,128)(2,1)S(1)}, bf16[176,256]{1,0:T(8,128)(2,1)}, u32[]{:S(2)}) copy-start(bf16[176,256]{1,0:T(8,128)(2,1)} %get-tuple-element.90) | copy-start | bytes 270340
  60.8 20.2 %copy-start.12 = (bf16[176,256]{1,0:T(8,128)(2,1)S(1)}, bf16[176,256]{1,0:T(8,128)(2,1)}, u32[]{:S(2)}) copy-start(bf16[176,256]{1,0:T(8,128)(2,1)} %get-tuple-element.99) | copy-start | bytes 270340
  68.2 41.7 %collective-permute-start.9 = (bf16[1,4,640,256]{3,2,1,0:T(8,128)(2,1)}, bf16[1,4,640,256]{3,2,1,0:T(8,128)(2,1)S(1)}, u32[]{:S(2)}, u32[]{:S(2)}) collective-permute-start(bf16[1,4,640,256]{3,2,1,0:T(8,128)(2,1)} %conv_hist1.1), channel_id=1, source_target_pairs={{0,8},{8,16},{16,24},{1,9},{9,17},{17,25},{2,10},{10,18},{18,26},{... | collective-permute-start | bytes 3932168 | tf_op jit(solution)/shard_map/hist1/ppermute | solution.py:18
  70.9 10.1 %collective-permute-start.10 = (bf16[176,256]{1,0:T(8,128)(2,1)S(1)}, bf16[176,256]{1,0:T(8,128)(2,1)S(1)}, u32[]{:S(2)}, u32[]{:S(2)}) collective-permute-start(bf16[176,256]{1,0:T(8,128)(2,1)S(1)} %copy-done.15), channel_id=1, source_target_pairs={{0,7},{1,6},{2,5},{3,4},{4,3},{5,2},{6,1},{7,0},{8,15},{9,14},{10,... | collective-permute-start | bytes 270344 | tf_op jit(solution)/shard_map/t7/ppermute | solution.py:23
  78.1 10.9 %collective-permute-start.12 = (bf16[176,256]{1,0:T(8,128)(2,1)S(1)}, bf16[176,256]{1,0:T(8,128)(2,1)S(1)}, u32[]{:S(2)}, u32[]{:S(2)}) collective-permute-start(bf16[176,256]{1,0:T(8,128)(2,1)S(1)} %copy-done.14), channel_id=1, source_target_pairs={{0,5},{1,4},{2,7},{3,6},{4,1},{5,0},{6,3},{7,2},{8,13},{9,12},{10,... | collective-permute-start | bytes 270344 | tf_op jit(solution)/shard_map/t5/ppermute | solution.py:23
  78.1 10.9 %collective-permute-start.11 = (bf16[176,256]{1,0:T(8,128)(2,1)S(1)}, bf16[176,256]{1,0:T(8,128)(2,1)S(1)}, u32[]{:S(2)}, u32[]{:S(2)}) collective-permute-start(bf16[176,256]{1,0:T(8,128)(2,1)S(1)} %copy-done.13), channel_id=1, source_target_pairs={{0,6},{1,7},{2,4},{3,5},{4,2},{5,3},{6,0},{7,1},{8,14},{9,15},{10,... | collective-permute-start | bytes 270344 | tf_op jit(solution)/shard_map/t6/ppermute | solution.py:23
  81.1 12.9 %collective-permute-start.13 = (bf16[176,256]{1,0:T(8,128)(2,1)S(1)}, bf16[176,256]{1,0:T(8,128)(2,1)S(1)}, u32[]{:S(2)}, u32[]{:S(2)}) collective-permute-start(bf16[176,256]{1,0:T(8,128)(2,1)S(1)} %copy-done.12), channel_id=1, source_target_pairs={{0,4},{1,5},{2,6},{3,7},{4,0},{5,1},{6,2},{7,3},{8,12},{9,13},{10,... | collective-permute-start | bytes 270344 | tf_op jit(solution)/shard_map/t4/ppermute | solution.py:23
  94.0 14.7 %collective-permute-start.14 = (bf16[512,256]{1,0:T(8,128)(2,1)}, bf16[512,256]{1,0:T(8,128)(2,1)S(1)}, u32[]{:S(2)}, u32[]{:S(2)}) collective-permute-start(bf16[512,256]{1,0:T(8,128)(2,1)} %get-tuple-element.100), channel_id=1, source_target_pairs={{0,1},{1,0},{2,3},{3,2},{4,5},{5,4},{6,7},{7,6},{8,9},{9,8},{10,11... | collective-permute-start | bytes 786440 | tf_op jit(solution)/shard_map/tb1/ppermute | solution.py:23
  94.2 8.4 %collective-permute-start.22 = (bf16[336,256]{1,0:T(8,128)(2,1)}, bf16[336,256]{1,0:T(8,128)(2,1)S(1)}, u32[]{:S(2)}, u32[]{:S(2)}) collective-permute-start(bf16[336,256]{1,0:T(8,128)(2,1)} %get-tuple-element.117), channel_id=1, source_target_pairs={{0,7},{1,6},{2,5},{3,4},{4,3},{5,2},{6,1},{7,0},{8,15},{9,14},{10,... | collective-permute-start | bytes 516104 | tf_op jit(solution)/shard_map/b7/ppermute | solution.py:23
  97.1 11.9 %collective-permute-start.15 = (bf16[512,256]{1,0:T(8,128)(2,1)}, bf16[512,256]{1,0:T(8,128)(2,1)S(1)}, u32[]{:S(2)}, u32[]{:S(2)}) collective-permute-start(bf16[512,256]{1,0:T(8,128)(2,1)} %get-tuple-element.102), channel_id=1, source_target_pairs={{0,2},{1,3},{2,0},{3,1},{4,6},{5,7},{6,4},{7,5},{8,10},{9,11},{10,... | collective-permute-start | bytes 786440 | tf_op jit(solution)/shard_map/tb2/ppermute | solution.py:23
  99.0 17.0 %collective-permute-start.19 = (bf16[336,256]{1,0:T(8,128)(2,1)}, bf16[336,256]{1,0:T(8,128)(2,1)S(1)}, u32[]{:S(2)}, u32[]{:S(2)}) collective-permute-start(bf16[336,256]{1,0:T(8,128)(2,1)} %get-tuple-element.111), channel_id=1, source_target_pairs={{0,6},{1,7},{2,4},{3,5},{4,2},{5,3},{6,0},{7,1},{8,14},{9,15},{10,... | collective-permute-start | bytes 516104 | tf_op jit(solution)/shard_map/b6/ppermute | solution.py:23
  102.6 19.0 %collective-permute-start.25 = (bf16[336,256]{1,0:T(8,128)(2,1)}, bf16[336,256]{1,0:T(8,128)(2,1)S(1)}, u32[]{:S(2)}, u32[]{:S(2)}) collective-permute-start(bf16[336,256]{1,0:T(8,128)(2,1)} %get-tuple-element.122), channel_id=1, source_target_pairs={{0,5},{1,4},{2,7},{3,6},{4,1},{5,0},{6,3},{7,2},{8,13},{9,12},{10,... | collective-permute-start | bytes 516104 | tf_op jit(solution)/shard_map/b5/ppermute | solution.py:23
  108.7 35.4 %collective-permute-start.27 = (bf16[512,256]{1,0:T(8,128)(2,1)}, bf16[512,256]{1,0:T(8,128)(2,1)S(1)}, u32[]{:S(2)}, u32[]{:S(2)}) collective-permute-start(bf16[512,256]{1,0:T(8,128)(2,1)} %get-tuple-element.126), channel_id=1, source_target_pairs={{0,3},{1,2},{2,1},{3,0},{4,7},{5,6},{6,5},{7,4},{8,11},{9,10},{10,... | collective-permute-start | bytes 786440 | tf_op jit(solution)/shard_map/tb3/ppermute | solution.py:23
  108.7 40.9 %copy-start = (bf16[512,256]{1,0:T(8,128)(2,1)S(1)}, bf16[512,256]{1,0:T(8,128)(2,1)}, u32[]{:S(2)}) copy-start(bf16[512,256]{1,0:T(8,128)(2,1)} %get-tuple-element.124.refs_0_) | copy-start | bytes 786436
  108.7 40.9 %copy-start.1 = (bf16[480,256]{1,0:T(8,128)(2,1)S(1)}, bf16[480,256]{1,0:T(8,128)(2,1)}, u32[]{:S(2)}) copy-start(bf16[480,256]{1,0:T(8,128)(2,1)} %get-tuple-element.127.refs_8_) | copy-start | bytes 737284
  108.7 40.9 %copy-start.3 = (bf16[480,256]{1,0:T(8,128)(2,1)S(1)}, bf16[480,256]{1,0:T(8,128)(2,1)}, u32[]{:S(2)}) copy-start(bf16[480,256]{1,0:T(8,128)(2,1)} %copy-done.2) | copy-start | bytes 737284
  108.7 40.9 %copy-start.5 = (f32[256]{0:T(256)S(1)}, f32[256]{0:T(256)}, u32[]{:S(2)}) copy-start(f32[256]{0:T(256)} %param.8) | copy-start | bytes 3076
  108.7 40.8 %copy-start.6 = (f32[256]{0:T(256)S(1)}, f32[256]{0:T(256)}, u32[]{:S(2)}) copy-start(f32[256]{0:T(256)} %param.9) | copy-start | bytes 3076
  109.0 27.1 %collective-permute-start.23 = (bf16[336,256]{1,0:T(8,128)(2,1)}, bf16[336,256]{1,0:T(8,128)(2,1)S(1)}, u32[]{:S(2)}, u32[]{:S(2)}) collective-permute-start(bf16[336,256]{1,0:T(8,128)(2,1)} %get-tuple-element.118), channel_id=1, source_target_pairs={{0,4},{1,5},{2,6},{3,7},{4,0},{5,1},{6,2},{7,3},{8,12},{9,13},{10,... | collective-permute-start | bytes 516104 | tf_op jit(solution)/shard_map/b4/ppermute | solution.py:23
  109.9 1.1 copy-start.8
  116.0 20.2 %collective-permute-start.20 = (bf16[336,256]{1,0:T(8,128)(2,1)}, bf16[336,256]{1,0:T(8,128)(2,1)S(1)}, u32[]{:S(2)}, u32[]{:S(2)}) collective-permute-start(bf16[336,256]{1,0:T(8,128)(2,1)} %get-tuple-element.112), channel_id=1, source_target_pairs={{0,7},{1,6},{2,5},{3,4},{4,3},{5,2},{6,1},{7,0},{8,15},{9,14},{10,... | collective-permute-start | bytes 516104 | tf_op jit(solution)/shard_map/c7/ppermute | solution.py:23
  121.6 22.5 %collective-permute-start.26 = (bf16[336,256]{1,0:T(8,128)(2,1)}, bf16[336,256]{1,0:T(8,128)(2,1)S(1)}, u32[]{:S(2)}, u32[]{:S(2)}) collective-permute-start(bf16[336,256]{1,0:T(8,128)(2,1)} %get-tuple-element.123), channel_id=1, source_target_pairs={{0,6},{1,7},{2,4},{3,5},{4,2},{5,3},{6,0},{7,1},{8,14},{9,15},{10,... | collective-permute-start | bytes 516104 | tf_op jit(solution)/shard_map/c6/ppermute | solution.py:23
  136.1 20.3 %collective-permute-start.24 = (bf16[336,256]{1,0:T(8,128)(2,1)}, bf16[336,256]{1,0:T(8,128)(2,1)S(1)}, u32[]{:S(2)}, u32[]{:S(2)}) collective-permute-start(bf16[336,256]{1,0:T(8,128)(2,1)} %get-tuple-element.119), channel_id=1, source_target_pairs={{0,5},{1,4},{2,7},{3,6},{4,1},{5,0},{6,3},{7,2},{8,13},{9,12},{10,... | collective-permute-start | bytes 516104 | tf_op jit(solution)/shard_map/c5/ppermute | solution.py:23
  136.1 20.3 %collective-permute-start.16 = (bf16[336,256]{1,0:T(8,128)(2,1)}, bf16[336,256]{1,0:T(8,128)(2,1)S(1)}, u32[]{:S(2)}, u32[]{:S(2)}) collective-permute-start(bf16[336,256]{1,0:T(8,128)(2,1)} %get-tuple-element.105), channel_id=1, source_target_pairs={{0,1},{1,0},{2,3},{3,2},{4,5},{5,4},{6,7},{7,6},{8,9},{9,8},{10,11... | collective-permute-start | bytes 516104 | tf_op jit(solution)/shard_map/c1/ppermute | solution.py:23
  136.2 20.6 %collective-permute-start.17 = (bf16[336,256]{1,0:T(8,128)(2,1)}, bf16[336,256]{1,0:T(8,128)(2,1)S(1)}, u32[]{:S(2)}, u32[]{:S(2)}) collective-permute-start(bf16[336,256]{1,0:T(8,128)(2,1)} %get-tuple-element.106), channel_id=1, source_target_pairs={{0,2},{1,3},{2,0},{3,1},{4,6},{5,7},{6,4},{7,5},{8,10},{9,11},{10,... | collective-permute-start | bytes 516104 | tf_op jit(solution)/shard_map/c2/ppermute | solution.py:23
  144.1 15.2 %collective-permute-start.18 = (bf16[336,256]{1,0:T(8,128)(2,1)}, bf16[336,256]{1,0:T(8,128)(2,1)S(1)}, u32[]{:S(2)}, u32[]{:S(2)}) collective-permute-start(bf16[336,256]{1,0:T(8,128)(2,1)} %get-tuple-element.107), channel_id=1, source_target_pairs={{0,3},{1,2},{2,1},{3,0},{4,7},{5,6},{6,5},{7,4},{8,11},{9,10},{10,... | collective-permute-start | bytes 516104 | tf_op jit(solution)/shard_map/c3/ppermute | solution.py:23
  144.1 15.2 %collective-permute-start.21 = (bf16[336,256]{1,0:T(8,128)(2,1)}, bf16[336,256]{1,0:T(8,128)(2,1)S(1)}, u32[]{:S(2)}, u32[]{:S(2)}) collective-permute-start(bf16[336,256]{1,0:T(8,128)(2,1)} %get-tuple-element.113), channel_id=1, source_target_pairs={{0,4},{1,5},{2,6},{3,7},{4,0},{5,1},{6,2},{7,3},{8,12},{9,13},{10,... | collective-permute-start | bytes 516104 | tf_op jit(solution)/shard_map/c4/ppermute | solution.py:23
  154.3 4.9 %copy-start.4 = (bf16[336,256]{1,0:T(8,128)(2,1)S(1)}, bf16[336,256]{1,0:T(8,128)(2,1)}, u32[]{:S(2)}) copy-start(bf16[336,256]{1,0:T(8,128)(2,1)} %get-tuple-element.104.refs_0_) | copy-start | bytes 516100

commit v9 on v8

--- a/solution.py
+++ b/solution.py
@@ -434,12 +434,12 @@
         "conv_top", run, 0, 4, later, steps=1, sums=(a_sums,), weigh=20, vmem=56,
         layout=layout((0, STAT_ROWS, top_rows), (0, STAT_ROWS, near_rows)))
     t_got = send_far("t", t_sent)
-    run = functools.partial(conv_frames, frames, after(halo, t_sent[0], a_got[near[2]]), weight, clip_ids, parts)
+    run = functools.partial(conv_frames, frames, after(halo, t_sent[0], a_sums), weight, clip_ids, parts)
     onward, = named("conv_hist1", run, 3, 1, [], [(5, [(0, 0)], ())], weigh=20, vmem=56)
     second_add = named("hist1", passed_along, after(onward, first_add, *[a_got[flip] for flip in far]), "tm", 1)
     kept = {flip: t_sent[flip] for flip in range(parts) if flip not in far}
     b_sent = named(
-        "add_b", run, 0, 0, [(0, [], (0, 1))], addends=(own[0], after(first_add, t_got[far[0]], t_got[far[1]], t_got[far[2]])), kept=kept,
+        "add_b", run, 0, 0, [(0, [], (0, 1))], addends=(own[0], after(first_add, a_sums)), kept=kept,
         weigh=20, vmem=56,
         layout=layout((0, STAT_ROWS, one_rows), (top_rows, top_rows + STAT_ROWS, near_rows)))
     b_got = send_far("b", b_sent)

time: 165 us -> 163 us (0.988); the launches traced: 161 us -> 161 us
  waiting for transfers between devices: 33.3 us -> 43.8 us
  starting transfers between devices: 57.6 us -> 47.7 us
    ppermute x25, starting transfers between devices: 49.7 us -> 39.8 us  [exchanged(): return lax.ppermute(array, axis, [(i, i ^ flip) for i in range(length)])]
    ppermute x25, waiting for transfers between devices: 32.4 us -> 42.2 us  [exchanged(): return lax.ppermute(array, axis, [(i, i ^ flip) for i in range(length)])]
  transfers between devices with their start and end apart: 28 -> 28, of which waited for: 10 -> 9; matrix products, arithmetic and copies ran while one was open for 0% -> 0% of each run, Pallas kernels for 40% -> 40%
where the time goes in v9:
time: 163 us; the launch traced here: 161 us
  Pallas kernels  66.8 us (41%)
  starting transfers between devices  47.7 us (29%)
  waiting for transfers between devices  43.8 us (27%)
  local copies, waits for them, and re-layouts  2.65 us (2%)
    pallas_call x7, Pallas kernels, conv_frames(): pl.pallas_call(functools.partial(conv_kernel, plan), out_shape=out_shape,...  57.8 us
    ppermute x25, waiting for transfers between devices, exchanged(): return lax.ppermute(array, axis, [(i, i ^ flip) for i in range(length)])  42.2 us
    ppermute x25, starting transfers between devices, exchanged(): return lax.ppermute(array, axis, [(i, i ^ flip) for i in range(length)])  39.8 us
    pallas_call x3, Pallas kernels, norm_frames(): pl.pallas_call(functools.partial(norm_kernel, plan), out_shape=[jax.Shape...  9 us
    ppermute x3, starting transfers between devices, passed_along(): return lax.ppermute(array, axis, pairs)  7.89 us
  transfers between devices with their start and end apart: 28, of which 9 were waited for; matrix products, arithmetic and copies ran while one was open for 0% of the time, Pallas kernels for 40%

profile of v9, /device:TPU:4, one launch (start us, length us, event | category | flops | bytes accessed | tf_op | source)
XLA Modules:
  0.0 161.3 jit_solution(14136964767555601167)
XLA Ops:
  0.0 1.4 slice.3
  1.4 1.8 %collective-permute-start = (bf16[4,1,1280,128]{3,2,1,0:T(8,128)(2,1)S(1)}, bf16[4,1,1280,128]{3,2,1,0:T(8,128)(2,1)S(1)}, u32[]{:S(2)}, u32[]{:S(2)}) collective-permute-start(bf16[4,1,1280,128]{3,2,1,0:T(8,128)(2,1)S(1)} %slice.3), channel_id=1, source_target_pairs={{0,1},{1,2},{2,3},{3,4},{4,5},{5,6},{6,7},{8,9},{9,10},{10,11},{11... | collective-permute-start | bytes 3932168 | tf_op jit(solution)/shard_map/halo/ppermute | solution.py:18
  3.2 15.2 %conv_a.1 = (bf16[480,256]{1,0:T(8,128)(2,1)}, bf16[480,256]{1,0:T(8,128)(2,1)}, bf16[480,256]{1,0:T(8,128)(2,1)}, bf16[480,256]{1,0:T(8,128)(2,1)}, bf16[480,25...) custom-call(s32[16]{0:T(128)} %clip_ref.13, ...), custom_call_target="tpu_custom_call" | custom-call | flops 6794772480 | bytes 9830400 | tf_op jit(solution)/shard_map/conv_a/pallas_call | solution.py:226
  18.4 1.8 %collective-permute-start.1 = (bf16[480,256]{1,0:T(8,128)(2,1)}, bf16[480,256]{1,0:T(8,128)(2,1)S(1)}, u32[]{:S(2)}, u32[]{:S(2)}) collective-permute-start(bf16[480,256]{1,0:T(8,128)(2,1)} %get-tuple-element.70), channel_id=1, source_target_pairs={{0,1},{1,0},{2,3},{3,2},{4,5},{5,4},{6,7},{7,6},{8,9},{9,8},{10,11... | collective-permute-start | bytes 737288 | tf_op jit(solution)/shard_map/a1/ppermute | solution.py:23
  20.3 2.1 %collective-permute-start.4 = (bf16[480,256]{1,0:T(8,128)(2,1)}, bf16[480,256]{1,0:T(8,128)(2,1)S(1)}, u32[]{:S(2)}, u32[]{:S(2)}) collective-permute-start(bf16[480,256]{1,0:T(8,128)(2,1)} %get-tuple-element.79), channel_id=1, source_target_pairs={{0,7},{1,6},{2,5},{3,4},{4,3},{5,2},{6,1},{7,0},{8,15},{9,14},{10,... | collective-permute-start | bytes 737288 | tf_op jit(solution)/shard_map/a7/ppermute | solution.py:23
  22.3 1.5 collective-permute-start.5
  23.8 0.6 collective-permute-start.6
  24.3 0.0 collective-permute-done.refs_2_.refs_3_.refs_4_.refs_5_.refs_6_.refs_7_.refs_1_
  24.3 1.1 copy-done.7
  25.5 8.6 %conv_hist0.1 = bf16[1,4,640,256]{3,2,1,0:T(8,128)(2,1)} custom-call(s32[16]{0:T(128)} %clip_ref.13, bf16[4,8,1280,128]{3,2,1,0:T(8,128)(2,1)} %refs_0_.9, bf16[4,8,1280,128]{3,2,1,0:T(8,128)(2,1)} %refs_0_.9, bf16[4,1,1280,128]{3,2,1,0:T(8,128)(2,1)} %copy-done.7, bf16[4,1,1280,128]{3,2,1,0:T(8,128)(2,1)} %copy-done.7, bf16[3,1152,256]{2,1,0:T(8,128)(2,1)} %bitcast.13, ...), custom_call_target="tpu_custom_call" | custom-call | flops 3019898880 | bytes 6553600 | tf_op jit(solution)/shard_map/conv_hist0/pallas_call | solution.py:226
  34.1 3.4 %collective-permute-start.3 = (bf16[1,4,640,256]{3,2,1,0:T(8,128)(2,1)}, bf16[1,4,640,256]{3,2,1,0:T(8,128)(2,1)}, u32[]{:S(2)}, u32[]{:S(2)}) collective-permute-start(bf16[1,4,640,256]{3,2,1,0:T(8,128)(2,1)} %conv_hist0.1), channel_id=1, source_target_pairs={{0,8},{8,16},{16,24},{1,9},{9,17},{17,25},{2,10},{10,18},{18,26},{... | collective-permute-start | bytes 3932168 | tf_op jit(solution)/shard_map/hist0/ppermute | solution.py:18
  37.5 0.0 collective-permute-done.1.refs_9_
  37.6 1.8 %collective-permute-start.2 = (bf16[480,256]{1,0:T(8,128)(2,1)S(1)}, bf16[480,256]{1,0:T(8,128)(2,1)S(1)}, u32[]{:S(2)}, u32[]{:S(2)}) collective-permute-start(bf16[480,256]{1,0:T(8,128)(2,1)S(1)} %copy-done.11), channel_id=1, source_target_pairs={{0,2},{1,3},{2,0},{3,1},{4,6},{5,7},{6,4},{7,5},{8,10},{9,11},{10,... | collective-permute-start | bytes 737288 | tf_op jit(solution)/shard_map/a2/ppermute | solution.py:23
  39.4 10.1 %conv_own.1 = (f32[1,4,640,256]{3,2,1,0:T(8,128)}, f32[1,4,640,256]{3,2,1,0:T(8,128)}) custom-call(s32[16]{0:T(128)} %clip_ref.13, bf16[4,8,1280,128]{3,2,1,0:T(8,128)(2,1)} %refs_0_.9, bf16[4,8,1280,128]{3,2,1,0:T(8,128)(2,1)} %refs_0_.9, bf16[4,1,1280,128]{3,2,1,0:T(8,128)(2,1)} %copy-done.7, bf16[4,1,1280,128]{3,2,1,0:T(8,128)(2,1)} %copy-done.7, ...), custom_call_target="tpu_custom_call" | custom-call | flops 90596966400 | bytes 157286400 | tf_op jit(solution)/shard_map/conv_own/pallas_call | solution.py:226
  49.5 0.7 collective-permute-start.7
  50.2 7.3 %conv_top.1 = (bf16[512,256]{1,0:T(8,128)(2,1)}, bf16[512,256]{1,0:T(8,128)(2,1)}, bf16[512,256]{1,0:T(8,128)(2,1)}, bf16[512,256]{1,0:T(8,128)(2,1)}, bf16[176,...) custom-call(s32[16]{0:T(128)} %clip_ref.13, ...), custom_call_target="tpu_custom_call" | custom-call | flops 45298483200 | bytes 65536000 | tf_op jit(solution)/shard_map/conv_top/pallas_call | solution.py:226
  57.5 6.5 %conv_hist1.1 = bf16[1,4,640,256]{3,2,1,0:T(8,128)(2,1)} custom-call(s32[16]{0:T(128)} %clip_ref.13, bf16[4,8,1280,128]{3,2,1,0:T(8,128)(2,1)} %refs_0_.9, bf16[4,1,1280,128]{3,2,1,0:T(8,128)(2,1)} %copy-done.7, bf16[3,1152,256]{2,1,0:T(8,128)(2,1)} %bitcast.20), custom_call_target="tpu_custom_call" | custom-call | flops 30198988800 | bytes 78643200 | tf_op jit(solution)/shard_map/conv_hist1/pallas_call | solution.py:226
  64.0 0.0 collective-permute-done.6.refs_13_
  64.0 2.6 %collective-permute-done.7.refs_12_ = bf16[480,256]{1,0:T(8,128)(2,1)S(1)} collective-permute-done((bf16[480,256]{1,0:T(8,128)(2,1)S(1)}, bf16[480,256]{1,0:T(8,128)(2,1)S(1)}, u32[]{:S(2)}, u32[]{:S(2)}) %collective-permute-start.7) | collective-permute-done | bytes 245792 | tf_op jit(solution)/shard_map/a4/ppermute | solution.py:23
  66.6 1.6 %collective-permute-done.3.refs_1_ = bf16[1,4,640,256]{3,2,1,0:T(8,128)(2,1)} collective-permute-done((bf16[1,4,640,256]{3,2,1,0:T(8,128)(2,1)}, bf16[1,4,640,256]{3,2,1,0:T(8,128)(2,1)}, u32[]{:S(2)}, u32[]{:S(2)}) %collective-permute-start.3) | collective-permute-done | bytes 1310752 | tf_op jit(solution)/shard_map/hist0/ppermute | solution.py:18
  68.2 2.7 %collective-permute-start.8 = (bf16[1,4,640,256]{3,2,1,0:T(8,128)(2,1)}, bf16[1,4,640,256]{3,2,1,0:T(8,128)(2,1)S(1)}, u32[]{:S(2)}, u32[]{:S(2)}) collective-permute-start(bf16[1,4,640,256]{3,2,1,0:T(8,128)(2,1)} %conv_hist1.1), channel_id=1, source_target_pairs={{0,8},{8,16},{16,24},{1,9},{9,17},{17,25},{2,10},{10,18},{18,26},{... | collective-permute-start | bytes 3932168 | tf_op jit(solution)/shard_map/hist1/ppermute | solution.py:18
  70.9 1.0 collective-permute-start.9
  71.9 5.3 %collective-permute-done.9.refs_7_ = bf16[176,256]{1,0:T(8,128)(2,1)S(1)} collective-permute-done((bf16[176,256]{1,0:T(8,128)(2,1)S(1)}, bf16[176,256]{1,0:T(8,128)(2,1)S(1)}, u32[]{:S(2)}, u32[]{:S(2)}) %collective-permute-start.9) | collective-permute-done | bytes 90144 | tf_op jit(solution)/shard_map/t7/ppermute | solution.py:23
  77.3 2.7 %collective-permute-start.10 = (bf16[176,256]{1,0:T(8,128)(2,1)S(1)}, bf16[176,256]{1,0:T(8,128)(2,1)S(1)}, u32[]{:S(2)}, u32[]{:S(2)}) collective-permute-start(bf16[176,256]{1,0:T(8,128)(2,1)S(1)} %copy-done.14), channel_id=1, source_target_pairs={{0,4},{1,5},{2,6},{3,7},{4,0},{5,1},{6,2},{7,3},{8,12},{9,13},{10,... | collective-permute-start | bytes 270344 | tf_op jit(solution)/shard_map/t4/ppermute | solution.py:23
  80.0 2.1 %collective-permute-start.20 = (bf16[176,256]{1,0:T(8,128)(2,1)S(1)}, bf16[176,256]{1,0:T(8,128)(2,1)S(1)}, u32[]{:S(2)}, u32[]{:S(2)}) collective-permute-start(bf16[176,256]{1,0:T(8,128)(2,1)S(1)} %copy-done.13), channel_id=1, source_target_pairs={{0,6},{1,7},{2,4},{3,5},{4,2},{5,3},{6,0},{7,1},{8,14},{9,15},{10,... | collective-permute-start | bytes 270344 | tf_op jit(solution)/shard_map/t6/ppermute | solution.py:23
  82.0 5.2 %add_b.1 = (bf16[512,256]{1,0:T(8,128)(2,1)}, bf16[512,256]{1,0:T(8,128)(2,1)}, bf16[512,256]{1,0:T(8,128)(2,1)}, bf16[512,256]{1,0:T(8,128)(2,1)}, bf16[336,256...) custom-call(s32[16]{0:T(128)} %clip_ref.13, ...), custom_call_target="tpu_custom_call", output_to_operand_aliasing={{0}: (3, {}), {1}: (4, {}), {2}: (5, {}), {3}: (6, {})} | custom-call | bytes 26214400 | tf_op jit(solution)/shard_map/add_b/pallas_call | solution.py:226
  87.2 0.3 collective-permute-done.10.refs_4_
  87.5 0.0 collective-permute-start.11
  87.5 0.0 collective-permute-done.20.refs_6_
  87.5 2.2 %collective-permute-start.21 = (bf16[336,256]{1,0:T(8,128)(2,1)}, bf16[336,256]{1,0:T(8,128)(2,1)S(1)}, u32[]{:S(2)}, u32[]{:S(2)}) collective-permute-start(bf16[336,256]{1,0:T(8,128)(2,1)} %get-tuple-element.115), channel_id=1, source_target_pairs={{0,7},{1,6},{2,5},{3,4},{4,3},{5,2},{6,1},{7,0},{8,15},{9,14},{10,... | collective-permute-start | bytes 516104 | tf_op jit(solution)/shard_map/b7/ppermute | solution.py:23
  89.7 0.0 collective-permute-start.12
  89.7 1.6 %collective-permute-start.16 = (bf16[176,256]{1,0:T(8,128)(2,1)S(1)}, bf16[176,256]{1,0:T(8,128)(2,1)S(1)}, u32[]{:S(2)}, u32[]{:S(2)}) collective-permute-start(bf16[176,256]{1,0:T(8,128)(2,1)S(1)} %copy-done.12), channel_id=1, source_target_pairs={{0,5},{1,4},{2,7},{3,6},{4,1},{5,0},{6,3},{7,2},{8,13},{9,12},{10,... | collective-permute-start | bytes 270344 | tf_op jit(solution)/shard_map/t5/ppermute | solution.py:23
  91.3 10.2 %collective-permute-done.16.refs_5_ = bf16[176,256]{1,0:T(8,128)(2,1)S(1)} collective-permute-done((bf16[176,256]{1,0:T(8,128)(2,1)S(1)}, bf16[176,256]{1,0:T(8,128)(2,1)S(1)}, u32[]{:S(2)}, u32[]{:S(2)}) %collective-permute-start.16) | collective-permute-done | bytes 90144 | tf_op jit(solution)/shard_map/t5/ppermute | solution.py:23
  101.6 1.7 %collective-permute-start.17 = (bf16[336,256]{1,0:T(8,128)(2,1)}, bf16[336,256]{1,0:T(8,128)(2,1)S(1)}, u32[]{:S(2)}, u32[]{:S(2)}) collective-permute-start(bf16[336,256]{1,0:T(8,128)(2,1)} %get-tuple-element.107), channel_id=1, source_target_pairs={{0,6},{1,7},{2,4},{3,5},{4,2},{5,3},{6,0},{7,1},{8,14},{9,15},{10,... | collective-permute-start | bytes 516104 | tf_op jit(solution)/shard_map/b6/ppermute | solution.py:23
  103.3 0.0 collective-permute-done.21.refs_7_
  103.3 1.6 %collective-permute-start.24 = (bf16[336,256]{1,0:T(8,128)(2,1)}, bf16[336,256]{1,0:T(8,128)(2,1)S(1)}, u32[]{:S(2)}, u32[]{:S(2)}) collective-permute-start(bf16[336,256]{1,0:T(8,128)(2,1)} %get-tuple-element.120), channel_id=1, source_target_pairs={{0,5},{1,4},{2,7},{3,6},{4,1},{5,0},{6,3},{7,2},{8,13},{9,12},{10,... | collective-permute-start | bytes 516104 | tf_op jit(solution)/shard_map/b5/ppermute | solution.py:23
  104.9 0.0 collective-permute-done.11.refs_1_
  104.9 0.7 collective-permute-start.26
  105.7 0.0 collective-permute-done.12.refs_2_
  105.7 1.0 collective-permute-start.27
  106.7 0.0 copy-start.6
  106.7 0.0 copy-start.8
  106.7 1.0 collective-permute-start.22
  107.7 0.1 copy-done.8
  107.8 5.0 %add_c.1 = (bf16[336,256]{1,0:T(8,128)(2,1)}, bf16[336,256]{1,0:T(8,128)(2,1)}, bf16[336,256]{1,0:T(8,128)(2,1)}, bf16[336,256]{1,0:T(8,128)(2,1)}, bf16[336,256...) custom-call(s32[16]{0:T(128)} %clip_ref.13, ...), custom_call_target="tpu_custom_call" | custom-call | bytes 26214400 | tf_op jit(solution)/shard_map/add_c/pallas_call | solution.py:226
  112.8 0.0 collective-permute-done.17.refs_6_
  112.8 2.1 %collective-permute-start.18 = (bf16[336,256]{1,0:T(8,128)(2,1)}, bf16[336,256]{1,0:T(8,128)(2,1)S(1)}, u32[]{:S(2)}, u32[]{:S(2)}) collective-permute-start(bf16[336,256]{1,0:T(8,128)(2,1)} %get-tuple-element.108), channel_id=1, source_target_pairs={{0,7},{1,6},{2,5},{3,4},{4,3},{5,2},{6,1},{7,0},{8,15},{9,14},{10,... | collective-permute-start | bytes 516104 | tf_op jit(solution)/shard_map/c7/ppermute | solution.py:23
  114.9 5.5 %collective-permute-done.24.refs_5_ = bf16[336,256]{1,0:T(8,128)(2,1)S(1)} collective-permute-done((bf16[336,256]{1,0:T(8,128)(2,1)}, bf16[336,256]{1,0:T(8,128)(2,1)S(1)}, u32[]{:S(2)}, u32[]{:S(2)}) %collective-permute-start.24) | collective-permute-done | bytes 172064 | tf_op jit(solution)/shard_map/b5/ppermute | solution.py:23
  120.4 1.7 %collective-permute-start.25 = (bf16[336,256]{1,0:T(8,128)(2,1)}, bf16[336,256]{1,0:T(8,128)(2,1)S(1)}, u32[]{:S(2)}, u32[]{:S(2)}) collective-permute-start(bf16[336,256]{1,0:T(8,128)(2,1)} %get-tuple-element.121), channel_id=1, source_target_pairs={{0,6},{1,7},{2,4},{3,5},{4,2},{5,3},{6,0},{7,1},{8,14},{9,15},{10,... | collective-permute-start | bytes 516104 | tf_op jit(solution)/shard_map/c6/ppermute | solution.py:23
  122.2 13.0 %collective-permute-done.22.refs_4_ = bf16[336,256]{1,0:T(8,128)(2,1)S(1)} collective-permute-done((bf16[336,256]{1,0:T(8,128)(2,1)}, bf16[336,256]{1,0:T(8,128)(2,1)S(1)}, u32[]{:S(2)}, u32[]{:S(2)}) %collective-permute-start.22) | collective-permute-done | bytes 172064 | tf_op jit(solution)/shard_map/b4/ppermute | solution.py:23
  135.2 0.0 collective-permute-start.23
  135.2 0.0 collective-permute-start.13
  135.2 0.0 collective-permute-done.27.refs_11_
  135.2 8.0 %collective-permute-start.14 = (bf16[336,256]{1,0:T(8,128)(2,1)}, bf16[336,256]{1,0:T(8,128)(2,1)S(1)}, u32[]{:S(2)}, u32[]{:S(2)}) collective-permute-start(bf16[336,256]{1,0:T(8,128)(2,1)} %get-tuple-element.100), channel_id=1, source_target_pairs={{0,2},{1,3},{2,0},{3,1},{4,6},{5,7},{6,4},{7,5},{8,10},{9,11},{10,... | collective-permute-start | bytes 516104 | tf_op jit(solution)/shard_map/c2/ppermute | solution.py:23
  143.2 0.0 collective-permute-done.26.refs_3_
  143.2 0.0 collective-permute-start.15
  143.2 0.0 collective-permute-done.25.refs_6_
  143.2 3.9 %collective-permute-start.19 = (bf16[336,256]{1,0:T(8,128)(2,1)}, bf16[336,256]{1,0:T(8,128)(2,1)S(1)}, u32[]{:S(2)}, u32[]{:S(2)}) collective-permute-start(bf16[336,256]{1,0:T(8,128)(2,1)} %get-tuple-element.109), channel_id=1, source_target_pairs={{0,4},{1,5},{2,6},{3,7},{4,0},{5,1},{6,2},{7,3},{8,12},{9,13},{10,... | collective-permute-start | bytes 516104 | tf_op jit(solution)/shard_map/c4/ppermute | solution.py:23
  147.1 4.7 %norm_a.1 = (bf16[4,8,4,80,256]{4,3,2,1,0:T(8,128)(2,1)}, f32[8,256]{1,0:T(8,128)}) custom-call(bf16[512,256]{1,0:T(8,128)(2,1)S(1)} %copy-done, bf16[512,256]{1,0:T(8,128)(2,1)S(1)} %collective-permute-done.11.refs_1_, bf16[512,256]{1,0:T(8,128)(2,1)S(1)} %collective-permute-done.12.refs_2_, bf16[512,256]{1,0:T(8,128)(2,1)S(1)} %collective-permute-done.26.refs_3_, ...), custom_call_target="tpu_custom_call" | custom-call | flops 10485760 | bytes 5242880 | tf_op jit(solution)/shard_map/norm_a/pallas_call | solution.py:338
  151.8 2.1 %norm_b.1 = (bf16[4,8,4,80,256]{4,3,2,1,0:T(8,128)(2,1)}, f32[8,256]{1,0:T(8,128)}) custom-call(bf16[512,256]{1,0:T(8,128)(2,1)S(1)} %copy-done, bf16[512,256]{1,0:T(8,128)(2,1)S(1)} %collective-permute-done.11.refs_1_, bf16[512,256]{1,0:T(8,128)(2,1)S(1)} %collective-permute-done.12.refs_2_, ...), custom_call_target="tpu_custom_call", output_to_operand_aliasing={{0}: (10, {})} | custom-call | flops 5242880 | bytes 2621440 | tf_op jit(solution)/shard_map/norm_b/pallas_call | solution.py:338
  154.0 1.9 %collective-permute-done.14.refs_2_ = bf16[336,256]{1,0:T(8,128)(2,1)S(1)} collective-permute-done((bf16[336,256]{1,0:T(8,128)(2,1)}, bf16[336,256]{1,0:T(8,128)(2,1)S(1)}, u32[]{:S(2)}, u32[]{:S(2)}) %collective-permute-start.14) | collective-permute-done | bytes 172064 | tf_op jit(solution)/shard_map/c2/ppermute | solution.py:23
  155.9 3.2 %collective-permute-done.15.refs_3_ = bf16[336,256]{1,0:T(8,128)(2,1)S(1)} collective-permute-done((bf16[336,256]{1,0:T(8,128)(2,1)}, bf16[336,256]{1,0:T(8,128)(2,1)S(1)}, u32[]{:S(2)}, u32[]{:S(2)}) %collective-permute-start.15) | collective-permute-done | bytes 172064 | tf_op jit(solution)/shard_map/c3/ppermute | solution.py:23
  159.1 0.0 collective-permute-done.19.refs_4_
  159.1 2.2 %norm_c.1 = (bf16[4,8,4,80,256]{4,3,2,1,0:T(8,128)(2,1)}, f32[8,256]{1,0:T(8,128)}) custom-call(bf16[336,256]{1,0:T(8,128)(2,1)S(1)} %copy-done.4, bf16[336,256]{1,0:T(8,128)(2,1)S(1)} %collective-permute-done.13.refs_1_, bf16[336,256]{1,0:T(8,128)(2,1)S(1)} %collective-permute-done.14.refs_2_, ...), custom_call_target="tpu_custom_call", output_to_operand_aliasing={{0}: (10, {})} | custom-call | flops 5242880 | bytes 2621440 | tf_op jit(solution)/shard_map/norm_c/pallas_call | solution.py:338
  (35 shorter events, 0.1 us)
Async XLA Ops:
  1.4 22.9 %collective-permute-start = (bf16[4,1,1280,128]{3,2,1,0:T(8,128)(2,1)S(1)}, bf16[4,1,1280,128]{3,2,1,0:T(8,128)(2,1)S(1)}, u32[]{:S(2)}, u32[]{:S(2)}) collective-permute-start(bf16[4,1,1280,128]{3,2,1,0:T(8,128)(2,1)S(1)} %slice.3), channel_id=1, source_target_pairs={{0,1},{1,2},{2,3},{3,4},{4,5},{5,6},{6,7},{8,9},{9,10},{10,11},{11... | collective-permute-start | bytes 3932168 | tf_op jit(solution)/shard_map/halo/ppermute | solution.py:18
  18.4 19.1 %collective-permute-start.1 = (bf16[480,256]{1,0:T(8,128)(2,1)}, bf16[480,256]{1,0:T(8,128)(2,1)S(1)}, u32[]{:S(2)}, u32[]{:S(2)}) collective-permute-start(bf16[480,256]{1,0:T(8,128)(2,1)} %get-tuple-element.70), channel_id=1, source_target_pairs={{0,1},{1,0},{2,3},{3,2},{4,5},{5,4},{6,7},{7,6},{8,9},{9,8},{10,11... | collective-permute-start | bytes 737288 | tf_op jit(solution)/shard_map/a1/ppermute | solution.py:23
  20.3 29.2 %collective-permute-start.4 = (bf16[480,256]{1,0:T(8,128)(2,1)}, bf16[480,256]{1,0:T(8,128)(2,1)S(1)}, u32[]{:S(2)}, u32[]{:S(2)}) collective-permute-start(bf16[480,256]{1,0:T(8,128)(2,1)} %get-tuple-element.79), channel_id=1, source_target_pairs={{0,7},{1,6},{2,5},{3,4},{4,3},{5,2},{6,1},{7,0},{8,15},{9,14},{10,... | collective-permute-start | bytes 737288 | tf_op jit(solution)/shard_map/a7/ppermute | solution.py:23
  22.3 41.7 %collective-permute-start.5 = (bf16[480,256]{1,0:T(8,128)(2,1)}, bf16[480,256]{1,0:T(8,128)(2,1)}, u32[]{:S(2)}, u32[]{:S(2)}) collective-permute-start(bf16[480,256]{1,0:T(8,128)(2,1)} %get-tuple-element.80), channel_id=1, source_target_pairs={{0,6},{1,7},{2,4},{3,5},{4,2},{5,3},{6,0},{7,1},{8,14},{9,15},{10,... | collective-permute-start | bytes 737288 | tf_op jit(solution)/shard_map/a6/ppermute | solution.py:23
  23.8 40.2 %collective-permute-start.6 = (bf16[480,256]{1,0:T(8,128)(2,1)}, bf16[480,256]{1,0:T(8,128)(2,1)}, u32[]{:S(2)}, u32[]{:S(2)}) collective-permute-start(bf16[480,256]{1,0:T(8,128)(2,1)} %get-tuple-element.81), channel_id=1, source_target_pairs={{0,5},{1,4},{2,7},{3,6},{4,1},{5,0},{6,3},{7,2},{8,13},{9,12},{10,... | collective-permute-start | bytes 737288 | tf_op jit(solution)/shard_map/a5/ppermute | solution.py:23
  24.3 1.1 copy-start.7
  25.5 12.1 %copy-start.11 = (bf16[480,256]{1,0:T(8,128)(2,1)S(1)}, bf16[480,256]{1,0:T(8,128)(2,1)}, u32[]{:S(2)}) copy-start(bf16[480,256]{1,0:T(8,128)(2,1)} %get-tuple-element.75) | copy-start | bytes 737284
  34.1 34.1 %collective-permute-start.3 = (bf16[1,4,640,256]{3,2,1,0:T(8,128)(2,1)}, bf16[1,4,640,256]{3,2,1,0:T(8,128)(2,1)}, u32[]{:S(2)}, u32[]{:S(2)}) collective-permute-start(bf16[1,4,640,256]{3,2,1,0:T(8,128)(2,1)} %conv_hist0.1), channel_id=1, source_target_pairs={{0,8},{8,16},{16,24},{1,9},{9,17},{17,25},{2,10},{10,18},{18,26},{... | collective-permute-start | bytes 3932168 | tf_op jit(solution)/shard_map/hist0/ppermute | solution.py:18
  37.5 11.9 %copy-start.2 = (bf16[480,256]{1,0:T(8,128)(2,1)}, bf16[480,256]{1,0:T(8,128)(2,1)S(1)}, u32[]{:S(2)}) copy-start(bf16[480,256]{1,0:T(8,128)(2,1)S(1)} %collective-permute-done.1.refs_9_) | copy-start | bytes 737284
  37.5 11.9 %copy-start.10 = (bf16[480,256]{1,0:T(8,128)(2,1)S(1)}, bf16[480,256]{1,0:T(8,128)(2,1)}, u32[]{:S(2)}) copy-start(bf16[480,256]{1,0:T(8,128)(2,1)} %get-tuple-element.83) | copy-start | bytes 737284
  37.6 12.6 %collective-permute-start.2 = (bf16[480,256]{1,0:T(8,128)(2,1)S(1)}, bf16[480,256]{1,0:T(8,128)(2,1)S(1)}, u32[]{:S(2)}, u32[]{:S(2)}) collective-permute-start(bf16[480,256]{1,0:T(8,128)(2,1)S(1)} %copy-done.11), channel_id=1, source_target_pairs={{0,2},{1,3},{2,0},{3,1},{4,6},{5,7},{6,4},{7,5},{8,10},{9,11},{10,... | collective-permute-start | bytes 737288 | tf_op jit(solution)/shard_map/a2/ppermute | solution.py:23
  49.5 17.1 %collective-permute-start.7 = (bf16[480,256]{1,0:T(8,128)(2,1)S(1)}, bf16[480,256]{1,0:T(8,128)(2,1)S(1)}, u32[]{:S(2)}, u32[]{:S(2)}) collective-permute-start(bf16[480,256]{1,0:T(8,128)(2,1)S(1)} %copy-done.10), channel_id=1, source_target_pairs={{0,4},{1,5},{2,6},{3,7},{4,0},{5,1},{6,2},{7,3},{8,12},{9,13},{10,... | collective-permute-start | bytes 737288 | tf_op jit(solution)/shard_map/a4/ppermute | solution.py:23
  57.4 13.5 %copy-start.15 = (bf16[176,256]{1,0:T(8,128)(2,1)S(1)}, bf16[176,256]{1,0:T(8,128)(2,1)}, u32[]{:S(2)}) copy-start(bf16[176,256]{1,0:T(8,128)(2,1)} %get-tuple-element.92) | copy-start | bytes 270340
  57.4 19.8 %copy-start.14 = (bf16[176,256]{1,0:T(8,128)(2,1)S(1)}, bf16[176,256]{1,0:T(8,128)(2,1)}, u32[]{:S(2)}) copy-start(bf16[176,256]{1,0:T(8,128)(2,1)} %get-tuple-element.93) | copy-start | bytes 270340
  57.4 22.5 %copy-start.13 = (bf16[176,256]{1,0:T(8,128)(2,1)S(1)}, bf16[176,256]{1,0:T(8,128)(2,1)}, u32[]{:S(2)}) copy-start(bf16[176,256]{1,0:T(8,128)(2,1)} %get-tuple-element.114) | copy-start | bytes 270340
  68.2 38.5 %collective-permute-start.8 = (bf16[1,4,640,256]{3,2,1,0:T(8,128)(2,1)}, bf16[1,4,640,256]{3,2,1,0:T(8,128)(2,1)S(1)}, u32[]{:S(2)}, u32[]{:S(2)}) collective-permute-start(bf16[1,4,640,256]{3,2,1,0:T(8,128)(2,1)} %conv_hist1.1), channel_id=1, source_target_pairs={{0,8},{8,16},{16,24},{1,9},{9,17},{17,25},{2,10},{10,18},{18,26},{... | collective-permute-start | bytes 3932168 | tf_op jit(solution)/shard_map/hist1/ppermute | solution.py:18
  70.9 6.3 %collective-permute-start.9 = (bf16[176,256]{1,0:T(8,128)(2,1)S(1)}, bf16[176,256]{1,0:T(8,128)(2,1)S(1)}, u32[]{:S(2)}, u32[]{:S(2)}) collective-permute-start(bf16[176,256]{1,0:T(8,128)(2,1)S(1)} %copy-done.15), channel_id=1, source_target_pairs={{0,7},{1,6},{2,5},{3,4},{4,3},{5,2},{6,1},{7,0},{8,15},{9,14},{10,... | collective-permute-start | bytes 270344 | tf_op jit(solution)/shard_map/t7/ppermute | solution.py:23
  77.3 10.2 %collective-permute-start.10 = (bf16[176,256]{1,0:T(8,128)(2,1)S(1)}, bf16[176,256]{1,0:T(8,128)(2,1)S(1)}, u32[]{:S(2)}, u32[]{:S(2)}) collective-permute-start(bf16[176,256]{1,0:T(8,128)(2,1)S(1)} %copy-done.14), channel_id=1, source_target_pairs={{0,4},{1,5},{2,6},{3,7},{4,0},{5,1},{6,2},{7,3},{8,12},{9,13},{10,... | collective-permute-start | bytes 270344 | tf_op jit(solution)/shard_map/t4/ppermute | solution.py:23
  80.0 7.5 %collective-permute-start.20 = (bf16[176,256]{1,0:T(8,128)(2,1)S(1)}, bf16[176,256]{1,0:T(8,128)(2,1)S(1)}, u32[]{:S(2)}, u32[]{:S(2)}) collective-permute-start(bf16[176,256]{1,0:T(8,128)(2,1)S(1)} %copy-done.13), channel_id=1, source_target_pairs={{0,6},{1,7},{2,4},{3,5},{4,2},{5,3},{6,0},{7,1},{8,14},{9,15},{10,... | collective-permute-start | bytes 270344 | tf_op jit(solution)/shard_map/t6/ppermute | solution.py:23
  82.0 7.7 %copy-start.12 = (bf16[176,256]{1,0:T(8,128)(2,1)S(1)}, bf16[176,256]{1,0:T(8,128)(2,1)}, u32[]{:S(2)}) copy-start(bf16[176,256]{1,0:T(8,128)(2,1)} %get-tuple-element.106) | copy-start | bytes 270340
  82.0 23.7 %copy-start.9 = (bf16[480,256]{1,0:T(8,128)(2,1)S(1)}, bf16[480,256]{1,0:T(8,128)(2,1)}, u32[]{:S(2)}) copy-start(bf16[480,256]{1,0:T(8,128)(2,1)} %get-tuple-element.127) | copy-start | bytes 737284
  87.5 17.5 %collective-permute-start.11 = (bf16[512,256]{1,0:T(8,128)(2,1)}, bf16[512,256]{1,0:T(8,128)(2,1)S(1)}, u32[]{:S(2)}, u32[]{:S(2)}) collective-permute-start(bf16[512,256]{1,0:T(8,128)(2,1)} %get-tuple-element.94), channel_id=1, source_target_pairs={{0,1},{1,0},{2,3},{3,2},{4,5},{5,4},{6,7},{7,6},{8,9},{9,8},{10,11... | collective-permute-start | bytes 786440 | tf_op jit(solution)/shard_map/tb1/ppermute | solution.py:23
  87.5 15.8 %collective-permute-start.21 = (bf16[336,256]{1,0:T(8,128)(2,1)}, bf16[336,256]{1,0:T(8,128)(2,1)S(1)}, u32[]{:S(2)}, u32[]{:S(2)}) collective-permute-start(bf16[336,256]{1,0:T(8,128)(2,1)} %get-tuple-element.115), channel_id=1, source_target_pairs={{0,7},{1,6},{2,5},{3,4},{4,3},{5,2},{6,1},{7,0},{8,15},{9,14},{10,... | collective-permute-start | bytes 516104 | tf_op jit(solution)/shard_map/b7/ppermute | solution.py:23
  89.7 16.0 %collective-permute-start.12 = (bf16[512,256]{1,0:T(8,128)(2,1)}, bf16[512,256]{1,0:T(8,128)(2,1)S(1)}, u32[]{:S(2)}, u32[]{:S(2)}) collective-permute-start(bf16[512,256]{1,0:T(8,128)(2,1)} %get-tuple-element.96), channel_id=1, source_target_pairs={{0,2},{1,3},{2,0},{3,1},{4,6},{5,7},{6,4},{7,5},{8,10},{9,11},{10,... | collective-permute-start | bytes 786440 | tf_op jit(solution)/shard_map/tb2/ppermute | solution.py:23
  89.7 11.9 %collective-permute-start.16 = (bf16[176,256]{1,0:T(8,128)(2,1)S(1)}, bf16[176,256]{1,0:T(8,128)(2,1)S(1)}, u32[]{:S(2)}, u32[]{:S(2)}) collective-permute-start(bf16[176,256]{1,0:T(8,128)(2,1)S(1)} %copy-done.12), channel_id=1, source_target_pairs={{0,5},{1,4},{2,7},{3,6},{4,1},{5,0},{6,3},{7,2},{8,13},{9,12},{10,... | collective-permute-start | bytes 270344 | tf_op jit(solution)/shard_map/t5/ppermute | solution.py:23
  101.6 11.3 %collective-permute-start.17 = (bf16[336,256]{1,0:T(8,128)(2,1)}, bf16[336,256]{1,0:T(8,128)(2,1)S(1)}, u32[]{:S(2)}, u32[]{:S(2)}) collective-permute-start(bf16[336,256]{1,0:T(8,128)(2,1)} %get-tuple-element.107), channel_id=1, source_target_pairs={{0,6},{1,7},{2,4},{3,5},{4,2},{5,3},{6,0},{7,1},{8,14},{9,15},{10,... | collective-permute-start | bytes 516104 | tf_op jit(solution)/shard_map/b6/ppermute | solution.py:23
  103.3 17.1 %collective-permute-start.24 = (bf16[336,256]{1,0:T(8,128)(2,1)}, bf16[336,256]{1,0:T(8,128)(2,1)S(1)}, u32[]{:S(2)}, u32[]{:S(2)}) collective-permute-start(bf16[336,256]{1,0:T(8,128)(2,1)} %get-tuple-element.120), channel_id=1, source_target_pairs={{0,5},{1,4},{2,7},{3,6},{4,1},{5,0},{6,3},{7,2},{8,13},{9,12},{10,... | collective-permute-start | bytes 516104 | tf_op jit(solution)/shard_map/b5/ppermute | solution.py:23
  104.9 38.3 %collective-permute-start.26 = (bf16[512,256]{1,0:T(8,128)(2,1)}, bf16[512,256]{1,0:T(8,128)(2,1)S(1)}, u32[]{:S(2)}, u32[]{:S(2)}) collective-permute-start(bf16[512,256]{1,0:T(8,128)(2,1)} %get-tuple-element.124), channel_id=1, source_target_pairs={{0,3},{1,2},{2,1},{3,0},{4,7},{5,6},{6,5},{7,4},{8,11},{9,10},{10,... | collective-permute-start | bytes 786440 | tf_op jit(solution)/shard_map/tb3/ppermute | solution.py:23
  105.7 29.6 %collective-permute-start.27 = (bf16[480,256]{1,0:T(8,128)(2,1)S(1)}, bf16[480,256]{1,0:T(8,128)(2,1)S(1)}, u32[]{:S(2)}, u32[]{:S(2)}) collective-permute-start(bf16[480,256]{1,0:T(8,128)(2,1)S(1)} %copy-done.9), channel_id=1, source_target_pairs={{0,3},{1,2},{2,1},{3,0},{4,7},{5,6},{6,5},{7,4},{8,11},{9,10},{10,... | collective-permute-start | bytes 737288 | tf_op jit(solution)/shard_map/a3/ppermute | solution.py:23
  106.7 40.4 %copy-start = (bf16[512,256]{1,0:T(8,128)(2,1)S(1)}, bf16[512,256]{1,0:T(8,128)(2,1)}, u32[]{:S(2)}) copy-start(bf16[512,256]{1,0:T(8,128)(2,1)} %get-tuple-element.122.refs_0_) | copy-start | bytes 786436
  106.7 40.4 %copy-start.1 = (bf16[480,256]{1,0:T(8,128)(2,1)S(1)}, bf16[480,256]{1,0:T(8,128)(2,1)}, u32[]{:S(2)}) copy-start(bf16[480,256]{1,0:T(8,128)(2,1)} %get-tuple-element.125.refs_8_) | copy-start | bytes 737284
  106.7 40.4 %copy-start.3 = (bf16[480,256]{1,0:T(8,128)(2,1)S(1)}, bf16[480,256]{1,0:T(8,128)(2,1)}, u32[]{:S(2)}) copy-start(bf16[480,256]{1,0:T(8,128)(2,1)} %copy-done.2) | copy-start | bytes 737284
  106.7 40.4 %copy-start.5 = (f32[256]{0:T(256)S(1)}, f32[256]{0:T(256)}, u32[]{:S(2)}) copy-start(f32[256]{0:T(256)} %param.8) | copy-start | bytes 3076
  106.7 40.4 %copy-start.6 = (f32[256]{0:T(256)S(1)}, f32[256]{0:T(256)}, u32[]{:S(2)}) copy-start(f32[256]{0:T(256)} %param.9) | copy-start | bytes 3076
  106.7 1.1 copy-start.8
  106.7 28.5 %collective-permute-start.22 = (bf16[336,256]{1,0:T(8,128)(2,1)}, bf16[336,256]{1,0:T(8,128)(2,1)S(1)}, u32[]{:S(2)}, u32[]{:S(2)}) collective-permute-start(bf16[336,256]{1,0:T(8,128)(2,1)} %get-tuple-element.116), channel_id=1, source_target_pairs={{0,4},{1,5},{2,6},{3,7},{4,0},{5,1},{6,2},{7,3},{8,12},{9,13},{10,... | collective-permute-start | bytes 516104 | tf_op jit(solution)/shard_map/b4/ppermute | solution.py:23
  112.8 22.4 %collective-permute-start.18 = (bf16[336,256]{1,0:T(8,128)(2,1)}, bf16[336,256]{1,0:T(8,128)(2,1)S(1)}, u32[]{:S(2)}, u32[]{:S(2)}) collective-permute-start(bf16[336,256]{1,0:T(8,128)(2,1)} %get-tuple-element.108), channel_id=1, source_target_pairs={{0,7},{1,6},{2,5},{3,4},{4,3},{5,2},{6,1},{7,0},{8,15},{9,14},{10,... | collective-permute-start | bytes 516104 | tf_op jit(solution)/shard_map/c7/ppermute | solution.py:23
  120.4 22.8 %collective-permute-start.25 = (bf16[336,256]{1,0:T(8,128)(2,1)}, bf16[336,256]{1,0:T(8,128)(2,1)S(1)}, u32[]{:S(2)}, u32[]{:S(2)}) collective-permute-start(bf16[336,256]{1,0:T(8,128)(2,1)} %get-tuple-element.121), channel_id=1, source_target_pairs={{0,6},{1,7},{2,4},{3,5},{4,2},{5,3},{6,0},{7,1},{8,14},{9,15},{10,... | collective-permute-start | bytes 516104 | tf_op jit(solution)/shard_map/c6/ppermute | solution.py:23
  135.2 18.8 %collective-permute-start.23 = (bf16[336,256]{1,0:T(8,128)(2,1)}, bf16[336,256]{1,0:T(8,128)(2,1)S(1)}, u32[]{:S(2)}, u32[]{:S(2)}) collective-permute-start(bf16[336,256]{1,0:T(8,128)(2,1)} %get-tuple-element.117), channel_id=1, source_target_pairs={{0,5},{1,4},{2,7},{3,6},{4,1},{5,0},{6,3},{7,2},{8,13},{9,12},{10,... | collective-permute-start | bytes 516104 | tf_op jit(solution)/shard_map/c5/ppermute | solution.py:23
  135.2 18.8 %collective-permute-start.13 = (bf16[336,256]{1,0:T(8,128)(2,1)}, bf16[336,256]{1,0:T(8,128)(2,1)S(1)}, u32[]{:S(2)}, u32[]{:S(2)}) collective-permute-start(bf16[336,256]{1,0:T(8,128)(2,1)} %get-tuple-element.99), channel_id=1, source_target_pairs={{0,1},{1,0},{2,3},{3,2},{4,5},{5,4},{6,7},{7,6},{8,9},{9,8},{10,11... | collective-permute-start | bytes 516104 | tf_op jit(solution)/shard_map/c1/ppermute | solution.py:23
  135.2 20.7 %collective-permute-start.14 = (bf16[336,256]{1,0:T(8,128)(2,1)}, bf16[336,256]{1,0:T(8,128)(2,1)S(1)}, u32[]{:S(2)}, u32[]{:S(2)}) collective-permute-start(bf16[336,256]{1,0:T(8,128)(2,1)} %get-tuple-element.100), channel_id=1, source_target_pairs={{0,2},{1,3},{2,0},{3,1},{4,6},{5,7},{6,4},{7,5},{8,10},{9,11},{10,... | collective-permute-start | bytes 516104 | tf_op jit(solution)/shard_map/c2/ppermute | solution.py:23
  143.2 15.9 %collective-permute-start.15 = (bf16[336,256]{1,0:T(8,128)(2,1)}, bf16[336,256]{1,0:T(8,128)(2,1)S(1)}, u32[]{:S(2)}, u32[]{:S(2)}) collective-permute-start(bf16[336,256]{1,0:T(8,128)(2,1)} %get-tuple-element.101), channel_id=1, source_target_pairs={{0,3},{1,2},{2,1},{3,0},{4,7},{5,6},{6,5},{7,4},{8,11},{9,10},{10,... | collective-permute-start | bytes 516104 | tf_op jit(solution)/shard_map/c3/ppermute | solution.py:23
  143.2 15.8 %collective-permute-start.19 = (bf16[336,256]{1,0:T(8,128)(2,1)}, bf16[336,256]{1,0:T(8,128)(2,1)S(1)}, u32[]{:S(2)}, u32[]{:S(2)}) collective-permute-start(bf16[336,256]{1,0:T(8,128)(2,1)} %get-tuple-element.109), channel_id=1, source_target_pairs={{0,4},{1,5},{2,6},{3,7},{4,0},{5,1},{6,2},{7,3},{8,12},{9,13},{10,... | collective-permute-start | bytes 516104 | tf_op jit(solution)/shard_map/c4/ppermute | solution.py:23
  151.8 7.2 %copy-start.4 = (bf16[336,256]{1,0:T(8,128)(2,1)S(1)}, bf16[336,256]{1,0:T(8,128)(2,1)}, u32[]{:S(2)}) copy-start(bf16[336,256]{1,0:T(8,128)(2,1)} %get-tuple-element.98.refs_0_) | copy-start | bytes 516100

commit v10 on v9

--- a/solution.py
+++ b/solution.py
@@ -382,10 +382,10 @@
     far = [flip for flip in range(parts - 1, 0, -1) if 2 * flip >= parts]
     chain = []
 
-    def send_far(name, sent):
+    def send_far(name, sent, deep=3):
         got = {}
         for flip in far:
-            before = chain[-3:][:1] if len(chain) >= 3 else []
+            before = chain[-deep:][:1] if len(chain) >= deep else []
             got[flip] = named(f"{name}{flip}", exchanged, after(sent[flip], *before), "rows", flip)
             chain.append(got[flip])
         return got
@@ -442,8 +442,8 @@
         "add_b", run, 0, 0, [(0, [], (0, 1))], addends=(own[0], after(first_add, a_sums)), kept=kept,
         weigh=20, vmem=56,
         layout=layout((0, STAT_ROWS, one_rows), (top_rows, top_rows + STAT_ROWS, near_rows)))
-    b_got = send_far("b", b_sent)
-    b_got.update(send_near("tb", b_sent, False, t_got[far[-1]]))
+    b_got = send_far("b", b_sent, 4)
+    b_got.update(send_near("tb", b_sent, False, b_got[far[0]]))
     c_sent = named(
         "add_c", run, 0, 0, [(1, [], (0, 1))], addends=(own[1], after(second_add, b_got[near[0]], b_got[near[1]])),
         weigh=20, vmem=56, layout=[(0, STAT_ROWS, one_rows)] * parts)

time: 163 us -> 163 us (level)
  waiting for transfers between devices: 43.8 us -> 28.3 us
  starting transfers between devices: 47.7 us -> 62.5 us
    ppermute x25, waiting for transfers between devices: 42.2 us -> 26.6 us  [exchanged(): return lax.ppermute(array, axis, [(i, i ^ flip) for i in range(length)])]
    ppermute x25, starting transfers between devices: 39.8 us -> 54.6 us  [exchanged(): return lax.ppermute(array, axis, [(i, i ^ flip) for i in range(length)])]
  transfers between devices with their start and end apart: 28 -> 28, of which waited for: 9 -> 10; matrix products, arithmetic and copies ran while one was open for 0% -> 0% of each run, Pallas kernels for 40% -> 40%
where the time goes in v10:
time: 163 us; the launch traced here: 160 us
  Pallas kernels  66.8 us (41%)
  starting transfers between devices  62.5 us (38%)
  waiting for transfers between devices  28.3 us (17%)
  local copies, waits for them, and re-layouts  2.59 us (2%)
    pallas_call x7, Pallas kernels, conv_frames(): pl.pallas_call(functools.partial(conv_kernel, plan), out_shape=out_shape,...  57.8 us
    ppermute x25, starting transfers between devices, exchanged(): return lax.ppermute(array, axis, [(i, i ^ flip) for i in range(length)])  54.6 us
    ppermute x25, waiting for transfers between devices, exchanged(): return lax.ppermute(array, axis, [(i, i ^ flip) for i in range(length)])  26.6 us
    pallas_call x3, Pallas kernels, norm_frames(): pl.pallas_call(functools.partial(norm_kernel, plan), out_shape=[jax.Shape...  9 us
    ppermute x3, starting transfers between devices, passed_along(): return lax.ppermute(array, axis, pairs)  7.89 us
  transfers between devices with their start and end apart: 28, of which 10 were waited for; matrix products, arithmetic and copies ran while one was open for 0% of the time, Pallas kernels for 40%

profile of v10, /device:TPU:4, one launch (start us, length us, event | category | flops | bytes accessed | tf_op | source)
XLA Modules:
  0.0 160.5 jit_solution(7657201812495784035)
XLA Ops:
  0.0 1.4 slice.3
  1.4 1.8 %collective-permute-start = (bf16[4,1,1280,128]{3,2,1,0:T(8,128)(2,1)S(1)}, bf16[4,1,1280,128]{3,2,1,0:T(8,128)(2,1)S(1)}, u32[]{:S(2)}, u32[]{:S(2)}) collective-permute-start(bf16[4,1,1280,128]{3,2,1,0:T(8,128)(2,1)S(1)} %slice.3), channel_id=1, source_target_pairs={{0,1},{1,2},{2,3},{3,4},{4,5},{5,6},{6,7},{8,9},{9,10},{10,11},{11... | collective-permute-start | bytes 3932168 | tf_op jit(solution)/shard_map/halo/ppermute | solution.py:18
  3.2 15.2 %conv_a.1 = (bf16[480,256]{1,0:T(8,128)(2,1)}, bf16[480,256]{1,0:T(8,128)(2,1)}, bf16[480,256]{1,0:T(8,128)(2,1)}, bf16[480,256]{1,0:T(8,128)(2,1)}, bf16[480,25...) custom-call(s32[16]{0:T(128)} %clip_ref.13, ...), custom_call_target="tpu_custom_call" | custom-call | flops 6794772480 | bytes 9830400 | tf_op jit(solution)/shard_map/conv_a/pallas_call | solution.py:226
  18.4 1.8 %collective-permute-start.1 = (bf16[480,256]{1,0:T(8,128)(2,1)}, bf16[480,256]{1,0:T(8,128)(2,1)S(1)}, u32[]{:S(2)}, u32[]{:S(2)}) collective-permute-start(bf16[480,256]{1,0:T(8,128)(2,1)} %get-tuple-element.70), channel_id=1, source_target_pairs={{0,1},{1,0},{2,3},{3,2},{4,5},{5,4},{6,7},{7,6},{8,9},{9,8},{10,11... | collective-permute-start | bytes 737288 | tf_op jit(solution)/shard_map/a1/ppermute | solution.py:23
  20.3 2.1 %collective-permute-start.4 = (bf16[480,256]{1,0:T(8,128)(2,1)}, bf16[480,256]{1,0:T(8,128)(2,1)S(1)}, u32[]{:S(2)}, u32[]{:S(2)}) collective-permute-start(bf16[480,256]{1,0:T(8,128)(2,1)} %get-tuple-element.79), channel_id=1, source_target_pairs={{0,7},{1,6},{2,5},{3,4},{4,3},{5,2},{6,1},{7,0},{8,15},{9,14},{10,... | collective-permute-start | bytes 737288 | tf_op jit(solution)/shard_map/a7/ppermute | solution.py:23
  22.3 1.5 collective-permute-start.5
  23.8 0.6 collective-permute-start.6
  24.3 0.0 collective-permute-done.refs_2_.refs_3_.refs_4_.refs_5_.refs_6_.refs_7_.refs_1_
  24.3 1.1 copy-done.7
  25.5 8.6 %conv_hist0.1 = bf16[1,4,640,256]{3,2,1,0:T(8,128)(2,1)} custom-call(s32[16]{0:T(128)} %clip_ref.13, bf16[4,8,1280,128]{3,2,1,0:T(8,128)(2,1)} %refs_0_.9, bf16[4,8,1280,128]{3,2,1,0:T(8,128)(2,1)} %refs_0_.9, bf16[4,1,1280,128]{3,2,1,0:T(8,128)(2,1)} %copy-done.7, bf16[4,1,1280,128]{3,2,1,0:T(8,128)(2,1)} %copy-done.7, bf16[3,1152,256]{2,1,0:T(8,128)(2,1)} %bitcast.13, ...), custom_call_target="tpu_custom_call" | custom-call | flops 3019898880 | bytes 6553600 | tf_op jit(solution)/shard_map/conv_hist0/pallas_call | solution.py:226
  34.1 3.4 %collective-permute-start.3 = (bf16[1,4,640,256]{3,2,1,0:T(8,128)(2,1)}, bf16[1,4,640,256]{3,2,1,0:T(8,128)(2,1)}, u32[]{:S(2)}, u32[]{:S(2)}) collective-permute-start(bf16[1,4,640,256]{3,2,1,0:T(8,128)(2,1)} %conv_hist0.1), channel_id=1, source_target_pairs={{0,8},{8,16},{16,24},{1,9},{9,17},{17,25},{2,10},{10,18},{18,26},{... | collective-permute-start | bytes 3932168 | tf_op jit(solution)/shard_map/hist0/ppermute | solution.py:18
  37.6 1.8 %collective-permute-start.2 = (bf16[480,256]{1,0:T(8,128)(2,1)S(1)}, bf16[480,256]{1,0:T(8,128)(2,1)S(1)}, u32[]{:S(2)}, u32[]{:S(2)}) collective-permute-start(bf16[480,256]{1,0:T(8,128)(2,1)S(1)} %copy-done.11), channel_id=1, source_target_pairs={{0,2},{1,3},{2,0},{3,1},{4,6},{5,7},{6,4},{7,5},{8,10},{9,11},{10,... | collective-permute-start | bytes 737288 | tf_op jit(solution)/shard_map/a2/ppermute | solution.py:23
  39.4 10.1 %conv_own.1 = (f32[1,4,640,256]{3,2,1,0:T(8,128)}, f32[1,4,640,256]{3,2,1,0:T(8,128)}) custom-call(s32[16]{0:T(128)} %clip_ref.13, bf16[4,8,1280,128]{3,2,1,0:T(8,128)(2,1)} %refs_0_.9, bf16[4,8,1280,128]{3,2,1,0:T(8,128)(2,1)} %refs_0_.9, bf16[4,1,1280,128]{3,2,1,0:T(8,128)(2,1)} %copy-done.7, bf16[4,1,1280,128]{3,2,1,0:T(8,128)(2,1)} %copy-done.7, ...), custom_call_target="tpu_custom_call" | custom-call | flops 90596966400 | bytes 157286400 | tf_op jit(solution)/shard_map/conv_own/pallas_call | solution.py:226
  49.5 0.7 collective-permute-start.7
  50.2 7.3 %conv_top.1 = (bf16[512,256]{1,0:T(8,128)(2,1)}, bf16[512,256]{1,0:T(8,128)(2,1)}, bf16[512,256]{1,0:T(8,128)(2,1)}, bf16[512,256]{1,0:T(8,128)(2,1)}, bf16[176,...) custom-call(s32[16]{0:T(128)} %clip_ref.13, ...), custom_call_target="tpu_custom_call" | custom-call | flops 45298483200 | bytes 65536000 | tf_op jit(solution)/shard_map/conv_top/pallas_call | solution.py:226
  57.4 6.5 %conv_hist1.1 = bf16[1,4,640,256]{3,2,1,0:T(8,128)(2,1)} custom-call(s32[16]{0:T(128)} %clip_ref.13, bf16[4,8,1280,128]{3,2,1,0:T(8,128)(2,1)} %refs_0_.9, bf16[4,1,1280,128]{3,2,1,0:T(8,128)(2,1)} %copy-done.7, bf16[3,1152,256]{2,1,0:T(8,128)(2,1)} %bitcast.20), custom_call_target="tpu_custom_call" | custom-call | flops 30198988800 | bytes 78643200 | tf_op jit(solution)/shard_map/conv_hist1/pallas_call | solution.py:226
  64.0 0.0 collective-permute-done.5.refs_14_
  64.0 0.0 collective-permute-done.6.refs_13_
  64.0 2.6 %collective-permute-done.7.refs_12_ = bf16[480,256]{1,0:T(8,128)(2,1)S(1)} collective-permute-done((bf16[480,256]{1,0:T(8,128)(2,1)S(1)}, bf16[480,256]{1,0:T(8,128)(2,1)S(1)}, u32[]{:S(2)}, u32[]{:S(2)}) %collective-permute-start.7) | collective-permute-done | bytes 245792 | tf_op jit(solution)/shard_map/a4/ppermute | solution.py:23
  66.6 1.6 %collective-permute-done.3.refs_1_ = bf16[1,4,640,256]{3,2,1,0:T(8,128)(2,1)} collective-permute-done((bf16[1,4,640,256]{3,2,1,0:T(8,128)(2,1)}, bf16[1,4,640,256]{3,2,1,0:T(8,128)(2,1)}, u32[]{:S(2)}, u32[]{:S(2)}) %collective-permute-start.3) | collective-permute-done | bytes 1310752 | tf_op jit(solution)/shard_map/hist0/ppermute | solution.py:18
  68.2 2.7 %collective-permute-start.8 = (bf16[1,4,640,256]{3,2,1,0:T(8,128)(2,1)}, bf16[1,4,640,256]{3,2,1,0:T(8,128)(2,1)S(1)}, u32[]{:S(2)}, u32[]{:S(2)}) collective-permute-start(bf16[1,4,640,256]{3,2,1,0:T(8,128)(2,1)} %conv_hist1.1), channel_id=1, source_target_pairs={{0,8},{8,16},{16,24},{1,9},{9,17},{17,25},{2,10},{10,18},{18,26},{... | collective-permute-start | bytes 3932168 | tf_op jit(solution)/shard_map/hist1/ppermute | solution.py:18
  70.9 1.0 collective-permute-start.9
  71.9 5.2 %add_b.1 = (bf16[512,256]{1,0:T(8,128)(2,1)}, bf16[512,256]{1,0:T(8,128)(2,1)}, bf16[512,256]{1,0:T(8,128)(2,1)}, bf16[512,256]{1,0:T(8,128)(2,1)}, bf16[336,256...) custom-call(s32[16]{0:T(128)} %clip_ref.13, ...), custom_call_target="tpu_custom_call", output_to_operand_aliasing={{0}: (3, {}), {1}: (4, {}), {2}: (5, {}), {3}: (6, {})} | custom-call | bytes 26214400 | tf_op jit(solution)/shard_map/add_b/pallas_call | solution.py:226
  77.1 0.1 collective-permute-done.9.refs_7_
  77.3 2.6 %collective-permute-start.10 = (bf16[336,256]{1,0:T(8,128)(2,1)}, bf16[336,256]{1,0:T(8,128)(2,1)S(1)}, u32[]{:S(2)}, u32[]{:S(2)}) collective-permute-start(bf16[336,256]{1,0:T(8,128)(2,1)} %get-tuple-element.93), channel_id=1, source_target_pairs={{0,7},{1,6},{2,5},{3,4},{4,3},{5,2},{6,1},{7,0},{8,15},{9,14},{10,... | collective-permute-start | bytes 516104 | tf_op jit(solution)/shard_map/b7/ppermute | solution.py:23
  79.8 1.8 %collective-permute-start.16 = (bf16[176,256]{1,0:T(8,128)(2,1)S(1)}, bf16[176,256]{1,0:T(8,128)(2,1)S(1)}, u32[]{:S(2)}, u32[]{:S(2)}) collective-permute-start(bf16[176,256]{1,0:T(8,128)(2,1)S(1)} %copy-done.14), channel_id=1, source_target_pairs={{0,6},{1,7},{2,4},{3,5},{4,2},{5,3},{6,0},{7,1},{8,14},{9,15},{10,... | collective-permute-start | bytes 270344 | tf_op jit(solution)/shard_map/t6/ppermute | solution.py:23
  81.6 3.4 %collective-permute-done.10.refs_7_ = bf16[336,256]{1,0:T(8,128)(2,1)S(1)} collective-permute-done((bf16[336,256]{1,0:T(8,128)(2,1)}, bf16[336,256]{1,0:T(8,128)(2,1)S(1)}, u32[]{:S(2)}, u32[]{:S(2)}) %collective-permute-start.10) | collective-permute-done | bytes 172064 | tf_op jit(solution)/shard_map/b7/ppermute | solution.py:23
  85.0 1.8 %collective-permute-start.11 = (bf16[512,256]{1,0:T(8,128)(2,1)}, bf16[512,256]{1,0:T(8,128)(2,1)S(1)}, u32[]{:S(2)}, u32[]{:S(2)}) collective-permute-start(bf16[512,256]{1,0:T(8,128)(2,1)} %get-tuple-element.94), channel_id=1, source_target_pairs={{0,1},{1,0},{2,3},{3,2},{4,5},{5,4},{6,7},{7,6},{8,9},{9,8},{10,11... | collective-permute-start | bytes 786440 | tf_op jit(solution)/shard_map/tb1/ppermute | solution.py:23
  86.8 5.4 %collective-permute-start.12 = (bf16[512,256]{1,0:T(8,128)(2,1)}, bf16[512,256]{1,0:T(8,128)(2,1)S(1)}, u32[]{:S(2)}, u32[]{:S(2)}) collective-permute-start(bf16[512,256]{1,0:T(8,128)(2,1)} %get-tuple-element.96), channel_id=1, source_target_pairs={{0,2},{1,3},{2,0},{3,1},{4,6},{5,7},{6,4},{7,5},{8,10},{9,11},{10,... | collective-permute-start | bytes 786440 | tf_op jit(solution)/shard_map/tb2/ppermute | solution.py:23
  92.3 0.3 collective-permute-start.23
  92.6 0.0 collective-permute-done.16.refs_6_
  92.6 2.3 %collective-permute-start.20 = (bf16[176,256]{1,0:T(8,128)(2,1)S(1)}, bf16[176,256]{1,0:T(8,128)(2,1)S(1)}, u32[]{:S(2)}, u32[]{:S(2)}) collective-permute-start(bf16[176,256]{1,0:T(8,128)(2,1)S(1)} %copy-done.12), channel_id=1, source_target_pairs={{0,4},{1,5},{2,6},{3,7},{4,0},{5,1},{6,2},{7,3},{8,12},{9,13},{10,... | collective-permute-start | bytes 270344 | tf_op jit(solution)/shard_map/t4/ppermute | solution.py:23
  94.9 6.2 %collective-permute-done.23.refs_5_ = bf16[176,256]{1,0:T(8,128)(2,1)S(1)} collective-permute-done((bf16[176,256]{1,0:T(8,128)(2,1)S(1)}, bf16[176,256]{1,0:T(8,128)(2,1)S(1)}, u32[]{:S(2)}, u32[]{:S(2)}) %collective-permute-start.23) | collective-permute-done | bytes 90144 | tf_op jit(solution)/shard_map/t5/ppermute | solution.py:23
  101.0 2.1 %collective-permute-start.17 = (bf16[336,256]{1,0:T(8,128)(2,1)}, bf16[336,256]{1,0:T(8,128)(2,1)S(1)}, u32[]{:S(2)}, u32[]{:S(2)}) collective-permute-start(bf16[336,256]{1,0:T(8,128)(2,1)} %get-tuple-element.107), channel_id=1, source_target_pairs={{0,6},{1,7},{2,4},{3,5},{4,2},{5,3},{6,0},{7,1},{8,14},{9,15},{10,... | collective-permute-start | bytes 516104 | tf_op jit(solution)/shard_map/b6/ppermute | solution.py:23
  103.2 1.8 %collective-permute-start.24 = (bf16[336,256]{1,0:T(8,128)(2,1)}, bf16[336,256]{1,0:T(8,128)(2,1)S(1)}, u32[]{:S(2)}, u32[]{:S(2)}) collective-permute-start(bf16[336,256]{1,0:T(8,128)(2,1)} %get-tuple-element.120), channel_id=1, source_target_pairs={{0,5},{1,4},{2,7},{3,6},{4,1},{5,0},{6,3},{7,2},{8,13},{9,12},{10,... | collective-permute-start | bytes 516104 | tf_op jit(solution)/shard_map/b5/ppermute | solution.py:23
  104.9 0.0 collective-permute-done.11.refs_1_
  104.9 0.2 collective-permute-start.26
  105.2 0.0 collective-permute-done.12.refs_2_
  105.2 1.5 collective-permute-start.27
  106.7 0.0 copy-start.6
  106.7 0.0 copy-start.8
  106.7 1.5 collective-permute-start.21
  108.2 5.0 %add_c.1 = (bf16[336,256]{1,0:T(8,128)(2,1)}, bf16[336,256]{1,0:T(8,128)(2,1)}, bf16[336,256]{1,0:T(8,128)(2,1)}, bf16[336,256]{1,0:T(8,128)(2,1)}, bf16[336,256...) custom-call(s32[16]{0:T(128)} %clip_ref.13, ...), custom_call_target="tpu_custom_call" | custom-call | bytes 26214400 | tf_op jit(solution)/shard_map/add_c/pallas_call | solution.py:226
  113.3 0.0 collective-permute-done.17.refs_6_
  113.3 1.9 %collective-permute-start.18 = (bf16[336,256]{1,0:T(8,128)(2,1)}, bf16[336,256]{1,0:T(8,128)(2,1)S(1)}, u32[]{:S(2)}, u32[]{:S(2)}) collective-permute-start(bf16[336,256]{1,0:T(8,128)(2,1)} %get-tuple-element.108), channel_id=1, source_target_pairs={{0,7},{1,6},{2,5},{3,4},{4,3},{5,2},{6,1},{7,0},{8,15},{9,14},{10,... | collective-permute-start | bytes 516104 | tf_op jit(solution)/shard_map/c7/ppermute | solution.py:23
  115.2 4.3 %collective-permute-done.24.refs_5_ = bf16[336,256]{1,0:T(8,128)(2,1)S(1)} collective-permute-done((bf16[336,256]{1,0:T(8,128)(2,1)}, bf16[336,256]{1,0:T(8,128)(2,1)S(1)}, u32[]{:S(2)}, u32[]{:S(2)}) %collective-permute-start.24) | collective-permute-done | bytes 172064 | tf_op jit(solution)/shard_map/b5/ppermute | solution.py:23
  119.5 2.0 %collective-permute-start.25 = (bf16[336,256]{1,0:T(8,128)(2,1)}, bf16[336,256]{1,0:T(8,128)(2,1)S(1)}, u32[]{:S(2)}, u32[]{:S(2)}) collective-permute-start(bf16[336,256]{1,0:T(8,128)(2,1)} %get-tuple-element.121), channel_id=1, source_target_pairs={{0,6},{1,7},{2,4},{3,5},{4,2},{5,3},{6,0},{7,1},{8,14},{9,15},{10,... | collective-permute-start | bytes 516104 | tf_op jit(solution)/shard_map/c6/ppermute | solution.py:23
  121.5 2.3 %collective-permute-done.21.refs_4_ = bf16[336,256]{1,0:T(8,128)(2,1)S(1)} collective-permute-done((bf16[336,256]{1,0:T(8,128)(2,1)}, bf16[336,256]{1,0:T(8,128)(2,1)S(1)}, u32[]{:S(2)}, u32[]{:S(2)}) %collective-permute-start.21) | collective-permute-done | bytes 172064 | tf_op jit(solution)/shard_map/b4/ppermute | solution.py:23
  123.9 4.4 %collective-permute-start.22 = (bf16[336,256]{1,0:T(8,128)(2,1)}, bf16[336,256]{1,0:T(8,128)(2,1)S(1)}, u32[]{:S(2)}, u32[]{:S(2)}) collective-permute-start(bf16[336,256]{1,0:T(8,128)(2,1)} %get-tuple-element.115), channel_id=1, source_target_pairs={{0,5},{1,4},{2,7},{3,6},{4,1},{5,0},{6,3},{7,2},{8,13},{9,12},{10,... | collective-permute-start | bytes 516104 | tf_op jit(solution)/shard_map/c5/ppermute | solution.py:23
  128.3 2.5 %collective-permute-done.18.refs_7_ = bf16[336,256]{1,0:T(8,128)(2,1)S(1)} collective-permute-done((bf16[336,256]{1,0:T(8,128)(2,1)}, bf16[336,256]{1,0:T(8,128)(2,1)S(1)}, u32[]{:S(2)}, u32[]{:S(2)}) %collective-permute-start.18) | collective-permute-done | bytes 172064 | tf_op jit(solution)/shard_map/c7/ppermute | solution.py:23
  130.8 6.9 %collective-permute-start.13 = (bf16[336,256]{1,0:T(8,128)(2,1)}, bf16[336,256]{1,0:T(8,128)(2,1)S(1)}, u32[]{:S(2)}, u32[]{:S(2)}) collective-permute-start(bf16[336,256]{1,0:T(8,128)(2,1)} %get-tuple-element.99), channel_id=1, source_target_pairs={{0,1},{1,0},{2,3},{3,2},{4,5},{5,4},{6,7},{7,6},{8,9},{9,8},{10,11... | collective-permute-start | bytes 516104 | tf_op jit(solution)/shard_map/c1/ppermute | solution.py:23
  137.7 0.0 collective-permute-done.27.refs_11_
  137.7 4.4 %collective-permute-start.14 = (bf16[336,256]{1,0:T(8,128)(2,1)}, bf16[336,256]{1,0:T(8,128)(2,1)S(1)}, u32[]{:S(2)}, u32[]{:S(2)}) collective-permute-start(bf16[336,256]{1,0:T(8,128)(2,1)} %get-tuple-element.100), channel_id=1, source_target_pairs={{0,2},{1,3},{2,0},{3,1},{4,6},{5,7},{6,4},{7,5},{8,10},{9,11},{10,... | collective-permute-start | bytes 516104 | tf_op jit(solution)/shard_map/c2/ppermute | solution.py:23
  142.2 0.0 collective-permute-done.26.refs_3_
  142.2 0.2 collective-permute-start.15
  142.4 0.0 collective-permute-done.25.refs_6_
  142.4 4.0 %collective-permute-start.19 = (bf16[336,256]{1,0:T(8,128)(2,1)}, bf16[336,256]{1,0:T(8,128)(2,1)S(1)}, u32[]{:S(2)}, u32[]{:S(2)}) collective-permute-start(bf16[336,256]{1,0:T(8,128)(2,1)} %get-tuple-element.109), channel_id=1, source_target_pairs={{0,4},{1,5},{2,6},{3,7},{4,0},{5,1},{6,2},{7,3},{8,12},{9,13},{10,... | collective-permute-start | bytes 516104 | tf_op jit(solution)/shard_map/c4/ppermute | solution.py:23
  146.4 4.7 %norm_a.1 = (bf16[4,8,4,80,256]{4,3,2,1,0:T(8,128)(2,1)}, f32[8,256]{1,0:T(8,128)}) custom-call(bf16[512,256]{1,0:T(8,128)(2,1)S(1)} %copy-done, bf16[512,256]{1,0:T(8,128)(2,1)S(1)} %collective-permute-done.11.refs_1_, bf16[512,256]{1,0:T(8,128)(2,1)S(1)} %collective-permute-done.12.refs_2_, bf16[512,256]{1,0:T(8,128)(2,1)S(1)} %collective-permute-done.26.refs_3_, ...), custom_call_target="tpu_custom_call" | custom-call | flops 10485760 | bytes 5242880 | tf_op jit(solution)/shard_map/norm_a/pallas_call | solution.py:338
  151.1 2.1 %norm_b.1 = (bf16[4,8,4,80,256]{4,3,2,1,0:T(8,128)(2,1)}, f32[8,256]{1,0:T(8,128)}) custom-call(bf16[512,256]{1,0:T(8,128)(2,1)S(1)} %copy-done, bf16[512,256]{1,0:T(8,128)(2,1)S(1)} %collective-permute-done.11.refs_1_, bf16[512,256]{1,0:T(8,128)(2,1)S(1)} %collective-permute-done.12.refs_2_, ...), custom_call_target="tpu_custom_call", output_to_operand_aliasing={{0}: (10, {})} | custom-call | flops 5242880 | bytes 2621440 | tf_op jit(solution)/shard_map/norm_b/pallas_call | solution.py:338
  153.2 0.0 collective-permute-done.22.refs_5_
  153.2 0.0 collective-permute-done.13.refs_1_
  153.2 0.4 collective-permute-done.14.refs_2_
  153.7 4.6 %collective-permute-done.15.refs_3_ = bf16[336,256]{1,0:T(8,128)(2,1)S(1)} collective-permute-done((bf16[336,256]{1,0:T(8,128)(2,1)}, bf16[336,256]{1,0:T(8,128)(2,1)S(1)}, u32[]{:S(2)}, u32[]{:S(2)}) %collective-permute-start.15) | collective-permute-done | bytes 172064 | tf_op jit(solution)/shard_map/c3/ppermute | solution.py:23
  158.3 2.2 %norm_c.1 = (bf16[4,8,4,80,256]{4,3,2,1,0:T(8,128)(2,1)}, f32[8,256]{1,0:T(8,128)}) custom-call(bf16[336,256]{1,0:T(8,128)(2,1)S(1)} %copy-done.4, bf16[336,256]{1,0:T(8,128)(2,1)S(1)} %collective-permute-done.13.refs_1_, bf16[336,256]{1,0:T(8,128)(2,1)S(1)} %collective-permute-done.14.refs_2_, ...), custom_call_target="tpu_custom_call", output_to_operand_aliasing={{0}: (10, {})} | custom-call | flops 5242880 | bytes 2621440 | tf_op jit(solution)/shard_map/norm_c/pallas_call | solution.py:338
  (35 shorter events, 0.1 us)
Async XLA Ops:
  1.4 22.9 %collective-permute-start = (bf16[4,1,1280,128]{3,2,1,0:T(8,128)(2,1)S(1)}, bf16[4,1,1280,128]{3,2,1,0:T(8,128)(2,1)S(1)}, u32[]{:S(2)}, u32[]{:S(2)}) collective-permute-start(bf16[4,1,1280,128]{3,2,1,0:T(8,128)(2,1)S(1)} %slice.3), channel_id=1, source_target_pairs={{0,1},{1,2},{2,3},{3,4},{4,5},{5,6},{6,7},{8,9},{9,10},{10,11},{11... | collective-permute-start | bytes 3932168 | tf_op jit(solution)/shard_map/halo/ppermute | solution.py:18
  18.4 19.1 %collective-permute-start.1 = (bf16[480,256]{1,0:T(8,128)(2,1)}, bf16[480,256]{1,0:T(8,128)(2,1)S(1)}, u32[]{:S(2)}, u32[]{:S(2)}) collective-permute-start(bf16[480,256]{1,0:T(8,128)(2,1)} %get-tuple-element.70), channel_id=1, source_target_pairs={{0,1},{1,0},{2,3},{3,2},{4,5},{5,4},{6,7},{7,6},{8,9},{9,8},{10,11... | collective-permute-start | bytes 737288 | tf_op jit(solution)/shard_map/a1/ppermute | solution.py:23
  20.3 29.2 %collective-permute-start.4 = (bf16[480,256]{1,0:T(8,128)(2,1)}, bf16[480,256]{1,0:T(8,128)(2,1)S(1)}, u32[]{:S(2)}, u32[]{:S(2)}) collective-permute-start(bf16[480,256]{1,0:T(8,128)(2,1)} %get-tuple-element.79), channel_id=1, source_target_pairs={{0,7},{1,6},{2,5},{3,4},{4,3},{5,2},{6,1},{7,0},{8,15},{9,14},{10,... | collective-permute-start | bytes 737288 | tf_op jit(solution)/shard_map/a7/ppermute | solution.py:23
  22.3 41.6 %collective-permute-start.5 = (bf16[480,256]{1,0:T(8,128)(2,1)}, bf16[480,256]{1,0:T(8,128)(2,1)}, u32[]{:S(2)}, u32[]{:S(2)}) collective-permute-start(bf16[480,256]{1,0:T(8,128)(2,1)} %get-tuple-element.80), channel_id=1, source_target_pairs={{0,6},{1,7},{2,4},{3,5},{4,2},{5,3},{6,0},{7,1},{8,14},{9,15},{10,... | collective-permute-start | bytes 737288 | tf_op jit(solution)/shard_map/a6/ppermute | solution.py:23
  23.8 40.2 %collective-permute-start.6 = (bf16[480,256]{1,0:T(8,128)(2,1)}, bf16[480,256]{1,0:T(8,128)(2,1)}, u32[]{:S(2)}, u32[]{:S(2)}) collective-permute-start(bf16[480,256]{1,0:T(8,128)(2,1)} %get-tuple-element.81), channel_id=1, source_target_pairs={{0,5},{1,4},{2,7},{3,6},{4,1},{5,0},{6,3},{7,2},{8,13},{9,12},{10,... | collective-permute-start | bytes 737288 | tf_op jit(solution)/shard_map/a5/ppermute | solution.py:23
  24.3 1.1 copy-start.7
  25.5 12.1 %copy-start.11 = (bf16[480,256]{1,0:T(8,128)(2,1)S(1)}, bf16[480,256]{1,0:T(8,128)(2,1)}, u32[]{:S(2)}) copy-start(bf16[480,256]{1,0:T(8,128)(2,1)} %get-tuple-element.75) | copy-start | bytes 737284
  34.1 34.1 %collective-permute-start.3 = (bf16[1,4,640,256]{3,2,1,0:T(8,128)(2,1)}, bf16[1,4,640,256]{3,2,1,0:T(8,128)(2,1)}, u32[]{:S(2)}, u32[]{:S(2)}) collective-permute-start(bf16[1,4,640,256]{3,2,1,0:T(8,128)(2,1)} %conv_hist0.1), channel_id=1, source_target_pairs={{0,8},{8,16},{16,24},{1,9},{9,17},{17,25},{2,10},{10,18},{18,26},{... | collective-permute-start | bytes 3932168 | tf_op jit(solution)/shard_map/hist0/ppermute | solution.py:18
  37.5 11.9 %copy-start.2 = (bf16[480,256]{1,0:T(8,128)(2,1)}, bf16[480,256]{1,0:T(8,128)(2,1)S(1)}, u32[]{:S(2)}) copy-start(bf16[480,256]{1,0:T(8,128)(2,1)S(1)} %collective-permute-done.1.refs_9_) | copy-start | bytes 737284
  37.5 11.9 %copy-start.10 = (bf16[480,256]{1,0:T(8,128)(2,1)S(1)}, bf16[480,256]{1,0:T(8,128)(2,1)}, u32[]{:S(2)}) copy-start(bf16[480,256]{1,0:T(8,128)(2,1)} %get-tuple-element.83) | copy-start | bytes 737284
  37.6 12.6 %collective-permute-start.2 = (bf16[480,256]{1,0:T(8,128)(2,1)S(1)}, bf16[480,256]{1,0:T(8,128)(2,1)S(1)}, u32[]{:S(2)}, u32[]{:S(2)}) collective-permute-start(bf16[480,256]{1,0:T(8,128)(2,1)S(1)} %copy-done.11), channel_id=1, source_target_pairs={{0,2},{1,3},{2,0},{3,1},{4,6},{5,7},{6,4},{7,5},{8,10},{9,11},{10,... | collective-permute-start | bytes 737288 | tf_op jit(solution)/shard_map/a2/ppermute | solution.py:23
  49.5 17.1 %collective-permute-start.7 = (bf16[480,256]{1,0:T(8,128)(2,1)S(1)}, bf16[480,256]{1,0:T(8,128)(2,1)S(1)}, u32[]{:S(2)}, u32[]{:S(2)}) collective-permute-start(bf16[480,256]{1,0:T(8,128)(2,1)S(1)} %copy-done.10), channel_id=1, source_target_pairs={{0,4},{1,5},{2,6},{3,7},{4,0},{5,1},{6,2},{7,3},{8,12},{9,13},{10,... | collective-permute-start | bytes 737288 | tf_op jit(solution)/shard_map/a4/ppermute | solution.py:23
  57.4 13.5 %copy-start.15 = (bf16[176,256]{1,0:T(8,128)(2,1)S(1)}, bf16[176,256]{1,0:T(8,128)(2,1)}, u32[]{:S(2)}) copy-start(bf16[176,256]{1,0:T(8,128)(2,1)} %get-tuple-element.92) | copy-start | bytes 270340
  68.2 38.5 %collective-permute-start.8 = (bf16[1,4,640,256]{3,2,1,0:T(8,128)(2,1)}, bf16[1,4,640,256]{3,2,1,0:T(8,128)(2,1)S(1)}, u32[]{:S(2)}, u32[]{:S(2)}) collective-permute-start(bf16[1,4,640,256]{3,2,1,0:T(8,128)(2,1)} %conv_hist1.1), channel_id=1, source_target_pairs={{0,8},{8,16},{16,24},{1,9},{9,17},{17,25},{2,10},{10,18},{18,26},{... | collective-permute-start | bytes 3932168 | tf_op jit(solution)/shard_map/hist1/ppermute | solution.py:18
  70.9 6.3 %collective-permute-start.9 = (bf16[176,256]{1,0:T(8,128)(2,1)S(1)}, bf16[176,256]{1,0:T(8,128)(2,1)S(1)}, u32[]{:S(2)}, u32[]{:S(2)}) collective-permute-start(bf16[176,256]{1,0:T(8,128)(2,1)S(1)} %copy-done.15), channel_id=1, source_target_pairs={{0,7},{1,6},{2,5},{3,4},{4,3},{5,2},{6,1},{7,0},{8,15},{9,14},{10,... | collective-permute-start | bytes 270344 | tf_op jit(solution)/shard_map/t7/ppermute | solution.py:23
  71.9 7.9 %copy-start.14 = (bf16[176,256]{1,0:T(8,128)(2,1)S(1)}, bf16[176,256]{1,0:T(8,128)(2,1)}, u32[]{:S(2)}) copy-start(bf16[176,256]{1,0:T(8,128)(2,1)} %get-tuple-element.106) | copy-start | bytes 270340
  71.9 20.3 %copy-start.13 = (bf16[176,256]{1,0:T(8,128)(2,1)S(1)}, bf16[176,256]{1,0:T(8,128)(2,1)}, u32[]{:S(2)}) copy-start(bf16[176,256]{1,0:T(8,128)(2,1)} %get-tuple-element.119) | copy-start | bytes 270340
  71.9 20.6 %copy-start.12 = (bf16[176,256]{1,0:T(8,128)(2,1)S(1)}, bf16[176,256]{1,0:T(8,128)(2,1)}, u32[]{:S(2)}) copy-start(bf16[176,256]{1,0:T(8,128)(2,1)} %get-tuple-element.113) | copy-start | bytes 270340
  71.9 33.2 %copy-start.9 = (bf16[480,256]{1,0:T(8,128)(2,1)S(1)}, bf16[480,256]{1,0:T(8,128)(2,1)}, u32[]{:S(2)}) copy-start(bf16[480,256]{1,0:T(8,128)(2,1)} %get-tuple-element.127) | copy-start | bytes 737284
  77.3 7.7 %collective-permute-start.10 = (bf16[336,256]{1,0:T(8,128)(2,1)}, bf16[336,256]{1,0:T(8,128)(2,1)S(1)}, u32[]{:S(2)}, u32[]{:S(2)}) collective-permute-start(bf16[336,256]{1,0:T(8,128)(2,1)} %get-tuple-element.93), channel_id=1, source_target_pairs={{0,7},{1,6},{2,5},{3,4},{4,3},{5,2},{6,1},{7,0},{8,15},{9,14},{10,... | collective-permute-start | bytes 516104 | tf_op jit(solution)/shard_map/b7/ppermute | solution.py:23
  79.8 12.8 %collective-permute-start.16 = (bf16[176,256]{1,0:T(8,128)(2,1)S(1)}, bf16[176,256]{1,0:T(8,128)(2,1)S(1)}, u32[]{:S(2)}, u32[]{:S(2)}) collective-permute-start(bf16[176,256]{1,0:T(8,128)(2,1)S(1)} %copy-done.14), channel_id=1, source_target_pairs={{0,6},{1,7},{2,4},{3,5},{4,2},{5,3},{6,0},{7,1},{8,14},{9,15},{10,... | collective-permute-start | bytes 270344 | tf_op jit(solution)/shard_map/t6/ppermute | solution.py:23
  85.0 20.0 %collective-permute-start.11 = (bf16[512,256]{1,0:T(8,128)(2,1)}, bf16[512,256]{1,0:T(8,128)(2,1)S(1)}, u32[]{:S(2)}, u32[]{:S(2)}) collective-permute-start(bf16[512,256]{1,0:T(8,128)(2,1)} %get-tuple-element.94), channel_id=1, source_target_pairs={{0,1},{1,0},{2,3},{3,2},{4,5},{5,4},{6,7},{7,6},{8,9},{9,8},{10,11... | collective-permute-start | bytes 786440 | tf_op jit(solution)/shard_map/tb1/ppermute | solution.py:23
  86.8 18.3 %collective-permute-start.12 = (bf16[512,256]{1,0:T(8,128)(2,1)}, bf16[512,256]{1,0:T(8,128)(2,1)S(1)}, u32[]{:S(2)}, u32[]{:S(2)}) collective-permute-start(bf16[512,256]{1,0:T(8,128)(2,1)} %get-tuple-element.96), channel_id=1, source_target_pairs={{0,2},{1,3},{2,0},{3,1},{4,6},{5,7},{6,4},{7,5},{8,10},{9,11},{10,... | collective-permute-start | bytes 786440 | tf_op jit(solution)/shard_map/tb2/ppermute | solution.py:23
  92.3 8.8 %collective-permute-start.23 = (bf16[176,256]{1,0:T(8,128)(2,1)S(1)}, bf16[176,256]{1,0:T(8,128)(2,1)S(1)}, u32[]{:S(2)}, u32[]{:S(2)}) collective-permute-start(bf16[176,256]{1,0:T(8,128)(2,1)S(1)} %copy-done.13), channel_id=1, source_target_pairs={{0,5},{1,4},{2,7},{3,6},{4,1},{5,0},{6,3},{7,2},{8,13},{9,12},{10,... | collective-permute-start | bytes 270344 | tf_op jit(solution)/shard_map/t5/ppermute | solution.py:23
  92.6 10.6 %collective-permute-start.20 = (bf16[176,256]{1,0:T(8,128)(2,1)S(1)}, bf16[176,256]{1,0:T(8,128)(2,1)S(1)}, u32[]{:S(2)}, u32[]{:S(2)}) collective-permute-start(bf16[176,256]{1,0:T(8,128)(2,1)S(1)} %copy-done.12), channel_id=1, source_target_pairs={{0,4},{1,5},{2,6},{3,7},{4,0},{5,1},{6,2},{7,3},{8,12},{9,13},{10,... | collective-permute-start | bytes 270344 | tf_op jit(solution)/shard_map/t4/ppermute | solution.py:23
  101.0 12.2 %collective-permute-start.17 = (bf16[336,256]{1,0:T(8,128)(2,1)}, bf16[336,256]{1,0:T(8,128)(2,1)S(1)}, u32[]{:S(2)}, u32[]{:S(2)}) collective-permute-start(bf16[336,256]{1,0:T(8,128)(2,1)} %get-tuple-element.107), channel_id=1, source_target_pairs={{0,6},{1,7},{2,4},{3,5},{4,2},{5,3},{6,0},{7,1},{8,14},{9,15},{10,... | collective-permute-start | bytes 516104 | tf_op jit(solution)/shard_map/b6/ppermute | solution.py:23
  103.2 16.4 %collective-permute-start.24 = (bf16[336,256]{1,0:T(8,128)(2,1)}, bf16[336,256]{1,0:T(8,128)(2,1)S(1)}, u32[]{:S(2)}, u32[]{:S(2)}) collective-permute-start(bf16[336,256]{1,0:T(8,128)(2,1)} %get-tuple-element.120), channel_id=1, source_target_pairs={{0,5},{1,4},{2,7},{3,6},{4,1},{5,0},{6,3},{7,2},{8,13},{9,12},{10,... | collective-permute-start | bytes 516104 | tf_op jit(solution)/shard_map/b5/ppermute | solution.py:23
  104.9 37.2 %collective-permute-start.26 = (bf16[512,256]{1,0:T(8,128)(2,1)}, bf16[512,256]{1,0:T(8,128)(2,1)S(1)}, u32[]{:S(2)}, u32[]{:S(2)}) collective-permute-start(bf16[512,256]{1,0:T(8,128)(2,1)} %get-tuple-element.124), channel_id=1, source_target_pairs={{0,3},{1,2},{2,1},{3,0},{4,7},{5,6},{6,5},{7,4},{8,11},{9,10},{10,... | collective-permute-start | bytes 786440 | tf_op jit(solution)/shard_map/tb3/ppermute | solution.py:23
  105.2 32.6 %collective-permute-start.27 = (bf16[480,256]{1,0:T(8,128)(2,1)S(1)}, bf16[480,256]{1,0:T(8,128)(2,1)S(1)}, u32[]{:S(2)}, u32[]{:S(2)}) collective-permute-start(bf16[480,256]{1,0:T(8,128)(2,1)S(1)} %copy-done.9), channel_id=1, source_target_pairs={{0,3},{1,2},{2,1},{3,0},{4,7},{5,6},{6,5},{7,4},{8,11},{9,10},{10,... | collective-permute-start | bytes 737288 | tf_op jit(solution)/shard_map/a3/ppermute | solution.py:23
  106.7 39.7 %copy-start = (bf16[512,256]{1,0:T(8,128)(2,1)S(1)}, bf16[512,256]{1,0:T(8,128)(2,1)}, u32[]{:S(2)}) copy-start(bf16[512,256]{1,0:T(8,128)(2,1)} %get-tuple-element.122.refs_0_) | copy-start | bytes 786436
  106.7 39.7 %copy-start.1 = (bf16[480,256]{1,0:T(8,128)(2,1)S(1)}, bf16[480,256]{1,0:T(8,128)(2,1)}, u32[]{:S(2)}) copy-start(bf16[480,256]{1,0:T(8,128)(2,1)} %get-tuple-element.125.refs_8_) | copy-start | bytes 737284
  106.7 39.7 %copy-start.3 = (bf16[480,256]{1,0:T(8,128)(2,1)S(1)}, bf16[480,256]{1,0:T(8,128)(2,1)}, u32[]{:S(2)}) copy-start(bf16[480,256]{1,0:T(8,128)(2,1)} %copy-done.2) | copy-start | bytes 737284
  106.7 39.7 %copy-start.5 = (f32[256]{0:T(256)S(1)}, f32[256]{0:T(256)}, u32[]{:S(2)}) copy-start(f32[256]{0:T(256)} %param.8) | copy-start | bytes 3076
  106.7 39.7 %copy-start.6 = (f32[256]{0:T(256)S(1)}, f32[256]{0:T(256)}, u32[]{:S(2)}) copy-start(f32[256]{0:T(256)} %param.9) | copy-start | bytes 3076
  106.7 1.5 copy-start.8
  106.7 17.1 %collective-permute-start.21 = (bf16[336,256]{1,0:T(8,128)(2,1)}, bf16[336,256]{1,0:T(8,128)(2,1)S(1)}, u32[]{:S(2)}, u32[]{:S(2)}) collective-permute-start(bf16[336,256]{1,0:T(8,128)(2,1)} %get-tuple-element.114), channel_id=1, source_target_pairs={{0,4},{1,5},{2,6},{3,7},{4,0},{5,1},{6,2},{7,3},{8,12},{9,13},{10,... | collective-permute-start | bytes 516104 | tf_op jit(solution)/shard_map/b4/ppermute | solution.py:23
  113.3 17.5 %collective-permute-start.18 = (bf16[336,256]{1,0:T(8,128)(2,1)}, bf16[336,256]{1,0:T(8,128)(2,1)S(1)}, u32[]{:S(2)}, u32[]{:S(2)}) collective-permute-start(bf16[336,256]{1,0:T(8,128)(2,1)} %get-tuple-element.108), channel_id=1, source_target_pairs={{0,7},{1,6},{2,5},{3,4},{4,3},{5,2},{6,1},{7,0},{8,15},{9,14},{10,... | collective-permute-start | bytes 516104 | tf_op jit(solution)/shard_map/c7/ppermute | solution.py:23
  119.5 22.8 %collective-permute-start.25 = (bf16[336,256]{1,0:T(8,128)(2,1)}, bf16[336,256]{1,0:T(8,128)(2,1)S(1)}, u32[]{:S(2)}, u32[]{:S(2)}) collective-permute-start(bf16[336,256]{1,0:T(8,128)(2,1)} %get-tuple-element.121), channel_id=1, source_target_pairs={{0,6},{1,7},{2,4},{3,5},{4,2},{5,3},{6,0},{7,1},{8,14},{9,15},{10,... | collective-permute-start | bytes 516104 | tf_op jit(solution)/shard_map/c6/ppermute | solution.py:23
  123.9 29.4 %collective-permute-start.22 = (bf16[336,256]{1,0:T(8,128)(2,1)}, bf16[336,256]{1,0:T(8,128)(2,1)S(1)}, u32[]{:S(2)}, u32[]{:S(2)}) collective-permute-start(bf16[336,256]{1,0:T(8,128)(2,1)} %get-tuple-element.115), channel_id=1, source_target_pairs={{0,5},{1,4},{2,7},{3,6},{4,1},{5,0},{6,3},{7,2},{8,13},{9,12},{10,... | collective-permute-start | bytes 516104 | tf_op jit(solution)/shard_map/c5/ppermute | solution.py:23
  130.8 22.4 %collective-permute-start.13 = (bf16[336,256]{1,0:T(8,128)(2,1)}, bf16[336,256]{1,0:T(8,128)(2,1)S(1)}, u32[]{:S(2)}, u32[]{:S(2)}) collective-permute-start(bf16[336,256]{1,0:T(8,128)(2,1)} %get-tuple-element.99), channel_id=1, source_target_pairs={{0,1},{1,0},{2,3},{3,2},{4,5},{5,4},{6,7},{7,6},{8,9},{9,8},{10,11... | collective-permute-start | bytes 516104 | tf_op jit(solution)/shard_map/c1/ppermute | solution.py:23
  137.7 15.9 %collective-permute-start.14 = (bf16[336,256]{1,0:T(8,128)(2,1)}, bf16[336,256]{1,0:T(8,128)(2,1)S(1)}, u32[]{:S(2)}, u32[]{:S(2)}) collective-permute-start(bf16[336,256]{1,0:T(8,128)(2,1)} %get-tuple-element.100), channel_id=1, source_target_pairs={{0,2},{1,3},{2,0},{3,1},{4,6},{5,7},{6,4},{7,5},{8,10},{9,11},{10,... | collective-permute-start | bytes 516104 | tf_op jit(solution)/shard_map/c2/ppermute | solution.py:23
  142.2 16.1 %collective-permute-start.15 = (bf16[336,256]{1,0:T(8,128)(2,1)}, bf16[336,256]{1,0:T(8,128)(2,1)S(1)}, u32[]{:S(2)}, u32[]{:S(2)}) collective-permute-start(bf16[336,256]{1,0:T(8,128)(2,1)} %get-tuple-element.101), channel_id=1, source_target_pairs={{0,3},{1,2},{2,1},{3,0},{4,7},{5,6},{6,5},{7,4},{8,11},{9,10},{10,... | collective-permute-start | bytes 516104 | tf_op jit(solution)/shard_map/c3/ppermute | solution.py:23
  142.4 15.9 %collective-permute-start.19 = (bf16[336,256]{1,0:T(8,128)(2,1)}, bf16[336,256]{1,0:T(8,128)(2,1)S(1)}, u32[]{:S(2)}, u32[]{:S(2)}) collective-permute-start(bf16[336,256]{1,0:T(8,128)(2,1)} %get-tuple-element.109), channel_id=1, source_target_pairs={{0,4},{1,5},{2,6},{3,7},{4,0},{5,1},{6,2},{7,3},{8,12},{9,13},{10,... | collective-permute-start | bytes 516104 | tf_op jit(solution)/shard_map/c4/ppermute | solution.py:23
  151.1 7.2 %copy-start.4 = (bf16[336,256]{1,0:T(8,128)(2,1)S(1)}, bf16[336,256]{1,0:T(8,128)(2,1)}, u32[]{:S(2)}) copy-start(bf16[336,256]{1,0:T(8,128)(2,1)} %get-tuple-element.98.refs_0_) | copy-start | bytes 516100
